TPU v7x, 32 devices: a whole 2x2x4 slice. The times are simulated.
32 devices in a mesh: ctx: 8 (over y, x, core), ch: 4 (over z).
Axes of the slice: x: 2, y: 2, z: 4, core: 2. Of those that a mesh axis runs over, the one named last changes fastest.
Arguments:
- signal: bfloat16 [2048, 2048], P('ctx', 'ch'), may hold values from -8 to 8
- cotangent: bfloat16 [2048, 2048], P('ctx', 'ch'), may hold values from -8 to 8
- residue: float32 [16, 512], replicated, may hold values from -0.125 to 0.125
- decay: float32 [16, 512], replicated, may hold values from 0.00048828125 to 0.2
Outputs:
- conv_out: bfloat16 [2048, 2048], P('ctx', 'ch')
- signal_grad: bfloat16 [2048, 2048], P('ctx', 'ch')
- residue_grad: float32 [16, 512], replicated
All inputs are finite; a program needn't handle non-finite values.
Results may differ from a plain program's by a relative error of at most 0.0013.
Values sent between devices are 32-bit elements; how exact they have to be, the bound alone decides.
No kernel may reach another device: no remote copies, remote signals or barrier semaphores. Data moves between devices by JAX's collectives and lax.ppermute only.
A program may use at most 64 MiB of HBM per device.

v0:
```python
import jax
import jax.numpy as jnp
from jax import lax
from jax.sharding import PartitionSpec as P


def carried_in(x, axis, combine, identity, reverse):
    devices, place = (lax.axis_size(axis), lax.axis_index(axis))
    everything = jax.tree.map(lambda part: lax.all_gather(part, axis), x)
    start = jax.tree.map(
        lambda part, zero: jnp.broadcast_to(jnp.asarray(zero, part.dtype), part.shape), x, identity
    )

    def step(k, before):
        at = devices - 1 - k if reverse else k
        reached = at > place if reverse else at < place
        new = combine(before, jax.tree.map(lambda part: part[at], everything))
        return jax.tree.map(lambda a, b: jnp.where(reached, a, b), new, before)

    return lax.fori_loop(0, devices, step, start)


def combine_pairs(earlier, latter):
    return (earlier[0] * latter[0], earlier[1] * latter[0] + latter[1])


def local_block(signal, cotangent, residue, decay):
    values = signal.astype(jnp.float32)
    cotans = cotangent.astype(jnp.float32)

    def local_per_mode(totals, mode_params):
        residue_row, decay_row = mode_params
        step_decay = jnp.broadcast_to(jnp.exp(-decay_row), values.shape)
        forward_sum = lax.associative_scan(combine_pairs, (step_decay, values), axis=0)[1]
        backward_sum = lax.associative_scan(
            combine_pairs, (step_decay, cotans), axis=0, reverse=True
        )[1]
        out_acc, grad_acc = totals
        totals = (out_acc + residue_row * forward_sum, grad_acc + residue_row * backward_sum)
        return (totals, (forward_sum[-1], backward_sum[0], jnp.sum(cotans * forward_sum, axis=0)))

    empty_acc = jnp.zeros(values.shape, jnp.float32)
    (out_acc, grad_acc), (closing, opening, local_grad) = lax.scan(
        local_per_mode, (empty_acc, empty_acc), (residue, decay)
    )
    return (out_acc, grad_acc, closing, opening, local_grad)


def finish(out_acc, grad_acc, residue, decay, incoming, outgoing):
    block_len = out_acc.shape[0]
    offsets = jnp.arange(block_len, dtype=jnp.float32)[:, None]

    def finish_per_mode(totals, mode_params):
        residue_row, decay_row, arriving, leaving = mode_params
        first, second = totals
        first = first + residue_row * jnp.exp(-decay_row * (offsets + 1.0)) * arriving
        second = second + residue_row * jnp.exp(-decay_row * (block_len - offsets)) * leaving
        return ((first, second), None)

    (first, second), _ = lax.scan(
        finish_per_mode, (out_acc, grad_acc), (residue, decay, incoming, outgoing)
    )
    return (first.astype(jnp.bfloat16), second.astype(jnp.bfloat16))


def body(signal, cotangent, residue, decay):
    out_acc, grad_acc, closing, opening, local_grad = local_block(signal, cotangent, residue, decay)
    block_len = signal.shape[0]
    block_decay = jnp.exp(-decay * block_len)
    identity = (jnp.ones_like(block_decay), jnp.zeros_like(closing))
    _, incoming = carried_in((block_decay, closing), "ctx", combine_pairs, identity, False)
    _, outgoing = carried_in((block_decay, opening), "ctx", combine_pairs, identity, True)
    cross_part = jnp.exp(-decay) * opening * incoming
    summed = lax.psum(local_grad + cross_part, ("ctx", "ch"))
    residue_grad = summed / (block_len * lax.axis_size("ctx"))
    conv_out, signal_grad = finish(out_acc, grad_acc, residue, decay, incoming, outgoing)
    return (conv_out, signal_grad, residue_grad)


def solution(mesh):
    return jax.shard_map(
        body,
        mesh=mesh,
        in_specs=(P("ctx", "ch"), P("ctx", "ch"), P(), P()),
        out_specs=(P("ctx", "ch"), P("ctx", "ch"), P()),
        check_vma=False,
    )
```

profile of v0, /device:TPU:0, one launch (start us, length us, event | category | flops | bytes accessed | tf_op | source)
XLA Modules:
  0.0 294.1 jit_solution(2834179033882696012)
XLA Ops:
  0.6 1.8 convert_element_type.12
  3.2 200.1 %while.64 = (s32[]{:T(128)}, f32[256,512]{1,0:T(8,128)S(1)}, f32[256,512]{1,0:T(8,128)S(1)}, f32[16,512]{1,0:T(8,128)S(1)}, f32[16,512]{1,0:T(8,128)S(1)}, /*ind...) while((s32[]{:T(128)}, f32[256,512]{1,0:T(8,128)S(1)}, ...), condition=%wide.region_2.3_spmd.clone, body=%wide.region_0.2_spmd.clone.sunk | while | flops 3252227 | bytes 40309024 | solution.py:43
  9.1 0.7 copy-done
  12.3 1.9 slice.780
  21.6 0.7 copy-done
  24.8 1.9 slice.780
  34.1 0.7 copy-done
  37.3 1.9 slice.780
  49.8 1.9 slice.780
  62.3 1.9 slice.780
  71.7 0.7 copy-done
  74.8 1.9 slice.780
  84.2 0.7 copy-done
  87.3 1.9 slice.780
  96.7 0.7 copy-done
  99.8 1.9 slice.780
  109.2 0.7 copy-done
  112.3 1.9 slice.780
  124.8 1.9 slice.780
  137.3 1.9 slice.780
  146.7 0.7 copy-done
  149.8 1.9 slice.780
  159.2 0.7 copy-done
  162.3 1.9 slice.780
  174.8 1.9 slice.780
  187.3 1.9 slice.780
  199.8 1.9 slice.780
  203.3 10.8 %all-gather.1 = f32[128,512]{1,0:T(8,128)S(1)} all-gather(f32[16,512]{1,0:T(8,128)S(1)} %get-tuple-element.333), channel_id=3, replica_groups=mesh['ctx'=8,'ch'=4] {'ctx'}, dimensions={0}, use_global_device_ids=true | all-gather | bytes 294912 | tf_op jit(solution)/shard_map/all_gather | solution.py:9
  214.1 9.3 %all-gather = f32[128,512]{1,0:T(8,128)S(1)} all-gather(f32[16,512]{1,0:T(8,128)S(1)} %multiply_exponential_fusion), channel_id=2, replica_groups=mesh['ctx'=8,'ch'=4] {'ctx'}, dimensions={0}, use_global_device_ids=true | all-gather | bytes 294912 | tf_op jit(solution)/shard_map/all_gather | solution.py:9
  223.7 39.8 %psum.7 = f32[16,512]{1,0:T(8,128)S(1)} all-reduce(f32[16,512]{1,0:T(8,128)S(1)} %multiply_add_fusion.16), channel_id=1, replica_groups=mesh['ctx'=8,'ch'=4] {'ctx','ch'}, use_global_device_ids=true, to_apply=%region_9.10 | all-reduce | flops 8192 | bytes 65536 | tf_op jit(solution)/shard_map/psum | solution.py:74
  264.1 10.1 %all-gather.2 = f32[128,512]{1,0:T(8,128)S(1)} all-gather(f32[16,512]{1,0:T(8,128)S(1)} %get-tuple-element.335), channel_id=4, replica_groups=mesh['ctx'=8,'ch'=4] {'ctx'}, dimensions={0}, use_global_device_ids=true | all-gather | bytes 294912 | tf_op jit(solution)/shard_map/all_gather | solution.py:9
  274.6 18.1 %while.63 = (s32[]{:T(128)}, f32[256,512]{1,0:T(8,128)S(1)}, f32[256,512]{1,0:T(8,128)S(1)}, f32[16,512]{1,0:T(8,128)}, f32[16,512]{1,0:T(8,128)S(1)}, /*index=5...) while((s32[]{:T(128)}, f32[256,512]{1,0:T(8,128)S(1)}, ...), condition=%wide.region_8.9_spmd.clone.clone, body=%wide.region_7.8_spmd.clone.clone.sunk | while | flops 1049602 | bytes 2125917 | solution.py:60
  (2874 shorter events, 168.2 us)
Async XLA Ops:
  0.6 1.9 copy-start.1
  2.5 0.8 copy-start.2
  8.8 1.0 copy-start
  21.3 1.0 copy-start
  33.8 1.0 copy-start
  46.3 1.0 copy-start
  58.8 1.0 copy-start
  71.3 1.0 copy-start
  83.9 1.0 copy-start
  96.4 1.0 copy-start
  108.9 1.0 copy-start
  121.4 1.0 copy-start
  133.9 1.0 copy-start
  146.4 1.0 copy-start
  158.9 1.0 copy-start
  171.4 1.0 copy-start
  183.9 1.0 copy-start
  196.4 1.0 copy-start
where the time goes:
time: 299 us; the launch traced here: 294 us
  local copies, waits for them, and re-layouts  159 us (53%)
  blocking collectives  69.9 us (23%)
  other arithmetic  47.6 us (16%)
  loops' own time  16.5 us (6%)
    slice x448, local copies, waits for them, and re-layouts, local_per_mode(): lax.associative_scan(combine_pairs, (step_decay, values), axis=0)[1]  64.7 us
    slice x768, local copies, waits for them, and re-layouts, local_per_mode(): lax.associative_scan(combine_pairs, (step_decay, cotans), axis=0, reverse...  51.8 us
    psum x1, blocking collectives, body(): summed = lax.psum(local_grad + cross_part, ('ctx', 'ch'))  39.8 us
    all_gather x3, blocking collectives, carried_in(): everything = jax.tree.map(lambda part: lax.all_gather(part, axis), x)  30.1 us
    another operation x1, loops' own time, local_block(): lax.scan(local_per_mode, (empty_acc, empty_acc), (residue, decay))  15.5 us
    while x32, local copies, waits for them, and re-layouts  11.9 us
    exp x16, other arithmetic, local_per_mode(): step_decay = jnp.broadcast_to(jnp.exp(-decay_row), values.shape)  11.8 us
    dynamic_slice x16, local copies, waits for them, and re-layouts, local_block(): lax.scan(local_per_mode, (empty_acc, empty_acc), (residue, decay))  11.7 us

commit v1 on v0

v1 whole, which is shorter than its diff:
```python
import functools

import jax
import jax.numpy as jnp
from jax import lax
from jax.experimental import pallas as pl
from jax.experimental.pallas import tpu as pltpu
from jax.sharding import PartitionSpec as P

SUB = 8
LANES = 128
F32 = jnp.float32


def row(ref, *index):
    return jnp.broadcast_to(ref[index], (SUB, LANES))


def split_lanes(source, target, tile):
    lanes = pl.ds(pl.multiple_of(tile * LANES, LANES), LANES)
    target[...] = source[:, lanes].astype(F32)


def read_tokens(scratch, chunks):
    span = chunks * SUB
    return [[scratch[pl.ds(p * SUB + r, SUB, stride=span), :] for r in range(SUB)] for p in range(chunks)]


def powers(decay, pw):
    pw[0] = jnp.exp(-decay)
    pw[1] = jnp.exp(-decay * SUB)


def horner(terms, factor):
    total = terms[0]
    for term in terms[1:]:
        total = total * factor + term
    return total


def chunk_states(m, xs, gs, pw):
    a, a8 = row(pw, 0, pl.ds(m, 1)), row(pw, 1, pl.ds(m, 1))
    chunks = len(xs)
    held, back = [], [None] * chunks
    for p in range(chunks):
        own = horner(xs[p], a)
        held.append(own if p == 0 else held[-1] * a8 + own)
    opens = [horner(gs[p][::-1], a) for p in range(chunks)]
    for p in reversed(range(chunks)):
        back[p] = opens[p] if p == chunks - 1 else back[p + 1] * a8 + opens[p]
    return held, back, opens


def by_span(scratch, half, j):
    return scratch[pl.ds(half * SUB * SUB + j, SUB, stride=SUB), :]


def gather_kernel(direct, n, x_ref, g_ref, decay_ref, *refs):
    modes, channels = decay_ref.shape
    chunks = x_ref.shape[0] // (SUB * SUB)
    span = chunks * SUB
    if direct:
        place = lax.axis_index("ctx")
        share = modes // n
        *messages, own, xf, gf, pw, ends, starts, inner, closing, opening, grad, parts = refs
    else:
        closing, opening, grad, xf, gf, pw, ends, starts, inner = refs

    def tile_step(tile, _):
        lanes = pl.ds(pl.multiple_of(tile * LANES, LANES), LANES)
        split_lanes(x_ref, xf, tile)
        split_lanes(g_ref, gf, tile)
        decay = decay_ref[:, lanes]
        powers(decay, pw)
        xs, gs = read_tokens(xf, chunks), read_tokens(gf, chunks)
        for m in range(modes):
            held, back, opens = chunk_states(m, xs, gs, pw)
            rows = pl.ds(m * SUB, SUB)
            ends[rows, :] = held[-1]
            starts[rows, :] = back[0]
            inner[rows, :] = sum(opens[p] * held[p - 1] for p in range(1, chunks))
        lagged = []
        for lag in range(SUB):
            pairs = [gs[p][r] * xs[p][r - lag] for p in range(chunks) for r in range(lag, SUB)]
            lagged.append(jnp.sum(sum(pairs), axis=0, keepdims=True))
        for half in range(modes // SUB):
            some = pl.ds(half * SUB, SUB)
            a = pw[0, some, :]
            across = jnp.exp(-decay[half * SUB:(half + 1) * SUB] * span)
            arriving = jnp.zeros((SUB, LANES), F32)
            cross = jnp.zeros((SUB, LANES), F32)
            for j in range(SUB):
                cross = cross + (by_span(inner, half, j) + by_span(starts, half, j) * arriving)
                arriving = arriving * across + by_span(ends, half, j)
            leaving = horner([by_span(starts, half, j) for j in reversed(range(SUB))], across)
            near = horner([jnp.broadcast_to(v, (SUB, LANES)) for v in reversed(lagged)], a)
            closing[some, lanes] = arriving
            opening[some, lanes] = leaving
            grad[some, lanes] = near + a * cross
        return 0

    lax.fori_loop(0, channels // LANES, tile_step, 0)

    if direct:
        for owner in range(n):
            rows = slice(owner * share, (owner + 1) * share)
            parts[owner, 0:share] = closing[rows]
            parts[owner, share:2 * share] = opening[rows]
            parts[owner, 2 * share:3 * share] = grad[rows]
            parts[owner, 3 * share:4 * share] = decay_ref[rows]
        own[...] = parts[place]
        for k in range(1, n):
            message = messages[k - 1]
            message[0:modes] = jnp.where(place + k < n, closing[...], opening[...])
            message[modes:] = parts[lax.rem(place + k, n)]


def local_kernel(x_ref, g_ref, residue_ref, decay_ref, out_ref, back_ref,
                 xf, gf, pw, ends, starts, before, after, arrive, leave):
    modes, channels = decay_ref.shape
    chunks = x_ref.shape[0] // (SUB * SUB)
    span = chunks * SUB

    def tile_step(tile, _):
        lanes = pl.ds(pl.multiple_of(tile * LANES, LANES), LANES)
        split_lanes(x_ref, xf, tile)
        split_lanes(g_ref, gf, tile)
        decay = decay_ref[:, lanes]
        residue = residue_ref[:, lanes]
        powers(decay, pw)
        pw[2] = residue * pw[0]
        xs, gs = read_tokens(xf, chunks), read_tokens(gf, chunks)
        for m in range(modes):
            held, back, _ = chunk_states(m, xs, gs, pw)
            rows = pl.ds(m * SUB, SUB)
            ends[rows, :] = held[-1]
            starts[rows, :] = back[0]
            for p in range(1, chunks):
                before[m, p - 1] = held[p - 1]
                after[m, p - 1] = back[p]
        for half in range(modes // SUB):
            across = jnp.exp(-decay[half * SUB:(half + 1) * SUB] * span)
            for target, source, order in ((arrive, ends, range(SUB)), (leave, starts, range(SUB - 1, -1, -1))):
                running = jnp.zeros((SUB, LANES), F32)
                for j in order:
                    target[pl.ds(half * SUB * SUB + j, SUB, stride=SUB), :] = running
                    running = running * across + by_span(source, half, j)
        taps = []
        weight = residue
        for lag in range(SUB):
            taps.append(jnp.broadcast_to(jnp.sum(weight, axis=0, keepdims=True), (SUB, LANES)))
            weight = weight * pw[0]
        for values, carried, inside, target, forward in (
            (xs, arrive, before, out_ref, True), (gs, leave, after, back_ref, False)
        ):
            order = range(SUB) if forward else range(SUB - 1, -1, -1)
            totals = []
            for p in range(chunks):
                seq = [values[p][r] for r in order]
                totals.append([sum(taps[lag] * seq[r - lag] for lag in range(r + 1)) for r in range(SUB)])
            for m in range(modes):
                a, a8, first = (row(pw, i, pl.ds(m, 1)) for i in range(3))
                edge = carried[pl.ds(m * SUB, SUB), :]
                for q in range(chunks):
                    p = q if forward else chunks - 1 - q
                    if q == 0:
                        state = edge
                    else:
                        edge = edge * a8
                        state = edge + inside[m, p - 1 if forward else p]
                    wave = state * first
                    for r in range(SUB):
                        totals[p][r] = totals[p][r] + wave
                        if r < SUB - 1:
                            wave = wave * a
            for p in range(chunks):
                for r, at in enumerate(order):
                    target[p * SUB + at, :, lanes] = totals[p][r]
        return 0

    lax.fori_loop(0, channels // LANES, tile_step, 0)


def owner_kernel(n, scale, *refs):
    *messages, own, out_ref, held, back = refs
    place = lax.axis_index("ctx")
    share = own.shape[0] // 4
    decay = own[3 * share:]
    total = own[2 * share:3 * share]
    held[place] = own[0:share]
    back[place] = own[share:2 * share]
    for k in range(1, n):
        source = lax.rem(place - k + n, n)
        held[source] = messages[k - 1][0:share]
        back[source] = messages[k - 1][share:2 * share]
        total = total + messages[k - 1][2 * share:3 * share]
    a = jnp.exp(-decay)
    block = jnp.exp(-decay * scale[0])
    arriving = jnp.zeros_like(decay)
    cross = jnp.zeros_like(decay)
    for j in range(n):
        cross = cross + back[j] * arriving
        arriving = arriving * block + held[j]
    out_ref[...] = (total + a * cross) * (1.0 / (scale[0] * n))


def finish_kernel(direct, n, residue_ref, decay_ref, near_out, near_back, *refs):
    modes, channels = decay_ref.shape
    chunks = near_out.shape[0] // SUB
    span = chunks * SUB
    *sources, out_ref, back_ref, result, pw, arrive, leave = refs
    decay = decay_ref[...]
    if direct:
        place = lax.axis_index("ctx")
        block = jnp.exp(-decay * (span * SUB))
        incoming = jnp.zeros_like(decay)
        outgoing = jnp.zeros_like(decay)
        for k in range(n - 1, 0, -1):
            incoming = incoming * block + jnp.where(place >= k, sources[k - 1][...], 0.0)
        for k in range(1, n):
            outgoing = outgoing * block + jnp.where(place < k, sources[k - 1][...], 0.0)
    else:
        incoming, outgoing = sources[0][...], sources[1][...]
    first = residue_ref[...] * jnp.exp(-decay)
    arrive[...] = incoming * first
    leave[...] = outgoing * first

    def tile_step(tile, _):
        lanes = pl.ds(pl.multiple_of(tile * LANES, LANES), LANES)
        decay = decay_ref[:, lanes]
        powers(decay, pw)
        pw[2] = decay * (-1.0 * span)
        pw[3] = arrive[:, lanes]
        pw[4] = leave[:, lanes]
        level = lax.broadcasted_iota(jnp.int32, (SUB, LANES), 0).astype(F32)
        for near, target, forward in ((near_out, out_ref, True), (near_back, back_ref, False)):
            order = range(SUB) if forward else range(SUB - 1, -1, -1)
            spans = level if forward else SUB - 1.0 - level
            totals = [[near[p * SUB + r, :, lanes] for r in range(SUB)] for p in range(chunks)]
            for m in range(modes):
                a, a8, rate = (row(pw, i, pl.ds(m, 1)) for i in range(3))
                state = row(pw, 3 if forward else 4, pl.ds(m, 1)) * jnp.exp(rate * spans)
                for q in range(chunks):
                    p = q if forward else chunks - 1 - q
                    wave = state
                    for r in order:
                        totals[p][r] = totals[p][r] + wave
                        wave = wave * a
                    if q < chunks - 1:
                        state = state * a8
            for p in range(chunks):
                for r in range(SUB):
                    result[pl.ds(p * SUB + r, SUB, stride=span), :] = totals[p][r]
            target[:, lanes] = result[...].astype(target.dtype)
        return 0

    lax.fori_loop(0, channels // LANES, tile_step, 0)


def assemble_kernel(n, *refs):
    *pieces, out_ref, parts = refs
    place = lax.axis_index("ctx")
    share = pieces[0].shape[0]
    for k in range(n):
        parts[lax.rem(place - k + n, n)] = pieces[k][...]
    for j in range(n):
        out_ref[j * share:(j + 1) * share] = parts[j]


def vmem(*shape):
    return pltpu.VMEM(shape, F32)


def shaped(*shape):
    return jax.ShapeDtypeStruct(shape, F32)


def cost(flops, transcendentals, nbytes):
    return pl.CostEstimate(flops=flops, transcendentals=transcendentals, bytes_accessed=nbytes)


PARAMS = pltpu.CompilerParams(vmem_limit_bytes=32 * 1024 * 1024)
WHOLE = pl.BlockSpec(memory_space=pltpu.VMEM)


def carried_in(own, block_decay, reverse):
    devices, place = lax.axis_size("ctx"), lax.axis_index("ctx")
    everything = lax.all_gather(own, "ctx")

    def step(k, before):
        at = devices - 1 - k if reverse else k
        reached = at > place if reverse else at < place
        return jnp.where(reached, block_decay * before + everything[at], before)

    return lax.fori_loop(0, devices, step, jnp.zeros_like(own))


def body(signal, cotangent, residue, decay):
    tokens, channels = signal.shape
    modes = decay.shape[0]
    n, n_ch = lax.axis_size("ctx"), lax.axis_size("ch")
    chunks = tokens // (SUB * SUB)
    direct = n <= SUB and modes % n == 0
    elements = tokens * channels
    tokens_scratch = [vmem(tokens, LANES), vmem(tokens, LANES)]
    spans = vmem(modes * SUB, LANES)

    if direct:
        share = modes // n
        gathered = pl.pallas_call(
            functools.partial(gather_kernel, True, n),
            out_shape=[shaped(modes + 4 * share, channels)] * (n - 1) + [shaped(4 * share, channels)],
            scratch_shapes=tokens_scratch + [vmem(2, modes, LANES), spans, spans, spans]
            + [vmem(modes, channels)] * 3 + [vmem(n, 4 * share, channels)],
            compiler_params=PARAMS,
            cost_estimate=cost(elements * modes * 5, modes * channels * 3, elements * 6),
            name="block_states",
        )(signal, cotangent, decay)
        *messages, own = gathered
        arrived = [
            lax.ppermute(messages[k - 1], "ctx", [(i, (i + k) % n) for i in range(n)]) for k in range(1, n)
        ]
    else:
        closing, opening, local_grad = pl.pallas_call(
            functools.partial(gather_kernel, False, n),
            out_shape=[shaped(modes, channels)] * 3,
            scratch_shapes=tokens_scratch + [vmem(2, modes, LANES), spans, spans, spans],
            compiler_params=PARAMS,
            cost_estimate=cost(elements * modes * 5, modes * channels * 3, elements * 6),
            name="block_states",
        )(signal, cotangent, decay)

    near_out, near_back = pl.pallas_call(
        local_kernel,
        out_shape=[shaped(chunks * SUB, SUB, channels)] * 2,
        scratch_shapes=tokens_scratch + [vmem(3, modes, LANES), spans, spans]
        + [vmem(modes, chunks - 1, SUB, LANES)] * 2 + [spans, spans],
        compiler_params=PARAMS,
        cost_estimate=cost(elements * modes * 10, modes * channels * 3, elements * 12),
        name="local_convolutions",
    )(signal, cotangent, residue, decay)

    if direct:
        part = pl.pallas_call(
            functools.partial(owner_kernel, n, (float(tokens),)),
            out_shape=shaped(share, channels),
            grid=(1,),
            in_specs=[pl.BlockSpec((4 * share, channels), lambda i: (modes // (4 * share), 0))] * (n - 1) + [WHOLE],
            out_specs=WHOLE,
            scratch_shapes=[vmem(n, share, channels)] * 2,
            compiler_params=PARAMS,
            cost_estimate=cost(elements, modes * channels, modes * channels * 16),
            name="owned_modes",
        )(*arrived, own)
        over_groups = [part]
        for k in range(1, n_ch):
            over_groups.append(lax.ppermute(part, "ch", [(i, i ^ k) for i in range(n_ch)]))
        while len(over_groups) > 1:
            over_groups = [a + b for a, b in zip(over_groups[::2], over_groups[1::2])]
        whole = over_groups[0]
        pieces = [whole] + [
            lax.ppermute(whole, "ctx", [(i, (i + k) % n) for i in range(n)]) for k in range(1, n)
        ]
        residue_grad = pl.pallas_call(
            functools.partial(assemble_kernel, n),
            out_shape=shaped(modes, channels),
            scratch_shapes=[vmem(n, share, channels)],
            compiler_params=PARAMS,
            cost_estimate=cost(modes * channels, 0, modes * channels * 8),
            name="assemble_gradient",
        )(*pieces)
        sources = arrived
        source_specs = [pl.BlockSpec((modes, channels), lambda i: (0, 0))] * (n - 1)
    else:
        block_decay = jnp.exp(-decay * tokens)
        incoming = carried_in(closing, block_decay, False)
        outgoing = carried_in(opening, block_decay, True)
        summed = lax.psum(local_grad + jnp.exp(-decay) * opening * incoming, ("ctx", "ch"))
        residue_grad = summed / (tokens * n)
        sources = [incoming, outgoing]
        source_specs = [WHOLE] * 2

    conv_out, signal_grad = pl.pallas_call(
        functools.partial(finish_kernel, direct, n),
        out_shape=[jax.ShapeDtypeStruct((tokens, channels), signal.dtype)] * 2,
        grid=(1,),
        in_specs=[WHOLE] * 4 + source_specs,
        out_specs=[WHOLE] * 2,
        scratch_shapes=[vmem(tokens, LANES), vmem(5, modes, LANES)] + [vmem(modes, channels)] * 2,
        compiler_params=PARAMS,
        cost_estimate=cost(elements * modes * 4, modes * channels * 10, elements * 12),
        name="add_arrivals",
    )(residue, decay, near_out, near_back, *sources)
    return conv_out, signal_grad, residue_grad


def solution(mesh):
    return jax.shard_map(
        body,
        mesh=mesh,
        in_specs=(P("ctx", "ch"), P("ctx", "ch"), P(), P()),
        out_specs=(P("ctx", "ch"), P("ctx", "ch"), P()),
        check_vma=False,
    )
```

time: 299 us -> 40.1 us (0.13); the launches traced: 294 us -> 39.9 us
  local copies, waits for them, and re-layouts: 159 us -> 2.67 us
  blocking collectives: 69.9 us -> 0 us
  other arithmetic: 47.6 us -> 0.01 us
  starting transfers between devices: 0 us -> 21.3 us
  loops' own time: 16.5 us -> 0 us
  Pallas kernels: 0 us -> 9.57 us
  waiting for transfers between devices: 0 us -> 5.6 us
    slice x1216 -> x0, local copies, waits for them, and re-layouts: 116 us -> none  [the longest x448 64.7 us: local_per_mode(): lax.associative_scan(combine_pairs, (step_decay, values), axis=0)[1]]
    psum x1 -> x0, blocking collectives: 39.8 us -> none  [body(): summed = lax.psum(local_grad + cross_part, ('ctx', 'ch'))]
    all_gather x3 -> x0, blocking collectives: 30.1 us -> none  [carried_in(): everything = jax.tree.map(lambda part: lax.all_gather(part, axis), x)]
    ppermute x0 -> x17, starting transfers between devices: none -> 21.3 us  [the longest x7 9.78 us: body(): lax.ppermute(messages[k - 1], 'ctx', [(i, (i + k) % n) for i in range(n)])]
    add x641 -> x1, other arithmetic: 18.2 us -> 0.01 us  [body(): over_groups = [a + b for a, b in zip(over_groups[::2], over_groups[1::2])]]
    another operation x4 -> x0, loops' own time: 16.5 us -> none  [the longest x1 15.5 us: local_block(): lax.scan(local_per_mode, (empty_acc, empty_acc), (residue, decay))]
    while x32 -> x0, local copies, waits for them, and re-layouts: 11.9 us -> none
    exp x17 -> x0, other arithmetic: 11.8 us -> none  [the longest x16 11.8 us: local_per_mode(): step_decay = jnp.broadcast_to(jnp.exp(-decay_row), values.shape)]
  transfers between devices with their start and end apart: 0 -> 17, of which waited for: 0 -> 4; matrix products, arithmetic and copies ran while one was open for 0% -> 0% of each run, Pallas kernels for 0% -> 16%
where the time goes in v1:
time: 40.1 us; the launch traced here: 39.9 us
  starting transfers between devices  21.3 us (53%)
  Pallas kernels  9.57 us (24%)
  waiting for transfers between devices  5.6 us (14%)
  local copies, waits for them, and re-layouts  2.67 us (7%)
  between operations  0.72 us (2%)
    ppermute x7, starting transfers between devices, body(): lax.ppermute(messages[k - 1], 'ctx', [(i, (i + k) % n) for i in range(n)])  9.78 us
    ppermute x7, starting transfers between devices, body(): lax.ppermute(whole, 'ctx', [(i, (i + k) % n) for i in range(n)])  7.31 us
    ppermute x3, starting transfers between devices, body(): lax.ppermute(part, 'ch', [(i, i ^ k) for i in range(n_ch)])  4.23 us
    ppermute x3, waiting for transfers between devices, body(): lax.ppermute(part, 'ch', [(i, i ^ k) for i in range(n_ch)])  3.83 us
    pallas_call x1, Pallas kernels, body(): pl.pallas_call(local_kernel, out_shape=[shaped(chunks * SUB, SUB, channel...  3.64 us
    pallas_call x1, Pallas kernels, body(): pl.pallas_call(functools.partial(finish_kernel, direct, n), out_shape=[ja...  2.72 us
    unnamed x14, local copies, waits for them, and re-layouts  2.67 us
    pallas_call x1, Pallas kernels, body(): pl.pallas_call(functools.partial(gather_kernel, True, n), out_shape=[shap...  2.47 us
  transfers between devices with their start and end apart: 17, of which 4 were waited for; matrix products, arithmetic and copies ran while one was open for 0% of the time, Pallas kernels for 16%

profile of v1, /device:TPU:0, one launch (start us, length us, event | category | flops | bytes accessed | tf_op | source)
XLA Modules:
  0.0 39.9 jit_solution(4431515495589914453)
XLA Ops:
  0.6 0.0 copy-start
  0.6 0.9 %copy-done = bf16[256,512]{1,0:T(8,128)(2,1)S(1)} copy-done((bf16[256,512]{1,0:T(8,128)(2,1)S(1)}, bf16[256,512]{1,0:T(8,128)(2,1)}, u32[]{:S(2)}) %copy-start) | copy-done | bytes 262168
  1.6 0.9 %copy-done.2 = bf16[256,512]{1,0:T(8,128)(2,1)S(1)} copy-done((bf16[256,512]{1,0:T(8,128)(2,1)S(1)}, bf16[256,512]{1,0:T(8,128)(2,1)}, u32[]{:S(2)}) %copy-start.2) | copy-done | bytes 262168
  2.5 0.8 %copy-done.4 = f32[16,512]{1,0:T(8,128)S(1)} copy-done((f32[16,512]{1,0:T(8,128)S(1)}, f32[16,512]{1,0:T(8,128)}, u32[]{:S(2)}) %copy-start.4) | copy-done | bytes 32792
  3.3 2.5 %block_states.1 = (f32[24,512]{1,0:T(8,128)S(1)}, f32[24,512]{1,0:T(8,128)S(1)}, f32[24,512]{1,0:T(8,128)S(1)}, f32[24,512]{1,0:T(8,128)S(1)}, f32[24,512]{1,0:T...) custom-call(bf16[256,512]{1,0:T(8,128)(2,1)S(1)} %copy-done, ...), custom_call_target="tpu_custom_call" | custom-call | flops 10485760 | bytes 786432 | tf_op jit(solution)/shard_map/block_states/pallas_call | solution.py:310
  5.8 0.0 copy-start.1
  5.8 0.5 %collective-permute-start = (f32[24,512]{1,0:T(8,128)S(1)}, f32[24,512]{1,0:T(8,128)S(1)}, u32[]{:S(2)}, u32[]{:S(2)}) collective-permute-start(f32[24,512]{1,0:T(8,128)S(1)} %get-tuple-element.17), channel_id=1, source_target_pairs={{0,4},{4,8},{8,12},{12,16},{16,20},{20,24},{24,28},{28,0},{1,5},{5... | collective-permute-start | bytes 147464 | tf_op jit(solution)/shard_map/ppermute | solution.py:321
  6.3 2.6 %collective-permute-start.1 = (f32[24,512]{1,0:T(8,128)S(1)}, f32[24,512]{1,0:T(8,128)S(1)}, u32[]{:S(2)}, u32[]{:S(2)}) collective-permute-start(f32[24,512]{1,0:T(8,128)S(1)} %get-tuple-element.18), channel_id=1, source_target_pairs={{0,8},{4,12},{8,16},{12,20},{16,24},{20,28},{24,0},{28,4},{1,9},{5... | collective-permute-start | bytes 147464 | tf_op jit(solution)/shard_map/ppermute | solution.py:321
  8.8 2.4 %collective-permute-start.2 = (f32[24,512]{1,0:T(8,128)S(1)}, f32[24,512]{1,0:T(8,128)S(1)}, u32[]{:S(2)}, u32[]{:S(2)}) collective-permute-start(f32[24,512]{1,0:T(8,128)S(1)} %get-tuple-element.19), channel_id=1, source_target_pairs={{0,12},{4,16},{8,20},{12,24},{16,28},{20,0},{24,4},{28,8},{1,13},{... | collective-permute-start | bytes 147464 | tf_op jit(solution)/shard_map/ppermute | solution.py:321
  11.2 0.5 %collective-permute-start.3 = (f32[24,512]{1,0:T(8,128)S(1)}, f32[24,512]{1,0:T(8,128)S(1)}, u32[]{:S(2)}, u32[]{:S(2)}) collective-permute-start(f32[24,512]{1,0:T(8,128)S(1)} %get-tuple-element.20), channel_id=1, source_target_pairs={{0,16},{4,20},{8,24},{12,28},{16,0},{20,4},{24,8},{28,12},{1,17},{... | collective-permute-start | bytes 147464 | tf_op jit(solution)/shard_map/ppermute | solution.py:321
  11.7 0.1 collective-permute-start.4
  11.8 0.0 collective-permute-done.refs_0_
  11.8 1.4 %collective-permute-start.5 = (f32[24,512]{1,0:T(8,128)S(1)}, f32[24,512]{1,0:T(8,128)S(1)}, u32[]{:S(2)}, u32[]{:S(2)}) collective-permute-start(f32[24,512]{1,0:T(8,128)S(1)} %get-tuple-element.22), channel_id=1, source_target_pairs={{0,24},{4,28},{8,0},{12,4},{16,8},{20,12},{24,16},{28,20},{1,25},{... | collective-permute-start | bytes 147464 | tf_op jit(solution)/shard_map/ppermute | solution.py:321
  13.3 0.0 collective-permute-done.1.refs_1_
  13.3 2.3 %collective-permute-start.6 = (f32[24,512]{1,0:T(8,128)S(1)}, f32[24,512]{1,0:T(8,128)S(1)}, u32[]{:S(2)}, u32[]{:S(2)}) collective-permute-start(f32[24,512]{1,0:T(8,128)S(1)} %get-tuple-element.23), channel_id=1, source_target_pairs={{0,28},{4,0},{8,4},{12,8},{16,12},{20,16},{24,20},{28,24},{1,29},{... | collective-permute-start | bytes 147464 | tf_op jit(solution)/shard_map/ppermute | solution.py:321
  15.6 0.6 %collective-permute-done.5.refs_5_ = f32[24,512]{1,0:T(8,128)S(1)} collective-permute-done((f32[24,512]{1,0:T(8,128)S(1)}, f32[24,512]{1,0:T(8,128)S(1)}, u32[]{:S(2)}, u32[]{:S(2)}) %collective-permute-start.5) | collective-permute-done | bytes 49184 | tf_op jit(solution)/shard_map/ppermute | solution.py:321
  16.2 1.2 %collective-permute-done.6.refs_6_ = f32[24,512]{1,0:T(8,128)S(1)} collective-permute-done((f32[24,512]{1,0:T(8,128)S(1)}, f32[24,512]{1,0:T(8,128)S(1)}, u32[]{:S(2)}, u32[]{:S(2)}) %collective-permute-start.6) | collective-permute-done | bytes 49184 | tf_op jit(solution)/shard_map/ppermute | solution.py:321
  17.3 0.1 owned_modes.1
  17.4 2.7 %collective-permute-start.8 = (f32[2,512]{1,0:T(2,128)S(1)}, f32[2,512]{1,0:T(2,128)S(1)}, u32[]{:S(2)}, u32[]{:S(2)}) collective-permute-start(f32[2,512]{1,0:T(2,128)S(1)} %owned_modes.1), channel_id=1, source_target_pairs={{0,2},{1,3},{2,0},{3,1},{4,6},{5,7},{6,4},{7,5},{8,10},{9,11},{10,... | collective-permute-start | bytes 12296 | tf_op jit(solution)/shard_map/ppermute | solution.py:357
  20.1 1.3 %collective-permute-start.9 = (f32[2,512]{1,0:T(2,128)S(1)}, f32[2,512]{1,0:T(2,128)S(1)}, u32[]{:S(2)}, u32[]{:S(2)}) collective-permute-start(f32[2,512]{1,0:T(2,128)S(1)} %owned_modes.1), channel_id=1, source_target_pairs={{0,3},{1,2},{2,1},{3,0},{4,7},{5,6},{6,5},{7,4},{8,11},{9,10},{10,... | collective-permute-start | bytes 12296 | tf_op jit(solution)/shard_map/ppermute | solution.py:357
  21.4 0.2 collective-permute-start.7
  21.6 0.3 collective-permute-done.8
  22.0 3.5 %collective-permute-done.9 = f32[2,512]{1,0:T(2,128)S(1)} collective-permute-done((f32[2,512]{1,0:T(2,128)S(1)}, f32[2,512]{1,0:T(2,128)S(1)}, u32[]{:S(2)}, u32[]{:S(2)}) %collective-permute-start.9) | collective-permute-done | bytes 4128 | tf_op jit(solution)/shard_map/ppermute | solution.py:357
  25.5 0.1 collective-permute-start.10
  25.5 1.4 %collective-permute-start.11 = (f32[2,512]{1,0:T(2,128)S(1)}, f32[2,512]{1,0:T(2,128)S(1)}, u32[]{:S(2)}, u32[]{:S(2)}) collective-permute-start(f32[2,512]{1,0:T(2,128)S(1)} %add_add_fusion.refs_0_), channel_id=1, source_target_pairs={{0,8},{4,12},{8,16},{12,20},{16,24},{20,28},{24,0},{28,4},{1,9},{5... | collective-permute-start | bytes 12296 | tf_op jit(solution)/shard_map/ppermute | solution.py:362
  26.9 1.0 %collective-permute-start.12 = (f32[2,512]{1,0:T(2,128)S(1)}, f32[2,512]{1,0:T(2,128)S(1)}, u32[]{:S(2)}, u32[]{:S(2)}) collective-permute-start(f32[2,512]{1,0:T(2,128)S(1)} %add_add_fusion.refs_0_), channel_id=1, source_target_pairs={{0,12},{4,16},{8,20},{12,24},{16,28},{20,0},{24,4},{28,8},{1,13},{... | collective-permute-start | bytes 12296 | tf_op jit(solution)/shard_map/ppermute | solution.py:362
  28.0 1.8 %collective-permute-start.13 = (f32[2,512]{1,0:T(2,128)S(1)}, f32[2,512]{1,0:T(2,128)S(1)}, u32[]{:S(2)}, u32[]{:S(2)}) collective-permute-start(f32[2,512]{1,0:T(2,128)S(1)} %add_add_fusion.refs_0_), channel_id=1, source_target_pairs={{0,16},{4,20},{8,24},{12,28},{16,0},{20,4},{24,8},{28,12},{1,17},{... | collective-permute-start | bytes 12296 | tf_op jit(solution)/shard_map/ppermute | solution.py:362
  29.8 1.6 %collective-permute-start.15 = (f32[2,512]{1,0:T(2,128)S(1)}, f32[2,512]{1,0:T(2,128)S(1)}, u32[]{:S(2)}, u32[]{:S(2)}) collective-permute-start(f32[2,512]{1,0:T(2,128)S(1)} %add_add_fusion.refs_0_), channel_id=1, source_target_pairs={{0,24},{4,28},{8,0},{12,4},{16,8},{20,12},{24,16},{28,20},{1,25},{... | collective-permute-start | bytes 12296 | tf_op jit(solution)/shard_map/ppermute | solution.py:362
  31.4 1.4 %collective-permute-start.16 = (f32[2,512]{1,0:T(2,128)S(1)}, f32[2,512]{1,0:T(2,128)S(1)}, u32[]{:S(2)}, u32[]{:S(2)}) collective-permute-start(f32[2,512]{1,0:T(2,128)S(1)} %add_add_fusion.refs_0_), channel_id=1, source_target_pairs={{0,28},{4,0},{8,4},{12,8},{16,12},{20,16},{24,20},{28,24},{1,29},{... | collective-permute-start | bytes 12296 | tf_op jit(solution)/shard_map/ppermute | solution.py:362
  32.8 3.6 %local_convolutions.1 = (f32[32,8,512]{2,1,0:T(8,128)S(1)}, f32[32,8,512]{2,1,0:T(8,128)S(1)}) custom-call(bf16[256,512]{1,0:T(8,128)(2,1)S(1)} %copy-done.1, bf16[256,512]{1,0:T(8,128)(2,1)S(1)} %copy-done.3, f32[16,512]{1,0:T(8,128)S(1)} %copy-done.6, f32[16,512]{1,0:T(8,128)S(1)} %copy-done.5), custom_call_target="tpu_custom_call" | custom-call | flops 20971520 | bytes 1572864 | tf_op jit(solution)/shard_map/local_convolutions/pallas_call | solution.py:333
  36.5 2.7 %add_arrivals.1 = (bf16[256,512]{1,0:T(8,128)(2,1)}, bf16[256,512]{1,0:T(8,128)(2,1)}) custom-call(f32[16,512]{1,0:T(8,128)S(1)} %copy-done.6, f32[16,512]{1,0:T(8,128)S(1)} %copy-done.5, f32[32,8,512]{2,1,0:T(8,128)S(1)} %get-tuple-element.15.near_out, f32[32,8,512]{2,1,0:T(8,128)S(1)} %get-tuple-element.16.near_back, ...), custom_call_target="tpu_custom_call" | custom-call | flops 8388608 | bytes 1572864 | tf_op jit(solution)/shard_map/add_arrivals/pallas_call | solution.py:383
  39.2 0.7 %assemble_gradient.1 = f32[16,512]{1,0:T(8,128)} custom-call(f32[2,512]{1,0:T(2,128)S(1)} %add_add_fusion.refs_0_, f32[2,512]{1,0:T(2,128)S(1)} %collective-permute-done.10.refs_1_, f32[2,512]{1,0:T(2,128)S(1)} %collective-permute-done.11.refs_2_, f32[2,512]{1,0:T(2,128)S(1)} %collective-permute-done.12.refs_3_, ...), custom_call_target="tpu_custom_call" | custom-call | flops 8192 | bytes 65536 | tf_op jit(solution)/shard_map/assemble_gradient/pallas_call | solution.py:364
  (22 shorter events, 0.1 us)
Async XLA Ops:
  0.6 1.0 %copy-start = (bf16[256,512]{1,0:T(8,128)(2,1)S(1)}, bf16[256,512]{1,0:T(8,128)(2,1)}, u32[]{:S(2)}) copy-start(bf16[256,512]{1,0:T(8,128)(2,1)} %x_ref.3) | copy-start | bytes 786436
  1.6 0.9 %copy-start.2 = (bf16[256,512]{1,0:T(8,128)(2,1)S(1)}, bf16[256,512]{1,0:T(8,128)(2,1)}, u32[]{:S(2)}) copy-start(bf16[256,512]{1,0:T(8,128)(2,1)} %g_ref.3) | copy-start | bytes 786436
  2.5 0.8 %copy-start.4 = (f32[16,512]{1,0:T(8,128)S(1)}, f32[16,512]{1,0:T(8,128)}, u32[]{:S(2)}) copy-start(f32[16,512]{1,0:T(8,128)} %decay_ref.5) | copy-start | bytes 98308
  3.3 29.5 %copy-start.3 = (bf16[256,512]{1,0:T(8,128)(2,1)S(1)}, bf16[256,512]{1,0:T(8,128)(2,1)}, u32[]{:S(2)}) copy-start(bf16[256,512]{1,0:T(8,128)(2,1)} %g_ref.3) | copy-start | bytes 786436
  5.8 27.0 %copy-start.1 = (bf16[256,512]{1,0:T(8,128)(2,1)S(1)}, bf16[256,512]{1,0:T(8,128)(2,1)}, u32[]{:S(2)}) copy-start(bf16[256,512]{1,0:T(8,128)(2,1)} %x_ref.3) | copy-start | bytes 786436
  5.8 6.0 %collective-permute-start = (f32[24,512]{1,0:T(8,128)S(1)}, f32[24,512]{1,0:T(8,128)S(1)}, u32[]{:S(2)}, u32[]{:S(2)}) collective-permute-start(f32[24,512]{1,0:T(8,128)S(1)} %get-tuple-element.17), channel_id=1, source_target_pairs={{0,4},{4,8},{8,12},{12,16},{16,20},{20,24},{24,28},{28,0},{1,5},{5... | collective-permute-start | bytes 147464 | tf_op jit(solution)/shard_map/ppermute | solution.py:321
  6.3 7.0 %collective-permute-start.1 = (f32[24,512]{1,0:T(8,128)S(1)}, f32[24,512]{1,0:T(8,128)S(1)}, u32[]{:S(2)}, u32[]{:S(2)}) collective-permute-start(f32[24,512]{1,0:T(8,128)S(1)} %get-tuple-element.18), channel_id=1, source_target_pairs={{0,8},{4,12},{8,16},{12,20},{16,24},{20,28},{24,0},{28,4},{1,9},{5... | collective-permute-start | bytes 147464 | tf_op jit(solution)/shard_map/ppermute | solution.py:321
  8.8 6.7 %collective-permute-start.2 = (f32[24,512]{1,0:T(8,128)S(1)}, f32[24,512]{1,0:T(8,128)S(1)}, u32[]{:S(2)}, u32[]{:S(2)}) collective-permute-start(f32[24,512]{1,0:T(8,128)S(1)} %get-tuple-element.19), channel_id=1, source_target_pairs={{0,12},{4,16},{8,20},{12,24},{16,28},{20,0},{24,4},{28,8},{1,13},{... | collective-permute-start | bytes 147464 | tf_op jit(solution)/shard_map/ppermute | solution.py:321
  11.2 4.4 %collective-permute-start.3 = (f32[24,512]{1,0:T(8,128)S(1)}, f32[24,512]{1,0:T(8,128)S(1)}, u32[]{:S(2)}, u32[]{:S(2)}) collective-permute-start(f32[24,512]{1,0:T(8,128)S(1)} %get-tuple-element.20), channel_id=1, source_target_pairs={{0,16},{4,20},{8,24},{12,28},{16,0},{20,4},{24,8},{28,12},{1,17},{... | collective-permute-start | bytes 147464 | tf_op jit(solution)/shard_map/ppermute | solution.py:321
  11.7 3.9 %collective-permute-start.4 = (f32[24,512]{1,0:T(8,128)S(1)}, f32[24,512]{1,0:T(8,128)S(1)}, u32[]{:S(2)}, u32[]{:S(2)}) collective-permute-start(f32[24,512]{1,0:T(8,128)S(1)} %get-tuple-element.21), channel_id=1, source_target_pairs={{0,20},{4,24},{8,28},{12,0},{16,4},{20,8},{24,12},{28,16},{1,21},{... | collective-permute-start | bytes 147464 | tf_op jit(solution)/shard_map/ppermute | solution.py:321
  11.8 4.3 %collective-permute-start.5 = (f32[24,512]{1,0:T(8,128)S(1)}, f32[24,512]{1,0:T(8,128)S(1)}, u32[]{:S(2)}, u32[]{:S(2)}) collective-permute-start(f32[24,512]{1,0:T(8,128)S(1)} %get-tuple-element.22), channel_id=1, source_target_pairs={{0,24},{4,28},{8,0},{12,4},{16,8},{20,12},{24,16},{28,20},{1,25},{... | collective-permute-start | bytes 147464 | tf_op jit(solution)/shard_map/ppermute | solution.py:321
  13.3 4.1 %collective-permute-start.6 = (f32[24,512]{1,0:T(8,128)S(1)}, f32[24,512]{1,0:T(8,128)S(1)}, u32[]{:S(2)}, u32[]{:S(2)}) collective-permute-start(f32[24,512]{1,0:T(8,128)S(1)} %get-tuple-element.23), channel_id=1, source_target_pairs={{0,28},{4,0},{8,4},{12,8},{16,12},{20,16},{24,20},{28,24},{1,29},{... | collective-permute-start | bytes 147464 | tf_op jit(solution)/shard_map/ppermute | solution.py:321
  17.3 15.5 %copy-start.5 = (f32[16,512]{1,0:T(8,128)S(1)}, f32[16,512]{1,0:T(8,128)}, u32[]{:S(2)}) copy-start(f32[16,512]{1,0:T(8,128)} %decay_ref.5) | copy-start | bytes 98308
  17.3 15.5 %copy-start.6 = (f32[16,512]{1,0:T(8,128)S(1)}, f32[16,512]{1,0:T(8,128)}, u32[]{:S(2)}) copy-start(f32[16,512]{1,0:T(8,128)} %residue_ref.3) | copy-start | bytes 98308
  17.4 4.6 %collective-permute-start.8 = (f32[2,512]{1,0:T(2,128)S(1)}, f32[2,512]{1,0:T(2,128)S(1)}, u32[]{:S(2)}, u32[]{:S(2)}) collective-permute-start(f32[2,512]{1,0:T(2,128)S(1)} %owned_modes.1), channel_id=1, source_target_pairs={{0,2},{1,3},{2,0},{3,1},{4,6},{5,7},{6,4},{7,5},{8,10},{9,11},{10,... | collective-permute-start | bytes 12296 | tf_op jit(solution)/shard_map/ppermute | solution.py:357
  20.1 5.4 %collective-permute-start.9 = (f32[2,512]{1,0:T(2,128)S(1)}, f32[2,512]{1,0:T(2,128)S(1)}, u32[]{:S(2)}, u32[]{:S(2)}) collective-permute-start(f32[2,512]{1,0:T(2,128)S(1)} %owned_modes.1), channel_id=1, source_target_pairs={{0,3},{1,2},{2,1},{3,0},{4,7},{5,6},{6,5},{7,4},{8,11},{9,10},{10,... | collective-permute-start | bytes 12296 | tf_op jit(solution)/shard_map/ppermute | solution.py:357
  21.4 4.1 %collective-permute-start.7 = (f32[2,512]{1,0:T(2,128)S(1)}, f32[2,512]{1,0:T(2,128)S(1)}, u32[]{:S(2)}, u32[]{:S(2)}) collective-permute-start(f32[2,512]{1,0:T(2,128)S(1)} %owned_modes.1), channel_id=1, source_target_pairs={{0,1},{1,0},{2,3},{3,2},{4,5},{5,4},{6,7},{7,6},{8,9},{9,8},{10,11... | collective-permute-start | bytes 12296 | tf_op jit(solution)/shard_map/ppermute | solution.py:357
  25.5 4.3 %collective-permute-start.10 = (f32[2,512]{1,0:T(2,128)S(1)}, f32[2,512]{1,0:T(2,128)S(1)}, u32[]{:S(2)}, u32[]{:S(2)}) collective-permute-start(f32[2,512]{1,0:T(2,128)S(1)} %add_add_fusion.refs_0_), channel_id=1, source_target_pairs={{0,4},{4,8},{8,12},{12,16},{16,20},{20,24},{24,28},{28,0},{1,5},{5... | collective-permute-start | bytes 12296 | tf_op jit(solution)/shard_map/ppermute | solution.py:362
  25.5 5.9 %collective-permute-start.11 = (f32[2,512]{1,0:T(2,128)S(1)}, f32[2,512]{1,0:T(2,128)S(1)}, u32[]{:S(2)}, u32[]{:S(2)}) collective-permute-start(f32[2,512]{1,0:T(2,128)S(1)} %add_add_fusion.refs_0_), channel_id=1, source_target_pairs={{0,8},{4,12},{8,16},{12,20},{16,24},{20,28},{24,0},{28,4},{1,9},{5... | collective-permute-start | bytes 12296 | tf_op jit(solution)/shard_map/ppermute | solution.py:362
  26.9 12.2 %collective-permute-start.12 = (f32[2,512]{1,0:T(2,128)S(1)}, f32[2,512]{1,0:T(2,128)S(1)}, u32[]{:S(2)}, u32[]{:S(2)}) collective-permute-start(f32[2,512]{1,0:T(2,128)S(1)} %add_add_fusion.refs_0_), channel_id=1, source_target_pairs={{0,12},{4,16},{8,20},{12,24},{16,28},{20,0},{24,4},{28,8},{1,13},{... | collective-permute-start | bytes 12296 | tf_op jit(solution)/shard_map/ppermute | solution.py:362
  28.0 11.2 %collective-permute-start.13 = (f32[2,512]{1,0:T(2,128)S(1)}, f32[2,512]{1,0:T(2,128)S(1)}, u32[]{:S(2)}, u32[]{:S(2)}) collective-permute-start(f32[2,512]{1,0:T(2,128)S(1)} %add_add_fusion.refs_0_), channel_id=1, source_target_pairs={{0,16},{4,20},{8,24},{12,28},{16,0},{20,4},{24,8},{28,12},{1,17},{... | collective-permute-start | bytes 12296 | tf_op jit(solution)/shard_map/ppermute | solution.py:362
  29.8 9.4 %collective-permute-start.14 = (f32[2,512]{1,0:T(2,128)S(1)}, f32[2,512]{1,0:T(2,128)S(1)}, u32[]{:S(2)}, u32[]{:S(2)}) collective-permute-start(f32[2,512]{1,0:T(2,128)S(1)} %add_add_fusion.refs_0_), channel_id=1, source_target_pairs={{0,20},{4,24},{8,28},{12,0},{16,4},{20,8},{24,12},{28,16},{1,21},{... | collective-permute-start | bytes 12296 | tf_op jit(solution)/shard_map/ppermute | solution.py:362
  29.8 9.4 %collective-permute-start.15 = (f32[2,512]{1,0:T(2,128)S(1)}, f32[2,512]{1,0:T(2,128)S(1)}, u32[]{:S(2)}, u32[]{:S(2)}) collective-permute-start(f32[2,512]{1,0:T(2,128)S(1)} %add_add_fusion.refs_0_), channel_id=1, source_target_pairs={{0,24},{4,28},{8,0},{12,4},{16,8},{20,12},{24,16},{28,20},{1,25},{... | collective-permute-start | bytes 12296 | tf_op jit(solution)/shard_map/ppermute | solution.py:362
  31.4 7.8 %collective-permute-start.16 = (f32[2,512]{1,0:T(2,128)S(1)}, f32[2,512]{1,0:T(2,128)S(1)}, u32[]{:S(2)}, u32[]{:S(2)}) collective-permute-start(f32[2,512]{1,0:T(2,128)S(1)} %add_add_fusion.refs_0_), channel_id=1, source_target_pairs={{0,28},{4,0},{8,4},{12,8},{16,12},{20,16},{24,20},{28,24},{1,29},{... | collective-permute-start | bytes 12296 | tf_op jit(solution)/shard_map/ppermute | solution.py:362

commit v2 on v1

--- a/solution.py
+++ b/solution.py
@@ -55,16 +55,25 @@
     return scratch[pl.ds(half * SUB * SUB + j, SUB, stride=SUB), :]
 
 
-def gather_kernel(direct, n, x_ref, g_ref, decay_ref, *refs):
+def gather_kernel(direct, n, x_hbm, g_hbm, decay_hbm, *refs):
+    *refs, x_ref, g_ref, decay_ref, sems = refs
+    copies = [
+        pltpu.make_async_copy(source, target, sems.at[i])
+        for i, (source, target) in enumerate(((x_hbm, x_ref), (g_hbm, g_ref), (decay_hbm, decay_ref)))
+    ]
+    for copy in copies:
+        copy.start()
     modes, channels = decay_ref.shape
     chunks = x_ref.shape[0] // (SUB * SUB)
     span = chunks * SUB
     if direct:
         place = lax.axis_index("ctx")
         share = modes // n
-        *messages, own, xf, gf, pw, ends, starts, inner, closing, opening, grad, parts = refs
+        messages, xf, gf, pw, ends, starts, inner, closing, opening, grad, parts = refs
     else:
         closing, opening, grad, xf, gf, pw, ends, starts, inner = refs
+    for copy in copies:
+        copy.wait()
 
     def tile_step(tile, _):
         lanes = pl.ds(pl.multiple_of(tile * LANES, LANES), LANES)
@@ -108,11 +117,9 @@
             parts[owner, share:2 * share] = opening[rows]
             parts[owner, 2 * share:3 * share] = grad[rows]
             parts[owner, 3 * share:4 * share] = decay_ref[rows]
-        own[...] = parts[place]
-        for k in range(1, n):
-            message = messages[k - 1]
-            message[0:modes] = jnp.where(place + k < n, closing[...], opening[...])
-            message[modes:] = parts[lax.rem(place + k, n)]
+        for k in range(n):
+            messages[k, 0:modes] = jnp.where(k > place, closing[...], opening[...])
+            messages[k, modes:] = parts[k]
 
 
 def local_kernel(x_ref, g_ref, residue_ref, decay_ref, out_ref, back_ref,
@@ -181,27 +188,20 @@
     lax.fori_loop(0, channels // LANES, tile_step, 0)
 
 
-def owner_kernel(n, scale, *refs):
-    *messages, own, out_ref, held, back = refs
-    place = lax.axis_index("ctx")
-    share = own.shape[0] // 4
-    decay = own[3 * share:]
-    total = own[2 * share:3 * share]
-    held[place] = own[0:share]
-    back[place] = own[share:2 * share]
-    for k in range(1, n):
-        source = lax.rem(place - k + n, n)
-        held[source] = messages[k - 1][0:share]
-        back[source] = messages[k - 1][share:2 * share]
-        total = total + messages[k - 1][2 * share:3 * share]
+def owner_kernel(scale, arrived, out_ref):
+    n, rows, _ = arrived.shape
+    share = rows // 4
+    decay = arrived[0, 3 * share:]
     a = jnp.exp(-decay)
-    block = jnp.exp(-decay * scale[0])
+    block = jnp.exp(-decay * scale)
     arriving = jnp.zeros_like(decay)
     cross = jnp.zeros_like(decay)
+    total = jnp.zeros_like(decay)
     for j in range(n):
-        cross = cross + back[j] * arriving
-        arriving = arriving * block + held[j]
-    out_ref[...] = (total + a * cross) * (1.0 / (scale[0] * n))
+        cross = cross + arrived[j, share:2 * share] * arriving
+        arriving = arriving * block + arrived[j, 0:share]
+        total = total + arrived[j, 2 * share:3 * share]
+    out_ref[...] = (total + a * cross) * (1.0 / (scale * n))
 
 
 def finish_kernel(direct, n, residue_ref, decay_ref, near_out, near_back, *refs):
@@ -215,10 +215,11 @@
         block = jnp.exp(-decay * (span * SUB))
         incoming = jnp.zeros_like(decay)
         outgoing = jnp.zeros_like(decay)
-        for k in range(n - 1, 0, -1):
-            incoming = incoming * block + jnp.where(place >= k, sources[k - 1][...], 0.0)
-        for k in range(1, n):
-            outgoing = outgoing * block + jnp.where(place < k, sources[k - 1][...], 0.0)
+        arrived, = sources
+        for k in range(n):
+            incoming = jnp.where(k < place, incoming * block + arrived[k], incoming)
+        for k in reversed(range(n)):
+            outgoing = jnp.where(k > place, outgoing * block + arrived[k], outgoing)
     else:
         incoming, outgoing = sources[0][...], sources[1][...]
     first = residue_ref[...] * jnp.exp(-decay)
@@ -257,14 +258,12 @@
     lax.fori_loop(0, channels // LANES, tile_step, 0)
 
 
-def assemble_kernel(n, *refs):
-    *pieces, out_ref, parts = refs
-    place = lax.axis_index("ctx")
-    share = pieces[0].shape[0]
-    for k in range(n):
-        parts[lax.rem(place - k + n, n)] = pieces[k][...]
-    for j in range(n):
-        out_ref[j * share:(j + 1) * share] = parts[j]
+def assemble_kernel(n, pieces, out_ref):
+    share = pieces.shape[1]
+    groups = pieces.shape[0] // n
+    for owner in range(n):
+        terms = [pieces[owner * groups + k] for k in range(groups)]
+        out_ref[owner * share:(owner + 1) * share] = sum(terms[1:], terms[0])
 
 
 def vmem(*shape):
@@ -281,6 +280,7 @@
 
 PARAMS = pltpu.CompilerParams(vmem_limit_bytes=32 * 1024 * 1024)
 WHOLE = pl.BlockSpec(memory_space=pltpu.VMEM)
+HBM = pl.BlockSpec(memory_space=pltpu.HBM)
 
 
 def carried_in(own, block_decay, reverse):
@@ -298,33 +298,38 @@
 def body(signal, cotangent, residue, decay):
     tokens, channels = signal.shape
     modes = decay.shape[0]
-    n, n_ch = lax.axis_size("ctx"), lax.axis_size("ch")
+    n = lax.axis_size("ctx")
     chunks = tokens // (SUB * SUB)
     direct = n <= SUB and modes % n == 0
     elements = tokens * channels
     tokens_scratch = [vmem(tokens, LANES), vmem(tokens, LANES)]
     spans = vmem(modes * SUB, LANES)
+    staging = [
+        pltpu.VMEM(signal.shape, signal.dtype),
+        pltpu.VMEM(cotangent.shape, cotangent.dtype),
+        vmem(modes, channels),
+        pltpu.SemaphoreType.DMA((3,)),
+    ]
 
     if direct:
         share = modes // n
-        gathered = pl.pallas_call(
+        messages = pl.pallas_call(
             functools.partial(gather_kernel, True, n),
-            out_shape=[shaped(modes + 4 * share, channels)] * (n - 1) + [shaped(4 * share, channels)],
+            out_shape=shaped(n, modes + 4 * share, channels),
+            in_specs=[HBM] * 3,
             scratch_shapes=tokens_scratch + [vmem(2, modes, LANES), spans, spans, spans]
-            + [vmem(modes, channels)] * 3 + [vmem(n, 4 * share, channels)],
+            + [vmem(modes, channels)] * 3 + [vmem(n, 4 * share, channels)] + staging,
             compiler_params=PARAMS,
             cost_estimate=cost(elements * modes * 5, modes * channels * 3, elements * 6),
             name="block_states",
         )(signal, cotangent, decay)
-        *messages, own = gathered
-        arrived = [
-            lax.ppermute(messages[k - 1], "ctx", [(i, (i + k) % n) for i in range(n)]) for k in range(1, n)
-        ]
+        arrived = lax.all_to_all(messages, "ctx", 0, 0)
     else:
         closing, opening, local_grad = pl.pallas_call(
             functools.partial(gather_kernel, False, n),
             out_shape=[shaped(modes, channels)] * 3,
-            scratch_shapes=tokens_scratch + [vmem(2, modes, LANES), spans, spans, spans],
+            in_specs=[HBM] * 3,
+            scratch_shapes=tokens_scratch + [vmem(2, modes, LANES), spans, spans, spans] + staging,
             compiler_params=PARAMS,
             cost_estimate=cost(elements * modes * 5, modes * channels * 3, elements * 6),
             name="block_states",
@@ -342,35 +347,25 @@
 
     if direct:
         part = pl.pallas_call(
-            functools.partial(owner_kernel, n, (float(tokens),)),
+            functools.partial(owner_kernel, float(tokens)),
             out_shape=shaped(share, channels),
             grid=(1,),
-            in_specs=[pl.BlockSpec((4 * share, channels), lambda i: (modes // (4 * share), 0))] * (n - 1) + [WHOLE],
+            in_specs=[pl.BlockSpec((n, 4 * share, channels), lambda i: (0, modes // (4 * share), 0))],
             out_specs=WHOLE,
-            scratch_shapes=[vmem(n, share, channels)] * 2,
             compiler_params=PARAMS,
             cost_estimate=cost(elements, modes * channels, modes * channels * 16),
             name="owned_modes",
-        )(*arrived, own)
-        over_groups = [part]
-        for k in range(1, n_ch):
-            over_groups.append(lax.ppermute(part, "ch", [(i, i ^ k) for i in range(n_ch)]))
-        while len(over_groups) > 1:
-            over_groups = [a + b for a, b in zip(over_groups[::2], over_groups[1::2])]
-        whole = over_groups[0]
-        pieces = [whole] + [
-            lax.ppermute(whole, "ctx", [(i, (i + k) % n) for i in range(n)]) for k in range(1, n)
-        ]
+        )(arrived)
+        pieces = lax.all_gather(part, ("ctx", "ch"))
         residue_grad = pl.pallas_call(
             functools.partial(assemble_kernel, n),
             out_shape=shaped(modes, channels),
-            scratch_shapes=[vmem(n, share, channels)],
             compiler_params=PARAMS,
             cost_estimate=cost(modes * channels, 0, modes * channels * 8),
             name="assemble_gradient",
-        )(*pieces)
-        sources = arrived
-        source_specs = [pl.BlockSpec((modes, channels), lambda i: (0, 0))] * (n - 1)
+        )(pieces)
+        sources = [arrived]
+        source_specs = [pl.BlockSpec((n, modes, channels), lambda i: (0, 0, 0))]
     else:
         block_decay = jnp.exp(-decay * tokens)
         incoming = carried_in(closing, block_decay, False)

time: 40.1 us -> 94.1 us (2.35)
  blocking collectives: 0 us -> 80.8 us
  starting transfers between devices: 21.3 us -> 0 us
  waiting for transfers between devices: 5.6 us -> 0 us
    all_gather x0 -> x1, blocking collectives: none -> 67.5 us  [body(): pieces = lax.all_gather(part, ('ctx', 'ch'))]
    ppermute x17 -> x0, starting transfers between devices: 21.3 us -> none  [the longest x7 9.78 us: body(): lax.ppermute(messages[k - 1], 'ctx', [(i, (i + k) % n) for i in range(n)])]
    all_to_all x0 -> x1, blocking collectives: none -> 13.3 us  [body(): arrived = lax.all_to_all(messages, 'ctx', 0, 0)]
    ppermute x17 -> x0, waiting for transfers between devices: 5.6 us -> none  [the longest x3 3.83 us: body(): lax.ppermute(part, 'ch', [(i, i ^ k) for i in range(n_ch)])]
    unnamed x14 -> x12, local copies, waits for them, and re-layouts: 2.67 us -> 2.67 us
  transfers between devices with their start and end apart: 17 -> 0, of which waited for: 4 -> 0; matrix products, arithmetic and copies ran while one was open for 0% -> 0% of each run, Pallas kernels for 16% -> 0%
where the time goes in v2:
time: 94.1 us; the launch traced here: 93.8 us
  blocking collectives  80.8 us (86%)
  Pallas kernels  9.64 us (10%)
  local copies, waits for them, and re-layouts  2.67 us (3%)
    all_gather x1, blocking collectives, body(): pieces = lax.all_gather(part, ('ctx', 'ch'))  67.5 us
    all_to_all x1, blocking collectives, body(): arrived = lax.all_to_all(messages, 'ctx', 0, 0)  13.3 us
    pallas_call x1, Pallas kernels, body(): pl.pallas_call(local_kernel, out_shape=[shaped(chunks * SUB, SUB, channel...  3.64 us
    pallas_call x1, Pallas kernels, body(): pl.pallas_call(functools.partial(finish_kernel, direct, n), out_shape=[ja...  2.72 us
    unnamed x12, local copies, waits for them, and re-layouts  2.67 us
    pallas_call x1, Pallas kernels, body(): pl.pallas_call(functools.partial(gather_kernel, True, n), out_shape=shape...  2.59 us

profile of v2, /device:TPU:0, one launch (start us, length us, event | category | flops | bytes accessed | tf_op | source)
XLA Modules:
  0.0 93.8 jit_solution(14297185221696959295)
XLA Ops:
  0.6 0.0 copy-start
  0.6 0.9 %copy-done = bf16[256,512]{1,0:T(8,128)(2,1)S(1)} copy-done((bf16[256,512]{1,0:T(8,128)(2,1)S(1)}, bf16[256,512]{1,0:T(8,128)(2,1)}, u32[]{:S(2)}) %copy-start) | copy-done | bytes 262168
  1.6 0.0 copy-start.1
  1.6 0.9 %copy-done.1 = bf16[256,512]{1,0:T(8,128)(2,1)S(1)} copy-done((bf16[256,512]{1,0:T(8,128)(2,1)S(1)}, bf16[256,512]{1,0:T(8,128)(2,1)}, u32[]{:S(2)}) %copy-start.1) | copy-done | bytes 262168
  2.5 0.0 copy-start.3
  2.5 0.8 copy-done.3
  3.3 2.6 %block_states.1 = f32[8,24,512]{2,1,0:T(8,128)S(1)} custom-call(bf16[256,512]{1,0:T(8,128)(2,1)S(1)} %copy-done, bf16[256,512]{1,0:T(8,128)(2,1)S(1)} %copy-done.1, f32[16,512]{1,0:T(8,128)S(1)} %copy-done.3), custom_call_target="tpu_custom_call" | custom-call | flops 10485760 | bytes 786432 | tf_op jit(solution)/shard_map/block_states/pallas_call | solution.py:316
  5.9 13.3 %all_to_all.5.refs_0_.arrived = f32[8,24,512]{2,1,0:T(8,128)S(1)} all-to-all(f32[8,24,512]{2,1,0:T(8,128)S(1)} %block_states.1), channel_id=1, replica_groups=mesh['ctx'=8,'ch'=4] {'ctx'}, dimensions={0} | all-to-all | bytes 786432 | tf_op jit(solution)/shard_map/all_to_all | solution.py:326
  19.2 0.0 copy-start.2
  19.2 0.1 owned_modes.1
  19.3 0.0 copy-start.4
  19.3 0.0 copy-start.5
  19.3 67.5 %all-gather.1.pieces = f32[32,2,512]{2,1,0:T(2,128)S(1)} all-gather(f32[1,2,512]{2,1,0:T(2,128)S(1)} %bitcast.1), channel_id=2, replica_groups=mesh['ctx'=8,'ch'=4] {'ctx','ch'}, dimensions={0}, use_global_device_ids=true | all-gather | bytes 135168 | tf_op jit(solution)/shard_map/all_gather | solution.py:359
  86.8 0.0 copy-done.2
  86.8 0.0 copy-done.4
  86.8 0.0 copy-done.5
  86.8 3.6 %local_convolutions.1 = (f32[32,8,512]{2,1,0:T(8,128)S(1)}, f32[32,8,512]{2,1,0:T(8,128)S(1)}) custom-call(bf16[256,512]{1,0:T(8,128)(2,1)S(1)} %copy-done, bf16[256,512]{1,0:T(8,128)(2,1)S(1)} %copy-done.2, f32[16,512]{1,0:T(8,128)S(1)} %copy-done.5, f32[16,512]{1,0:T(8,128)S(1)} %copy-done.4), custom_call_target="tpu_custom_call" | custom-call | flops 20971520 | bytes 1572864 | tf_op jit(solution)/shard_map/local_convolutions/pallas_call | solution.py:338
  90.4 0.6 assemble_gradient.1
  91.1 2.7 %add_arrivals.1 = (bf16[256,512]{1,0:T(8,128)(2,1)}, bf16[256,512]{1,0:T(8,128)(2,1)}) custom-call(f32[16,512]{1,0:T(8,128)S(1)} %copy-done.5, f32[16,512]{1,0:T(8,128)S(1)} %copy-done.4, f32[32,8,512]{2,1,0:T(8,128)S(1)} %get-tuple-element.7.near_out, f32[32,8,512]{2,1,0:T(8,128)S(1)} %get-tuple-element.8.near_back, f32[8,24,512]{2,1,0:T(8,128)S(1)} %all_to_all.5.refs_0_.arrived), custom_call_target="tpu_custom_call" | custom-call | flops 8388608 | bytes 1572864 | tf_op jit(solution)/shard_map/add_arrivals/pallas_call | solution.py:378
Async XLA Ops:
  0.6 1.0 %copy-start = (bf16[256,512]{1,0:T(8,128)(2,1)S(1)}, bf16[256,512]{1,0:T(8,128)(2,1)}, u32[]{:S(2)}) copy-start(bf16[256,512]{1,0:T(8,128)(2,1)} %x_hbm.1) | copy-start | bytes 786436
  1.6 0.9 %copy-start.1 = (bf16[256,512]{1,0:T(8,128)(2,1)S(1)}, bf16[256,512]{1,0:T(8,128)(2,1)}, u32[]{:S(2)}) copy-start(bf16[256,512]{1,0:T(8,128)(2,1)} %g_hbm.1) | copy-start | bytes 786436
  2.5 0.8 copy-start.3
  19.2 67.6 %copy-start.2 = (bf16[256,512]{1,0:T(8,128)(2,1)S(1)}, bf16[256,512]{1,0:T(8,128)(2,1)}, u32[]{:S(2)}) copy-start(bf16[256,512]{1,0:T(8,128)(2,1)} %g_hbm.1) | copy-start | bytes 786436
  19.3 67.5 %copy-start.4 = (f32[16,512]{1,0:T(8,128)S(1)}, f32[16,512]{1,0:T(8,128)}, u32[]{:S(2)}) copy-start(f32[16,512]{1,0:T(8,128)} %decay_ref.3) | copy-start | bytes 98308
  19.3 67.5 %copy-start.5 = (f32[16,512]{1,0:T(8,128)S(1)}, f32[16,512]{1,0:T(8,128)}, u32[]{:S(2)}) copy-start(f32[16,512]{1,0:T(8,128)} %residue_ref.3) | copy-start | bytes 98308

commit v3 on v2

v3 whole, which is shorter than its diff:
```python
import functools

import jax
import jax.numpy as jnp
from jax import lax
from jax.experimental import pallas as pl
from jax.experimental.pallas import tpu as pltpu
from jax.sharding import PartitionSpec as P

SUB = 8
LANES = 128
F32 = jnp.float32


def row(ref, *index):
    return jnp.broadcast_to(ref[index], (SUB, LANES))


def split_lanes(source, target, tile):
    lanes = pl.ds(pl.multiple_of(tile * LANES, LANES), LANES)
    target[...] = source[:, lanes].astype(F32)


def read_tokens(scratch, chunks):
    span = chunks * SUB
    return [[scratch[pl.ds(p * SUB + r, SUB, stride=span), :] for r in range(SUB)] for p in range(chunks)]


def powers(decay, pw):
    pw[0] = jnp.exp(-decay)
    pw[1] = jnp.exp(-decay * SUB)


def horner(terms, factor):
    total = terms[0]
    for term in terms[1:]:
        total = total * factor + term
    return total


def chunk_states(m, xs, gs, pw):
    a, a8 = row(pw, 0, pl.ds(m, 1)), row(pw, 1, pl.ds(m, 1))
    chunks = len(xs)
    held, back = [], [None] * chunks
    for p in range(chunks):
        own = horner(xs[p], a)
        held.append(own if p == 0 else held[-1] * a8 + own)
    opens = [horner(gs[p][::-1], a) for p in range(chunks)]
    for p in reversed(range(chunks)):
        back[p] = opens[p] if p == chunks - 1 else back[p + 1] * a8 + opens[p]
    return held, back, opens


def by_span(scratch, half, j):
    return scratch[pl.ds(half * SUB * SUB + j, SUB, stride=SUB), :]


def gather_kernel(x_hbm, g_hbm, decay_hbm, segment, *refs):
    xf, gf, pw, ends, starts, inner, x_ref, g_ref, decay_ref, sems = refs
    copies = [
        pltpu.make_async_copy(source, target, sems.at[i])
        for i, (source, target) in enumerate(((x_hbm, x_ref), (g_hbm, g_ref), (decay_hbm, decay_ref)))
    ]
    for copy in copies:
        copy.start()
    modes, channels = decay_ref.shape
    chunks = x_ref.shape[0] // (SUB * SUB)
    span = chunks * SUB
    closing, opening, grad = (segment.at[pl.ds(i * modes, modes)] for i in range(3))
    for copy in copies:
        copy.wait()

    def tile_step(tile, _):
        lanes = pl.ds(pl.multiple_of(tile * LANES, LANES), LANES)
        split_lanes(x_ref, xf, tile)
        split_lanes(g_ref, gf, tile)
        decay = decay_ref[:, lanes]
        powers(decay, pw)
        xs, gs = read_tokens(xf, chunks), read_tokens(gf, chunks)
        for m in range(modes):
            held, back, opens = chunk_states(m, xs, gs, pw)
            rows = pl.ds(m * SUB, SUB)
            ends[rows, :] = held[-1]
            starts[rows, :] = back[0]
            inner[rows, :] = sum(opens[p] * held[p - 1] for p in range(1, chunks))
        lagged = []
        for lag in range(SUB):
            pairs = [gs[p][r] * xs[p][r - lag] for p in range(chunks) for r in range(lag, SUB)]
            lagged.append(jnp.sum(sum(pairs), axis=0, keepdims=True))
        for half in range(modes // SUB):
            some = pl.ds(half * SUB, SUB)
            a = pw[0, some, :]
            across = jnp.exp(-decay[half * SUB:(half + 1) * SUB] * span)
            arriving = jnp.zeros((SUB, LANES), F32)
            cross = jnp.zeros((SUB, LANES), F32)
            for j in range(SUB):
                cross = cross + (by_span(inner, half, j) + by_span(starts, half, j) * arriving)
                arriving = arriving * across + by_span(ends, half, j)
            leaving = horner([by_span(starts, half, j) for j in reversed(range(SUB))], across)
            near = horner([jnp.broadcast_to(v, (SUB, LANES)) for v in reversed(lagged)], a)
            closing[some, lanes] = arriving
            opening[some, lanes] = leaving
            grad[some, lanes] = near + a * cross
        return 0

    lax.fori_loop(0, channels // LANES, tile_step, 0)


def local_kernel(tiles, x_ref, g_ref, residue_ref, decay_ref, _, out_ref, back_ref,
                 xf, gf, pw, ends, starts, before, after, arrive, leave):
    modes, channels = decay_ref.shape
    chunks = x_ref.shape[0] // (SUB * SUB)
    span = chunks * SUB

    def tile_step(tile, _):
        lanes = pl.ds(pl.multiple_of(tile * LANES, LANES), LANES)
        split_lanes(x_ref, xf, tile)
        split_lanes(g_ref, gf, tile)
        decay = decay_ref[:, lanes]
        residue = residue_ref[:, lanes]
        powers(decay, pw)
        pw[2] = residue * pw[0]
        xs, gs = read_tokens(xf, chunks), read_tokens(gf, chunks)
        for m in range(modes):
            held, back, _ = chunk_states(m, xs, gs, pw)
            rows = pl.ds(m * SUB, SUB)
            ends[rows, :] = held[-1]
            starts[rows, :] = back[0]
            for p in range(1, chunks):
                before[m, p - 1] = held[p - 1]
                after[m, p - 1] = back[p]
        for half in range(modes // SUB):
            across = jnp.exp(-decay[half * SUB:(half + 1) * SUB] * span)
            for target, source, order in ((arrive, ends, range(SUB)), (leave, starts, range(SUB - 1, -1, -1))):
                running = jnp.zeros((SUB, LANES), F32)
                for j in order:
                    target[pl.ds(half * SUB * SUB + j, SUB, stride=SUB), :] = running
                    running = running * across + by_span(source, half, j)
        taps = []
        weight = residue
        for lag in range(SUB):
            taps.append(jnp.broadcast_to(jnp.sum(weight, axis=0, keepdims=True), (SUB, LANES)))
            weight = weight * pw[0]
        for values, carried, inside, target, forward in (
            (xs, arrive, before, out_ref, True), (gs, leave, after, back_ref, False)
        ):
            order = range(SUB) if forward else range(SUB - 1, -1, -1)
            totals = []
            for p in range(chunks):
                seq = [values[p][r] for r in order]
                totals.append([sum(taps[lag] * seq[r - lag] for lag in range(r + 1)) for r in range(SUB)])
            for m in range(modes):
                a, a8, first = (row(pw, i, pl.ds(m, 1)) for i in range(3))
                edge = carried[pl.ds(m * SUB, SUB), :]
                for q in range(chunks):
                    p = q if forward else chunks - 1 - q
                    if q == 0:
                        state = edge
                    else:
                        edge = edge * a8
                        state = edge + inside[m, p - 1 if forward else p]
                    wave = state * first
                    for r in range(SUB):
                        totals[p][r] = totals[p][r] + wave
                        if r < SUB - 1:
                            wave = wave * a
            for p in range(chunks):
                for r, at in enumerate(order):
                    target[tile - tiles[0], p * SUB + at] = totals[p][r]
        return 0

    lax.fori_loop(tiles[0], tiles[1], tile_step, 0)


def join_kernel(tokens, bit, last, segment, other, decay_ref, carried, _, *outs):
    modes = decay_ref.shape[0]
    place = lax.axis_index("ctx")
    size = 1 << bit
    inside = lax.rem(place, size)
    late = lax.rem(lax.div(place, size), 2) == 1
    decay = decay_ref[...]
    parts = [slice(i * modes, (i + 1) * modes) for i in range(3)]
    mine = [segment[rows] for rows in parts]
    theirs = [other[rows] for rows in parts]
    behind = (inside * tokens).astype(F32)
    ahead = ((size - 1 - inside) * tokens).astype(F32)
    reach = jnp.exp(decay * -jnp.where(late, behind, ahead))
    first = reach * jnp.where(late, theirs[0], 0.0)
    second = reach * jnp.where(late, 0.0, theirs[1])
    if bit:
        first = first + carried[0:modes]
        second = second + carried[modes:]
    outs[0][0:modes] = first
    outs[0][modes:] = second
    early_close = jnp.where(late, theirs[0], mine[0])
    late_open = jnp.where(late, mine[1], theirs[1])
    grad = (mine[2] + theirs[2]) + jnp.exp(-decay) * late_open * early_close
    if last:
        outs[1][...] = grad
    else:
        block = jnp.exp(decay * (-1.0 * size * tokens))
        outs[1][parts[0]] = block * early_close + jnp.where(late, mine[0], theirs[0])
        outs[1][parts[1]] = jnp.where(late, theirs[1], mine[1]) + block * late_open
        outs[1][parts[2]] = grad


def finish_kernel(tiles, residue_ref, decay_ref, near_out, near_back, carried, _, *refs):
    out_ref, back_ref, result, pw, arrive, leave = refs[-6:]
    modes, channels = decay_ref.shape
    chunks = near_out.shape[1] // SUB
    span = chunks * SUB
    first = residue_ref[...] * jnp.exp(-decay_ref[...])
    arrive[...] = carried[0:modes] * first
    leave[...] = carried[modes:] * first

    def tile_step(tile, _):
        lanes = pl.ds(pl.multiple_of(tile * LANES, LANES), LANES)
        decay = decay_ref[:, lanes]
        powers(decay, pw)
        pw[2] = decay * (-1.0 * span)
        pw[3] = arrive[:, lanes]
        pw[4] = leave[:, lanes]
        level = lax.broadcasted_iota(jnp.int32, (SUB, LANES), 0).astype(F32)
        for near, target, forward in ((near_out, out_ref, True), (near_back, back_ref, False)):
            order = range(SUB) if forward else range(SUB - 1, -1, -1)
            spans = level if forward else SUB - 1.0 - level
            totals = [[near[tile - tiles[0], p * SUB + r] for r in range(SUB)] for p in range(chunks)]
            for m in range(modes):
                a, a8, rate = (row(pw, i, pl.ds(m, 1)) for i in range(3))
                state = row(pw, 3 if forward else 4, pl.ds(m, 1)) * jnp.exp(rate * spans)
                for q in range(chunks):
                    p = q if forward else chunks - 1 - q
                    wave = state
                    for r in order:
                        totals[p][r] = totals[p][r] + wave
                        wave = wave * a
                    if q < chunks - 1:
                        state = state * a8
            for p in range(chunks):
                for r in range(SUB):
                    result[pl.ds(p * SUB + r, SUB, stride=span), :] = totals[p][r]
            place = pl.ds(pl.multiple_of((tile - tiles[0]) * LANES, LANES), LANES)
            target[:, place] = result[...].astype(target.dtype)
        return 0

    lax.fori_loop(tiles[0], tiles[1], tile_step, 0)


def vmem(*shape):
    return pltpu.VMEM(shape, F32)


def shaped(*shape):
    return jax.ShapeDtypeStruct(shape, F32)


def cost(flops, transcendentals, nbytes):
    return pl.CostEstimate(flops=flops, transcendentals=transcendentals, bytes_accessed=nbytes)


PARAMS = pltpu.CompilerParams(vmem_limit_bytes=32 * 1024 * 1024)
WHOLE = pl.BlockSpec(memory_space=pltpu.VMEM)
HBM = pl.BlockSpec(memory_space=pltpu.HBM)


UNREAD = pl.BlockSpec(memory_space=pl.ANY)
PARTS = 2


def body(signal, cotangent, residue, decay):
    tokens, channels = signal.shape
    modes = decay.shape[0]
    n, groups = lax.axis_size("ctx"), lax.axis_size("ch")
    chunks = tokens // (SUB * SUB)
    elements = tokens * channels
    steps = n.bit_length() - 1
    tokens_scratch = [vmem(tokens, LANES), vmem(tokens, LANES)]
    spans = vmem(modes * SUB, LANES)
    width = channels // LANES // PARTS
    ranges = [(k * width, (k + 1) * width) for k in range(PARTS)]

    segment = pl.pallas_call(
        gather_kernel,
        out_shape=shaped(3 * modes, channels),
        in_specs=[HBM] * 3,
        scratch_shapes=tokens_scratch
        + [vmem(2, modes, LANES), spans, spans, spans]
        + [pltpu.VMEM(signal.shape, signal.dtype)] * 2
        + [vmem(modes, channels), pltpu.SemaphoreType.DMA((3,))],
        compiler_params=PARAMS,
        cost_estimate=cost(elements * modes * 5, modes * channels * 3, elements * 6),
        name="block_states",
    )(*(pltpu.with_memory_space_constraint(a, pltpu.HBM) for a in (signal, cotangent, decay)))

    def near_part(part, after):
        return pl.pallas_call(
            functools.partial(local_kernel, ranges[part]),
            out_shape=[shaped(width, chunks * SUB, SUB, LANES)] * 2,
            in_specs=[WHOLE] * 4 + [UNREAD],
            scratch_shapes=tokens_scratch
            + [vmem(3, modes, LANES), spans, spans]
            + [vmem(modes, chunks - 1, SUB, LANES)] * 2
            + [spans, spans],
            compiler_params=PARAMS,
            cost_estimate=cost(elements * modes * 400 // PARTS, 0, elements * 12 // PARTS),
            name="local_convolutions",
        )(signal, cotangent, residue, decay, after)

    near = [None] * PARTS
    carried = jnp.zeros((SUB, LANES), F32)
    pinned = segment
    for bit in range(steps):
        other = lax.ppermute(segment, "ctx", [(i, i ^ (1 << bit)) for i in range(n)])
        last = bit == steps - 1
        part = bit - (steps - PARTS)
        if part >= 0:
            near[part] = near_part(part, segment)
            pinned = near[part][0]
        carried, segment = pl.pallas_call(
            functools.partial(join_kernel, tokens, bit, last),
            out_shape=[shaped(2 * modes, channels), shaped(modes if last else 3 * modes, channels)],
            in_specs=[WHOLE] * 4 + [UNREAD],
            compiler_params=PARAMS,
            cost_estimate=cost(elements, modes * channels * 3, modes * channels * 48),
            name="join_segments",
        )(segment, other, decay, carried, pinned)

    def finish_part(part, after, done):
        spec = pl.BlockSpec((tokens, width * LANES), lambda i: (0, part))
        kept = [] if done is None else list(done)
        return pl.pallas_call(
            functools.partial(finish_kernel, ranges[part]),
            out_shape=[jax.ShapeDtypeStruct((tokens, channels), signal.dtype)] * 2,
            grid=(1,),
            in_specs=[WHOLE] * 5 + [UNREAD] + [UNREAD] * len(kept),
            out_specs=[spec] * 2,
            input_output_aliases={6 + i: i for i in range(len(kept))},
            scratch_shapes=[vmem(tokens, LANES), vmem(5, modes, LANES)] + [vmem(modes, channels)] * 2,
            compiler_params=PARAMS,
            cost_estimate=cost(elements * modes * 300 // PARTS, 0, elements * 12 // PARTS),
            name="add_arrivals",
        )(residue, decay, *near[part], carried, after, *kept)

    grad = segment
    results = None
    part = 0
    shift = 1
    while shift < groups:
        other = lax.ppermute(grad, "ch", [(i, i ^ shift) for i in range(groups)])
        if part < PARTS:
            results = finish_part(part, grad, results)
            part += 1
        grad = grad + other
        shift *= 2
    while part < PARTS:
        results = finish_part(part, grad, results)
        part += 1
    return results[0], results[1], grad / (tokens * n)


def solution(mesh):
    return jax.shard_map(
        body,
        mesh=mesh,
        in_specs=(P("ctx", "ch"), P("ctx", "ch"), P(), P()),
        out_specs=(P("ctx", "ch"), P("ctx", "ch"), P()),
        check_vma=False,
    )
```

time: 94.1 us -> 27.6 us (0.29)
  blocking collectives: 80.8 us -> 0 us
  starting transfers between devices: 0 us -> 10.2 us
  waiting for transfers between devices: 0 us -> 5.36 us
  local copies, waits for them, and re-layouts: 2.67 us -> 0.02 us
    all_gather x1 -> x0, blocking collectives: 67.5 us -> none  [body(): pieces = lax.all_gather(part, ('ctx', 'ch'))]
    all_to_all x1 -> x0, blocking collectives: 13.3 us -> none  [body(): arrived = lax.all_to_all(messages, 'ctx', 0, 0)]
    ppermute x0 -> x5, starting transfers between devices: none -> 10.2 us  [the longest x3 5.26 us: body(): other = lax.ppermute(segment, 'ctx', [(i, i ^ 1 << bit) for i in range(n)])]
    ppermute x0 -> x5, waiting for transfers between devices: none -> 5.36 us  [the longest x3 3.26 us: body(): other = lax.ppermute(segment, 'ctx', [(i, i ^ 1 << bit) for i in range(n)])]
    unnamed x12 -> x8, local copies, waits for them, and re-layouts: 2.67 us -> 0.02 us
    pallas_call x5 -> x8, Pallas kernels: 9.64 us -> 10.5 us  [the longest x2 3.62 us: near_part(): pl.pallas_call(functools.partial(local_kernel, ranges[part]), out_shape=[...]
  transfers between devices with their start and end apart: 0 -> 5, of which waited for: 0 -> 4; matrix products, arithmetic and copies ran while one was open for 0% -> 0% of each run, Pallas kernels for 0% -> 25%
where the time goes in v3:
time: 27.6 us; the launch traced here: 27.4 us
  Pallas kernels  10.5 us (38%)
  starting transfers between devices  10.2 us (37%)
  waiting for transfers between devices  5.36 us (19%)
  between operations  0.7 us (3%)
  other arithmetic  0.63 us (2%)
    ppermute x3, starting transfers between devices, body(): other = lax.ppermute(segment, 'ctx', [(i, i ^ 1 << bit) for i in range(n)])  5.26 us
    ppermute x2, starting transfers between devices, body(): other = lax.ppermute(grad, 'ch', [(i, i ^ shift) for i in range(groups)])  4.94 us
    pallas_call x2, Pallas kernels, near_part(): pl.pallas_call(functools.partial(local_kernel, ranges[part]), out_shape=[...  3.62 us
    pallas_call x1, Pallas kernels, body(): pl.pallas_call(gather_kernel, out_shape=shaped(3 * modes, channels), in_s...  3.5 us
    pallas_call x2, Pallas kernels, finish_part(): pl.pallas_call(functools.partial(finish_kernel, ranges[part]), out_shape=...  3.28 us
    ppermute x3, waiting for transfers between devices, body(): other = lax.ppermute(segment, 'ctx', [(i, i ^ 1 << bit) for i in range(n)])  3.26 us
    ppermute x2, waiting for transfers between devices, body(): other = lax.ppermute(grad, 'ch', [(i, i ^ shift) for i in range(groups)])  2.09 us
    div x1, other arithmetic, body(): return (results[0], results[1], grad / (tokens * n))  0.62 us
  transfers between devices with their start and end apart: 5, of which 4 were waited for; matrix products, arithmetic and copies ran while one was open for 0% of the time, Pallas kernels for 25%

profile of v3, /device:TPU:0, one launch (start us, length us, event | category | flops | bytes accessed | tf_op | source)
XLA Modules:
  0.0 27.4 jit_solution(11791441340808418070)
XLA Ops:
  0.6 0.0 copy-start
  0.6 0.0 copy-start.2
  0.7 3.5 %block_states.1.segment._ = f32[48,512]{1,0:T(8,128)S(1)} custom-call(bf16[256,512]{1,0:T(8,128)(2,1)} %x_ref.3, bf16[256,512]{1,0:T(8,128)(2,1)} %g_ref.3, f32[16,512]{1,0:T(8,128)} %decay_ref.13), custom_call_target="tpu_custom_call" | custom-call | flops 10485760 | bytes 786432 | tf_op jit(solution)/shard_map/block_states/pallas_call | solution.py:282
  4.2 0.0 copy-start.1
  4.2 0.5 %collective-permute-start = (f32[48,512]{1,0:T(8,128)S(1)}, f32[48,512]{1,0:T(8,128)S(1)}, u32[]{:S(2)}, u32[]{:S(2)}) collective-permute-start(f32[48,512]{1,0:T(8,128)S(1)} %block_states.1.segment._), channel_id=1, source_target_pairs={{0,4},{4,0},{8,12},{12,8},{16,20},{20,16},{24,28},{28,24},{1,5},{5... | collective-permute-start | bytes 294920 | tf_op jit(solution)/shard_map/ppermute | solution.py:313
  4.7 0.9 %collective-permute-done.other = f32[48,512]{1,0:T(8,128)S(1)} collective-permute-done((f32[48,512]{1,0:T(8,128)S(1)}, f32[48,512]{1,0:T(8,128)S(1)}, u32[]{:S(2)}, u32[]{:S(2)}) %collective-permute-start) | collective-permute-done | bytes 98336 | tf_op jit(solution)/shard_map/ppermute | solution.py:313
  5.6 0.0 copy-done
  5.6 0.0 copy-start.3
  5.7 2.9 %collective-permute-start.1 = (f32[48,512]{1,0:T(8,128)S(1)}, f32[48,512]{1,0:T(8,128)S(1)}, u32[]{:S(2)}, u32[]{:S(2)}) collective-permute-start(f32[48,512]{1,0:T(8,128)S(1)} %get-tuple-element.17._.segment), channel_id=1, source_target_pairs={{0,8},{4,12},{8,0},{12,4},{16,24},{20,28},{24,16},{28,20},{1,9},{5... | collective-permute-start | bytes 294920 | tf_op jit(solution)/shard_map/ppermute | solution.py:313
  8.6 0.0 copy-done.2
  8.6 0.0 copy-done.1
  8.6 0.0 copy-done.3
  8.6 1.8 %local_convolutions.2 = (f32[2,32,8,128]{3,2,1,0:T(8,128)S(1)}, f32[2,32,8,128]{3,2,1,0:T(8,128)S(1)}) custom-call(bf16[256,512]{1,0:T(8,128)(2,1)S(1)} %copy-done.1, bf16[256,512]{1,0:T(8,128)(2,1)S(1)} %copy-done.2, f32[16,512]{1,0:T(8,128)S(1)} %copy-done.3, f32[16,512]{1,0:T(8,128)S(1)} %copy-done, f32[48,512]{1,0:T(8,128)S(1)} %get-tuple-element.17._.segment), custom_call_target="tpu_custom_call" | custom-call | flops 419430400 | bytes 786432 | tf_op jit(solution)/shard_map/local_convolutions/pallas_call | solution.py:296
  10.4 1.3 %collective-permute-done.1.other = f32[48,512]{1,0:T(8,128)S(1)} collective-permute-done((f32[48,512]{1,0:T(8,128)S(1)}, f32[48,512]{1,0:T(8,128)S(1)}, u32[]{:S(2)}, u32[]{:S(2)}) %collective-permute-start.1) | collective-permute-done | bytes 98336 | tf_op jit(solution)/shard_map/ppermute | solution.py:313
  11.7 1.8 %collective-permute-start.2 = (f32[48,512]{1,0:T(8,128)S(1)}, f32[48,512]{1,0:T(8,128)S(1)}, u32[]{:S(2)}, u32[]{:S(2)}) collective-permute-start(f32[48,512]{1,0:T(8,128)S(1)} %get-tuple-element.20._.segment), channel_id=1, source_target_pairs={{0,16},{4,20},{8,24},{12,28},{16,0},{20,4},{24,8},{28,12},{1,17},{... | collective-permute-start | bytes 294920 | tf_op jit(solution)/shard_map/ppermute | solution.py:313
  13.6 1.8 %local_convolutions.3 = (f32[2,32,8,128]{3,2,1,0:T(8,128)S(1)}, f32[2,32,8,128]{3,2,1,0:T(8,128)S(1)}) custom-call(bf16[256,512]{1,0:T(8,128)(2,1)S(1)} %copy-done.1, bf16[256,512]{1,0:T(8,128)(2,1)S(1)} %copy-done.2, f32[16,512]{1,0:T(8,128)S(1)} %copy-done.3, f32[16,512]{1,0:T(8,128)S(1)} %copy-done, f32[48,512]{1,0:T(8,128)S(1)} %get-tuple-element.20._.segment), custom_call_target="tpu_custom_call" | custom-call | flops 419430400 | bytes 786432 | tf_op jit(solution)/shard_map/local_convolutions/pallas_call | solution.py:296
  15.4 1.0 %collective-permute-done.2.other = f32[48,512]{1,0:T(8,128)S(1)} collective-permute-done((f32[48,512]{1,0:T(8,128)S(1)}, f32[48,512]{1,0:T(8,128)S(1)}, u32[]{:S(2)}, u32[]{:S(2)}) %collective-permute-start.2) | collective-permute-done | bytes 98336 | tf_op jit(solution)/shard_map/ppermute | solution.py:313
  16.5 1.9 %collective-permute-start.3 = (f32[16,512]{1,0:T(8,128)S(1)}, f32[16,512]{1,0:T(8,128)S(1)}, u32[]{:S(2)}, u32[]{:S(2)}) collective-permute-start(f32[16,512]{1,0:T(8,128)S(1)} %get-tuple-element.25._), channel_id=1, source_target_pairs={{0,1},{1,0},{2,3},{3,2},{4,5},{5,4},{6,7},{7,6},{8,9},{9,8},{10,11... | collective-permute-start | bytes 98312 | tf_op jit(solution)/shard_map/ppermute | solution.py:349
  18.4 2.1 %collective-permute-done.3 = f32[16,512]{1,0:T(8,128)S(1)} collective-permute-done((f32[16,512]{1,0:T(8,128)S(1)}, f32[16,512]{1,0:T(8,128)S(1)}, u32[]{:S(2)}, u32[]{:S(2)}) %collective-permute-start.3) | collective-permute-done | bytes 32800 | tf_op jit(solution)/shard_map/ppermute | solution.py:349
  20.5 3.1 %collective-permute-start.4 = (f32[16,512]{1,0:T(8,128)S(1)}, f32[16,512]{1,0:T(8,128)S(1)}, u32[]{:S(2)}, u32[]{:S(2)}) collective-permute-start(f32[16,512]{1,0:T(8,128)S(1)} %add.6._), channel_id=1, source_target_pairs={{0,2},{1,3},{2,0},{3,1},{4,6},{5,7},{6,4},{7,5},{8,10},{9,11},{10,... | collective-permute-start | bytes 98312 | tf_op jit(solution)/shard_map/ppermute | solution.py:349
  23.5 1.6 %add_arrivals.2 = (bf16[256,512]{1,0:T(8,128)(2,1)}, bf16[256,512]{1,0:T(8,128)(2,1)}) custom-call(f32[16,512]{1,0:T(8,128)S(1)} %copy-done.3, f32[16,512]{1,0:T(8,128)S(1)} %copy-done, f32[2,32,8,128]{3,2,1,0:T(8,128)S(1)} %get-tuple-element.19._.near_out, f32[2,32,8,128]{3,2,1,0:T(8,128)S(1)} %get-tuple-element.26.near_back, ...), custom_call_target="tpu_custom_call" | custom-call | flops 314572800 | bytes 786432 | tf_op jit(solution)/shard_map/add_arrivals/pallas_call | solution.py:331
  25.1 1.7 %add_arrivals.3 = (bf16[256,512]{1,0:T(8,128)(2,1)}, bf16[256,512]{1,0:T(8,128)(2,1)}) custom-call(f32[16,512]{1,0:T(8,128)S(1)} %copy-done.3, f32[16,512]{1,0:T(8,128)S(1)} %copy-done, f32[2,32,8,128]{3,2,1,0:T(8,128)S(1)} %get-tuple-element.21._.near_out, ...), custom_call_target="tpu_custom_call", output_to_operand_aliasing={{0}: (6, {}), {1}: (7, {})} | custom-call | flops 314572800 | bytes 786432 | tf_op jit(solution)/shard_map/add_arrivals/pallas_call | solution.py:331
  26.8 0.0 collective-permute-done.4
  26.8 0.6 %add_multiply_fusion = f32[16,512]{1,0:T(8,128)} fusion(f32[16,512]{1,0:T(8,128)S(1)} %add.6._, f32[16,512]{1,0:T(8,128)S(1)} %collective-permute-done.4), kind=kLoop, calls=%fused_computation | loop fusion | flops 16384 | bytes 98304 | tf_op jit(solution)/shard_map/div | solution.py:358
  (5 shorter events, 0.1 us)
Async XLA Ops:
  0.6 5.0 %copy-start = (f32[16,512]{1,0:T(8,128)S(1)}, f32[16,512]{1,0:T(8,128)}, u32[]{:S(2)}) copy-start(f32[16,512]{1,0:T(8,128)} %decay_ref.13) | copy-start | bytes 98308
  0.6 7.9 %copy-start.2 = (bf16[256,512]{1,0:T(8,128)(2,1)S(1)}, bf16[256,512]{1,0:T(8,128)(2,1)}, u32[]{:S(2)}) copy-start(bf16[256,512]{1,0:T(8,128)(2,1)} %g_ref.3) | copy-start | bytes 786436
  4.2 4.4 %copy-start.1 = (bf16[256,512]{1,0:T(8,128)(2,1)S(1)}, bf16[256,512]{1,0:T(8,128)(2,1)}, u32[]{:S(2)}) copy-start(bf16[256,512]{1,0:T(8,128)(2,1)} %x_ref.3) | copy-start | bytes 786436
  4.2 1.5 %collective-permute-start = (f32[48,512]{1,0:T(8,128)S(1)}, f32[48,512]{1,0:T(8,128)S(1)}, u32[]{:S(2)}, u32[]{:S(2)}) collective-permute-start(f32[48,512]{1,0:T(8,128)S(1)} %block_states.1.segment._), channel_id=1, source_target_pairs={{0,4},{4,0},{8,12},{12,8},{16,20},{20,16},{24,28},{28,24},{1,5},{5... | collective-permute-start | bytes 294920 | tf_op jit(solution)/shard_map/ppermute | solution.py:313
  5.6 3.0 %copy-start.3 = (f32[16,512]{1,0:T(8,128)S(1)}, f32[16,512]{1,0:T(8,128)}, u32[]{:S(2)}) copy-start(f32[16,512]{1,0:T(8,128)} %residue_ref.7) | copy-start | bytes 98308
  5.7 6.0 %collective-permute-start.1 = (f32[48,512]{1,0:T(8,128)S(1)}, f32[48,512]{1,0:T(8,128)S(1)}, u32[]{:S(2)}, u32[]{:S(2)}) collective-permute-start(f32[48,512]{1,0:T(8,128)S(1)} %get-tuple-element.17._.segment), channel_id=1, source_target_pairs={{0,8},{4,12},{8,0},{12,4},{16,24},{20,28},{24,16},{28,20},{1,9},{5... | collective-permute-start | bytes 294920 | tf_op jit(solution)/shard_map/ppermute | solution.py:313
  11.7 4.7 %collective-permute-start.2 = (f32[48,512]{1,0:T(8,128)S(1)}, f32[48,512]{1,0:T(8,128)S(1)}, u32[]{:S(2)}, u32[]{:S(2)}) collective-permute-start(f32[48,512]{1,0:T(8,128)S(1)} %get-tuple-element.20._.segment), channel_id=1, source_target_pairs={{0,16},{4,20},{8,24},{12,28},{16,0},{20,4},{24,8},{28,12},{1,17},{... | collective-permute-start | bytes 294920 | tf_op jit(solution)/shard_map/ppermute | solution.py:313
  16.5 4.0 %collective-permute-start.3 = (f32[16,512]{1,0:T(8,128)S(1)}, f32[16,512]{1,0:T(8,128)S(1)}, u32[]{:S(2)}, u32[]{:S(2)}) collective-permute-start(f32[16,512]{1,0:T(8,128)S(1)} %get-tuple-element.25._), channel_id=1, source_target_pairs={{0,1},{1,0},{2,3},{3,2},{4,5},{5,4},{6,7},{7,6},{8,9},{9,8},{10,11... | collective-permute-start | bytes 98312 | tf_op jit(solution)/shard_map/ppermute | solution.py:349
  20.5 6.3 %collective-permute-start.4 = (f32[16,512]{1,0:T(8,128)S(1)}, f32[16,512]{1,0:T(8,128)S(1)}, u32[]{:S(2)}, u32[]{:S(2)}) collective-permute-start(f32[16,512]{1,0:T(8,128)S(1)} %add.6._), channel_id=1, source_target_pairs={{0,2},{1,3},{2,0},{3,1},{4,6},{5,7},{6,4},{7,5},{8,10},{9,11},{10,... | collective-permute-start | bytes 98312 | tf_op jit(solution)/shard_map/ppermute | solution.py:349

commit v4 on v3

--- a/solution.py
+++ b/solution.py
@@ -172,78 +172,107 @@
     lax.fori_loop(tiles[0], tiles[1], tile_step, 0)
 
 
-def join_kernel(tokens, bit, last, segment, other, decay_ref, carried, _, *outs):
+def join_kernel(tokens, bit, last, segment, other, decay_ref, carried, _, arrivals, joined, *message):
     modes = decay_ref.shape[0]
     place = lax.axis_index("ctx")
     size = 1 << bit
-    inside = lax.rem(place, size)
     late = lax.rem(lax.div(place, size), 2) == 1
     decay = decay_ref[...]
     parts = [slice(i * modes, (i + 1) * modes) for i in range(3)]
-    mine = [segment[rows] for rows in parts]
-    theirs = [other[rows] for rows in parts]
-    behind = (inside * tokens).astype(F32)
-    ahead = ((size - 1 - inside) * tokens).astype(F32)
-    reach = jnp.exp(decay * -jnp.where(late, behind, ahead))
-    first = reach * jnp.where(late, theirs[0], 0.0)
-    second = reach * jnp.where(late, 0.0, theirs[1])
+    compact = other.shape[0] == 2 * modes
+    close, begin, grad = (segment[rows] for rows in parts)
+    their_close = other[parts[0]]
+    their_begin = other[parts[0 if compact else 1]]
+    their_grad = other[parts[1 if compact else 2]]
+    first = jnp.where(late, their_close, 0.0)
+    second = jnp.where(late, 0.0, their_begin)
     if bit:
+        inside = lax.rem(place, size)
+        inside = inside - lax.rem(inside, 2)
+        between = (jnp.where(late, inside, size - 2 - inside) * tokens).astype(F32)
+        reach = jnp.exp(decay * -between)
+        first, second = reach * first, reach * second
+    if bit > 1:
         first = first + carried[0:modes]
         second = second + carried[modes:]
-    outs[0][0:modes] = first
-    outs[0][modes:] = second
-    early_close = jnp.where(late, theirs[0], mine[0])
-    late_open = jnp.where(late, mine[1], theirs[1])
-    grad = (mine[2] + theirs[2]) + jnp.exp(-decay) * late_open * early_close
+    arrivals[0:modes] = first
+    arrivals[modes:] = second
+    early_close = jnp.where(late, their_close, close)
+    late_begin = jnp.where(late, begin, their_begin)
+    grad = (grad + their_grad) + jnp.exp(-decay) * late_begin * early_close
     if last:
-        outs[1][...] = grad
-    else:
-        block = jnp.exp(decay * (-1.0 * size * tokens))
-        outs[1][parts[0]] = block * early_close + jnp.where(late, mine[0], theirs[0])
-        outs[1][parts[1]] = jnp.where(late, theirs[1], mine[1]) + block * late_open
-        outs[1][parts[2]] = grad
-
-
-def finish_kernel(tiles, residue_ref, decay_ref, near_out, near_back, carried, _, *refs):
-    out_ref, back_ref, result, pw, arrive, leave = refs[-6:]
+        joined[...] = grad
+        return
+    block = jnp.exp(decay * (-1.0 * size * tokens))
+    close = block * early_close + jnp.where(late, close, their_close)
+    begin = jnp.where(late, their_begin, begin) + block * late_begin
+    joined[parts[0]] = close
+    joined[parts[1]] = begin
+    joined[parts[2]] = grad
+    if message:
+        next_late = lax.rem(lax.div(place, 2 * size), 2) == 1
+        message[0][0:modes] = jnp.where(next_late, begin, close)
+        message[0][modes:] = grad
+
+
+def finish_kernel(ranges, residue_ref, decay_ref, core, chip, received, *refs):
+    near = refs[:2 * len(ranges)]
+    out_hbm, back_hbm, out_ref, back_ref, result, pw, arrive, leave, sems = refs[2 * len(ranges):]
     modes, channels = decay_ref.shape
-    chunks = near_out.shape[1] // SUB
+    chunks = near[0].shape[1] // SUB
     span = chunks * SUB
-    first = residue_ref[...] * jnp.exp(-decay_ref[...])
-    arrive[...] = carried[0:modes] * first
-    leave[...] = carried[modes:] * first
-
-    def tile_step(tile, _):
+    late = lax.rem(lax.axis_index("ctx"), 2) == 1
+    decay = decay_ref[...]
+    first = residue_ref[...] * jnp.exp(-decay)
+    block = jnp.exp(decay * (-1.0 * span * SUB))
+    incoming = jnp.where(late, chip[0:modes], received[0:modes])
+    outgoing = jnp.where(late, chip[modes:], received[modes:])
+    arrive[...] = (core[0:modes] + jnp.where(late, block, 1.0) * incoming) * first
+    leave[...] = (core[modes:] + jnp.where(late, 1.0, block) * outgoing) * first
+
+    def copy_out(tile, which):
         lanes = pl.ds(pl.multiple_of(tile * LANES, LANES), LANES)
-        decay = decay_ref[:, lanes]
-        powers(decay, pw)
-        pw[2] = decay * (-1.0 * span)
-        pw[3] = arrive[:, lanes]
-        pw[4] = leave[:, lanes]
-        level = lax.broadcasted_iota(jnp.int32, (SUB, LANES), 0).astype(F32)
-        for near, target, forward in ((near_out, out_ref, True), (near_back, back_ref, False)):
-            order = range(SUB) if forward else range(SUB - 1, -1, -1)
-            spans = level if forward else SUB - 1.0 - level
-            totals = [[near[tile - tiles[0], p * SUB + r] for r in range(SUB)] for p in range(chunks)]
-            for m in range(modes):
-                a, a8, rate = (row(pw, i, pl.ds(m, 1)) for i in range(3))
-                state = row(pw, 3 if forward else 4, pl.ds(m, 1)) * jnp.exp(rate * spans)
-                for q in range(chunks):
-                    p = q if forward else chunks - 1 - q
-                    wave = state
-                    for r in order:
-                        totals[p][r] = totals[p][r] + wave
-                        wave = wave * a
-                    if q < chunks - 1:
-                        state = state * a8
-            for p in range(chunks):
-                for r in range(SUB):
-                    result[pl.ds(p * SUB + r, SUB, stride=span), :] = totals[p][r]
-            place = pl.ds(pl.multiple_of((tile - tiles[0]) * LANES, LANES), LANES)
-            target[:, place] = result[...].astype(target.dtype)
-        return 0
-
-    lax.fori_loop(tiles[0], tiles[1], tile_step, 0)
+        source, target = ((out_ref, out_hbm), (back_ref, back_hbm))[which]
+        return pltpu.make_async_copy(source.at[:, lanes], target.at[:, lanes], sems.at[which, tile])
+
+    def run(tiles, near_out, near_back):
+        def tile_step(tile, _):
+            lanes = pl.ds(pl.multiple_of(tile * LANES, LANES), LANES)
+            decay = decay_ref[:, lanes]
+            powers(decay, pw)
+            pw[2] = decay * (-1.0 * span)
+            pw[3] = arrive[:, lanes]
+            pw[4] = leave[:, lanes]
+            level = lax.broadcasted_iota(jnp.int32, (SUB, LANES), 0).astype(F32)
+            for near, target, forward in ((near_out, out_ref, True), (near_back, back_ref, False)):
+                order = range(SUB) if forward else range(SUB - 1, -1, -1)
+                spans = level if forward else SUB - 1.0 - level
+                totals = [[near[tile - tiles[0], p * SUB + r] for r in range(SUB)] for p in range(chunks)]
+                for m in range(modes):
+                    a, a8, rate = (row(pw, i, pl.ds(m, 1)) for i in range(3))
+                    state = row(pw, 3 if forward else 4, pl.ds(m, 1)) * jnp.exp(rate * spans)
+                    for q in range(chunks):
+                        p = q if forward else chunks - 1 - q
+                        wave = state
+                        for r in order:
+                            totals[p][r] = totals[p][r] + wave
+                            wave = wave * a
+                        if q < chunks - 1:
+                            state = state * a8
+                for p in range(chunks):
+                    for r in range(SUB):
+                        result[pl.ds(p * SUB + r, SUB, stride=span), :] = totals[p][r]
+                target[:, lanes] = result[...].astype(target.dtype)
+                copy_out(tile, 0 if forward else 1).start()
+            return 0
+
+        lax.fori_loop(tiles[0], tiles[1], tile_step, 0)
+
+    for part, tiles in enumerate(ranges):
+        run(tiles, near[2 * part], near[2 * part + 1])
+    for tile in range(channels // LANES):
+        for which in range(2):
+            copy_out(tile, which).wait()
 
 
 def vmem(*shape):
@@ -306,56 +335,70 @@
             name="local_convolutions",
         )(signal, cotangent, residue, decay, after)
 
-    near = [None] * PARTS
+    def pairs(shift):
+        return [(i, i ^ shift) for i in range(n) if shift == 1 or i % 2]
+
+    to_first = [(i, i - 1) for i in range(n) if i % 2]
+
+    near = []
     carried = jnp.zeros((SUB, LANES), F32)
-    pinned = segment
+    pinned = message = segment
     for bit in range(steps):
-        other = lax.ppermute(segment, "ctx", [(i, i ^ (1 << bit)) for i in range(n)])
+        other = lax.ppermute(message, "ctx", pairs(1 << bit))
         last = bit == steps - 1
-        part = bit - (steps - PARTS)
-        if part >= 0:
-            near[part] = near_part(part, segment)
-            pinned = near[part][0]
-        carried, segment = pl.pallas_call(
+        if bit >= steps - PARTS:
+            near += near_part(len(near) // 2, segment)
+            pinned = near[-1]
+        rows = [2 * modes, modes if last else 3 * modes] + ([2 * modes] if bit == steps - 2 else [])
+        arrivals, segment, *message = pl.pallas_call(
             functools.partial(join_kernel, tokens, bit, last),
-            out_shape=[shaped(2 * modes, channels), shaped(modes if last else 3 * modes, channels)],
+            out_shape=[shaped(r, channels) for r in rows],
             in_specs=[WHOLE] * 4 + [UNREAD],
             compiler_params=PARAMS,
             cost_estimate=cost(elements, modes * channels * 3, modes * channels * 48),
             name="join_segments",
         )(segment, other, decay, carried, pinned)
-
-    def finish_part(part, after, done):
-        spec = pl.BlockSpec((tokens, width * LANES), lambda i: (0, part))
-        kept = [] if done is None else list(done)
-        return pl.pallas_call(
-            functools.partial(finish_kernel, ranges[part]),
-            out_shape=[jax.ShapeDtypeStruct((tokens, channels), signal.dtype)] * 2,
-            grid=(1,),
-            in_specs=[WHOLE] * 5 + [UNREAD] + [UNREAD] * len(kept),
-            out_specs=[spec] * 2,
-            input_output_aliases={6 + i: i for i in range(len(kept))},
-            scratch_shapes=[vmem(tokens, LANES), vmem(5, modes, LANES)] + [vmem(modes, channels)] * 2,
-            compiler_params=PARAMS,
-            cost_estimate=cost(elements * modes * 300 // PARTS, 0, elements * 12 // PARTS),
-            name="add_arrivals",
-        )(residue, decay, *near[part], carried, after, *kept)
+        message = message[0] if message else segment
+        if bit == 0:
+            from_core = arrivals
+        else:
+            carried = arrivals
 
     grad = segment
-    results = None
-    part = 0
-    shift = 1
-    while shift < groups:
-        other = lax.ppermute(grad, "ch", [(i, i ^ shift) for i in range(groups)])
-        if part < PARTS:
-            results = finish_part(part, grad, results)
-            part += 1
-        grad = grad + other
-        shift *= 2
-    while part < PARTS:
-        results = finish_part(part, grad, results)
-        part += 1
-    return results[0], results[1], grad / (tokens * n)
+    received = lax.ppermute(carried, "ctx", to_first)
+    stride = 1
+    while stride < groups:
+        count = min(4, groups // stride)
+        terms = [grad] + [
+            lax.ppermute(
+                grad,
+                ("ctx", "ch"),
+                [(i * groups + k, i * groups + (k ^ (stride * m))) for i in range(n) if i % 2 for k in range(groups)],
+            )
+            for m in range(1, count)
+        ]
+        while len(terms) > 1:
+            terms = [a + b for a, b in zip(terms[::2], terms[1::2])]
+        grad = terms[0]
+        stride *= count
+    other = lax.ppermute(grad, "ctx", to_first)
+    second = lax.rem(lax.axis_index("ctx"), 2) == 1
+    residue_grad = jnp.where(second, grad, other) / (tokens * n)
+
+    conv_out, signal_grad = pl.pallas_call(
+        functools.partial(finish_kernel, ranges),
+        out_shape=[jax.ShapeDtypeStruct((tokens, channels), signal.dtype)] * 2,
+        in_specs=[WHOLE] * (5 + 2 * PARTS),
+        out_specs=[HBM] * 2,
+        scratch_shapes=[pltpu.VMEM((tokens, channels), signal.dtype)] * 2
+        + [vmem(tokens, LANES), vmem(5, modes, LANES)]
+        + [vmem(modes, channels)] * 2
+        + [pltpu.SemaphoreType.DMA((2, channels // LANES))],
+        compiler_params=PARAMS,
+        cost_estimate=cost(elements * modes * 600, 0, elements * 12),
+        name="add_arrivals",
+    )(residue, decay, from_core, carried, received, *near)
+    return conv_out, signal_grad, residue_grad
 
 
 def solution(mesh):

time: 27.6 us -> 35.7 us (1.29)
  waiting for transfers between devices: 5.36 us -> 17.6 us
  starting transfers between devices: 10.2 us -> 6.42 us
  Pallas kernels: 10.5 us -> 9.85 us
    ppermute x5 -> x8, waiting for transfers between devices: 5.36 us -> 17.6 us  [the longest x1 16 us: body(): other = lax.ppermute(grad, 'ctx', to_first)]
    ppermute x5 -> x8, starting transfers between devices: 10.2 us -> 6.42 us  [the longest x3 1.99 us: body(): lax.ppermute(grad, ('ctx', 'ch'), [(i * groups + k, i * groups + (k ^ str...]
    pallas_call x2 -> x1, Pallas kernels: 3.28 us -> 2.6 us  [body(): pl.pallas_call(functools.partial(finish_kernel, ranges), out_shape=[jax.S...]
  transfers between devices with their start and end apart: 5 -> 8, of which waited for: 4 -> 3; matrix products, arithmetic and copies ran while one was open for 0% -> 2% of each run, Pallas kernels for 25% -> 10%
where the time goes in v4:
time: 35.7 us; the launch traced here: 35.4 us
  waiting for transfers between devices  17.6 us (49%)
  Pallas kernels  9.85 us (28%)
  starting transfers between devices  6.42 us (18%)
  between operations  0.82 us (2%)
  other arithmetic  0.64 us (2%)
    ppermute x1, waiting for transfers between devices, body(): other = lax.ppermute(grad, 'ctx', to_first)  16 us
    pallas_call x2, Pallas kernels, near_part(): pl.pallas_call(functools.partial(local_kernel, ranges[part]), out_shape=[...  3.63 us
    pallas_call x1, Pallas kernels, body(): pl.pallas_call(gather_kernel, out_shape=shaped(3 * modes, channels), in_s...  3.5 us
    pallas_call x1, Pallas kernels, body(): pl.pallas_call(functools.partial(finish_kernel, ranges), out_shape=[jax.S...  2.6 us
    ppermute x3, starting transfers between devices, body(): lax.ppermute(grad, ('ctx', 'ch'), [(i * groups + k, i * groups + (k ^ str...  1.99 us
    ppermute x3, starting transfers between devices, body(): other = lax.ppermute(message, 'ctx', pairs(1 << bit))  1.85 us
    ppermute x1, starting transfers between devices, body(): other = lax.ppermute(grad, 'ctx', to_first)  1.29 us
    ppermute x1, starting transfers between devices, body(): received = lax.ppermute(carried, 'ctx', to_first)  1.29 us
  transfers between devices with their start and end apart: 8, of which 3 were waited for; matrix products, arithmetic and copies ran while one was open for 2% of the time, Pallas kernels for 10%

profile of v4, /device:TPU:0, one launch (start us, length us, event | category | flops | bytes accessed | tf_op | source)
XLA Modules:
  0.0 35.4 jit_solution(12562235851283857393)
XLA Ops:
  0.6 0.0 copy-start
  0.6 0.0 copy-start.2
  0.7 3.5 %block_states.1.segment._ = f32[48,512]{1,0:T(8,128)S(1)} custom-call(bf16[256,512]{1,0:T(8,128)(2,1)} %x_ref.3, bf16[256,512]{1,0:T(8,128)(2,1)} %g_ref.3, f32[16,512]{1,0:T(8,128)} %decay_ref.11), custom_call_target="tpu_custom_call" | custom-call | flops 10485760 | bytes 786432 | tf_op jit(solution)/shard_map/block_states/pallas_call | solution.py:311
  4.2 0.0 copy-start.1
  4.2 0.5 %collective-permute-start = (f32[48,512]{1,0:T(8,128)S(1)}, f32[48,512]{1,0:T(8,128)S(1)}, u32[]{:S(2)}, u32[]{:S(2)}) collective-permute-start(f32[48,512]{1,0:T(8,128)S(1)} %block_states.1.segment._), channel_id=1, source_target_pairs={{0,4},{4,0},{8,12},{12,8},{16,20},{20,16},{24,28},{28,24},{1,5},{5... | collective-permute-start | bytes 294920 | tf_op jit(solution)/shard_map/ppermute | solution.py:347
  4.7 0.9 %collective-permute-done.other = f32[48,512]{1,0:T(8,128)S(1)} collective-permute-done((f32[48,512]{1,0:T(8,128)S(1)}, f32[48,512]{1,0:T(8,128)S(1)}, u32[]{:S(2)}, u32[]{:S(2)}) %collective-permute-start) | collective-permute-done | bytes 98336 | tf_op jit(solution)/shard_map/ppermute | solution.py:347
  5.6 0.0 copy-done
  5.6 0.0 copy-start.3
  5.7 0.7 %collective-permute-start.1 = (f32[48,512]{1,0:T(8,128)S(1)}, f32[48,512]{1,0:T(8,128)S(1)}, u32[]{:S(2)}, u32[]{:S(2)}) collective-permute-start(f32[48,512]{1,0:T(8,128)S(1)} %get-tuple-element.17._.segment), channel_id=1, source_target_pairs={{4,12},{12,4},{20,28},{28,20},{5,13},{13,5},{21,29},{29,21},{6,14}... | collective-permute-start | bytes 294920 | tf_op jit(solution)/shard_map/ppermute | solution.py:347
  6.3 0.0 copy-done.2
  6.4 0.0 copy-done.1
  6.4 0.0 copy-done.3
  6.4 1.8 %local_convolutions.2 = (f32[2,32,8,128]{3,2,1,0:T(8,128)S(1)}, f32[2,32,8,128]{3,2,1,0:T(8,128)S(1)}) custom-call(bf16[256,512]{1,0:T(8,128)(2,1)S(1)} %copy-done.1, bf16[256,512]{1,0:T(8,128)(2,1)S(1)} %copy-done.2, f32[16,512]{1,0:T(8,128)S(1)} %copy-done.3, f32[16,512]{1,0:T(8,128)S(1)} %copy-done, f32[48,512]{1,0:T(8,128)S(1)} %get-tuple-element.17._.segment), custom_call_target="tpu_custom_call" | custom-call | flops 419430400 | bytes 786432 | tf_op jit(solution)/shard_map/local_convolutions/pallas_call | solution.py:325
  8.2 0.0 collective-permute-done.1.other
  8.3 0.7 %collective-permute-start.2 = (f32[32,512]{1,0:T(8,128)S(1)}, f32[32,512]{1,0:T(8,128)S(1)}, u32[]{:S(2)}, u32[]{:S(2)}) collective-permute-start(f32[32,512]{1,0:T(8,128)S(1)} %get-tuple-element.20), channel_id=1, source_target_pairs={{4,20},{12,28},{20,4},{28,12},{5,21},{13,29},{21,5},{29,13},{6,22}... | collective-permute-start | bytes 196616 | tf_op jit(solution)/shard_map/ppermute | solution.py:347
  8.9 1.8 %local_convolutions.3 = (f32[2,32,8,128]{3,2,1,0:T(8,128)S(1)}, f32[2,32,8,128]{3,2,1,0:T(8,128)S(1)}) custom-call(bf16[256,512]{1,0:T(8,128)(2,1)S(1)} %copy-done.1, bf16[256,512]{1,0:T(8,128)(2,1)S(1)} %copy-done.2, f32[16,512]{1,0:T(8,128)S(1)} %copy-done.3, f32[16,512]{1,0:T(8,128)S(1)} %copy-done, f32[48,512]{1,0:T(8,128)S(1)} %get-tuple-element.19._.segment), custom_call_target="tpu_custom_call" | custom-call | flops 419430400 | bytes 786432 | tf_op jit(solution)/shard_map/local_convolutions/pallas_call | solution.py:325
  10.8 0.0 collective-permute-done.2.other
  10.8 0.7 %collective-permute-start.6 = (f32[16,512]{1,0:T(8,128)S(1)}, f32[16,512]{1,0:T(8,128)S(1)}, u32[]{:S(2)}, u32[]{:S(2)}) collective-permute-start(f32[16,512]{1,0:T(8,128)S(1)} %get-tuple-element.28), channel_id=1, source_target_pairs={{4,7},{5,6},{6,5},{7,4},{12,15},{13,14},{14,13},{15,12},{20,23},{2... | collective-permute-start | bytes 98312 | tf_op jit(solution)/shard_map/ppermute | solution.py:373
  11.5 0.7 %collective-permute-start.5 = (f32[16,512]{1,0:T(8,128)S(1)}, f32[16,512]{1,0:T(8,128)S(1)}, u32[]{:S(2)}, u32[]{:S(2)}) collective-permute-start(f32[16,512]{1,0:T(8,128)S(1)} %get-tuple-element.28), channel_id=1, source_target_pairs={{4,6},{5,7},{6,4},{7,5},{12,14},{13,15},{14,12},{15,13},{20,22},{2... | collective-permute-start | bytes 98312 | tf_op jit(solution)/shard_map/ppermute | solution.py:373
  12.2 0.7 %collective-permute-start.4 = (f32[16,512]{1,0:T(8,128)S(1)}, f32[16,512]{1,0:T(8,128)S(1)}, u32[]{:S(2)}, u32[]{:S(2)}) collective-permute-start(f32[16,512]{1,0:T(8,128)S(1)} %get-tuple-element.28), channel_id=1, source_target_pairs={{4,5},{5,4},{6,7},{7,6},{12,13},{13,12},{14,15},{15,14},{20,21},{2... | collective-permute-start | bytes 98312 | tf_op jit(solution)/shard_map/ppermute | solution.py:373
  12.8 0.0 collective-permute-done.6
  12.8 0.0 collective-permute-done.5
  12.9 0.0 collective-permute-done.4
  12.9 1.3 %collective-permute-start.7 = (f32[16,512]{1,0:T(8,128)S(1)}, f32[16,512]{1,0:T(8,128)S(1)}, u32[]{:S(2)}, u32[]{:S(2)}) collective-permute-start(f32[16,512]{1,0:T(8,128)S(1)} %add_add_fusion), channel_id=1, source_target_pairs={{4,0},{12,8},{20,16},{28,24},{5,1},{13,9},{21,17},{29,25},{6,2},{1... | collective-permute-start | bytes 98312 | tf_op jit(solution)/shard_map/ppermute | solution.py:384
  14.2 1.3 %collective-permute-start.3 = (f32[32,512]{1,0:T(8,128)S(1)}, f32[32,512]{1,0:T(8,128)S(1)}, u32[]{:S(2)}, u32[]{:S(2)}) collective-permute-start(f32[32,512]{1,0:T(8,128)S(1)} %get-tuple-element.23.chip), channel_id=1, source_target_pairs={{4,0},{12,8},{20,16},{28,24},{5,1},{13,9},{21,17},{29,25},{6,2},{1... | collective-permute-start | bytes 196616 | tf_op jit(solution)/shard_map/ppermute | solution.py:368
  15.5 16.0 %collective-permute-done.7 = f32[16,512]{1,0:T(8,128)S(1)} collective-permute-done((f32[16,512]{1,0:T(8,128)S(1)}, f32[16,512]{1,0:T(8,128)S(1)}, u32[]{:S(2)}, u32[]{:S(2)}) %collective-permute-start.7) | collective-permute-done | bytes 32800 | tf_op jit(solution)/shard_map/ppermute | solution.py:384
  31.5 0.6 %select_multiply_fusion = f32[16,512]{1,0:T(8,128)} fusion(f32[16,512]{1,0:T(8,128)S(1)} %add_add_fusion, f32[16,512]{1,0:T(8,128)S(1)} %collective-permute-done.7, pred[]{:T(512)S(6)} %eq.3), kind=kLoop, calls=%fused_computation | loop fusion | flops 16384 | bytes 98305 | tf_op jit(solution)/shard_map/div | solution.py:386
  32.1 0.7 %collective-permute-done.3.received = f32[32,512]{1,0:T(8,128)S(1)} collective-permute-done((f32[32,512]{1,0:T(8,128)S(1)}, f32[32,512]{1,0:T(8,128)S(1)}, u32[]{:S(2)}, u32[]{:S(2)}) %collective-permute-start.3) | collective-permute-done | bytes 65568 | tf_op jit(solution)/shard_map/ppermute | solution.py:368
  32.8 2.6 %add_arrivals.1 = (bf16[256,512]{1,0:T(8,128)(2,1)}, bf16[256,512]{1,0:T(8,128)(2,1)}) custom-call(f32[16,512]{1,0:T(8,128)S(1)} %copy-done.3, f32[16,512]{1,0:T(8,128)S(1)} %copy-done, f32[32,512]{1,0:T(8,128)S(1)} %get-tuple-element.16.core, f32[32,512]{1,0:T(8,128)S(1)} %get-tuple-element.23.chip, f32[32,512]{1,0:T(8,128)S(1)} %collective-permute-done.3.received, ...), custom_call_target="tpu_custom_call" | custom-call | flops 1258291200 | bytes 1572864 | tf_op jit(solution)/shard_map/add_arrivals/pallas_call | solution.py:388
  (5 shorter events, 0.1 us)
Async XLA Ops:
  0.6 5.0 %copy-start = (f32[16,512]{1,0:T(8,128)S(1)}, f32[16,512]{1,0:T(8,128)}, u32[]{:S(2)}) copy-start(f32[16,512]{1,0:T(8,128)} %decay_ref.11) | copy-start | bytes 98308
  0.6 5.7 %copy-start.2 = (bf16[256,512]{1,0:T(8,128)(2,1)S(1)}, bf16[256,512]{1,0:T(8,128)(2,1)}, u32[]{:S(2)}) copy-start(bf16[256,512]{1,0:T(8,128)(2,1)} %g_ref.3) | copy-start | bytes 786436
  4.2 2.2 %copy-start.1 = (bf16[256,512]{1,0:T(8,128)(2,1)S(1)}, bf16[256,512]{1,0:T(8,128)(2,1)}, u32[]{:S(2)}) copy-start(bf16[256,512]{1,0:T(8,128)(2,1)} %x_ref.3) | copy-start | bytes 786436
  4.2 1.5 %collective-permute-start = (f32[48,512]{1,0:T(8,128)S(1)}, f32[48,512]{1,0:T(8,128)S(1)}, u32[]{:S(2)}, u32[]{:S(2)}) collective-permute-start(f32[48,512]{1,0:T(8,128)S(1)} %block_states.1.segment._), channel_id=1, source_target_pairs={{0,4},{4,0},{8,12},{12,8},{16,20},{20,16},{24,28},{28,24},{1,5},{5... | collective-permute-start | bytes 294920 | tf_op jit(solution)/shard_map/ppermute | solution.py:347
  5.6 0.8 %copy-start.3 = (f32[16,512]{1,0:T(8,128)S(1)}, f32[16,512]{1,0:T(8,128)}, u32[]{:S(2)}) copy-start(f32[16,512]{1,0:T(8,128)} %residue_ref.5) | copy-start | bytes 98308
  5.7 2.5 %collective-permute-start.1 = (f32[48,512]{1,0:T(8,128)S(1)}, f32[48,512]{1,0:T(8,128)S(1)}, u32[]{:S(2)}, u32[]{:S(2)}) collective-permute-start(f32[48,512]{1,0:T(8,128)S(1)} %get-tuple-element.17._.segment), channel_id=1, source_target_pairs={{4,12},{12,4},{20,28},{28,20},{5,13},{13,5},{21,29},{29,21},{6,14}... | collective-permute-start | bytes 294920 | tf_op jit(solution)/shard_map/ppermute | solution.py:347
  8.3 2.5 %collective-permute-start.2 = (f32[32,512]{1,0:T(8,128)S(1)}, f32[32,512]{1,0:T(8,128)S(1)}, u32[]{:S(2)}, u32[]{:S(2)}) collective-permute-start(f32[32,512]{1,0:T(8,128)S(1)} %get-tuple-element.20), channel_id=1, source_target_pairs={{4,20},{12,28},{20,4},{28,12},{5,21},{13,29},{21,5},{29,13},{6,22}... | collective-permute-start | bytes 196616 | tf_op jit(solution)/shard_map/ppermute | solution.py:347
  10.8 2.0 %collective-permute-start.6 = (f32[16,512]{1,0:T(8,128)S(1)}, f32[16,512]{1,0:T(8,128)S(1)}, u32[]{:S(2)}, u32[]{:S(2)}) collective-permute-start(f32[16,512]{1,0:T(8,128)S(1)} %get-tuple-element.28), channel_id=1, source_target_pairs={{4,7},{5,6},{6,5},{7,4},{12,15},{13,14},{14,13},{15,12},{20,23},{2... | collective-permute-start | bytes 98312 | tf_op jit(solution)/shard_map/ppermute | solution.py:373
  11.5 1.4 %collective-permute-start.5 = (f32[16,512]{1,0:T(8,128)S(1)}, f32[16,512]{1,0:T(8,128)S(1)}, u32[]{:S(2)}, u32[]{:S(2)}) collective-permute-start(f32[16,512]{1,0:T(8,128)S(1)} %get-tuple-element.28), channel_id=1, source_target_pairs={{4,6},{5,7},{6,4},{7,5},{12,14},{13,15},{14,12},{15,13},{20,22},{2... | collective-permute-start | bytes 98312 | tf_op jit(solution)/shard_map/ppermute | solution.py:373
  12.2 0.7 %collective-permute-start.4 = (f32[16,512]{1,0:T(8,128)S(1)}, f32[16,512]{1,0:T(8,128)S(1)}, u32[]{:S(2)}, u32[]{:S(2)}) collective-permute-start(f32[16,512]{1,0:T(8,128)S(1)} %get-tuple-element.28), channel_id=1, source_target_pairs={{4,5},{5,4},{6,7},{7,6},{12,13},{13,12},{14,15},{15,14},{20,21},{2... | collective-permute-start | bytes 98312 | tf_op jit(solution)/shard_map/ppermute | solution.py:373
  12.9 18.6 %collective-permute-start.7 = (f32[16,512]{1,0:T(8,128)S(1)}, f32[16,512]{1,0:T(8,128)S(1)}, u32[]{:S(2)}, u32[]{:S(2)}) collective-permute-start(f32[16,512]{1,0:T(8,128)S(1)} %add_add_fusion), channel_id=1, source_target_pairs={{4,0},{12,8},{20,16},{28,24},{5,1},{13,9},{21,17},{29,25},{6,2},{1... | collective-permute-start | bytes 98312 | tf_op jit(solution)/shard_map/ppermute | solution.py:384
  14.2 18.6 %collective-permute-start.3 = (f32[32,512]{1,0:T(8,128)S(1)}, f32[32,512]{1,0:T(8,128)S(1)}, u32[]{:S(2)}, u32[]{:S(2)}) collective-permute-start(f32[32,512]{1,0:T(8,128)S(1)} %get-tuple-element.23.chip), channel_id=1, source_target_pairs={{4,0},{12,8},{20,16},{28,24},{5,1},{13,9},{21,17},{29,25},{6,2},{1... | collective-permute-start | bytes 196616 | tf_op jit(solution)/shard_map/ppermute | solution.py:368

commit v5 on v4

--- a/solution.py
+++ b/solution.py
@@ -217,7 +217,7 @@
 
 def finish_kernel(ranges, residue_ref, decay_ref, core, chip, received, *refs):
     near = refs[:2 * len(ranges)]
-    out_hbm, back_hbm, out_ref, back_ref, result, pw, arrive, leave, sems = refs[2 * len(ranges):]
+    out_hbm, back_hbm, finished, out_ref, back_ref, result, pw, arrive, leave, sems = refs[2 * len(ranges):]
     modes, channels = decay_ref.shape
     chunks = near[0].shape[1] // SUB
     span = chunks * SUB
@@ -273,6 +273,7 @@
     for tile in range(channels // LANES):
         for which in range(2):
             copy_out(tile, which).wait()
+    finished[...] = jnp.zeros(finished.shape, F32)
 
 
 def vmem(*shape):
@@ -336,9 +337,7 @@
         )(signal, cotangent, residue, decay, after)
 
     def pairs(shift):
-        return [(i, i ^ shift) for i in range(n) if shift == 1 or i % 2]
-
-    to_first = [(i, i - 1) for i in range(n) if i % 2]
+        return [(i, i ^ shift if shift == 1 or i % 2 else i) for i in range(n)]
 
     near = []
     carried = jnp.zeros((SUB, LANES), F32)
@@ -364,32 +363,21 @@
         else:
             carried = arrivals
 
-    grad = segment
-    received = lax.ppermute(carried, "ctx", to_first)
-    stride = 1
-    while stride < groups:
-        count = min(4, groups // stride)
-        terms = [grad] + [
-            lax.ppermute(
-                grad,
-                ("ctx", "ch"),
-                [(i * groups + k, i * groups + (k ^ (stride * m))) for i in range(n) if i % 2 for k in range(groups)],
-            )
-            for m in range(1, count)
-        ]
+    received = lax.ppermute(carried, "ctx", pairs(1))
+
+    def summed(*terms):
         while len(terms) > 1:
             terms = [a + b for a, b in zip(terms[::2], terms[1::2])]
-        grad = terms[0]
-        stride *= count
-    other = lax.ppermute(grad, "ctx", to_first)
-    second = lax.rem(lax.axis_index("ctx"), 2) == 1
-    residue_grad = jnp.where(second, grad, other) / (tokens * n)
-
-    conv_out, signal_grad = pl.pallas_call(
+        return terms[0]
+
+    def sum_kernel(*refs):
+        refs[-1][...] = summed(*(ref[...] for ref in refs[:-2]))
+
+    conv_out, signal_grad, finished = pl.pallas_call(
         functools.partial(finish_kernel, ranges),
-        out_shape=[jax.ShapeDtypeStruct((tokens, channels), signal.dtype)] * 2,
+        out_shape=[jax.ShapeDtypeStruct((tokens, channels), signal.dtype)] * 2 + [shaped(SUB, LANES)],
         in_specs=[WHOLE] * (5 + 2 * PARTS),
-        out_specs=[HBM] * 2,
+        out_specs=[HBM] * 2 + [WHOLE],
         scratch_shapes=[pltpu.VMEM((tokens, channels), signal.dtype)] * 2
         + [vmem(tokens, LANES), vmem(5, modes, LANES)]
         + [vmem(modes, channels)] * 2
@@ -398,6 +386,31 @@
         cost_estimate=cost(elements * modes * 600, 0, elements * 12),
         name="add_arrivals",
     )(residue, decay, from_core, carried, received, *near)
+
+    grad = segment
+    stride = 1
+    while stride < groups:
+        count = min(4, groups // stride)
+        terms = [grad] + [
+            lax.ppermute(
+                grad,
+                ("ctx", "ch"),
+                [(i * groups + k, i * groups + (k ^ (stride * m if i % 2 else 0))) for i in range(n) for k in range(groups)],
+            )
+            for m in range(1, count)
+        ]
+        grad = pl.pallas_call(
+            sum_kernel,
+            out_shape=shaped(modes, channels),
+            in_specs=[WHOLE] * count + [UNREAD],
+            compiler_params=PARAMS,
+            cost_estimate=cost(modes * channels * count, 0, modes * channels * 4 * count),
+            name="sum_groups",
+        )(*terms, finished)
+        stride *= count
+    other = lax.ppermute(grad, "ctx", pairs(1))
+    second = lax.rem(lax.axis_index("ctx"), 2) == 1
+    residue_grad = jnp.where(second, grad, other) / (tokens * n)
     return conv_out, signal_grad, residue_grad
 
 

time: 35.7 us -> 33.5 us (0.938)
  waiting for transfers between devices: 17.6 us -> 1.82 us
  starting transfers between devices: 6.42 us -> 20 us
    ppermute x5, waiting for transfers between devices: 16.7 us -> 0.87 us  [the longest x1 0.86 us: body(): other = lax.ppermute(grad, 'ctx', pairs(1))]
    ppermute x5, starting transfers between devices: 4.57 us -> 18.2 us  [the longest x1 9.32 us: body(): other = lax.ppermute(grad, 'ctx', pairs(1))]
  transfers between devices with their start and end apart: 8 -> 8, of which waited for: 3 -> 2; matrix products, arithmetic and copies ran while one was open for 2% -> 0% of each run, Pallas kernels for 10% -> 19%
where the time goes in v5:
time: 33.5 us; the launch traced here: 33.2 us
  starting transfers between devices  20 us (60%)
  Pallas kernels  9.87 us (29%)
  waiting for transfers between devices  1.82 us (5%)
  between operations  0.82 us (2%)
  other arithmetic  0.62 us (2%)
    ppermute x1, starting transfers between devices, body(): other = lax.ppermute(grad, 'ctx', pairs(1))  9.32 us
    ppermute x1, starting transfers between devices, body(): received = lax.ppermute(carried, 'ctx', pairs(1))  6.86 us
    pallas_call x2, Pallas kernels, near_part(): pl.pallas_call(functools.partial(local_kernel, ranges[part]), out_shape=[...  3.62 us
    pallas_call x1, Pallas kernels, body(): pl.pallas_call(gather_kernel, out_shape=shaped(3 * modes, channels), in_s...  3.5 us
    pallas_call x1, Pallas kernels, body(): pl.pallas_call(functools.partial(finish_kernel, ranges), out_shape=[jax.S...  2.61 us
    ppermute x3, starting transfers between devices, body(): lax.ppermute(grad, ('ctx', 'ch'), [(i * groups + k, i * groups + (k ^ (st...  1.98 us
    ppermute x3, starting transfers between devices, body(): other = lax.ppermute(message, 'ctx', pairs(1 << bit))  1.85 us
    ppermute x3, waiting for transfers between devices, body(): other = lax.ppermute(message, 'ctx', pairs(1 << bit))  0.95 us
  transfers between devices with their start and end apart: 8, of which 2 were waited for; matrix products, arithmetic and copies ran while one was open for 0% of the time, Pallas kernels for 19%

profile of v5, /device:TPU:0, one launch (start us, length us, event | category | flops | bytes accessed | tf_op | source)
XLA Modules:
  0.0 33.2 jit_solution(15588727691280399435)
XLA Ops:
  0.6 0.0 copy-start
  0.6 0.0 copy-start.2
  0.7 3.5 %block_states.1.segment._ = f32[48,512]{1,0:T(8,128)S(1)} custom-call(bf16[256,512]{1,0:T(8,128)(2,1)} %x_ref.3, bf16[256,512]{1,0:T(8,128)(2,1)} %g_ref.3, f32[16,512]{1,0:T(8,128)} %decay_ref.11), custom_call_target="tpu_custom_call" | custom-call | flops 10485760 | bytes 786432 | tf_op jit(solution)/shard_map/block_states/pallas_call | solution.py:312
  4.2 0.0 copy-start.1
  4.2 0.5 %collective-permute-start = (f32[48,512]{1,0:T(8,128)S(1)}, f32[48,512]{1,0:T(8,128)S(1)}, u32[]{:S(2)}, u32[]{:S(2)}) collective-permute-start(f32[48,512]{1,0:T(8,128)S(1)} %block_states.1.segment._), channel_id=1, source_target_pairs={{0,4},{4,0},{8,12},{12,8},{16,20},{20,16},{24,28},{28,24},{1,5},{5... | collective-permute-start | bytes 294920 | tf_op jit(solution)/shard_map/ppermute | solution.py:346
  4.7 0.9 %collective-permute-done.other = f32[48,512]{1,0:T(8,128)S(1)} collective-permute-done((f32[48,512]{1,0:T(8,128)S(1)}, f32[48,512]{1,0:T(8,128)S(1)}, u32[]{:S(2)}, u32[]{:S(2)}) %collective-permute-start) | collective-permute-done | bytes 98336 | tf_op jit(solution)/shard_map/ppermute | solution.py:346
  5.6 0.0 copy-done
  5.6 0.0 copy-start.3
  5.7 0.7 %collective-permute-start.1 = (f32[48,512]{1,0:T(8,128)S(1)}, f32[48,512]{1,0:T(8,128)S(1)}, u32[]{:S(2)}, u32[]{:S(2)}) collective-permute-start(f32[48,512]{1,0:T(8,128)S(1)} %get-tuple-element.18._.segment), channel_id=1, source_target_pairs={{0,0},{4,12},{8,8},{12,4},{16,16},{20,28},{24,24},{28,20},{1,1},{5... | collective-permute-start | bytes 294920 | tf_op jit(solution)/shard_map/ppermute | solution.py:346
  6.3 0.0 copy-done.2
  6.4 0.0 copy-done.1
  6.4 0.0 copy-done.3
  6.4 1.8 %local_convolutions.2 = (f32[2,32,8,128]{3,2,1,0:T(8,128)S(1)}, f32[2,32,8,128]{3,2,1,0:T(8,128)S(1)}) custom-call(bf16[256,512]{1,0:T(8,128)(2,1)S(1)} %copy-done.1, bf16[256,512]{1,0:T(8,128)(2,1)S(1)} %copy-done.2, f32[16,512]{1,0:T(8,128)S(1)} %copy-done.3, f32[16,512]{1,0:T(8,128)S(1)} %copy-done, f32[48,512]{1,0:T(8,128)S(1)} %get-tuple-element.18._.segment), custom_call_target="tpu_custom_call" | custom-call | flops 419430400 | bytes 786432 | tf_op jit(solution)/shard_map/local_convolutions/pallas_call | solution.py:326
  8.2 0.0 collective-permute-done.1.other
  8.3 0.7 %collective-permute-start.2 = (f32[32,512]{1,0:T(8,128)S(1)}, f32[32,512]{1,0:T(8,128)S(1)}, u32[]{:S(2)}, u32[]{:S(2)}) collective-permute-start(f32[32,512]{1,0:T(8,128)S(1)} %get-tuple-element.21), channel_id=1, source_target_pairs={{0,0},{4,20},{8,8},{12,28},{16,16},{20,4},{24,24},{28,12},{1,1},{5... | collective-permute-start | bytes 196616 | tf_op jit(solution)/shard_map/ppermute | solution.py:346
  8.9 1.8 %local_convolutions.3 = (f32[2,32,8,128]{3,2,1,0:T(8,128)S(1)}, f32[2,32,8,128]{3,2,1,0:T(8,128)S(1)}) custom-call(bf16[256,512]{1,0:T(8,128)(2,1)S(1)} %copy-done.1, bf16[256,512]{1,0:T(8,128)(2,1)S(1)} %copy-done.2, f32[16,512]{1,0:T(8,128)S(1)} %copy-done.3, f32[16,512]{1,0:T(8,128)S(1)} %copy-done, f32[48,512]{1,0:T(8,128)S(1)} %get-tuple-element.20._.segment), custom_call_target="tpu_custom_call" | custom-call | flops 419430400 | bytes 786432 | tf_op jit(solution)/shard_map/local_convolutions/pallas_call | solution.py:326
  10.8 0.0 collective-permute-done.2.other
  10.8 6.9 %collective-permute-start.3 = (f32[32,512]{1,0:T(8,128)S(1)}, f32[32,512]{1,0:T(8,128)S(1)}, u32[]{:S(2)}, u32[]{:S(2)}) collective-permute-start(f32[32,512]{1,0:T(8,128)S(1)} %get-tuple-element.24.chip), channel_id=1, source_target_pairs={{0,4},{4,0},{8,12},{12,8},{16,20},{20,16},{24,28},{28,24},{1,5},{5... | collective-permute-start | bytes 196616 | tf_op jit(solution)/shard_map/ppermute | solution.py:366
  17.7 0.7 %collective-permute-start.4 = (f32[16,512]{1,0:T(8,128)S(1)}, f32[16,512]{1,0:T(8,128)S(1)}, u32[]{:S(2)}, u32[]{:S(2)}) collective-permute-start(f32[16,512]{1,0:T(8,128)S(1)} %get-tuple-element.29.refs_0_), channel_id=1, source_target_pairs={{0,0},{1,1},{2,2},{3,3},{4,5},{5,4},{6,7},{7,6},{8,8},{9,9},{10,10... | collective-permute-start | bytes 98312 | tf_op jit(solution)/shard_map/ppermute | solution.py:395
  18.3 0.7 %collective-permute-start.5 = (f32[16,512]{1,0:T(8,128)S(1)}, f32[16,512]{1,0:T(8,128)S(1)}, u32[]{:S(2)}, u32[]{:S(2)}) collective-permute-start(f32[16,512]{1,0:T(8,128)S(1)} %get-tuple-element.29.refs_0_), channel_id=1, source_target_pairs={{0,0},{1,1},{2,2},{3,3},{4,6},{5,7},{6,4},{7,5},{8,8},{9,9},{10,10... | collective-permute-start | bytes 98312 | tf_op jit(solution)/shard_map/ppermute | solution.py:395
  19.0 0.7 %collective-permute-start.6 = (f32[16,512]{1,0:T(8,128)S(1)}, f32[16,512]{1,0:T(8,128)S(1)}, u32[]{:S(2)}, u32[]{:S(2)}) collective-permute-start(f32[16,512]{1,0:T(8,128)S(1)} %get-tuple-element.29.refs_0_), channel_id=1, source_target_pairs={{0,0},{1,1},{2,2},{3,3},{4,7},{5,6},{6,5},{7,4},{8,8},{9,9},{10,10... | collective-permute-start | bytes 98312 | tf_op jit(solution)/shard_map/ppermute | solution.py:395
  19.7 0.0 collective-permute-done.3.received
  19.7 2.6 %add_arrivals.1 = (bf16[256,512]{1,0:T(8,128)(2,1)}, bf16[256,512]{1,0:T(8,128)(2,1)}, f32[8,128]{1,0:T(8,128)S(1)}) custom-call(f32[16,512]{1,0:T(8,128)S(1)} %copy-done.3, f32[16,512]{1,0:T(8,128)S(1)} %copy-done, f32[32,512]{1,0:T(8,128)S(1)} %get-tuple-element.17.core, f32[32,512]{1,0:T(8,128)S(1)} %get-tuple-element.24.chip, ...), custom_call_target="tpu_custom_call" | custom-call | flops 1258291200 | bytes 1572864 | tf_op jit(solution)/shard_map/add_arrivals/pallas_call | solution.py:376
  22.3 0.0 collective-permute-done.4.refs_1_
  22.3 0.0 collective-permute-done.5.refs_2_
  22.3 0.0 collective-permute-done.6.refs_3_
  22.4 9.3 %collective-permute-start.7 = (f32[16,512]{1,0:T(8,128)S(1)}, f32[16,512]{1,0:T(8,128)S(1)}, u32[]{:S(2)}, u32[]{:S(2)}) collective-permute-start(f32[16,512]{1,0:T(8,128)S(1)} %sum_groups.1), channel_id=1, source_target_pairs={{0,4},{4,0},{8,12},{12,8},{16,20},{20,16},{24,28},{28,24},{1,5},{5... | collective-permute-start | bytes 98312 | tf_op jit(solution)/shard_map/ppermute | solution.py:411
  31.7 0.9 %collective-permute-done.7 = f32[16,512]{1,0:T(8,128)S(1)} collective-permute-done((f32[16,512]{1,0:T(8,128)S(1)}, f32[16,512]{1,0:T(8,128)S(1)}, u32[]{:S(2)}, u32[]{:S(2)}) %collective-permute-start.7) | collective-permute-done | bytes 32800 | tf_op jit(solution)/shard_map/ppermute | solution.py:411
  32.6 0.6 %select_multiply_fusion = f32[16,512]{1,0:T(8,128)} fusion(f32[16,512]{1,0:T(8,128)S(1)} %sum_groups.1, f32[16,512]{1,0:T(8,128)S(1)} %collective-permute-done.7, pred[]{:T(512)S(6)} %eq.3), kind=kLoop, calls=%fused_computation | loop fusion | flops 16384 | bytes 98305 | tf_op jit(solution)/shard_map/div | solution.py:413
  (5 shorter events, 0.1 us)
Async XLA Ops:
  0.6 5.0 %copy-start = (f32[16,512]{1,0:T(8,128)S(1)}, f32[16,512]{1,0:T(8,128)}, u32[]{:S(2)}) copy-start(f32[16,512]{1,0:T(8,128)} %decay_ref.11) | copy-start | bytes 98308
  0.6 5.7 %copy-start.2 = (bf16[256,512]{1,0:T(8,128)(2,1)S(1)}, bf16[256,512]{1,0:T(8,128)(2,1)}, u32[]{:S(2)}) copy-start(bf16[256,512]{1,0:T(8,128)(2,1)} %g_ref.3) | copy-start | bytes 786436
  4.2 2.2 %copy-start.1 = (bf16[256,512]{1,0:T(8,128)(2,1)S(1)}, bf16[256,512]{1,0:T(8,128)(2,1)}, u32[]{:S(2)}) copy-start(bf16[256,512]{1,0:T(8,128)(2,1)} %x_ref.3) | copy-start | bytes 786436
  4.2 1.5 %collective-permute-start = (f32[48,512]{1,0:T(8,128)S(1)}, f32[48,512]{1,0:T(8,128)S(1)}, u32[]{:S(2)}, u32[]{:S(2)}) collective-permute-start(f32[48,512]{1,0:T(8,128)S(1)} %block_states.1.segment._), channel_id=1, source_target_pairs={{0,4},{4,0},{8,12},{12,8},{16,20},{20,16},{24,28},{28,24},{1,5},{5... | collective-permute-start | bytes 294920 | tf_op jit(solution)/shard_map/ppermute | solution.py:346
  5.6 0.8 %copy-start.3 = (f32[16,512]{1,0:T(8,128)S(1)}, f32[16,512]{1,0:T(8,128)}, u32[]{:S(2)}) copy-start(f32[16,512]{1,0:T(8,128)} %residue_ref.5) | copy-start | bytes 98308
  5.7 2.5 %collective-permute-start.1 = (f32[48,512]{1,0:T(8,128)S(1)}, f32[48,512]{1,0:T(8,128)S(1)}, u32[]{:S(2)}, u32[]{:S(2)}) collective-permute-start(f32[48,512]{1,0:T(8,128)S(1)} %get-tuple-element.18._.segment), channel_id=1, source_target_pairs={{0,0},{4,12},{8,8},{12,4},{16,16},{20,28},{24,24},{28,20},{1,1},{5... | collective-permute-start | bytes 294920 | tf_op jit(solution)/shard_map/ppermute | solution.py:346
  8.3 2.5 %collective-permute-start.2 = (f32[32,512]{1,0:T(8,128)S(1)}, f32[32,512]{1,0:T(8,128)S(1)}, u32[]{:S(2)}, u32[]{:S(2)}) collective-permute-start(f32[32,512]{1,0:T(8,128)S(1)} %get-tuple-element.21), channel_id=1, source_target_pairs={{0,0},{4,20},{8,8},{12,28},{16,16},{20,4},{24,24},{28,12},{1,1},{5... | collective-permute-start | bytes 196616 | tf_op jit(solution)/shard_map/ppermute | solution.py:346
  10.8 8.9 %collective-permute-start.3 = (f32[32,512]{1,0:T(8,128)S(1)}, f32[32,512]{1,0:T(8,128)S(1)}, u32[]{:S(2)}, u32[]{:S(2)}) collective-permute-start(f32[32,512]{1,0:T(8,128)S(1)} %get-tuple-element.24.chip), channel_id=1, source_target_pairs={{0,4},{4,0},{8,12},{12,8},{16,20},{20,16},{24,28},{28,24},{1,5},{5... | collective-permute-start | bytes 196616 | tf_op jit(solution)/shard_map/ppermute | solution.py:366
  17.7 4.6 %collective-permute-start.4 = (f32[16,512]{1,0:T(8,128)S(1)}, f32[16,512]{1,0:T(8,128)S(1)}, u32[]{:S(2)}, u32[]{:S(2)}) collective-permute-start(f32[16,512]{1,0:T(8,128)S(1)} %get-tuple-element.29.refs_0_), channel_id=1, source_target_pairs={{0,0},{1,1},{2,2},{3,3},{4,5},{5,4},{6,7},{7,6},{8,8},{9,9},{10,10... | collective-permute-start | bytes 98312 | tf_op jit(solution)/shard_map/ppermute | solution.py:395
  18.3 4.0 %collective-permute-start.5 = (f32[16,512]{1,0:T(8,128)S(1)}, f32[16,512]{1,0:T(8,128)S(1)}, u32[]{:S(2)}, u32[]{:S(2)}) collective-permute-start(f32[16,512]{1,0:T(8,128)S(1)} %get-tuple-element.29.refs_0_), channel_id=1, source_target_pairs={{0,0},{1,1},{2,2},{3,3},{4,6},{5,7},{6,4},{7,5},{8,8},{9,9},{10,10... | collective-permute-start | bytes 98312 | tf_op jit(solution)/shard_map/ppermute | solution.py:395
  19.0 3.3 %collective-permute-start.6 = (f32[16,512]{1,0:T(8,128)S(1)}, f32[16,512]{1,0:T(8,128)S(1)}, u32[]{:S(2)}, u32[]{:S(2)}) collective-permute-start(f32[16,512]{1,0:T(8,128)S(1)} %get-tuple-element.29.refs_0_), channel_id=1, source_target_pairs={{0,0},{1,1},{2,2},{3,3},{4,7},{5,6},{6,5},{7,4},{8,8},{9,9},{10,10... | collective-permute-start | bytes 98312 | tf_op jit(solution)/shard_map/ppermute | solution.py:395
  22.4 10.2 %collective-permute-start.7 = (f32[16,512]{1,0:T(8,128)S(1)}, f32[16,512]{1,0:T(8,128)S(1)}, u32[]{:S(2)}, u32[]{:S(2)}) collective-permute-start(f32[16,512]{1,0:T(8,128)S(1)} %sum_groups.1), channel_id=1, source_target_pairs={{0,4},{4,0},{8,12},{12,8},{16,20},{20,16},{24,28},{28,24},{1,5},{5... | collective-permute-start | bytes 98312 | tf_op jit(solution)/shard_map/ppermute | solution.py:411

commit v6 on v5

--- a/solution.py
+++ b/solution.py
@@ -55,7 +55,7 @@
     return scratch[pl.ds(half * SUB * SUB + j, SUB, stride=SUB), :]
 
 
-def gather_kernel(x_hbm, g_hbm, decay_hbm, segment, *refs):
+def gather_kernel(x_hbm, g_hbm, decay_hbm, segment, message, *refs):
     xf, gf, pw, ends, starts, inner, x_ref, g_ref, decay_ref, sems = refs
     copies = [
         pltpu.make_async_copy(source, target, sems.at[i])
@@ -104,6 +104,26 @@
         return 0
 
     lax.fori_loop(0, channels // LANES, tile_step, 0)
+
+
+    second = on_second()
+    half = modes // 2
+    for i in range(3):
+        low, high = segment[pl.ds(i * modes, half)], segment[pl.ds(i * modes + half, half)]
+        message[pl.ds(i * half, half)] = jnp.where(second, low, high)
+
+
+def on_second():
+    return lax.rem(lax.axis_index("ctx"), 2) == 1
+
+
+def own_half(second, values):
+    half = values.shape[0] // 2
+    return jnp.where(second, values[half:], values[:half])
+
+
+def both_halves(second, own, other):
+    return jnp.where(second, other, own), jnp.where(second, own, other)
 
 
 def local_kernel(tiles, x_ref, g_ref, residue_ref, decay_ref, _, out_ref, back_ref,
@@ -172,63 +192,83 @@
     lax.fori_loop(tiles[0], tiles[1], tile_step, 0)
 
 
-def join_kernel(tokens, bit, last, segment, other, decay_ref, carried, _, arrivals, joined, *message):
+def join_chip_kernel(tokens, segment, other, decay_ref, _, joined, core):
     modes = decay_ref.shape[0]
-    place = lax.axis_index("ctx")
-    size = 1 << bit
-    late = lax.rem(lax.div(place, size), 2) == 1
-    decay = decay_ref[...]
-    parts = [slice(i * modes, (i + 1) * modes) for i in range(3)]
-    compact = other.shape[0] == 2 * modes
-    close, begin, grad = (segment[rows] for rows in parts)
-    their_close = other[parts[0]]
-    their_begin = other[parts[0 if compact else 1]]
-    their_grad = other[parts[1 if compact else 2]]
-    first = jnp.where(late, their_close, 0.0)
-    second = jnp.where(late, 0.0, their_begin)
-    if bit:
-        inside = lax.rem(place, size)
-        inside = inside - lax.rem(inside, 2)
-        between = (jnp.where(late, inside, size - 2 - inside) * tokens).astype(F32)
-        reach = jnp.exp(decay * -between)
-        first, second = reach * first, reach * second
-    if bit > 1:
-        first = first + carried[0:modes]
-        second = second + carried[modes:]
-    arrivals[0:modes] = first
-    arrivals[modes:] = second
-    early_close = jnp.where(late, their_close, close)
-    late_begin = jnp.where(late, begin, their_begin)
-    grad = (grad + their_grad) + jnp.exp(-decay) * late_begin * early_close
-    if last:
-        joined[...] = grad
+    half = modes // 2
+    second = on_second()
+    decay = own_half(second, decay_ref[...])
+    mine = [own_half(second, segment[i * modes:(i + 1) * modes]) for i in range(3)]
+    theirs = [other[i * half:(i + 1) * half] for i in range(3)]
+    (close0, close1), (open0, open1), _ = (both_halves(second, a, b) for a, b in zip(mine, theirs))
+    block = jnp.exp(decay * (-1.0 * tokens))
+    joined[0:half] = block * close0 + close1
+    joined[half:2 * half] = open0 + block * open1
+    joined[2 * half:] = (mine[2] + theirs[2]) + jnp.exp(-decay) * open1 * close0
+    core[0:half] = close0
+    core[half:] = open1
+
+
+def join_kernel(tokens, size, count, last, *refs):
+    segments = refs[:count]
+    core, decay_ref, carried, _ = refs[count:count + 4]
+    *outs, ordered = refs[count + 4:]
+    second = on_second()
+    decay = own_half(second, decay_ref[...])
+    half = decay.shape[0]
+    chip = lax.div(lax.axis_index("ctx"), 2)
+    place = lax.rem(lax.div(chip, size), count)
+    for m in range(count):
+        ordered[place ^ m] = segments[m][...]
+    block = jnp.exp(decay * (-2.0 * size * tokens))
+    zero = jnp.zeros_like(decay)
+    close, cross, grad, incoming = zero, zero, zero, zero
+    for k in range(count):
+        grad = grad + ordered[k, 2 * half:]
+        if k:
+            cross = cross + ordered[k, half:2 * half] * close
+            incoming = jnp.where(place == k, close, incoming)
+        close = close * block + ordered[k, 0:half]
+    begin, outgoing = zero, zero
+    for k in reversed(range(count)):
+        outgoing = jnp.where(place == k, begin, outgoing)
+        begin = begin * block + ordered[k, half:2 * half]
+    grad = grad + jnp.exp(-decay) * cross
+    if size > 1:
+        inside = lax.rem(chip, size)
+        incoming = carried[0:half] + incoming * jnp.exp(decay * (inside * (-2 * tokens)).astype(F32))
+        outgoing = carried[half:] + outgoing * jnp.exp(decay * ((size - 1 - inside) * (-2 * tokens)).astype(F32))
+    if not last:
+        joined, arrivals = outs
+        joined[0:half] = close
+        joined[half:2 * half] = begin
+        joined[2 * half:] = grad
+        arrivals[0:half] = incoming
+        arrivals[half:] = outgoing
         return
-    block = jnp.exp(decay * (-1.0 * size * tokens))
-    close = block * early_close + jnp.where(late, close, their_close)
-    begin = jnp.where(late, their_begin, begin) + block * late_begin
-    joined[parts[0]] = close
-    joined[parts[1]] = begin
-    joined[parts[2]] = grad
-    if message:
-        next_late = lax.rem(lax.div(place, 2 * size), 2) == 1
-        message[0][0:modes] = jnp.where(next_late, begin, close)
-        message[0][modes:] = grad
-
-
-def finish_kernel(ranges, residue_ref, decay_ref, core, chip, received, *refs):
+    total, own, message = outs
+    total[...] = grad
+    block = jnp.exp(decay * (-1.0 * tokens))
+    into = incoming, block * incoming + core[0:half]
+    out = block * outgoing + core[half:], outgoing
+    own[0:half] = jnp.where(second, into[1], into[0])
+    own[half:] = jnp.where(second, out[1], out[0])
+    message[0:half] = jnp.where(second, into[0], into[1])
+    message[half:] = jnp.where(second, out[0], out[1])
+
+
+def finish_kernel(ranges, residue_ref, decay_ref, own, other, *refs):
     near = refs[:2 * len(ranges)]
     out_hbm, back_hbm, finished, out_ref, back_ref, result, pw, arrive, leave, sems = refs[2 * len(ranges):]
     modes, channels = decay_ref.shape
+    half = modes // 2
     chunks = near[0].shape[1] // SUB
     span = chunks * SUB
-    late = lax.rem(lax.axis_index("ctx"), 2) == 1
-    decay = decay_ref[...]
-    first = residue_ref[...] * jnp.exp(-decay)
-    block = jnp.exp(decay * (-1.0 * span * SUB))
-    incoming = jnp.where(late, chip[0:modes], received[0:modes])
-    outgoing = jnp.where(late, chip[modes:], received[modes:])
-    arrive[...] = (core[0:modes] + jnp.where(late, block, 1.0) * incoming) * first
-    leave[...] = (core[modes:] + jnp.where(late, 1.0, block) * outgoing) * first
+    second = on_second()
+    first = residue_ref[...] * jnp.exp(-decay_ref[...])
+    for target, rows in ((arrive, slice(0, half)), (leave, slice(half, modes))):
+        low, high = both_halves(second, own[rows], other[rows])
+        target[0:half] = low * first[0:half]
+        target[half:] = high * first[half:]
 
     def copy_out(tile, which):
         lanes = pl.ds(pl.multiple_of(tile * LANES, LANES), LANES)
@@ -276,6 +316,23 @@
     finished[...] = jnp.zeros(finished.shape, F32)
 
 
+def balanced(terms):
+    while len(terms) > 1:
+        terms = [a + b for a, b in zip(terms[::2], terms[1::2])]
+    return terms[0]
+
+
+def sum_kernel(*refs):
+    refs[-1][...] = balanced([ref[...] for ref in refs[:-2]])
+
+
+def assemble_kernel(scale, own, other, out_ref):
+    half = own.shape[0]
+    low, high = both_halves(on_second(), own[...], other[...])
+    out_ref[0:half] = low * scale
+    out_ref[half:] = high * scale
+
+
 def vmem(*shape):
     return pltpu.VMEM(shape, F32)
 
@@ -294,24 +351,43 @@
 
 
 UNREAD = pl.BlockSpec(memory_space=pl.ANY)
-PARTS = 2
 
 
 def body(signal, cotangent, residue, decay):
     tokens, channels = signal.shape
     modes = decay.shape[0]
+    half = modes // 2
     n, groups = lax.axis_size("ctx"), lax.axis_size("ch")
     chunks = tokens // (SUB * SUB)
     elements = tokens * channels
-    steps = n.bit_length() - 1
     tokens_scratch = [vmem(tokens, LANES), vmem(tokens, LANES)]
     spans = vmem(modes * SUB, LANES)
-    width = channels // LANES // PARTS
-    ranges = [(k * width, (k + 1) * width) for k in range(PARTS)]
-
-    segment = pl.pallas_call(
+    tiles = channels // LANES
+    ranges = [(0, tiles // 4), (tiles // 4, tiles)]
+    small = dict(compiler_params=PARAMS, cost_estimate=cost(elements, modes * channels, modes * channels * 32))
+
+    def swap(x, axis, size, mask):
+        return lax.ppermute(x, axis, [(i, i ^ mask) for i in range(size)])
+
+    def near_part(part, after):
+        first, last = ranges[part]
+        share = elements * modes * (last - first) // tiles
+        return pl.pallas_call(
+            functools.partial(local_kernel, ranges[part]),
+            out_shape=[shaped(last - first, chunks * SUB, SUB, LANES)] * 2,
+            in_specs=[WHOLE] * 4 + [UNREAD],
+            scratch_shapes=tokens_scratch
+            + [vmem(3, modes, LANES), spans, spans]
+            + [vmem(modes, chunks - 1, SUB, LANES)] * 2
+            + [spans, spans],
+            compiler_params=PARAMS,
+            cost_estimate=cost(share * 400, 0, share),
+            name="local_convolutions",
+        )(signal, cotangent, residue, decay, after)
+
+    segment, message = pl.pallas_call(
         gather_kernel,
-        out_shape=shaped(3 * modes, channels),
+        out_shape=[shaped(3 * modes, channels), shaped(3 * half, channels)],
         in_specs=[HBM] * 3,
         scratch_shapes=tokens_scratch
         + [vmem(2, modes, LANES), spans, spans, spans]
@@ -322,95 +398,70 @@
         name="block_states",
     )(*(pltpu.with_memory_space_constraint(a, pltpu.HBM) for a in (signal, cotangent, decay)))
 
-    def near_part(part, after):
-        return pl.pallas_call(
-            functools.partial(local_kernel, ranges[part]),
-            out_shape=[shaped(width, chunks * SUB, SUB, LANES)] * 2,
-            in_specs=[WHOLE] * 4 + [UNREAD],
-            scratch_shapes=tokens_scratch
-            + [vmem(3, modes, LANES), spans, spans]
-            + [vmem(modes, chunks - 1, SUB, LANES)] * 2
-            + [spans, spans],
-            compiler_params=PARAMS,
-            cost_estimate=cost(elements * modes * 400 // PARTS, 0, elements * 12 // PARTS),
-            name="local_convolutions",
-        )(signal, cotangent, residue, decay, after)
-
-    def pairs(shift):
-        return [(i, i ^ shift if shift == 1 or i % 2 else i) for i in range(n)]
-
-    near = []
-    carried = jnp.zeros((SUB, LANES), F32)
-    pinned = message = segment
-    for bit in range(steps):
-        other = lax.ppermute(message, "ctx", pairs(1 << bit))
-        last = bit == steps - 1
-        if bit >= steps - PARTS:
-            near += near_part(len(near) // 2, segment)
-            pinned = near[-1]
-        rows = [2 * modes, modes if last else 3 * modes] + ([2 * modes] if bit == steps - 2 else [])
-        arrivals, segment, *message = pl.pallas_call(
-            functools.partial(join_kernel, tokens, bit, last),
+    other = swap(message, "ctx", n, 1)
+    near = near_part(0, segment)
+    joined, core = pl.pallas_call(
+        functools.partial(join_chip_kernel, tokens),
+        out_shape=[shaped(3 * half, channels), shaped(2 * half, channels)],
+        in_specs=[WHOLE] * 3 + [UNREAD],
+        name="join_chip",
+        **small,
+    )(segment, other, decay, near[0])
+
+    chips = n // 2
+    size = 1
+    carried = core
+    while size < chips:
+        count = min(4, chips // size)
+        last = size * count == chips
+        others = [swap(joined, "ctx", n, 2 * size * m) for m in range(1, count)]
+        if last:
+            near = near + near_part(1, joined)
+        rows = [half, 2 * half, 2 * half] if last else [3 * half, 2 * half]
+        joined, carried, *message = pl.pallas_call(
+            functools.partial(join_kernel, tokens, size, count, last),
             out_shape=[shaped(r, channels) for r in rows],
-            in_specs=[WHOLE] * 4 + [UNREAD],
-            compiler_params=PARAMS,
-            cost_estimate=cost(elements, modes * channels * 3, modes * channels * 48),
-            name="join_segments",
-        )(segment, other, decay, carried, pinned)
-        message = message[0] if message else segment
-        if bit == 0:
-            from_core = arrivals
-        else:
-            carried = arrivals
-
-    received = lax.ppermute(carried, "ctx", pairs(1))
-
-    def summed(*terms):
-        while len(terms) > 1:
-            terms = [a + b for a, b in zip(terms[::2], terms[1::2])]
-        return terms[0]
-
-    def sum_kernel(*refs):
-        refs[-1][...] = summed(*(ref[...] for ref in refs[:-2]))
-
+            in_specs=[WHOLE] * (count + 3) + [UNREAD],
+            scratch_shapes=[vmem(count, 3 * half, channels)],
+            name="join_chips",
+            **small,
+        )(joined, *others, core, decay, carried, near[-1])
+        size *= count
+
+    received = swap(message[0], "ctx", n, 1)
     conv_out, signal_grad, finished = pl.pallas_call(
         functools.partial(finish_kernel, ranges),
         out_shape=[jax.ShapeDtypeStruct((tokens, channels), signal.dtype)] * 2 + [shaped(SUB, LANES)],
-        in_specs=[WHOLE] * (5 + 2 * PARTS),
+        in_specs=[WHOLE] * (4 + 2 * len(ranges)),
         out_specs=[HBM] * 2 + [WHOLE],
         scratch_shapes=[pltpu.VMEM((tokens, channels), signal.dtype)] * 2
         + [vmem(tokens, LANES), vmem(5, modes, LANES)]
         + [vmem(modes, channels)] * 2
-        + [pltpu.SemaphoreType.DMA((2, channels // LANES))],
+        + [pltpu.SemaphoreType.DMA((2, tiles))],
         compiler_params=PARAMS,
         cost_estimate=cost(elements * modes * 600, 0, elements * 12),
         name="add_arrivals",
-    )(residue, decay, from_core, carried, received, *near)
-
-    grad = segment
+    )(residue, decay, carried, received, *near)
+
+    grad = joined
     stride = 1
     while stride < groups:
         count = min(4, groups // stride)
-        terms = [grad] + [
-            lax.ppermute(
-                grad,
-                ("ctx", "ch"),
-                [(i * groups + k, i * groups + (k ^ (stride * m if i % 2 else 0))) for i in range(n) for k in range(groups)],
-            )
-            for m in range(1, count)
-        ]
+        others = [swap(grad, "ch", groups, stride * m) for m in range(1, count)]
         grad = pl.pallas_call(
             sum_kernel,
-            out_shape=shaped(modes, channels),
+            out_shape=shaped(half, channels),
             in_specs=[WHOLE] * count + [UNREAD],
-            compiler_params=PARAMS,
-            cost_estimate=cost(modes * channels * count, 0, modes * channels * 4 * count),
             name="sum_groups",
-        )(*terms, finished)
+            **small,
+        )(grad, *others, finished)
         stride *= count
-    other = lax.ppermute(grad, "ctx", pairs(1))
-    second = lax.rem(lax.axis_index("ctx"), 2) == 1
-    residue_grad = jnp.where(second, grad, other) / (tokens * n)
+    residue_grad = pl.pallas_call(
+        functools.partial(assemble_kernel, 1.0 / (tokens * n)),
+        out_shape=shaped(modes, channels),
+        name="assemble_gradient",
+        **small,
+    )(grad, swap(grad, "ctx", n, 1))
     return conv_out, signal_grad, residue_grad
 
 

time: 33.5 us -> 27.5 us (0.82)
  starting transfers between devices: 20 us -> 9.24 us
  waiting for transfers between devices: 1.82 us -> 6.18 us
  local copies, waits for them, and re-layouts: 0.04 us -> 0.77 us
  other arithmetic: 0.62 us -> 0 us
  Pallas kernels: 9.87 us -> 10.4 us
    ppermute x8 -> x9, starting transfers between devices: 20 us -> 9.24 us  [swap(): return lax.ppermute(x, axis, [(i, i ^ mask) for i in range(size)])]
    ppermute x8 -> x9, waiting for transfers between devices: 1.82 us -> 6.18 us  [swap(): return lax.ppermute(x, axis, [(i, i ^ mask) for i in range(size)])]
    unnamed x8 -> x10, local copies, waits for them, and re-layouts: 0.04 us -> 0.77 us
    div x1 -> x0, other arithmetic: 0.62 us -> none  [body(): residue_grad = jnp.where(second, grad, other) / (tokens * n)]
    pallas_call x5, Pallas kernels: 3.63 us -> 4.23 us  [the longest x1 3.52 us: body(): pl.pallas_call(gather_kernel, out_shape=[shaped(3 * modes, channels), sha...]
  transfers between devices with their start and end apart: 8 -> 9, of which waited for: 2 -> 3; matrix products, arithmetic and copies ran while one was open for 0% -> 0% of each run, Pallas kernels for 19% -> 22%
where the time goes in v6:
time: 27.5 us; the launch traced here: 27.3 us
  Pallas kernels  10.4 us (38%)
  starting transfers between devices  9.24 us (34%)
  waiting for transfers between devices  6.18 us (22%)
  local copies, waits for them, and re-layouts  0.77 us (3%)
  between operations  0.77 us (3%)
    ppermute x9, starting transfers between devices, swap(): return lax.ppermute(x, axis, [(i, i ^ mask) for i in range(size)])  9.24 us
    ppermute x9, waiting for transfers between devices, swap(): return lax.ppermute(x, axis, [(i, i ^ mask) for i in range(size)])  6.18 us
    pallas_call x2, Pallas kernels, near_part(): pl.pallas_call(functools.partial(local_kernel, ranges[part]), out_shape=[...  3.62 us
    pallas_call x1, Pallas kernels, body(): pl.pallas_call(gather_kernel, out_shape=[shaped(3 * modes, channels), sha...  3.52 us
    pallas_call x1, Pallas kernels, body(): pl.pallas_call(functools.partial(finish_kernel, ranges), out_shape=[jax.S...  2.51 us
    unnamed x10, local copies, waits for them, and re-layouts  0.77 us
    pallas_call x1, Pallas kernels, body(): pl.pallas_call(functools.partial(assemble_kernel, 1.0 / (tokens * n)), ou...  0.62 us
  transfers between devices with their start and end apart: 9, of which 3 were waited for; matrix products, arithmetic and copies ran while one was open for 0% of the time, Pallas kernels for 22%

profile of v6, /device:TPU:0, one launch (start us, length us, event | category | flops | bytes accessed | tf_op | source)
XLA Modules:
  0.0 27.3 jit_solution(7833254869979442758)
XLA Ops:
  0.6 0.0 copy-start.1
  0.6 0.0 copy-start.2
  0.7 0.0 copy-start
  0.7 3.5 %block_states.1 = (f32[48,512]{1,0:T(8,128)S(1)}, f32[24,512]{1,0:T(8,128)S(1)}) custom-call(bf16[256,512]{1,0:T(8,128)(2,1)} %x_ref.3, bf16[256,512]{1,0:T(8,128)(2,1)} %g_ref.3, f32[16,512]{1,0:T(8,128)} %decay_ref.7), custom_call_target="tpu_custom_call" | custom-call | flops 10485760 | bytes 786432 | tf_op jit(solution)/shard_map/block_states/pallas_call | solution.py:388
  4.2 0.5 %collective-permute-start = (f32[24,512]{1,0:T(8,128)S(1)}, f32[24,512]{1,0:T(8,128)S(1)}, u32[]{:S(2)}, u32[]{:S(2)}) collective-permute-start(f32[24,512]{1,0:T(8,128)S(1)} %get-tuple-element.18), channel_id=1, source_target_pairs={{0,4},{4,0},{8,12},{12,8},{16,20},{20,16},{24,28},{28,24},{1,5},{5... | collective-permute-start | bytes 147464 | tf_op jit(solution)/shard_map/ppermute | solution.py:370
  4.7 0.0 copy-done.1
  4.7 0.0 copy-done.2
  4.7 0.0 copy-done
  4.7 0.8 %copy-done.3 = f32[16,512]{1,0:T(8,128)S(1)} copy-done((f32[16,512]{1,0:T(8,128)S(1)}, f32[16,512]{1,0:T(8,128)}, u32[]{:S(2)}) %copy-start.3) | copy-done | bytes 32792
  5.5 0.9 %local_convolutions.2 = (f32[1,32,8,128]{3,2,1,0:T(8,128)S(1)}, f32[1,32,8,128]{3,2,1,0:T(8,128)S(1)}) custom-call(bf16[256,512]{1,0:T(8,128)(2,1)S(1)} %copy-done.1, bf16[256,512]{1,0:T(8,128)(2,1)S(1)} %copy-done.2, f32[16,512]{1,0:T(8,128)S(1)} %copy-done.3, f32[16,512]{1,0:T(8,128)S(1)} %copy-done, f32[48,512]{1,0:T(8,128)S(1)} %get-tuple-element.17._.segment), custom_call_target="tpu_custom_call" | custom-call | flops 209715200 | bytes 524288 | tf_op jit(solution)/shard_map/local_convolutions/pallas_call | solution.py:375
  6.4 0.0 collective-permute-done.other
  6.4 0.0 copy-start.4
  6.4 2.6 %collective-permute-start.1 = (f32[24,512]{1,0:T(8,128)S(1)}, f32[24,512]{1,0:T(8,128)S(1)}, u32[]{:S(2)}, u32[]{:S(2)}) collective-permute-start(f32[24,512]{1,0:T(8,128)S(1)} %get-tuple-element.20._.refs_0_), channel_id=1, source_target_pairs={{0,8},{4,12},{8,0},{12,4},{16,24},{20,28},{24,16},{28,20},{1,9},{5... | collective-permute-start | bytes 147464 | tf_op jit(solution)/shard_map/ppermute | solution.py:370
  9.0 1.5 %collective-permute-start.2 = (f32[24,512]{1,0:T(8,128)S(1)}, f32[24,512]{1,0:T(8,128)S(1)}, u32[]{:S(2)}, u32[]{:S(2)}) collective-permute-start(f32[24,512]{1,0:T(8,128)S(1)} %get-tuple-element.20._.refs_0_), channel_id=1, source_target_pairs={{0,16},{4,20},{8,24},{12,28},{16,0},{20,4},{24,8},{28,12},{1,17},{... | collective-permute-start | bytes 147464 | tf_op jit(solution)/shard_map/ppermute | solution.py:370
  10.6 0.0 collective-permute-start.3
  10.6 0.0 copy-done.4
  10.6 2.7 %local_convolutions.3 = (f32[3,32,8,128]{3,2,1,0:T(8,128)S(1)}, f32[3,32,8,128]{3,2,1,0:T(8,128)S(1)}) custom-call(bf16[256,512]{1,0:T(8,128)(2,1)S(1)} %copy-done.1, bf16[256,512]{1,0:T(8,128)(2,1)S(1)} %copy-done.2, f32[16,512]{1,0:T(8,128)S(1)} %copy-done.4, f32[16,512]{1,0:T(8,128)S(1)} %copy-done, f32[24,512]{1,0:T(8,128)S(1)} %get-tuple-element.20._.refs_0_), custom_call_target="tpu_custom_call" | custom-call | flops 629145600 | bytes 1572864 | tf_op jit(solution)/shard_map/local_convolutions/pallas_call | solution.py:375
  13.3 0.0 collective-permute-done.1.refs_1_
  13.3 0.0 collective-permute-done.2.refs_2_
  13.3 2.2 %collective-permute-done.3.refs_3_ = f32[24,512]{1,0:T(8,128)S(1)} collective-permute-done((f32[24,512]{1,0:T(8,128)S(1)}, f32[24,512]{1,0:T(8,128)S(1)}, u32[]{:S(2)}, u32[]{:S(2)}) %collective-permute-start.3) | collective-permute-done | bytes 49184 | tf_op jit(solution)/shard_map/ppermute | solution.py:370
  15.6 0.1 collective-permute-start.4
  15.7 1.6 %collective-permute-start.5 = (f32[8,512]{1,0:T(8,128)S(1)}, f32[8,512]{1,0:T(8,128)S(1)}, u32[]{:S(2)}, u32[]{:S(2)}) collective-permute-start(f32[8,512]{1,0:T(8,128)S(1)} %get-tuple-element.29.refs_0_), channel_id=1, source_target_pairs={{0,1},{1,0},{2,3},{3,2},{4,5},{5,4},{6,7},{7,6},{8,9},{9,8},{10,11... | collective-permute-start | bytes 49160 | tf_op jit(solution)/shard_map/ppermute | solution.py:370
  17.3 2.6 %collective-permute-start.6 = (f32[8,512]{1,0:T(8,128)S(1)}, f32[8,512]{1,0:T(8,128)S(1)}, u32[]{:S(2)}, u32[]{:S(2)}) collective-permute-start(f32[8,512]{1,0:T(8,128)S(1)} %get-tuple-element.29.refs_0_), channel_id=1, source_target_pairs={{0,2},{1,3},{2,0},{3,1},{4,6},{5,7},{6,4},{7,5},{8,10},{9,11},{10,... | collective-permute-start | bytes 49160 | tf_op jit(solution)/shard_map/ppermute | solution.py:370
  19.9 0.2 collective-permute-start.7
  20.1 0.0 collective-permute-done.4.other
  20.1 2.5 %add_arrivals.1 = (bf16[256,512]{1,0:T(8,128)(2,1)}, bf16[256,512]{1,0:T(8,128)(2,1)}, f32[8,128]{1,0:T(8,128)S(1)}) custom-call(f32[16,512]{1,0:T(8,128)S(1)} %copy-done.4, f32[16,512]{1,0:T(8,128)S(1)} %copy-done, f32[16,512]{1,0:T(8,128)S(1)} %get-tuple-element.23.own, f32[16,512]{1,0:T(8,128)S(1)} %collective-permute-done.4.other, ...), custom_call_target="tpu_custom_call" | custom-call | flops 1258291200 | bytes 1572864 | tf_op jit(solution)/shard_map/add_arrivals/pallas_call | solution.py:432
  22.7 0.0 collective-permute-done.5.refs_1_
  22.7 0.0 collective-permute-done.6.refs_2_
  22.7 2.8 %collective-permute-done.7.refs_3_ = f32[8,512]{1,0:T(8,128)S(1)} collective-permute-done((f32[8,512]{1,0:T(8,128)S(1)}, f32[8,512]{1,0:T(8,128)S(1)}, u32[]{:S(2)}, u32[]{:S(2)}) %collective-permute-start.7) | collective-permute-done | bytes 16416 | tf_op jit(solution)/shard_map/ppermute | solution.py:370
  25.5 0.1 collective-permute-start.8
  25.5 1.2 %collective-permute-done.8.other = f32[8,512]{1,0:T(8,128)S(1)} collective-permute-done((f32[8,512]{1,0:T(8,128)S(1)}, f32[8,512]{1,0:T(8,128)S(1)}, u32[]{:S(2)}, u32[]{:S(2)}) %collective-permute-start.8) | collective-permute-done | bytes 16416 | tf_op jit(solution)/shard_map/ppermute | solution.py:370
  26.7 0.6 %assemble_gradient.1 = f32[16,512]{1,0:T(8,128)} custom-call(f32[8,512]{1,0:T(8,128)S(1)} %sum_groups.1.own, f32[8,512]{1,0:T(8,128)S(1)} %collective-permute-done.8.other), custom_call_target="tpu_custom_call" | custom-call | flops 131072 | bytes 262144 | tf_op jit(solution)/shard_map/assemble_gradient/pallas_call | solution.py:459
  (4 shorter events, 0.1 us)
Async XLA Ops:
  0.6 4.1 %copy-start.1 = (bf16[256,512]{1,0:T(8,128)(2,1)S(1)}, bf16[256,512]{1,0:T(8,128)(2,1)}, u32[]{:S(2)}) copy-start(bf16[256,512]{1,0:T(8,128)(2,1)} %x_ref.3) | copy-start | bytes 786436
  0.6 4.1 %copy-start.2 = (bf16[256,512]{1,0:T(8,128)(2,1)S(1)}, bf16[256,512]{1,0:T(8,128)(2,1)}, u32[]{:S(2)}) copy-start(bf16[256,512]{1,0:T(8,128)(2,1)} %g_ref.3) | copy-start | bytes 786436
  0.7 4.1 %copy-start = (f32[16,512]{1,0:T(8,128)S(1)}, f32[16,512]{1,0:T(8,128)}, u32[]{:S(2)}) copy-start(f32[16,512]{1,0:T(8,128)} %decay_ref.7) | copy-start | bytes 98308
  4.2 2.2 %collective-permute-start = (f32[24,512]{1,0:T(8,128)S(1)}, f32[24,512]{1,0:T(8,128)S(1)}, u32[]{:S(2)}, u32[]{:S(2)}) collective-permute-start(f32[24,512]{1,0:T(8,128)S(1)} %get-tuple-element.18), channel_id=1, source_target_pairs={{0,4},{4,0},{8,12},{12,8},{16,20},{20,16},{24,28},{28,24},{1,5},{5... | collective-permute-start | bytes 147464 | tf_op jit(solution)/shard_map/ppermute | solution.py:370
  4.7 0.8 %copy-start.3 = (f32[16,512]{1,0:T(8,128)S(1)}, f32[16,512]{1,0:T(8,128)}, u32[]{:S(2)}) copy-start(f32[16,512]{1,0:T(8,128)} %residue_ref.5) | copy-start | bytes 98308
  6.4 4.2 %copy-start.4 = (f32[16,512]{1,0:T(8,128)S(1)}, f32[16,512]{1,0:T(8,128)}, u32[]{:S(2)}) copy-start(f32[16,512]{1,0:T(8,128)} %residue_ref.5) | copy-start | bytes 98308
  6.4 6.9 %collective-permute-start.1 = (f32[24,512]{1,0:T(8,128)S(1)}, f32[24,512]{1,0:T(8,128)S(1)}, u32[]{:S(2)}, u32[]{:S(2)}) collective-permute-start(f32[24,512]{1,0:T(8,128)S(1)} %get-tuple-element.20._.refs_0_), channel_id=1, source_target_pairs={{0,8},{4,12},{8,0},{12,4},{16,24},{20,28},{24,16},{28,20},{1,9},{5... | collective-permute-start | bytes 147464 | tf_op jit(solution)/shard_map/ppermute | solution.py:370
  9.0 4.3 %collective-permute-start.2 = (f32[24,512]{1,0:T(8,128)S(1)}, f32[24,512]{1,0:T(8,128)S(1)}, u32[]{:S(2)}, u32[]{:S(2)}) collective-permute-start(f32[24,512]{1,0:T(8,128)S(1)} %get-tuple-element.20._.refs_0_), channel_id=1, source_target_pairs={{0,16},{4,20},{8,24},{12,28},{16,0},{20,4},{24,8},{28,12},{1,17},{... | collective-permute-start | bytes 147464 | tf_op jit(solution)/shard_map/ppermute | solution.py:370
  10.6 5.0 %collective-permute-start.3 = (f32[24,512]{1,0:T(8,128)S(1)}, f32[24,512]{1,0:T(8,128)S(1)}, u32[]{:S(2)}, u32[]{:S(2)}) collective-permute-start(f32[24,512]{1,0:T(8,128)S(1)} %get-tuple-element.20._.refs_0_), channel_id=1, source_target_pairs={{0,24},{4,28},{8,16},{12,20},{16,8},{20,12},{24,0},{28,4},{1,25},{... | collective-permute-start | bytes 147464 | tf_op jit(solution)/shard_map/ppermute | solution.py:370
  15.6 4.5 %collective-permute-start.4 = (f32[16,512]{1,0:T(8,128)S(1)}, f32[16,512]{1,0:T(8,128)S(1)}, u32[]{:S(2)}, u32[]{:S(2)}) collective-permute-start(f32[16,512]{1,0:T(8,128)S(1)} %get-tuple-element.24), channel_id=1, source_target_pairs={{0,4},{4,0},{8,12},{12,8},{16,20},{20,16},{24,28},{28,24},{1,5},{5... | collective-permute-start | bytes 98312 | tf_op jit(solution)/shard_map/ppermute | solution.py:370
  15.7 7.0 %collective-permute-start.5 = (f32[8,512]{1,0:T(8,128)S(1)}, f32[8,512]{1,0:T(8,128)S(1)}, u32[]{:S(2)}, u32[]{:S(2)}) collective-permute-start(f32[8,512]{1,0:T(8,128)S(1)} %get-tuple-element.29.refs_0_), channel_id=1, source_target_pairs={{0,1},{1,0},{2,3},{3,2},{4,5},{5,4},{6,7},{7,6},{8,9},{9,8},{10,11... | collective-permute-start | bytes 49160 | tf_op jit(solution)/shard_map/ppermute | solution.py:370
  17.3 5.3 %collective-permute-start.6 = (f32[8,512]{1,0:T(8,128)S(1)}, f32[8,512]{1,0:T(8,128)S(1)}, u32[]{:S(2)}, u32[]{:S(2)}) collective-permute-start(f32[8,512]{1,0:T(8,128)S(1)} %get-tuple-element.29.refs_0_), channel_id=1, source_target_pairs={{0,2},{1,3},{2,0},{3,1},{4,6},{5,7},{6,4},{7,5},{8,10},{9,11},{10,... | collective-permute-start | bytes 49160 | tf_op jit(solution)/shard_map/ppermute | solution.py:370
  19.9 5.5 %collective-permute-start.7 = (f32[8,512]{1,0:T(8,128)S(1)}, f32[8,512]{1,0:T(8,128)S(1)}, u32[]{:S(2)}, u32[]{:S(2)}) collective-permute-start(f32[8,512]{1,0:T(8,128)S(1)} %get-tuple-element.29.refs_0_), channel_id=1, source_target_pairs={{0,3},{1,2},{2,1},{3,0},{4,7},{5,6},{6,5},{7,4},{8,11},{9,10},{10,... | collective-permute-start | bytes 49160 | tf_op jit(solution)/shard_map/ppermute | solution.py:370
  25.5 1.2 %collective-permute-start.8 = (f32[8,512]{1,0:T(8,128)S(1)}, f32[8,512]{1,0:T(8,128)S(1)}, u32[]{:S(2)}, u32[]{:S(2)}) collective-permute-start(f32[8,512]{1,0:T(8,128)S(1)} %sum_groups.1.own), channel_id=1, source_target_pairs={{0,4},{4,0},{8,12},{12,8},{16,20},{20,16},{24,28},{28,24},{1,5},{5... | collective-permute-start | bytes 49160 | tf_op jit(solution)/shard_map/ppermute | solution.py:370

commit v7 on v6

--- a/solution.py
+++ b/solution.py
@@ -55,12 +55,11 @@
     return scratch[pl.ds(half * SUB * SUB + j, SUB, stride=SUB), :]
 
 
-def gather_kernel(x_hbm, g_hbm, decay_hbm, segment, message, *refs):
-    xf, gf, pw, ends, starts, inner, x_ref, g_ref, decay_ref, sems = refs
-    copies = [
-        pltpu.make_async_copy(source, target, sems.at[i])
-        for i, (source, target) in enumerate(((x_hbm, x_ref), (g_hbm, g_ref), (decay_hbm, decay_ref)))
-    ]
+def gather_kernel(*refs):
+    sources, staged = refs[:4], refs[4:8]
+    segment, message, xf, gf, pw, ends, starts, inner, sems = refs[8:]
+    x_ref, g_ref, _, decay_ref = staged
+    copies = [pltpu.make_async_copy(*pair, sems.at[i]) for i, pair in enumerate(zip(sources, staged))]
     for copy in copies:
         copy.start()
     modes, channels = decay_ref.shape
@@ -208,7 +207,8 @@
     core[half:] = open1
 
 
-def join_kernel(tokens, size, count, last, *refs):
+def join_kernel(tokens, size, masks, last, *refs):
+    count = len(masks)
     segments = refs[:count]
     core, decay_ref, carried, _ = refs[count:count + 4]
     *outs, ordered = refs[count + 4:]
@@ -217,8 +217,8 @@
     half = decay.shape[0]
     chip = lax.div(lax.axis_index("ctx"), 2)
     place = lax.rem(lax.div(chip, size), count)
-    for m in range(count):
-        ordered[place ^ m] = segments[m][...]
+    for mask, segment in zip(masks, segments):
+        ordered[place ^ mask] = segment[...]
     block = jnp.exp(decay * (-2.0 * size * tokens))
     zero = jnp.zeros_like(decay)
     close, cross, grad, incoming = zero, zero, zero, zero
@@ -258,7 +258,7 @@
 
 def finish_kernel(ranges, residue_ref, decay_ref, own, other, *refs):
     near = refs[:2 * len(ranges)]
-    out_hbm, back_hbm, finished, out_ref, back_ref, result, pw, arrive, leave, sems = refs[2 * len(ranges):]
+    _, out_hbm, back_hbm, finished, out_ref, back_ref, result, pw, arrive, leave, sems = refs[2 * len(ranges):]
     modes, channels = decay_ref.shape
     half = modes // 2
     chunks = near[0].shape[1] // SUB
@@ -316,14 +316,8 @@
     finished[...] = jnp.zeros(finished.shape, F32)
 
 
-def balanced(terms):
-    while len(terms) > 1:
-        terms = [a + b for a, b in zip(terms[::2], terms[1::2])]
-    return terms[0]
-
-
-def sum_kernel(*refs):
-    refs[-1][...] = balanced([ref[...] for ref in refs[:-2]])
+def sum_kernel(own, other, _, out_ref):
+    out_ref[...] = own[...] + other[...]
 
 
 def assemble_kernel(scale, own, other, out_ref):
@@ -363,7 +357,8 @@
     tokens_scratch = [vmem(tokens, LANES), vmem(tokens, LANES)]
     spans = vmem(modes * SUB, LANES)
     tiles = channels // LANES
-    ranges = [(0, tiles // 4), (tiles // 4, tiles)]
+    quarter = tiles // 4
+    ranges = [(0, quarter), (quarter, 3 * quarter), (3 * quarter, tiles)]
     small = dict(compiler_params=PARAMS, cost_estimate=cost(elements, modes * channels, modes * channels * 32))
 
     def swap(x, axis, size, mask):
@@ -385,18 +380,18 @@
             name="local_convolutions",
         )(signal, cotangent, residue, decay, after)
 
-    segment, message = pl.pallas_call(
+    inputs = signal, cotangent, residue, decay
+    signal, cotangent, residue, decay, segment, message = pl.pallas_call(
         gather_kernel,
-        out_shape=[shaped(3 * modes, channels), shaped(3 * half, channels)],
-        in_specs=[HBM] * 3,
+        out_shape=[jax.ShapeDtypeStruct(a.shape, a.dtype) for a in inputs]
+        + [shaped(3 * modes, channels), shaped(3 * half, channels)],
+        in_specs=[HBM] * 4,
         scratch_shapes=tokens_scratch
-        + [vmem(2, modes, LANES), spans, spans, spans]
-        + [pltpu.VMEM(signal.shape, signal.dtype)] * 2
-        + [vmem(modes, channels), pltpu.SemaphoreType.DMA((3,))],
+        + [vmem(2, modes, LANES), spans, spans, spans, pltpu.SemaphoreType.DMA((4,))],
         compiler_params=PARAMS,
         cost_estimate=cost(elements * modes * 5, modes * channels * 3, elements * 6),
         name="block_states",
-    )(*(pltpu.with_memory_space_constraint(a, pltpu.HBM) for a in (signal, cotangent, decay)))
+    )(*(pltpu.with_memory_space_constraint(a, pltpu.HBM) for a in inputs))
 
     other = swap(message, "ctx", n, 1)
     near = near_part(0, segment)
@@ -414,12 +409,13 @@
     while size < chips:
         count = min(4, chips // size)
         last = size * count == chips
-        others = [swap(joined, "ctx", n, 2 * size * m) for m in range(1, count)]
+        masks = [3, 1, 2] if count == 4 else [1]
+        others = [swap(joined, "ctx", n, 2 * size * m) for m in masks]
         if last:
             near = near + near_part(1, joined)
         rows = [half, 2 * half, 2 * half] if last else [3 * half, 2 * half]
         joined, carried, *message = pl.pallas_call(
-            functools.partial(join_kernel, tokens, size, count, last),
+            functools.partial(join_kernel, tokens, size, [0] + masks, last),
             out_shape=[shaped(r, channels) for r in rows],
             in_specs=[WHOLE] * (count + 3) + [UNREAD],
             scratch_shapes=[vmem(count, 3 * half, channels)],
@@ -428,34 +424,36 @@
         )(joined, *others, core, decay, carried, near[-1])
         size *= count
 
-    received = swap(message[0], "ctx", n, 1)
-    conv_out, signal_grad, finished = pl.pallas_call(
-        functools.partial(finish_kernel, ranges),
-        out_shape=[jax.ShapeDtypeStruct((tokens, channels), signal.dtype)] * 2 + [shaped(SUB, LANES)],
-        in_specs=[WHOLE] * (4 + 2 * len(ranges)),
-        out_specs=[HBM] * 2 + [WHOLE],
-        scratch_shapes=[pltpu.VMEM((tokens, channels), signal.dtype)] * 2
-        + [vmem(tokens, LANES), vmem(5, modes, LANES)]
-        + [vmem(modes, channels)] * 2
-        + [pltpu.SemaphoreType.DMA((2, tiles))],
-        compiler_params=PARAMS,
-        cost_estimate=cost(elements * modes * 600, 0, elements * 12),
-        name="add_arrivals",
-    )(residue, decay, carried, received, *near)
-
     grad = joined
     stride = 1
     while stride < groups:
-        count = min(4, groups // stride)
-        others = [swap(grad, "ch", groups, stride * m) for m in range(1, count)]
+        other = swap(grad, "ch", groups, stride)
+        if stride == 1:
+            received = swap(message[0], "ctx", n, 1)
+            near = near + near_part(2, grad)
+            pinned = near[-1]
+        stride *= 2
+        if stride == groups:
+            conv_out, signal_grad, pinned = pl.pallas_call(
+                functools.partial(finish_kernel, ranges),
+                out_shape=[jax.ShapeDtypeStruct((tokens, channels), signal.dtype)] * 2 + [shaped(SUB, LANES)],
+                in_specs=[WHOLE] * (4 + 2 * len(ranges)) + [UNREAD],
+                out_specs=[HBM] * 2 + [WHOLE],
+                scratch_shapes=[pltpu.VMEM((tokens, channels), signal.dtype)] * 2
+                + [vmem(tokens, LANES), vmem(5, modes, LANES)]
+                + [vmem(modes, channels)] * 2
+                + [pltpu.SemaphoreType.DMA((2, tiles))],
+                compiler_params=PARAMS,
+                cost_estimate=cost(elements * modes * 600, 0, elements * 12),
+                name="add_arrivals",
+            )(residue, decay, carried, received, *near, grad)
         grad = pl.pallas_call(
             sum_kernel,
             out_shape=shaped(half, channels),
-            in_specs=[WHOLE] * count + [UNREAD],
+            in_specs=[WHOLE] * 2 + [UNREAD],
             name="sum_groups",
             **small,
-        )(grad, *others, finished)
-        stride *= count
+        )(grad, other, pinned)
     residue_grad = pl.pallas_call(
         functools.partial(assemble_kernel, 1.0 / (tokens * n)),
         out_shape=shaped(modes, channels),

time: 27.5 us -> 25.2 us (0.916)
  waiting for transfers between devices: 6.18 us -> 4.59 us
  local copies, waits for them, and re-layouts: 0.77 us -> 0 us
    ppermute x9 -> x8, waiting for transfers between devices: 6.18 us -> 4.59 us  [swap(): return lax.ppermute(x, axis, [(i, i ^ mask) for i in range(size)])]
    unnamed x10 -> x0, local copies, waits for them, and re-layouts: 0.77 us -> none
    ppermute x9 -> x8, starting transfers between devices: 9.24 us -> 9.34 us  [swap(): return lax.ppermute(x, axis, [(i, i ^ mask) for i in range(size)])]
    pallas_call x2 -> x3, Pallas kernels: 3.62 us -> 3.62 us  [near_part(): pl.pallas_call(functools.partial(local_kernel, ranges[part]), out_shape=[...]
  transfers between devices with their start and end apart: 9 -> 8, of which waited for: 3 -> 4; matrix products, arithmetic and copies ran while one was open for 0% -> 0% of each run, Pallas kernels for 22% -> 25%
where the time goes in v7:
time: 25.2 us; the launch traced here: 25 us
  Pallas kernels  10.3 us (41%)
  starting transfers between devices  9.34 us (37%)
  waiting for transfers between devices  4.59 us (18%)
  between operations  0.72 us (3%)
    ppermute x8, starting transfers between devices, swap(): return lax.ppermute(x, axis, [(i, i ^ mask) for i in range(size)])  9.34 us
    ppermute x8, waiting for transfers between devices, swap(): return lax.ppermute(x, axis, [(i, i ^ mask) for i in range(size)])  4.59 us
    pallas_call x3, Pallas kernels, near_part(): pl.pallas_call(functools.partial(local_kernel, ranges[part]), out_shape=[...  3.62 us
    pallas_call x1, Pallas kernels, body(): pl.pallas_call(gather_kernel, out_shape=[jax.ShapeDtypeStruct(a.shape, a....  3.48 us
    pallas_call x1, Pallas kernels, body(): pl.pallas_call(functools.partial(finish_kernel, ranges), out_shape=[jax.S...  2.54 us
    pallas_call x1, Pallas kernels, body(): pl.pallas_call(functools.partial(assemble_kernel, 1.0 / (tokens * n)), ou...  0.62 us
  transfers between devices with their start and end apart: 8, of which 4 were waited for; matrix products, arithmetic and copies ran while one was open for 0% of the time, Pallas kernels for 25%

profile of v7, /device:TPU:0, one launch (start us, length us, event | category | flops | bytes accessed | tf_op | source)
XLA Modules:
  0.0 25.0 jit_solution(14088730384793408031)
XLA Ops:
  0.6 3.5 %block_states.1 = (bf16[256,512]{1,0:T(8,128)(2,1)S(1)}, bf16[256,512]{1,0:T(8,128)(2,1)S(1)}, f32[16,512]{1,0:T(8,128)S(1)}, f32[16,512]{1,0:T(8,128)S(1)}, f32...) custom-call(bf16[256,512]{1,0:T(8,128)(2,1)} %refs_0_.1, bf16[256,512]{1,0:T(8,128)(2,1)} %refs_1_.1, f32[16,512]{1,0:T(8,128)} %refs_2_.1, ...), custom_call_target="tpu_custom_call" | custom-call | flops 10485760 | bytes 786432 | tf_op jit(solution)/shard_map/block_states/pallas_call | solution.py:384
  4.1 0.5 %collective-permute-start = (f32[24,512]{1,0:T(8,128)S(1)}, f32[24,512]{1,0:T(8,128)S(1)}, u32[]{:S(2)}, u32[]{:S(2)}) collective-permute-start(f32[24,512]{1,0:T(8,128)S(1)} %get-tuple-element.26), channel_id=1, source_target_pairs={{0,4},{4,0},{8,12},{12,8},{16,20},{20,16},{24,28},{28,24},{1,5},{5... | collective-permute-start | bytes 147464 | tf_op jit(solution)/shard_map/ppermute | solution.py:365
  4.6 0.9 %local_convolutions.3 = (f32[1,32,8,128]{3,2,1,0:T(8,128)S(1)}, f32[1,32,8,128]{3,2,1,0:T(8,128)S(1)}) custom-call(bf16[256,512]{1,0:T(8,128)(2,1)S(1)} %get-tuple-element.27.x_ref, bf16[256,512]{1,0:T(8,128)(2,1)S(1)} %get-tuple-element.28.g_ref, f32[16,512]{1,0:T(8,128)S(1)} %get-tuple-element.23.residue_ref, ...), custom_call_target="tpu_custom_call" | custom-call | flops 209715200 | bytes 524288 | tf_op jit(solution)/shard_map/local_convolutions/pallas_call | solution.py:370
  5.5 0.0 collective-permute-done.other
  5.6 3.8 %collective-permute-start.1 = (f32[24,512]{1,0:T(8,128)S(1)}, f32[24,512]{1,0:T(8,128)S(1)}, u32[]{:S(2)}, u32[]{:S(2)}) collective-permute-start(f32[24,512]{1,0:T(8,128)S(1)} %get-tuple-element.30._.refs_0_), channel_id=1, source_target_pairs={{0,24},{4,28},{8,16},{12,20},{16,8},{20,12},{24,0},{28,4},{1,25},{... | collective-permute-start | bytes 147464 | tf_op jit(solution)/shard_map/ppermute | solution.py:365
  9.4 0.5 %collective-permute-start.2 = (f32[24,512]{1,0:T(8,128)S(1)}, f32[24,512]{1,0:T(8,128)S(1)}, u32[]{:S(2)}, u32[]{:S(2)}) collective-permute-start(f32[24,512]{1,0:T(8,128)S(1)} %get-tuple-element.30._.refs_0_), channel_id=1, source_target_pairs={{0,8},{4,12},{8,0},{12,4},{16,24},{20,28},{24,16},{28,20},{1,9},{5... | collective-permute-start | bytes 147464 | tf_op jit(solution)/shard_map/ppermute | solution.py:365
  9.9 0.1 collective-permute-start.3
  10.0 1.8 %local_convolutions.4 = (f32[2,32,8,128]{3,2,1,0:T(8,128)S(1)}, f32[2,32,8,128]{3,2,1,0:T(8,128)S(1)}) custom-call(bf16[256,512]{1,0:T(8,128)(2,1)S(1)} %get-tuple-element.27.x_ref, bf16[256,512]{1,0:T(8,128)(2,1)S(1)} %get-tuple-element.28.g_ref, f32[16,512]{1,0:T(8,128)S(1)} %get-tuple-element.23.residue_ref, ...), custom_call_target="tpu_custom_call" | custom-call | flops 419430400 | bytes 1048576 | tf_op jit(solution)/shard_map/local_convolutions/pallas_call | solution.py:370
  11.9 0.0 collective-permute-done.1.refs_1_
  11.9 1.6 %collective-permute-done.2.refs_2_ = f32[24,512]{1,0:T(8,128)S(1)} collective-permute-done((f32[24,512]{1,0:T(8,128)S(1)}, f32[24,512]{1,0:T(8,128)S(1)}, u32[]{:S(2)}, u32[]{:S(2)}) %collective-permute-start.2) | collective-permute-done | bytes 49184 | tf_op jit(solution)/shard_map/ppermute | solution.py:365
  13.5 0.5 %collective-permute-done.3.refs_3_ = f32[24,512]{1,0:T(8,128)S(1)} collective-permute-done((f32[24,512]{1,0:T(8,128)S(1)}, f32[24,512]{1,0:T(8,128)S(1)}, u32[]{:S(2)}, u32[]{:S(2)}) %collective-permute-start.3) | collective-permute-done | bytes 49184 | tf_op jit(solution)/shard_map/ppermute | solution.py:365
  14.1 0.1 collective-permute-start.4
  14.2 1.6 %collective-permute-start.5 = (f32[8,512]{1,0:T(8,128)S(1)}, f32[8,512]{1,0:T(8,128)S(1)}, u32[]{:S(2)}, u32[]{:S(2)}) collective-permute-start(f32[8,512]{1,0:T(8,128)S(1)} %get-tuple-element.37._.own), channel_id=1, source_target_pairs={{0,1},{1,0},{2,3},{3,2},{4,5},{5,4},{6,7},{7,6},{8,9},{9,8},{10,11... | collective-permute-start | bytes 49160 | tf_op jit(solution)/shard_map/ppermute | solution.py:365
  15.8 0.9 %local_convolutions.5 = (f32[1,32,8,128]{3,2,1,0:T(8,128)S(1)}, f32[1,32,8,128]{3,2,1,0:T(8,128)S(1)}) custom-call(bf16[256,512]{1,0:T(8,128)(2,1)S(1)} %get-tuple-element.27.x_ref, bf16[256,512]{1,0:T(8,128)(2,1)S(1)} %get-tuple-element.28.g_ref, f32[16,512]{1,0:T(8,128)S(1)} %get-tuple-element.23.residue_ref, ...), custom_call_target="tpu_custom_call" | custom-call | flops 209715200 | bytes 524288 | tf_op jit(solution)/shard_map/local_convolutions/pallas_call | solution.py:370
  16.7 1.3 %collective-permute-done.5.other = f32[8,512]{1,0:T(8,128)S(1)} collective-permute-done((f32[8,512]{1,0:T(8,128)S(1)}, f32[8,512]{1,0:T(8,128)S(1)}, u32[]{:S(2)}, u32[]{:S(2)}) %collective-permute-start.5) | collective-permute-done | bytes 16416 | tf_op jit(solution)/shard_map/ppermute | solution.py:365
  18.0 2.6 %collective-permute-start.6 = (f32[8,512]{1,0:T(8,128)S(1)}, f32[8,512]{1,0:T(8,128)S(1)}, u32[]{:S(2)}, u32[]{:S(2)}) collective-permute-start(f32[8,512]{1,0:T(8,128)S(1)} %sum_groups.2.refs_6_.own), channel_id=1, source_target_pairs={{0,2},{1,3},{2,0},{3,1},{4,6},{5,7},{6,4},{7,5},{8,10},{9,11},{10,... | collective-permute-start | bytes 49160 | tf_op jit(solution)/shard_map/ppermute | solution.py:365
  20.6 0.0 collective-permute-done.4.other
  20.6 2.5 %add_arrivals.1 = (bf16[256,512]{1,0:T(8,128)(2,1)}, bf16[256,512]{1,0:T(8,128)(2,1)}, f32[8,128]{1,0:T(8,128)S(1)}) custom-call(f32[16,512]{1,0:T(8,128)S(1)} %get-tuple-element.23.residue_ref, f32[16,512]{1,0:T(8,128)S(1)} %get-tuple-element.24.decay_ref.refs_5_, f32[16,512]{1,0:T(8,128)S(1)} %get-tuple-element.33.own, ...), custom_call_target="tpu_custom_call" | custom-call | flops 1258291200 | bytes 1572864 | tf_op jit(solution)/shard_map/add_arrivals/pallas_call | solution.py:437
  23.1 0.0 collective-permute-done.6.other
  23.1 0.1 collective-permute-start.7
  23.2 1.2 %collective-permute-done.7.other = f32[8,512]{1,0:T(8,128)S(1)} collective-permute-done((f32[8,512]{1,0:T(8,128)S(1)}, f32[8,512]{1,0:T(8,128)S(1)}, u32[]{:S(2)}, u32[]{:S(2)}) %collective-permute-start.7) | collective-permute-done | bytes 16416 | tf_op jit(solution)/shard_map/ppermute | solution.py:365
  24.4 0.6 %assemble_gradient.1 = f32[16,512]{1,0:T(8,128)} custom-call(f32[8,512]{1,0:T(8,128)S(1)} %sum_groups.3.own, f32[8,512]{1,0:T(8,128)S(1)} %collective-permute-done.7.other), custom_call_target="tpu_custom_call" | custom-call | flops 131072 | bytes 262144 | tf_op jit(solution)/shard_map/assemble_gradient/pallas_call | solution.py:457
  (4 shorter events, 0.1 us)
Async XLA Ops:
  4.1 1.4 %collective-permute-start = (f32[24,512]{1,0:T(8,128)S(1)}, f32[24,512]{1,0:T(8,128)S(1)}, u32[]{:S(2)}, u32[]{:S(2)}) collective-permute-start(f32[24,512]{1,0:T(8,128)S(1)} %get-tuple-element.26), channel_id=1, source_target_pairs={{0,4},{4,0},{8,12},{12,8},{16,20},{20,16},{24,28},{28,24},{1,5},{5... | collective-permute-start | bytes 147464 | tf_op jit(solution)/shard_map/ppermute | solution.py:365
  5.6 6.3 %collective-permute-start.1 = (f32[24,512]{1,0:T(8,128)S(1)}, f32[24,512]{1,0:T(8,128)S(1)}, u32[]{:S(2)}, u32[]{:S(2)}) collective-permute-start(f32[24,512]{1,0:T(8,128)S(1)} %get-tuple-element.30._.refs_0_), channel_id=1, source_target_pairs={{0,24},{4,28},{8,16},{12,20},{16,8},{20,12},{24,0},{28,4},{1,25},{... | collective-permute-start | bytes 147464 | tf_op jit(solution)/shard_map/ppermute | solution.py:365
  9.4 4.1 %collective-permute-start.2 = (f32[24,512]{1,0:T(8,128)S(1)}, f32[24,512]{1,0:T(8,128)S(1)}, u32[]{:S(2)}, u32[]{:S(2)}) collective-permute-start(f32[24,512]{1,0:T(8,128)S(1)} %get-tuple-element.30._.refs_0_), channel_id=1, source_target_pairs={{0,8},{4,12},{8,0},{12,4},{16,24},{20,28},{24,16},{28,20},{1,9},{5... | collective-permute-start | bytes 147464 | tf_op jit(solution)/shard_map/ppermute | solution.py:365
  9.9 4.1 %collective-permute-start.3 = (f32[24,512]{1,0:T(8,128)S(1)}, f32[24,512]{1,0:T(8,128)S(1)}, u32[]{:S(2)}, u32[]{:S(2)}) collective-permute-start(f32[24,512]{1,0:T(8,128)S(1)} %get-tuple-element.30._.refs_0_), channel_id=1, source_target_pairs={{0,16},{4,20},{8,24},{12,28},{16,0},{20,4},{24,8},{28,12},{1,17},{... | collective-permute-start | bytes 147464 | tf_op jit(solution)/shard_map/ppermute | solution.py:365
  14.1 6.5 %collective-permute-start.4 = (f32[16,512]{1,0:T(8,128)S(1)}, f32[16,512]{1,0:T(8,128)S(1)}, u32[]{:S(2)}, u32[]{:S(2)}) collective-permute-start(f32[16,512]{1,0:T(8,128)S(1)} %get-tuple-element.34), channel_id=1, source_target_pairs={{0,4},{4,0},{8,12},{12,8},{16,20},{20,16},{24,28},{28,24},{1,5},{5... | collective-permute-start | bytes 98312 | tf_op jit(solution)/shard_map/ppermute | solution.py:365
  14.2 3.8 %collective-permute-start.5 = (f32[8,512]{1,0:T(8,128)S(1)}, f32[8,512]{1,0:T(8,128)S(1)}, u32[]{:S(2)}, u32[]{:S(2)}) collective-permute-start(f32[8,512]{1,0:T(8,128)S(1)} %get-tuple-element.37._.own), channel_id=1, source_target_pairs={{0,1},{1,0},{2,3},{3,2},{4,5},{5,4},{6,7},{7,6},{8,9},{9,8},{10,11... | collective-permute-start | bytes 49160 | tf_op jit(solution)/shard_map/ppermute | solution.py:365
  18.0 5.1 %collective-permute-start.6 = (f32[8,512]{1,0:T(8,128)S(1)}, f32[8,512]{1,0:T(8,128)S(1)}, u32[]{:S(2)}, u32[]{:S(2)}) collective-permute-start(f32[8,512]{1,0:T(8,128)S(1)} %sum_groups.2.refs_6_.own), channel_id=1, source_target_pairs={{0,2},{1,3},{2,0},{3,1},{4,6},{5,7},{6,4},{7,5},{8,10},{9,11},{10,... | collective-permute-start | bytes 49160 | tf_op jit(solution)/shard_map/ppermute | solution.py:365
  23.1 1.2 %collective-permute-start.7 = (f32[8,512]{1,0:T(8,128)S(1)}, f32[8,512]{1,0:T(8,128)S(1)}, u32[]{:S(2)}, u32[]{:S(2)}) collective-permute-start(f32[8,512]{1,0:T(8,128)S(1)} %sum_groups.3.own), channel_id=1, source_target_pairs={{0,4},{4,0},{8,12},{12,8},{16,20},{20,16},{24,28},{28,24},{1,5},{5... | collective-permute-start | bytes 49160 | tf_op jit(solution)/shard_map/ppermute | solution.py:365

commit v8 on v7

--- a/solution.py
+++ b/solution.py
@@ -105,23 +105,31 @@
     lax.fori_loop(0, channels // LANES, tile_step, 0)
 
 
-    second = on_second()
+    own_high = owns_high()
     half = modes // 2
     for i in range(3):
         low, high = segment[pl.ds(i * modes, half)], segment[pl.ds(i * modes + half, half)]
-        message[pl.ds(i * half, half)] = jnp.where(second, low, high)
+        message[pl.ds(i * half, half)] = jnp.where(own_high, low, high)
 
 
 def on_second():
     return lax.rem(lax.axis_index("ctx"), 2) == 1
 
 
-def own_half(second, values):
+def owns_high():
+    place, group = lax.axis_index("ctx"), lax.axis_index("ch")
+    bits = place ^ group
+    for shift in (16, 8, 4, 2, 1):
+        bits = bits ^ lax.shift_right_logical(bits, jnp.int32(shift))
+    return lax.rem(bits, 2) == 1
+
+
+def own_half(high, values):
     half = values.shape[0] // 2
-    return jnp.where(second, values[half:], values[:half])
-
-
-def both_halves(second, own, other):
+    return jnp.where(high, values[half:], values[:half])
+
+
+def in_order(second, own, other):
     return jnp.where(second, other, own), jnp.where(second, own, other)
 
 
@@ -194,11 +202,11 @@
 def join_chip_kernel(tokens, segment, other, decay_ref, _, joined, core):
     modes = decay_ref.shape[0]
     half = modes // 2
-    second = on_second()
-    decay = own_half(second, decay_ref[...])
-    mine = [own_half(second, segment[i * modes:(i + 1) * modes]) for i in range(3)]
+    high = owns_high()
+    decay = own_half(high, decay_ref[...])
+    mine = [own_half(high, segment[i * modes:(i + 1) * modes]) for i in range(3)]
     theirs = [other[i * half:(i + 1) * half] for i in range(3)]
-    (close0, close1), (open0, open1), _ = (both_halves(second, a, b) for a, b in zip(mine, theirs))
+    (close0, close1), (open0, open1), _ = (in_order(on_second(), a, b) for a, b in zip(mine, theirs))
     block = jnp.exp(decay * (-1.0 * tokens))
     joined[0:half] = block * close0 + close1
     joined[half:2 * half] = open0 + block * open1
@@ -213,7 +221,7 @@
     core, decay_ref, carried, _ = refs[count:count + 4]
     *outs, ordered = refs[count + 4:]
     second = on_second()
-    decay = own_half(second, decay_ref[...])
+    decay = own_half(owns_high(), decay_ref[...])
     half = decay.shape[0]
     chip = lax.div(lax.axis_index("ctx"), 2)
     place = lax.rem(lax.div(chip, size), count)
@@ -263,10 +271,10 @@
     half = modes // 2
     chunks = near[0].shape[1] // SUB
     span = chunks * SUB
-    second = on_second()
+    own_high = owns_high()
     first = residue_ref[...] * jnp.exp(-decay_ref[...])
     for target, rows in ((arrive, slice(0, half)), (leave, slice(half, modes))):
-        low, high = both_halves(second, own[rows], other[rows])
+        low, high = in_order(own_high, own[rows], other[rows])
         target[0:half] = low * first[0:half]
         target[half:] = high * first[half:]
 
@@ -322,7 +330,7 @@
 
 def assemble_kernel(scale, own, other, out_ref):
     half = own.shape[0]
-    low, high = both_halves(on_second(), own[...], other[...])
+    low, high = in_order(owns_high(), own[...], other[...])
     out_ref[0:half] = low * scale
     out_ref[half:] = high * scale
 
@@ -361,8 +369,11 @@
     ranges = [(0, quarter), (quarter, 3 * quarter), (3 * quarter, tiles)]
     small = dict(compiler_params=PARAMS, cost_estimate=cost(elements, modes * channels, modes * channels * 32))
 
-    def swap(x, axis, size, mask):
-        return lax.ppermute(x, axis, [(i, i ^ mask) for i in range(size)])
+    def swap(x, ctx_mask, ch_mask=0):
+        if ctx_mask != 1:
+            ctx_mask |= (ctx_mask.bit_count() + ch_mask.bit_count()) % 2
+        mask = ctx_mask * groups + ch_mask
+        return lax.ppermute(x, ("ctx", "ch"), [(i, i ^ mask) for i in range(n * groups)])
 
     def near_part(part, after):
         first, last = ranges[part]
@@ -393,7 +404,7 @@
         name="block_states",
     )(*(pltpu.with_memory_space_constraint(a, pltpu.HBM) for a in inputs))
 
-    other = swap(message, "ctx", n, 1)
+    other = swap(message, 1)
     near = near_part(0, segment)
     joined, core = pl.pallas_call(
         functools.partial(join_chip_kernel, tokens),
@@ -410,7 +421,7 @@
         count = min(4, chips // size)
         last = size * count == chips
         masks = [3, 1, 2] if count == 4 else [1]
-        others = [swap(joined, "ctx", n, 2 * size * m) for m in masks]
+        others = [swap(joined, 2 * size * m) for m in masks]
         if last:
             near = near + near_part(1, joined)
         rows = [half, 2 * half, 2 * half] if last else [3 * half, 2 * half]
@@ -427,9 +438,9 @@
     grad = joined
     stride = 1
     while stride < groups:
-        other = swap(grad, "ch", groups, stride)
+        other = swap(grad, 0, stride)
         if stride == 1:
-            received = swap(message[0], "ctx", n, 1)
+            received = swap(message[0], 1)
             near = near + near_part(2, grad)
             pinned = near[-1]
         stride *= 2
@@ -459,7 +470,7 @@
         out_shape=shaped(modes, channels),
         name="assemble_gradient",
         **small,
-    )(grad, swap(grad, "ctx", n, 1))
+    )(grad, swap(grad, 1))
     return conv_out, signal_grad, residue_grad
 
 

time: 25.2 us -> 23.9 us (0.948)
  waiting for transfers between devices: 4.59 us -> 3.5 us
    ppermute x8, waiting for transfers between devices: 4.59 us -> 3.5 us  [swap(): lax.ppermute(x, ('ctx', 'ch'), [(i, i ^ mask) for i in range(n * groups)])]
  transfers between devices with their start and end apart: 8 -> 8, of which waited for: 4 -> 3; matrix products, arithmetic and copies ran while one was open for 0% -> 0% of each run, Pallas kernels for 25% -> 26%
where the time goes in v8:
time: 23.9 us; the launch traced here: 23.8 us
  Pallas kernels  10.4 us (44%)
  starting transfers between devices  9.21 us (39%)
  waiting for transfers between devices  3.5 us (15%)
  between operations  0.71 us (3%)
    ppermute x8, starting transfers between devices, swap(): lax.ppermute(x, ('ctx', 'ch'), [(i, i ^ mask) for i in range(n * groups)])  9.21 us
    pallas_call x3, Pallas kernels, near_part(): pl.pallas_call(functools.partial(local_kernel, ranges[part]), out_shape=[...  3.62 us
    ppermute x8, waiting for transfers between devices, swap(): lax.ppermute(x, ('ctx', 'ch'), [(i, i ^ mask) for i in range(n * groups)])  3.5 us
    pallas_call x1, Pallas kernels, body(): pl.pallas_call(gather_kernel, out_shape=[jax.ShapeDtypeStruct(a.shape, a....  3.48 us
    pallas_call x1, Pallas kernels, body(): pl.pallas_call(functools.partial(finish_kernel, ranges), out_shape=[jax.S...  2.53 us
    pallas_call x1, Pallas kernels, body(): pl.pallas_call(functools.partial(assemble_kernel, 1.0 / (tokens * n)), ou...  0.62 us
  transfers between devices with their start and end apart: 8, of which 3 were waited for; matrix products, arithmetic and copies ran while one was open for 0% of the time, Pallas kernels for 26%

profile of v8, /device:TPU:0, one launch (start us, length us, event | category | flops | bytes accessed | tf_op | source)
XLA Modules:
  0.0 23.8 jit_solution(17853214546376003617)
XLA Ops:
  0.6 3.5 %block_states.1 = (bf16[256,512]{1,0:T(8,128)(2,1)S(1)}, bf16[256,512]{1,0:T(8,128)(2,1)S(1)}, f32[16,512]{1,0:T(8,128)S(1)}, f32[16,512]{1,0:T(8,128)S(1)}, f32...) custom-call(bf16[256,512]{1,0:T(8,128)(2,1)} %refs_0_.1, bf16[256,512]{1,0:T(8,128)(2,1)} %refs_1_.1, f32[16,512]{1,0:T(8,128)} %refs_2_.1, ...), custom_call_target="tpu_custom_call" | custom-call | flops 10485760 | bytes 786432 | tf_op jit(solution)/shard_map/block_states/pallas_call | solution.py:395
  4.1 0.5 %collective-permute-start = (f32[24,512]{1,0:T(8,128)S(1)}, f32[24,512]{1,0:T(8,128)S(1)}, u32[]{:S(2)}, u32[]{:S(2)}) collective-permute-start(f32[24,512]{1,0:T(8,128)S(1)} %get-tuple-element.26), channel_id=1, source_target_pairs={{0,4},{1,5},{2,6},{3,7},{4,0},{5,1},{6,2},{7,3},{8,12},{9,13},{10,... | collective-permute-start | bytes 147464 | tf_op jit(solution)/shard_map/ppermute | solution.py:376
  4.6 0.9 %local_convolutions.3 = (f32[1,32,8,128]{3,2,1,0:T(8,128)S(1)}, f32[1,32,8,128]{3,2,1,0:T(8,128)S(1)}) custom-call(bf16[256,512]{1,0:T(8,128)(2,1)S(1)} %get-tuple-element.27.x_ref, bf16[256,512]{1,0:T(8,128)(2,1)S(1)} %get-tuple-element.28.g_ref, f32[16,512]{1,0:T(8,128)S(1)} %get-tuple-element.23.residue_ref, ...), custom_call_target="tpu_custom_call" | custom-call | flops 209715200 | bytes 524288 | tf_op jit(solution)/shard_map/local_convolutions/pallas_call | solution.py:381
  5.5 0.0 collective-permute-done.other
  5.6 3.8 %collective-permute-start.1 = (f32[24,512]{1,0:T(8,128)S(1)}, f32[24,512]{1,0:T(8,128)S(1)}, u32[]{:S(2)}, u32[]{:S(2)}) collective-permute-start(f32[24,512]{1,0:T(8,128)S(1)} %get-tuple-element.30._.refs_0_), channel_id=1, source_target_pairs={{0,24},{1,25},{2,26},{3,27},{4,28},{5,29},{6,30},{7,31},{8,16},{9,... | collective-permute-start | bytes 147464 | tf_op jit(solution)/shard_map/ppermute | solution.py:376
  9.4 0.1 collective-permute-start.2
  9.5 0.3 %collective-permute-start.3 = (f32[24,512]{1,0:T(8,128)S(1)}, f32[24,512]{1,0:T(8,128)S(1)}, u32[]{:S(2)}, u32[]{:S(2)}) collective-permute-start(f32[24,512]{1,0:T(8,128)S(1)} %get-tuple-element.30._.refs_0_), channel_id=1, source_target_pairs={{0,20},{1,21},{2,22},{3,23},{4,16},{5,17},{6,18},{7,19},{8,28},{9,... | collective-permute-start | bytes 147464 | tf_op jit(solution)/shard_map/ppermute | solution.py:376
  9.8 1.8 %local_convolutions.4 = (f32[2,32,8,128]{3,2,1,0:T(8,128)S(1)}, f32[2,32,8,128]{3,2,1,0:T(8,128)S(1)}) custom-call(bf16[256,512]{1,0:T(8,128)(2,1)S(1)} %get-tuple-element.27.x_ref, bf16[256,512]{1,0:T(8,128)(2,1)S(1)} %get-tuple-element.28.g_ref, f32[16,512]{1,0:T(8,128)S(1)} %get-tuple-element.23.residue_ref, ...), custom_call_target="tpu_custom_call" | custom-call | flops 419430400 | bytes 1048576 | tf_op jit(solution)/shard_map/local_convolutions/pallas_call | solution.py:381
  11.6 0.0 collective-permute-done.1.refs_1_
  11.6 1.7 %collective-permute-done.2.refs_2_ = f32[24,512]{1,0:T(8,128)S(1)} collective-permute-done((f32[24,512]{1,0:T(8,128)S(1)}, f32[24,512]{1,0:T(8,128)S(1)}, u32[]{:S(2)}, u32[]{:S(2)}) %collective-permute-start.2) | collective-permute-done | bytes 49184 | tf_op jit(solution)/shard_map/ppermute | solution.py:376
  13.3 0.0 collective-permute-done.3.refs_3_
  13.3 0.1 join_chips.1
  13.4 0.3 %collective-permute-start.4 = (f32[16,512]{1,0:T(8,128)S(1)}, f32[16,512]{1,0:T(8,128)S(1)}, u32[]{:S(2)}, u32[]{:S(2)}) collective-permute-start(f32[16,512]{1,0:T(8,128)S(1)} %get-tuple-element.34), channel_id=1, source_target_pairs={{0,4},{1,5},{2,6},{3,7},{4,0},{5,1},{6,2},{7,3},{8,12},{9,13},{10,... | collective-permute-start | bytes 98312 | tf_op jit(solution)/shard_map/ppermute | solution.py:376
  13.7 1.5 %collective-permute-start.5 = (f32[8,512]{1,0:T(8,128)S(1)}, f32[8,512]{1,0:T(8,128)S(1)}, u32[]{:S(2)}, u32[]{:S(2)}) collective-permute-start(f32[8,512]{1,0:T(8,128)S(1)} %get-tuple-element.37._.own), channel_id=1, source_target_pairs={{0,5},{1,4},{2,7},{3,6},{4,1},{5,0},{6,3},{7,2},{8,13},{9,12},{10,... | collective-permute-start | bytes 49160 | tf_op jit(solution)/shard_map/ppermute | solution.py:376
  15.2 0.9 %local_convolutions.5 = (f32[1,32,8,128]{3,2,1,0:T(8,128)S(1)}, f32[1,32,8,128]{3,2,1,0:T(8,128)S(1)}) custom-call(bf16[256,512]{1,0:T(8,128)(2,1)S(1)} %get-tuple-element.27.x_ref, bf16[256,512]{1,0:T(8,128)(2,1)S(1)} %get-tuple-element.28.g_ref, f32[16,512]{1,0:T(8,128)S(1)} %get-tuple-element.23.residue_ref, ...), custom_call_target="tpu_custom_call" | custom-call | flops 209715200 | bytes 524288 | tf_op jit(solution)/shard_map/local_convolutions/pallas_call | solution.py:381
  16.1 0.8 %collective-permute-done.5.other = f32[8,512]{1,0:T(8,128)S(1)} collective-permute-done((f32[8,512]{1,0:T(8,128)S(1)}, f32[8,512]{1,0:T(8,128)S(1)}, u32[]{:S(2)}, u32[]{:S(2)}) %collective-permute-start.5) | collective-permute-done | bytes 16416 | tf_op jit(solution)/shard_map/ppermute | solution.py:376
  16.9 2.5 %collective-permute-start.6 = (f32[8,512]{1,0:T(8,128)S(1)}, f32[8,512]{1,0:T(8,128)S(1)}, u32[]{:S(2)}, u32[]{:S(2)}) collective-permute-start(f32[8,512]{1,0:T(8,128)S(1)} %sum_groups.2.refs_6_.own), channel_id=1, source_target_pairs={{0,6},{1,7},{2,4},{3,5},{4,2},{5,3},{6,0},{7,1},{8,14},{9,15},{10,... | collective-permute-start | bytes 49160 | tf_op jit(solution)/shard_map/ppermute | solution.py:376
  19.3 0.0 collective-permute-done.4.other
  19.3 2.5 %add_arrivals.1 = (bf16[256,512]{1,0:T(8,128)(2,1)}, bf16[256,512]{1,0:T(8,128)(2,1)}, f32[8,128]{1,0:T(8,128)S(1)}) custom-call(f32[16,512]{1,0:T(8,128)S(1)} %get-tuple-element.23.residue_ref, f32[16,512]{1,0:T(8,128)S(1)} %get-tuple-element.24.decay_ref.refs_5_, f32[16,512]{1,0:T(8,128)S(1)} %get-tuple-element.33.own, ...), custom_call_target="tpu_custom_call" | custom-call | flops 1258291200 | bytes 1572864 | tf_op jit(solution)/shard_map/add_arrivals/pallas_call | solution.py:448
  21.9 0.0 collective-permute-done.6.other
  21.9 0.3 %collective-permute-start.7 = (f32[8,512]{1,0:T(8,128)S(1)}, f32[8,512]{1,0:T(8,128)S(1)}, u32[]{:S(2)}, u32[]{:S(2)}) collective-permute-start(f32[8,512]{1,0:T(8,128)S(1)} %sum_groups.3.own), channel_id=1, source_target_pairs={{0,4},{1,5},{2,6},{3,7},{4,0},{5,1},{6,2},{7,3},{8,12},{9,13},{10,... | collective-permute-start | bytes 49160 | tf_op jit(solution)/shard_map/ppermute | solution.py:376
  22.2 0.9 %collective-permute-done.7.other = f32[8,512]{1,0:T(8,128)S(1)} collective-permute-done((f32[8,512]{1,0:T(8,128)S(1)}, f32[8,512]{1,0:T(8,128)S(1)}, u32[]{:S(2)}, u32[]{:S(2)}) %collective-permute-start.7) | collective-permute-done | bytes 16416 | tf_op jit(solution)/shard_map/ppermute | solution.py:376
  23.2 0.6 %assemble_gradient.1 = f32[16,512]{1,0:T(8,128)} custom-call(f32[8,512]{1,0:T(8,128)S(1)} %sum_groups.3.own, f32[8,512]{1,0:T(8,128)S(1)} %collective-permute-done.7.other), custom_call_target="tpu_custom_call" | custom-call | flops 131072 | bytes 262144 | tf_op jit(solution)/shard_map/assemble_gradient/pallas_call | solution.py:468
  (3 shorter events, 0.1 us)
Async XLA Ops:
  4.1 1.4 %collective-permute-start = (f32[24,512]{1,0:T(8,128)S(1)}, f32[24,512]{1,0:T(8,128)S(1)}, u32[]{:S(2)}, u32[]{:S(2)}) collective-permute-start(f32[24,512]{1,0:T(8,128)S(1)} %get-tuple-element.26), channel_id=1, source_target_pairs={{0,4},{1,5},{2,6},{3,7},{4,0},{5,1},{6,2},{7,3},{8,12},{9,13},{10,... | collective-permute-start | bytes 147464 | tf_op jit(solution)/shard_map/ppermute | solution.py:376
  5.6 6.0 %collective-permute-start.1 = (f32[24,512]{1,0:T(8,128)S(1)}, f32[24,512]{1,0:T(8,128)S(1)}, u32[]{:S(2)}, u32[]{:S(2)}) collective-permute-start(f32[24,512]{1,0:T(8,128)S(1)} %get-tuple-element.30._.refs_0_), channel_id=1, source_target_pairs={{0,24},{1,25},{2,26},{3,27},{4,28},{5,29},{6,30},{7,31},{8,16},{9,... | collective-permute-start | bytes 147464 | tf_op jit(solution)/shard_map/ppermute | solution.py:376
  9.4 3.9 %collective-permute-start.2 = (f32[24,512]{1,0:T(8,128)S(1)}, f32[24,512]{1,0:T(8,128)S(1)}, u32[]{:S(2)}, u32[]{:S(2)}) collective-permute-start(f32[24,512]{1,0:T(8,128)S(1)} %get-tuple-element.30._.refs_0_), channel_id=1, source_target_pairs={{0,12},{1,13},{2,14},{3,15},{4,8},{5,9},{6,10},{7,11},{8,4},{9,5},... | collective-permute-start | bytes 147464 | tf_op jit(solution)/shard_map/ppermute | solution.py:376
  9.5 3.9 %collective-permute-start.3 = (f32[24,512]{1,0:T(8,128)S(1)}, f32[24,512]{1,0:T(8,128)S(1)}, u32[]{:S(2)}, u32[]{:S(2)}) collective-permute-start(f32[24,512]{1,0:T(8,128)S(1)} %get-tuple-element.30._.refs_0_), channel_id=1, source_target_pairs={{0,20},{1,21},{2,22},{3,23},{4,16},{5,17},{6,18},{7,19},{8,28},{9,... | collective-permute-start | bytes 147464 | tf_op jit(solution)/shard_map/ppermute | solution.py:376
  13.4 5.9 %collective-permute-start.4 = (f32[16,512]{1,0:T(8,128)S(1)}, f32[16,512]{1,0:T(8,128)S(1)}, u32[]{:S(2)}, u32[]{:S(2)}) collective-permute-start(f32[16,512]{1,0:T(8,128)S(1)} %get-tuple-element.34), channel_id=1, source_target_pairs={{0,4},{1,5},{2,6},{3,7},{4,0},{5,1},{6,2},{7,3},{8,12},{9,13},{10,... | collective-permute-start | bytes 98312 | tf_op jit(solution)/shard_map/ppermute | solution.py:376
  13.7 3.2 %collective-permute-start.5 = (f32[8,512]{1,0:T(8,128)S(1)}, f32[8,512]{1,0:T(8,128)S(1)}, u32[]{:S(2)}, u32[]{:S(2)}) collective-permute-start(f32[8,512]{1,0:T(8,128)S(1)} %get-tuple-element.37._.own), channel_id=1, source_target_pairs={{0,5},{1,4},{2,7},{3,6},{4,1},{5,0},{6,3},{7,2},{8,13},{9,12},{10,... | collective-permute-start | bytes 49160 | tf_op jit(solution)/shard_map/ppermute | solution.py:376
  16.9 5.0 %collective-permute-start.6 = (f32[8,512]{1,0:T(8,128)S(1)}, f32[8,512]{1,0:T(8,128)S(1)}, u32[]{:S(2)}, u32[]{:S(2)}) collective-permute-start(f32[8,512]{1,0:T(8,128)S(1)} %sum_groups.2.refs_6_.own), channel_id=1, source_target_pairs={{0,6},{1,7},{2,4},{3,5},{4,2},{5,3},{6,0},{7,1},{8,14},{9,15},{10,... | collective-permute-start | bytes 49160 | tf_op jit(solution)/shard_map/ppermute | solution.py:376
  21.9 1.2 %collective-permute-start.7 = (f32[8,512]{1,0:T(8,128)S(1)}, f32[8,512]{1,0:T(8,128)S(1)}, u32[]{:S(2)}, u32[]{:S(2)}) collective-permute-start(f32[8,512]{1,0:T(8,128)S(1)} %sum_groups.3.own), channel_id=1, source_target_pairs={{0,4},{1,5},{2,6},{3,7},{4,0},{5,1},{6,2},{7,3},{8,12},{9,13},{10,... | collective-permute-start | bytes 49160 | tf_op jit(solution)/shard_map/ppermute | solution.py:376

commit v9 on v8

--- a/solution.py
+++ b/solution.py
@@ -16,14 +16,15 @@
     return jnp.broadcast_to(ref[index], (SUB, LANES))
 
 
-def split_lanes(source, target, tile):
-    lanes = pl.ds(pl.multiple_of(tile * LANES, LANES), LANES)
-    target[...] = source[:, lanes].astype(F32)
-
-
-def read_tokens(scratch, chunks):
-    span = chunks * SUB
-    return [[scratch[pl.ds(p * SUB + r, SUB, stride=span), :] for r in range(SUB)] for p in range(chunks)]
+def token_order(tokens):
+    rows = lax.broadcasted_iota(jnp.int32, (tokens, tokens), 0)
+    columns = lax.broadcasted_iota(jnp.int32, (tokens, tokens), 1)
+    wanted = lax.rem(rows, SUB) * (tokens // SUB) + lax.div(rows, SUB)
+    return jnp.where(columns == wanted, 1.0, 0.0).astype(jnp.bfloat16)
+
+
+def read_tokens(ref, chunks, lanes):
+    return [[ref[pl.ds((p * SUB + r) * SUB, SUB), lanes] for r in range(SUB)] for p in range(chunks)]
 
 
 def powers(decay, pw):
@@ -56,26 +57,28 @@
 
 
 def gather_kernel(*refs):
-    sources, staged = refs[:4], refs[4:8]
-    segment, message, xf, gf, pw, ends, starts, inner, sems = refs[8:]
-    x_ref, g_ref, _, decay_ref = staged
+    sources = refs[:4]
+    xf, gf, residue_ref, decay_ref, segment, message, pw, ends, starts, inner, x_ref, g_ref, sems = refs[4:]
+    staged = x_ref, g_ref, residue_ref, decay_ref
     copies = [pltpu.make_async_copy(*pair, sems.at[i]) for i, pair in enumerate(zip(sources, staged))]
     for copy in copies:
         copy.start()
     modes, channels = decay_ref.shape
-    chunks = x_ref.shape[0] // (SUB * SUB)
+    tokens = x_ref.shape[0]
+    chunks = tokens // (SUB * SUB)
     span = chunks * SUB
     closing, opening, grad = (segment.at[pl.ds(i * modes, modes)] for i in range(3))
+    order = token_order(tokens)
     for copy in copies:
         copy.wait()
+    xf[...] = jnp.dot(order, x_ref[...], preferred_element_type=F32)
+    gf[...] = jnp.dot(order, g_ref[...], preferred_element_type=F32)
 
     def tile_step(tile, _):
         lanes = pl.ds(pl.multiple_of(tile * LANES, LANES), LANES)
-        split_lanes(x_ref, xf, tile)
-        split_lanes(g_ref, gf, tile)
         decay = decay_ref[:, lanes]
         powers(decay, pw)
-        xs, gs = read_tokens(xf, chunks), read_tokens(gf, chunks)
+        xs, gs = read_tokens(xf, chunks, lanes), read_tokens(gf, chunks, lanes)
         for m in range(modes):
             held, back, opens = chunk_states(m, xs, gs, pw)
             rows = pl.ds(m * SUB, SUB)
@@ -133,21 +136,19 @@
     return jnp.where(second, other, own), jnp.where(second, own, other)
 
 
-def local_kernel(tiles, x_ref, g_ref, residue_ref, decay_ref, _, out_ref, back_ref,
-                 xf, gf, pw, ends, starts, before, after, arrive, leave):
+def local_kernel(tiles, xf, gf, residue_ref, decay_ref, _, out_ref, back_ref,
+                 pw, ends, starts, before, after, arrive, leave):
     modes, channels = decay_ref.shape
-    chunks = x_ref.shape[0] // (SUB * SUB)
+    chunks = xf.shape[0] // (SUB * SUB)
     span = chunks * SUB
 
     def tile_step(tile, _):
         lanes = pl.ds(pl.multiple_of(tile * LANES, LANES), LANES)
-        split_lanes(x_ref, xf, tile)
-        split_lanes(g_ref, gf, tile)
         decay = decay_ref[:, lanes]
         residue = residue_ref[:, lanes]
         powers(decay, pw)
         pw[2] = residue * pw[0]
-        xs, gs = read_tokens(xf, chunks), read_tokens(gf, chunks)
+        xs, gs = read_tokens(xf, chunks, lanes), read_tokens(gf, chunks, lanes)
         for m in range(modes):
             held, back, _ = chunk_states(m, xs, gs, pw)
             rows = pl.ds(m * SUB, SUB)
@@ -362,7 +363,6 @@
     n, groups = lax.axis_size("ctx"), lax.axis_size("ch")
     chunks = tokens // (SUB * SUB)
     elements = tokens * channels
-    tokens_scratch = [vmem(tokens, LANES), vmem(tokens, LANES)]
     spans = vmem(modes * SUB, LANES)
     tiles = channels // LANES
     quarter = tiles // 4
@@ -382,27 +382,29 @@
             functools.partial(local_kernel, ranges[part]),
             out_shape=[shaped(last - first, chunks * SUB, SUB, LANES)] * 2,
             in_specs=[WHOLE] * 4 + [UNREAD],
-            scratch_shapes=tokens_scratch
-            + [vmem(3, modes, LANES), spans, spans]
+            scratch_shapes=[vmem(3, modes, LANES), spans, spans]
             + [vmem(modes, chunks - 1, SUB, LANES)] * 2
             + [spans, spans],
             compiler_params=PARAMS,
             cost_estimate=cost(share * 400, 0, share),
             name="local_convolutions",
-        )(signal, cotangent, residue, decay, after)
-
-    inputs = signal, cotangent, residue, decay
-    signal, cotangent, residue, decay, segment, message = pl.pallas_call(
+        )(*inputs, after)
+
+    values = shaped(tokens, channels)
+    *inputs, segment, message = pl.pallas_call(
         gather_kernel,
-        out_shape=[jax.ShapeDtypeStruct(a.shape, a.dtype) for a in inputs]
+        out_shape=[values, values]
+        + [shaped(modes, channels)] * 2
         + [shaped(3 * modes, channels), shaped(3 * half, channels)],
         in_specs=[HBM] * 4,
-        scratch_shapes=tokens_scratch
-        + [vmem(2, modes, LANES), spans, spans, spans, pltpu.SemaphoreType.DMA((4,))],
+        scratch_shapes=[vmem(2, modes, LANES), spans, spans, spans]
+        + [pltpu.VMEM(signal.shape, signal.dtype)] * 2
+        + [pltpu.SemaphoreType.DMA((4,))],
         compiler_params=PARAMS,
         cost_estimate=cost(elements * modes * 5, modes * channels * 3, elements * 6),
         name="block_states",
-    )(*(pltpu.with_memory_space_constraint(a, pltpu.HBM) for a in inputs))
+    )(*(pltpu.with_memory_space_constraint(a, pltpu.HBM) for a in (signal, cotangent, residue, decay)))
+    residue, decay = inputs[2:]
 
     other = swap(message, 1)
     near = near_part(0, segment)

time: 23.9 us -> 23.7 us (level)
  Pallas kernels: 10.4 us -> 9.55 us
  waiting for transfers between devices: 3.5 us -> 4.04 us
    ppermute x8, waiting for transfers between devices: 3.5 us -> 4.04 us  [swap(): lax.ppermute(x, ('ctx', 'ch'), [(i, i ^ mask) for i in range(n * groups)])]
    pallas_call x3, Pallas kernels: 3.62 us -> 3.11 us  [near_part(): pl.pallas_call(functools.partial(local_kernel, ranges[part]), out_shape=[...]
    pallas_call x1, Pallas kernels: 3.48 us -> 3.19 us  [body(): pl.pallas_call(gather_kernel, out_shape=[values, values] + [shaped(modes,...]
  transfers between devices with their start and end apart: 8 -> 8, of which waited for: 3 -> 5; matrix products, arithmetic and copies ran while one was open for 0% -> 0% of each run, Pallas kernels for 26% -> 24%
where the time goes in v9:
time: 23.7 us; the launch traced here: 23.5 us
  Pallas kernels  9.55 us (40%)
  starting transfers between devices  9.26 us (39%)
  waiting for transfers between devices  4.04 us (17%)
  between operations  0.69 us (3%)
    ppermute x8, starting transfers between devices, swap(): lax.ppermute(x, ('ctx', 'ch'), [(i, i ^ mask) for i in range(n * groups)])  9.26 us
    ppermute x8, waiting for transfers between devices, swap(): lax.ppermute(x, ('ctx', 'ch'), [(i, i ^ mask) for i in range(n * groups)])  4.04 us
    pallas_call x1, Pallas kernels, body(): pl.pallas_call(gather_kernel, out_shape=[values, values] + [shaped(modes,...  3.19 us
    pallas_call x3, Pallas kernels, near_part(): pl.pallas_call(functools.partial(local_kernel, ranges[part]), out_shape=[...  3.11 us
    pallas_call x1, Pallas kernels, body(): pl.pallas_call(functools.partial(finish_kernel, ranges), out_shape=[jax.S...  2.53 us
    pallas_call x1, Pallas kernels, body(): pl.pallas_call(functools.partial(assemble_kernel, 1.0 / (tokens * n)), ou...  0.62 us
  transfers between devices with their start and end apart: 8, of which 5 were waited for; matrix products, arithmetic and copies ran while one was open for 0% of the time, Pallas kernels for 24%

profile of v9, /device:TPU:0, one launch (start us, length us, event | category | flops | bytes accessed | tf_op | source)
XLA Modules:
  0.0 23.5 jit_solution(1917958738019607568)
XLA Ops:
  0.6 3.2 %block_states.1 = (f32[256,512]{1,0:T(8,128)S(1)}, f32[256,512]{1,0:T(8,128)S(1)}, f32[16,512]{1,0:T(8,128)S(1)}, f32[16,512]{1,0:T(8,128)S(1)}, f32[48,512]{1,0:T(8,128)S(1)}, /*index=5*/f32[24,512]{1,0:T(8,128)S(1)}) custom-call(bf16[256,512]{1,0:T(8,128)(2,1)} %refs_0_.1, bf16[256,512]{1,0:T(8,128)(2,1)} %refs_1_.1, f32[16,512]{1,0:T(8,128)} %refs_2_.1, ...), custom_call_target="tpu_custom_call" | custom-call | flops 10485760 | bytes 786432 | tf_op jit(solution)/shard_map/block_states/pallas_call | solution.py:394
  3.8 0.5 %collective-permute-start = (f32[24,512]{1,0:T(8,128)S(1)}, f32[24,512]{1,0:T(8,128)S(1)}, u32[]{:S(2)}, u32[]{:S(2)}) collective-permute-start(f32[24,512]{1,0:T(8,128)S(1)} %get-tuple-element.26), channel_id=1, source_target_pairs={{0,4},{1,5},{2,6},{3,7},{4,0},{5,1},{6,2},{7,3},{8,12},{9,13},{10,... | collective-permute-start | bytes 147464 | tf_op jit(solution)/shard_map/ppermute | solution.py:376
  4.4 0.8 %local_convolutions.3 = (f32[1,32,8,128]{3,2,1,0:T(8,128)S(1)}, f32[1,32,8,128]{3,2,1,0:T(8,128)S(1)}) custom-call(f32[256,512]{1,0:T(8,128)S(1)} %get-tuple-element.27.xf, f32[256,512]{1,0:T(8,128)S(1)} %get-tuple-element.28.gf, f32[16,512]{1,0:T(8,128)S(1)} %get-tuple-element.23.residue_ref, f32[16,512]{1,0:T(8,128)S(1)} %get-tuple-element.24.decay_ref.refs_5_, ...), custom_call_target="tpu_custom_call" | custom-call | flops 209715200 | bytes 524288 | tf_op jit(solution)/shard_map/local_convolutions/pallas_call | solution.py:381
  5.1 0.1 collective-permute-done.other
  5.3 3.9 %collective-permute-start.1 = (f32[24,512]{1,0:T(8,128)S(1)}, f32[24,512]{1,0:T(8,128)S(1)}, u32[]{:S(2)}, u32[]{:S(2)}) collective-permute-start(f32[24,512]{1,0:T(8,128)S(1)} %get-tuple-element.30._.refs_0_), channel_id=1, source_target_pairs={{0,24},{1,25},{2,26},{3,27},{4,28},{5,29},{6,30},{7,31},{8,16},{9,... | collective-permute-start | bytes 147464 | tf_op jit(solution)/shard_map/ppermute | solution.py:376
  9.1 0.0 collective-permute-start.2
  9.1 0.3 %collective-permute-start.3 = (f32[24,512]{1,0:T(8,128)S(1)}, f32[24,512]{1,0:T(8,128)S(1)}, u32[]{:S(2)}, u32[]{:S(2)}) collective-permute-start(f32[24,512]{1,0:T(8,128)S(1)} %get-tuple-element.30._.refs_0_), channel_id=1, source_target_pairs={{0,20},{1,21},{2,22},{3,23},{4,16},{5,17},{6,18},{7,19},{8,28},{9,... | collective-permute-start | bytes 147464 | tf_op jit(solution)/shard_map/ppermute | solution.py:376
  9.5 1.6 %local_convolutions.4 = (f32[2,32,8,128]{3,2,1,0:T(8,128)S(1)}, f32[2,32,8,128]{3,2,1,0:T(8,128)S(1)}) custom-call(f32[256,512]{1,0:T(8,128)S(1)} %get-tuple-element.27.xf, f32[256,512]{1,0:T(8,128)S(1)} %get-tuple-element.28.gf, f32[16,512]{1,0:T(8,128)S(1)} %get-tuple-element.23.residue_ref, f32[16,512]{1,0:T(8,128)S(1)} %get-tuple-element.24.decay_ref.refs_5_, ...), custom_call_target="tpu_custom_call" | custom-call | flops 419430400 | bytes 1048576 | tf_op jit(solution)/shard_map/local_convolutions/pallas_call | solution.py:381
  11.0 0.2 collective-permute-done.1.refs_1_
  11.2 1.9 %collective-permute-done.2.refs_2_ = f32[24,512]{1,0:T(8,128)S(1)} collective-permute-done((f32[24,512]{1,0:T(8,128)S(1)}, f32[24,512]{1,0:T(8,128)S(1)}, u32[]{:S(2)}, u32[]{:S(2)}) %collective-permute-start.2) | collective-permute-done | bytes 49184 | tf_op jit(solution)/shard_map/ppermute | solution.py:376
  13.1 0.0 collective-permute-done.3.refs_3_
  13.1 0.1 join_chips.1
  13.2 0.2 %collective-permute-start.4 = (f32[16,512]{1,0:T(8,128)S(1)}, f32[16,512]{1,0:T(8,128)S(1)}, u32[]{:S(2)}, u32[]{:S(2)}) collective-permute-start(f32[16,512]{1,0:T(8,128)S(1)} %get-tuple-element.34), channel_id=1, source_target_pairs={{0,4},{1,5},{2,6},{3,7},{4,0},{5,1},{6,2},{7,3},{8,12},{9,13},{10,... | collective-permute-start | bytes 98312 | tf_op jit(solution)/shard_map/ppermute | solution.py:376
  13.4 1.5 %collective-permute-start.5 = (f32[8,512]{1,0:T(8,128)S(1)}, f32[8,512]{1,0:T(8,128)S(1)}, u32[]{:S(2)}, u32[]{:S(2)}) collective-permute-start(f32[8,512]{1,0:T(8,128)S(1)} %get-tuple-element.37._.own), channel_id=1, source_target_pairs={{0,5},{1,4},{2,7},{3,6},{4,1},{5,0},{6,3},{7,2},{8,13},{9,12},{10,... | collective-permute-start | bytes 49160 | tf_op jit(solution)/shard_map/ppermute | solution.py:376
  14.9 0.8 %local_convolutions.5 = (f32[1,32,8,128]{3,2,1,0:T(8,128)S(1)}, f32[1,32,8,128]{3,2,1,0:T(8,128)S(1)}) custom-call(f32[256,512]{1,0:T(8,128)S(1)} %get-tuple-element.27.xf, f32[256,512]{1,0:T(8,128)S(1)} %get-tuple-element.28.gf, f32[16,512]{1,0:T(8,128)S(1)} %get-tuple-element.23.residue_ref, f32[16,512]{1,0:T(8,128)S(1)} %get-tuple-element.24.decay_ref.refs_5_, ...), custom_call_target="tpu_custom_call" | custom-call | flops 209715200 | bytes 524288 | tf_op jit(solution)/shard_map/local_convolutions/pallas_call | solution.py:381
  15.7 0.9 %collective-permute-done.5.other = f32[8,512]{1,0:T(8,128)S(1)} collective-permute-done((f32[8,512]{1,0:T(8,128)S(1)}, f32[8,512]{1,0:T(8,128)S(1)}, u32[]{:S(2)}, u32[]{:S(2)}) %collective-permute-start.5) | collective-permute-done | bytes 16416 | tf_op jit(solution)/shard_map/ppermute | solution.py:376
  16.6 2.5 %collective-permute-start.6 = (f32[8,512]{1,0:T(8,128)S(1)}, f32[8,512]{1,0:T(8,128)S(1)}, u32[]{:S(2)}, u32[]{:S(2)}) collective-permute-start(f32[8,512]{1,0:T(8,128)S(1)} %sum_groups.2.refs_6_.own), channel_id=1, source_target_pairs={{0,6},{1,7},{2,4},{3,5},{4,2},{5,3},{6,0},{7,1},{8,14},{9,15},{10,... | collective-permute-start | bytes 49160 | tf_op jit(solution)/shard_map/ppermute | solution.py:376
  19.1 0.0 collective-permute-done.4.other
  19.1 2.5 %add_arrivals.1 = (bf16[256,512]{1,0:T(8,128)(2,1)}, bf16[256,512]{1,0:T(8,128)(2,1)}, f32[8,128]{1,0:T(8,128)S(1)}) custom-call(f32[16,512]{1,0:T(8,128)S(1)} %get-tuple-element.23.residue_ref, f32[16,512]{1,0:T(8,128)S(1)} %get-tuple-element.24.decay_ref.refs_5_, f32[16,512]{1,0:T(8,128)S(1)} %get-tuple-element.33.own, ...), custom_call_target="tpu_custom_call" | custom-call | flops 1258291200 | bytes 1572864 | tf_op jit(solution)/shard_map/add_arrivals/pallas_call | solution.py:450
  21.6 0.0 collective-permute-done.6.other
  21.7 0.2 %collective-permute-start.7 = (f32[8,512]{1,0:T(8,128)S(1)}, f32[8,512]{1,0:T(8,128)S(1)}, u32[]{:S(2)}, u32[]{:S(2)}) collective-permute-start(f32[8,512]{1,0:T(8,128)S(1)} %sum_groups.3.own), channel_id=1, source_target_pairs={{0,4},{1,5},{2,6},{3,7},{4,0},{5,1},{6,2},{7,3},{8,12},{9,13},{10,... | collective-permute-start | bytes 49160 | tf_op jit(solution)/shard_map/ppermute | solution.py:376
  21.9 1.0 %collective-permute-done.7.other = f32[8,512]{1,0:T(8,128)S(1)} collective-permute-done((f32[8,512]{1,0:T(8,128)S(1)}, f32[8,512]{1,0:T(8,128)S(1)}, u32[]{:S(2)}, u32[]{:S(2)}) %collective-permute-start.7) | collective-permute-done | bytes 16416 | tf_op jit(solution)/shard_map/ppermute | solution.py:376
  22.9 0.6 %assemble_gradient.1 = f32[16,512]{1,0:T(8,128)} custom-call(f32[8,512]{1,0:T(8,128)S(1)} %sum_groups.3.own, f32[8,512]{1,0:T(8,128)S(1)} %collective-permute-done.7.other), custom_call_target="tpu_custom_call" | custom-call | flops 131072 | bytes 262144 | tf_op jit(solution)/shard_map/assemble_gradient/pallas_call | solution.py:470
  (3 shorter events, 0.0 us)
Async XLA Ops:
  3.8 1.4 %collective-permute-start = (f32[24,512]{1,0:T(8,128)S(1)}, f32[24,512]{1,0:T(8,128)S(1)}, u32[]{:S(2)}, u32[]{:S(2)}) collective-permute-start(f32[24,512]{1,0:T(8,128)S(1)} %get-tuple-element.26), channel_id=1, source_target_pairs={{0,4},{1,5},{2,6},{3,7},{4,0},{5,1},{6,2},{7,3},{8,12},{9,13},{10,... | collective-permute-start | bytes 147464 | tf_op jit(solution)/shard_map/ppermute | solution.py:376
  5.3 6.0 %collective-permute-start.1 = (f32[24,512]{1,0:T(8,128)S(1)}, f32[24,512]{1,0:T(8,128)S(1)}, u32[]{:S(2)}, u32[]{:S(2)}) collective-permute-start(f32[24,512]{1,0:T(8,128)S(1)} %get-tuple-element.30._.refs_0_), channel_id=1, source_target_pairs={{0,24},{1,25},{2,26},{3,27},{4,28},{5,29},{6,30},{7,31},{8,16},{9,... | collective-permute-start | bytes 147464 | tf_op jit(solution)/shard_map/ppermute | solution.py:376
  9.1 4.0 %collective-permute-start.2 = (f32[24,512]{1,0:T(8,128)S(1)}, f32[24,512]{1,0:T(8,128)S(1)}, u32[]{:S(2)}, u32[]{:S(2)}) collective-permute-start(f32[24,512]{1,0:T(8,128)S(1)} %get-tuple-element.30._.refs_0_), channel_id=1, source_target_pairs={{0,12},{1,13},{2,14},{3,15},{4,8},{5,9},{6,10},{7,11},{8,4},{9,5},... | collective-permute-start | bytes 147464 | tf_op jit(solution)/shard_map/ppermute | solution.py:376
  9.1 4.0 %collective-permute-start.3 = (f32[24,512]{1,0:T(8,128)S(1)}, f32[24,512]{1,0:T(8,128)S(1)}, u32[]{:S(2)}, u32[]{:S(2)}) collective-permute-start(f32[24,512]{1,0:T(8,128)S(1)} %get-tuple-element.30._.refs_0_), channel_id=1, source_target_pairs={{0,20},{1,21},{2,22},{3,23},{4,16},{5,17},{6,18},{7,19},{8,28},{9,... | collective-permute-start | bytes 147464 | tf_op jit(solution)/shard_map/ppermute | solution.py:376
  13.2 5.9 %collective-permute-start.4 = (f32[16,512]{1,0:T(8,128)S(1)}, f32[16,512]{1,0:T(8,128)S(1)}, u32[]{:S(2)}, u32[]{:S(2)}) collective-permute-start(f32[16,512]{1,0:T(8,128)S(1)} %get-tuple-element.34), channel_id=1, source_target_pairs={{0,4},{1,5},{2,6},{3,7},{4,0},{5,1},{6,2},{7,3},{8,12},{9,13},{10,... | collective-permute-start | bytes 98312 | tf_op jit(solution)/shard_map/ppermute | solution.py:376
  13.4 3.2 %collective-permute-start.5 = (f32[8,512]{1,0:T(8,128)S(1)}, f32[8,512]{1,0:T(8,128)S(1)}, u32[]{:S(2)}, u32[]{:S(2)}) collective-permute-start(f32[8,512]{1,0:T(8,128)S(1)} %get-tuple-element.37._.own), channel_id=1, source_target_pairs={{0,5},{1,4},{2,7},{3,6},{4,1},{5,0},{6,3},{7,2},{8,13},{9,12},{10,... | collective-permute-start | bytes 49160 | tf_op jit(solution)/shard_map/ppermute | solution.py:376
  16.6 5.1 %collective-permute-start.6 = (f32[8,512]{1,0:T(8,128)S(1)}, f32[8,512]{1,0:T(8,128)S(1)}, u32[]{:S(2)}, u32[]{:S(2)}) collective-permute-start(f32[8,512]{1,0:T(8,128)S(1)} %sum_groups.2.refs_6_.own), channel_id=1, source_target_pairs={{0,6},{1,7},{2,4},{3,5},{4,2},{5,3},{6,0},{7,1},{8,14},{9,15},{10,... | collective-permute-start | bytes 49160 | tf_op jit(solution)/shard_map/ppermute | solution.py:376
  21.7 1.2 %collective-permute-start.7 = (f32[8,512]{1,0:T(8,128)S(1)}, f32[8,512]{1,0:T(8,128)S(1)}, u32[]{:S(2)}, u32[]{:S(2)}) collective-permute-start(f32[8,512]{1,0:T(8,128)S(1)} %sum_groups.3.own), channel_id=1, source_target_pairs={{0,4},{1,5},{2,6},{3,7},{4,0},{5,1},{6,2},{7,3},{8,12},{9,13},{10,... | collective-permute-start | bytes 49160 | tf_op jit(solution)/shard_map/ppermute | solution.py:376

commit v10 on v9

--- a/solution.py
+++ b/solution.py
@@ -23,8 +23,12 @@
     return jnp.where(columns == wanted, 1.0, 0.0).astype(jnp.bfloat16)
 
 
+def read_chunk(ref, p, lanes):
+    return [ref[pl.ds((p * SUB + r) * SUB, SUB), lanes] for r in range(SUB)]
+
+
 def read_tokens(ref, chunks, lanes):
-    return [[ref[pl.ds((p * SUB + r) * SUB, SUB), lanes] for r in range(SUB)] for p in range(chunks)]
+    return [read_chunk(ref, p, lanes) for p in range(chunks)]
 
 
 def powers(decay, pw):
@@ -39,17 +43,22 @@
     return total
 
 
-def chunk_states(m, xs, gs, pw):
+def held_states(m, xs, pw):
     a, a8 = row(pw, 0, pl.ds(m, 1)), row(pw, 1, pl.ds(m, 1))
-    chunks = len(xs)
-    held, back = [], [None] * chunks
-    for p in range(chunks):
-        own = horner(xs[p], a)
-        held.append(own if p == 0 else held[-1] * a8 + own)
-    opens = [horner(gs[p][::-1], a) for p in range(chunks)]
-    for p in reversed(range(chunks)):
-        back[p] = opens[p] if p == chunks - 1 else back[p + 1] * a8 + opens[p]
-    return held, back, opens
+    held = []
+    for chunk in xs:
+        own = horner(chunk, a)
+        held.append(held[-1] * a8 + own if held else own)
+    return held
+
+
+def back_states(m, gs, pw):
+    a, a8 = row(pw, 0, pl.ds(m, 1)), row(pw, 1, pl.ds(m, 1))
+    opens = [horner(chunk[::-1], a) for chunk in gs]
+    back = opens[-1:]
+    for own in reversed(opens[:-1]):
+        back.insert(0, back[0] * a8 + own)
+    return back, opens
 
 
 def by_span(scratch, half, j):
@@ -58,7 +67,7 @@
 
 def gather_kernel(*refs):
     sources = refs[:4]
-    xf, gf, residue_ref, decay_ref, segment, message, pw, ends, starts, inner, x_ref, g_ref, sems = refs[4:]
+    xf, gf, residue_ref, decay_ref, segment, message, *scratch, x_ref, g_ref, sems = refs[4:]
     staged = x_ref, g_ref, residue_ref, decay_ref
     copies = [pltpu.make_async_copy(*pair, sems.at[i]) for i, pair in enumerate(zip(sources, staged))]
     for copy in copies:
@@ -74,21 +83,29 @@
     xf[...] = jnp.dot(order, x_ref[...], preferred_element_type=F32)
     gf[...] = jnp.dot(order, g_ref[...], preferred_element_type=F32)
 
-    def tile_step(tile, _):
-        lanes = pl.ds(pl.multiple_of(tile * LANES, LANES), LANES)
+    def tile_step(tile):
+        lanes = pl.ds(tile * LANES, LANES)
+        pw, ends, starts, inner, before = (ref.at[tile % 2] for ref in scratch)
         decay = decay_ref[:, lanes]
         powers(decay, pw)
-        xs, gs = read_tokens(xf, chunks, lanes), read_tokens(gf, chunks, lanes)
+        xs = read_tokens(xf, chunks, lanes)
         for m in range(modes):
-            held, back, opens = chunk_states(m, xs, gs, pw)
+            held = held_states(m, xs, pw)
+            ends[pl.ds(m * SUB, SUB), :] = held[-1]
+            for p in range(chunks - 1):
+                before[m, p] = held[p]
+        gs = read_tokens(gf, chunks, lanes)
+        for m in range(modes):
+            back, opens = back_states(m, gs, pw)
             rows = pl.ds(m * SUB, SUB)
-            ends[rows, :] = held[-1]
             starts[rows, :] = back[0]
-            inner[rows, :] = sum(opens[p] * held[p - 1] for p in range(1, chunks))
-        lagged = []
-        for lag in range(SUB):
-            pairs = [gs[p][r] * xs[p][r - lag] for p in range(chunks) for r in range(lag, SUB)]
-            lagged.append(jnp.sum(sum(pairs), axis=0, keepdims=True))
+            inner[rows, :] = sum(opens[p] * before[m, p - 1] for p in range(1, chunks))
+        lagged = [0.0] * SUB
+        for p in range(chunks):
+            xs, gs = read_chunk(xf, p, lanes), read_chunk(gf, p, lanes)
+            for lag in range(SUB):
+                lagged[lag] = lagged[lag] + sum(gs[r] * xs[r - lag] for r in range(lag, SUB))
+        lagged = [jnp.sum(total, axis=0, keepdims=True) for total in lagged]
         for half in range(modes // SUB):
             some = pl.ds(half * SUB, SUB)
             a = pw[0, some, :]
@@ -103,10 +120,9 @@
             closing[some, lanes] = arriving
             opening[some, lanes] = leaving
             grad[some, lanes] = near + a * cross
-        return 0
-
-    lax.fori_loop(0, channels // LANES, tile_step, 0)
-
+
+    for tile in range(channels // LANES):
+        tile_step(tile)
 
     own_high = owns_high()
     half = modes // 2
@@ -150,7 +166,7 @@
         pw[2] = residue * pw[0]
         xs, gs = read_tokens(xf, chunks, lanes), read_tokens(gf, chunks, lanes)
         for m in range(modes):
-            held, back, _ = chunk_states(m, xs, gs, pw)
+            held, (back, _) = held_states(m, xs, pw), back_states(m, gs, pw)
             rows = pl.ds(m * SUB, SUB)
             ends[rows, :] = held[-1]
             starts[rows, :] = back[0]
@@ -397,7 +413,9 @@
         + [shaped(modes, channels)] * 2
         + [shaped(3 * modes, channels), shaped(3 * half, channels)],
         in_specs=[HBM] * 4,
-        scratch_shapes=[vmem(2, modes, LANES), spans, spans, spans]
+        scratch_shapes=[vmem(2, 2, modes, LANES)]
+        + [vmem(2, modes * SUB, LANES)] * 3
+        + [vmem(2, modes, chunks - 1, SUB, LANES)]
         + [pltpu.VMEM(signal.shape, signal.dtype)] * 2
         + [pltpu.SemaphoreType.DMA((4,))],
         compiler_params=PARAMS,

time: 23.7 us -> 23.4 us (0.987)
  Pallas kernels: 9.55 us -> 9.27 us
    pallas_call x1, Pallas kernels: 3.19 us -> 2.91 us  [body(): pl.pallas_call(gather_kernel, out_shape=[values, values] + [shaped(modes,...]
where the time goes in v10:
time: 23.4 us; the launch traced here: 23.3 us
  Pallas kernels  9.27 us (40%)
  starting transfers between devices  9.26 us (40%)
  waiting for transfers between devices  4.04 us (17%)
  between operations  0.69 us (3%)
    ppermute x8, starting transfers between devices, swap(): lax.ppermute(x, ('ctx', 'ch'), [(i, i ^ mask) for i in range(n * groups)])  9.26 us
    ppermute x8, waiting for transfers between devices, swap(): lax.ppermute(x, ('ctx', 'ch'), [(i, i ^ mask) for i in range(n * groups)])  4.04 us
    pallas_call x3, Pallas kernels, near_part(): pl.pallas_call(functools.partial(local_kernel, ranges[part]), out_shape=[...  3.11 us
    pallas_call x1, Pallas kernels, body(): pl.pallas_call(gather_kernel, out_shape=[values, values] + [shaped(modes,...  2.91 us
    pallas_call x1, Pallas kernels, body(): pl.pallas_call(functools.partial(finish_kernel, ranges), out_shape=[jax.S...  2.53 us
    pallas_call x1, Pallas kernels, body(): pl.pallas_call(functools.partial(assemble_kernel, 1.0 / (tokens * n)), ou...  0.62 us
  transfers between devices with their start and end apart: 8, of which 5 were waited for; matrix products, arithmetic and copies ran while one was open for 0% of the time, Pallas kernels for 24%

profile of v10, /device:TPU:0, one launch (start us, length us, event | category | flops | bytes accessed | tf_op | source)
XLA Modules:
  0.0 23.3 jit_solution(9340645887740533252)
XLA Ops:
  0.6 2.9 %block_states.1 = (f32[256,512]{1,0:T(8,128)S(1)}, f32[256,512]{1,0:T(8,128)S(1)}, f32[16,512]{1,0:T(8,128)S(1)}, f32[16,512]{1,0:T(8,128)S(1)}, f32[48,512]{1,0:T(8,128)S(1)}, /*index=5*/f32[24,512]{1,0:T(8,128)S(1)}) custom-call(bf16[256,512]{1,0:T(8,128)(2,1)} %refs_0_.1, bf16[256,512]{1,0:T(8,128)(2,1)} %refs_1_.1, f32[16,512]{1,0:T(8,128)} %refs_2_.1, ...), custom_call_target="tpu_custom_call" | custom-call | flops 10485760 | bytes 786432 | tf_op jit(solution)/shard_map/block_states/pallas_call | solution.py:410
  3.6 0.5 %collective-permute-start = (f32[24,512]{1,0:T(8,128)S(1)}, f32[24,512]{1,0:T(8,128)S(1)}, u32[]{:S(2)}, u32[]{:S(2)}) collective-permute-start(f32[24,512]{1,0:T(8,128)S(1)} %get-tuple-element.26), channel_id=1, source_target_pairs={{0,4},{1,5},{2,6},{3,7},{4,0},{5,1},{6,2},{7,3},{8,12},{9,13},{10,... | collective-permute-start | bytes 147464 | tf_op jit(solution)/shard_map/ppermute | solution.py:392
  4.1 0.8 %local_convolutions.3 = (f32[1,32,8,128]{3,2,1,0:T(8,128)S(1)}, f32[1,32,8,128]{3,2,1,0:T(8,128)S(1)}) custom-call(f32[256,512]{1,0:T(8,128)S(1)} %get-tuple-element.27.xf, f32[256,512]{1,0:T(8,128)S(1)} %get-tuple-element.28.gf, f32[16,512]{1,0:T(8,128)S(1)} %get-tuple-element.23.residue_ref, f32[16,512]{1,0:T(8,128)S(1)} %get-tuple-element.24.decay_ref.refs_5_, ...), custom_call_target="tpu_custom_call" | custom-call | flops 209715200 | bytes 524288 | tf_op jit(solution)/shard_map/local_convolutions/pallas_call | solution.py:397
  4.8 0.1 collective-permute-done.other
  5.0 3.9 %collective-permute-start.1 = (f32[24,512]{1,0:T(8,128)S(1)}, f32[24,512]{1,0:T(8,128)S(1)}, u32[]{:S(2)}, u32[]{:S(2)}) collective-permute-start(f32[24,512]{1,0:T(8,128)S(1)} %get-tuple-element.30._.refs_0_), channel_id=1, source_target_pairs={{0,24},{1,25},{2,26},{3,27},{4,28},{5,29},{6,30},{7,31},{8,16},{9,... | collective-permute-start | bytes 147464 | tf_op jit(solution)/shard_map/ppermute | solution.py:392
  8.8 0.0 collective-permute-start.2
  8.9 0.3 %collective-permute-start.3 = (f32[24,512]{1,0:T(8,128)S(1)}, f32[24,512]{1,0:T(8,128)S(1)}, u32[]{:S(2)}, u32[]{:S(2)}) collective-permute-start(f32[24,512]{1,0:T(8,128)S(1)} %get-tuple-element.30._.refs_0_), channel_id=1, source_target_pairs={{0,20},{1,21},{2,22},{3,23},{4,16},{5,17},{6,18},{7,19},{8,28},{9,... | collective-permute-start | bytes 147464 | tf_op jit(solution)/shard_map/ppermute | solution.py:392
  9.2 1.6 %local_convolutions.4 = (f32[2,32,8,128]{3,2,1,0:T(8,128)S(1)}, f32[2,32,8,128]{3,2,1,0:T(8,128)S(1)}) custom-call(f32[256,512]{1,0:T(8,128)S(1)} %get-tuple-element.27.xf, f32[256,512]{1,0:T(8,128)S(1)} %get-tuple-element.28.gf, f32[16,512]{1,0:T(8,128)S(1)} %get-tuple-element.23.residue_ref, f32[16,512]{1,0:T(8,128)S(1)} %get-tuple-element.24.decay_ref.refs_5_, ...), custom_call_target="tpu_custom_call" | custom-call | flops 419430400 | bytes 1048576 | tf_op jit(solution)/shard_map/local_convolutions/pallas_call | solution.py:397
  10.8 0.2 collective-permute-done.1.refs_1_
  11.0 1.9 %collective-permute-done.2.refs_2_ = f32[24,512]{1,0:T(8,128)S(1)} collective-permute-done((f32[24,512]{1,0:T(8,128)S(1)}, f32[24,512]{1,0:T(8,128)S(1)}, u32[]{:S(2)}, u32[]{:S(2)}) %collective-permute-start.2) | collective-permute-done | bytes 49184 | tf_op jit(solution)/shard_map/ppermute | solution.py:392
  12.8 0.0 collective-permute-done.3.refs_3_
  12.8 0.1 join_chips.1
  12.9 0.2 %collective-permute-start.4 = (f32[16,512]{1,0:T(8,128)S(1)}, f32[16,512]{1,0:T(8,128)S(1)}, u32[]{:S(2)}, u32[]{:S(2)}) collective-permute-start(f32[16,512]{1,0:T(8,128)S(1)} %get-tuple-element.34), channel_id=1, source_target_pairs={{0,4},{1,5},{2,6},{3,7},{4,0},{5,1},{6,2},{7,3},{8,12},{9,13},{10,... | collective-permute-start | bytes 98312 | tf_op jit(solution)/shard_map/ppermute | solution.py:392
  13.1 1.5 %collective-permute-start.5 = (f32[8,512]{1,0:T(8,128)S(1)}, f32[8,512]{1,0:T(8,128)S(1)}, u32[]{:S(2)}, u32[]{:S(2)}) collective-permute-start(f32[8,512]{1,0:T(8,128)S(1)} %get-tuple-element.37._.own), channel_id=1, source_target_pairs={{0,5},{1,4},{2,7},{3,6},{4,1},{5,0},{6,3},{7,2},{8,13},{9,12},{10,... | collective-permute-start | bytes 49160 | tf_op jit(solution)/shard_map/ppermute | solution.py:392
  14.6 0.8 %local_convolutions.5 = (f32[1,32,8,128]{3,2,1,0:T(8,128)S(1)}, f32[1,32,8,128]{3,2,1,0:T(8,128)S(1)}) custom-call(f32[256,512]{1,0:T(8,128)S(1)} %get-tuple-element.27.xf, f32[256,512]{1,0:T(8,128)S(1)} %get-tuple-element.28.gf, f32[16,512]{1,0:T(8,128)S(1)} %get-tuple-element.23.residue_ref, f32[16,512]{1,0:T(8,128)S(1)} %get-tuple-element.24.decay_ref.refs_5_, ...), custom_call_target="tpu_custom_call" | custom-call | flops 209715200 | bytes 524288 | tf_op jit(solution)/shard_map/local_convolutions/pallas_call | solution.py:397
  15.4 0.9 %collective-permute-done.5.other = f32[8,512]{1,0:T(8,128)S(1)} collective-permute-done((f32[8,512]{1,0:T(8,128)S(1)}, f32[8,512]{1,0:T(8,128)S(1)}, u32[]{:S(2)}, u32[]{:S(2)}) %collective-permute-start.5) | collective-permute-done | bytes 16416 | tf_op jit(solution)/shard_map/ppermute | solution.py:392
  16.3 2.5 %collective-permute-start.6 = (f32[8,512]{1,0:T(8,128)S(1)}, f32[8,512]{1,0:T(8,128)S(1)}, u32[]{:S(2)}, u32[]{:S(2)}) collective-permute-start(f32[8,512]{1,0:T(8,128)S(1)} %sum_groups.2.refs_6_.own), channel_id=1, source_target_pairs={{0,6},{1,7},{2,4},{3,5},{4,2},{5,3},{6,0},{7,1},{8,14},{9,15},{10,... | collective-permute-start | bytes 49160 | tf_op jit(solution)/shard_map/ppermute | solution.py:392
  18.8 0.0 collective-permute-done.4.other
  18.8 2.5 %add_arrivals.1 = (bf16[256,512]{1,0:T(8,128)(2,1)}, bf16[256,512]{1,0:T(8,128)(2,1)}, f32[8,128]{1,0:T(8,128)S(1)}) custom-call(f32[16,512]{1,0:T(8,128)S(1)} %get-tuple-element.23.residue_ref, f32[16,512]{1,0:T(8,128)S(1)} %get-tuple-element.24.decay_ref.refs_5_, f32[16,512]{1,0:T(8,128)S(1)} %get-tuple-element.33.own, ...), custom_call_target="tpu_custom_call" | custom-call | flops 1258291200 | bytes 1572864 | tf_op jit(solution)/shard_map/add_arrivals/pallas_call | solution.py:468
  21.4 0.0 collective-permute-done.6.other
  21.4 0.2 %collective-permute-start.7 = (f32[8,512]{1,0:T(8,128)S(1)}, f32[8,512]{1,0:T(8,128)S(1)}, u32[]{:S(2)}, u32[]{:S(2)}) collective-permute-start(f32[8,512]{1,0:T(8,128)S(1)} %sum_groups.3.own), channel_id=1, source_target_pairs={{0,4},{1,5},{2,6},{3,7},{4,0},{5,1},{6,2},{7,3},{8,12},{9,13},{10,... | collective-permute-start | bytes 49160 | tf_op jit(solution)/shard_map/ppermute | solution.py:392
  21.6 1.0 %collective-permute-done.7.other = f32[8,512]{1,0:T(8,128)S(1)} collective-permute-done((f32[8,512]{1,0:T(8,128)S(1)}, f32[8,512]{1,0:T(8,128)S(1)}, u32[]{:S(2)}, u32[]{:S(2)}) %collective-permute-start.7) | collective-permute-done | bytes 16416 | tf_op jit(solution)/shard_map/ppermute | solution.py:392
  22.6 0.6 %assemble_gradient.1 = f32[16,512]{1,0:T(8,128)} custom-call(f32[8,512]{1,0:T(8,128)S(1)} %sum_groups.3.own, f32[8,512]{1,0:T(8,128)S(1)} %collective-permute-done.7.other), custom_call_target="tpu_custom_call" | custom-call | flops 131072 | bytes 262144 | tf_op jit(solution)/shard_map/assemble_gradient/pallas_call | solution.py:488
  (3 shorter events, 0.0 us)
Async XLA Ops:
  3.6 1.4 %collective-permute-start = (f32[24,512]{1,0:T(8,128)S(1)}, f32[24,512]{1,0:T(8,128)S(1)}, u32[]{:S(2)}, u32[]{:S(2)}) collective-permute-start(f32[24,512]{1,0:T(8,128)S(1)} %get-tuple-element.26), channel_id=1, source_target_pairs={{0,4},{1,5},{2,6},{3,7},{4,0},{5,1},{6,2},{7,3},{8,12},{9,13},{10,... | collective-permute-start | bytes 147464 | tf_op jit(solution)/shard_map/ppermute | solution.py:392
  5.0 6.0 %collective-permute-start.1 = (f32[24,512]{1,0:T(8,128)S(1)}, f32[24,512]{1,0:T(8,128)S(1)}, u32[]{:S(2)}, u32[]{:S(2)}) collective-permute-start(f32[24,512]{1,0:T(8,128)S(1)} %get-tuple-element.30._.refs_0_), channel_id=1, source_target_pairs={{0,24},{1,25},{2,26},{3,27},{4,28},{5,29},{6,30},{7,31},{8,16},{9,... | collective-permute-start | bytes 147464 | tf_op jit(solution)/shard_map/ppermute | solution.py:392
  8.8 4.0 %collective-permute-start.2 = (f32[24,512]{1,0:T(8,128)S(1)}, f32[24,512]{1,0:T(8,128)S(1)}, u32[]{:S(2)}, u32[]{:S(2)}) collective-permute-start(f32[24,512]{1,0:T(8,128)S(1)} %get-tuple-element.30._.refs_0_), channel_id=1, source_target_pairs={{0,12},{1,13},{2,14},{3,15},{4,8},{5,9},{6,10},{7,11},{8,4},{9,5},... | collective-permute-start | bytes 147464 | tf_op jit(solution)/shard_map/ppermute | solution.py:392
  8.9 4.0 %collective-permute-start.3 = (f32[24,512]{1,0:T(8,128)S(1)}, f32[24,512]{1,0:T(8,128)S(1)}, u32[]{:S(2)}, u32[]{:S(2)}) collective-permute-start(f32[24,512]{1,0:T(8,128)S(1)} %get-tuple-element.30._.refs_0_), channel_id=1, source_target_pairs={{0,20},{1,21},{2,22},{3,23},{4,16},{5,17},{6,18},{7,19},{8,28},{9,... | collective-permute-start | bytes 147464 | tf_op jit(solution)/shard_map/ppermute | solution.py:392
  12.9 5.9 %collective-permute-start.4 = (f32[16,512]{1,0:T(8,128)S(1)}, f32[16,512]{1,0:T(8,128)S(1)}, u32[]{:S(2)}, u32[]{:S(2)}) collective-permute-start(f32[16,512]{1,0:T(8,128)S(1)} %get-tuple-element.34), channel_id=1, source_target_pairs={{0,4},{1,5},{2,6},{3,7},{4,0},{5,1},{6,2},{7,3},{8,12},{9,13},{10,... | collective-permute-start | bytes 98312 | tf_op jit(solution)/shard_map/ppermute | solution.py:392
  13.1 3.2 %collective-permute-start.5 = (f32[8,512]{1,0:T(8,128)S(1)}, f32[8,512]{1,0:T(8,128)S(1)}, u32[]{:S(2)}, u32[]{:S(2)}) collective-permute-start(f32[8,512]{1,0:T(8,128)S(1)} %get-tuple-element.37._.own), channel_id=1, source_target_pairs={{0,5},{1,4},{2,7},{3,6},{4,1},{5,0},{6,3},{7,2},{8,13},{9,12},{10,... | collective-permute-start | bytes 49160 | tf_op jit(solution)/shard_map/ppermute | solution.py:392
  16.3 5.1 %collective-permute-start.6 = (f32[8,512]{1,0:T(8,128)S(1)}, f32[8,512]{1,0:T(8,128)S(1)}, u32[]{:S(2)}, u32[]{:S(2)}) collective-permute-start(f32[8,512]{1,0:T(8,128)S(1)} %sum_groups.2.refs_6_.own), channel_id=1, source_target_pairs={{0,6},{1,7},{2,4},{3,5},{4,2},{5,3},{6,0},{7,1},{8,14},{9,15},{10,... | collective-permute-start | bytes 49160 | tf_op jit(solution)/shard_map/ppermute | solution.py:392
  21.4 1.2 %collective-permute-start.7 = (f32[8,512]{1,0:T(8,128)S(1)}, f32[8,512]{1,0:T(8,128)S(1)}, u32[]{:S(2)}, u32[]{:S(2)}) collective-permute-start(f32[8,512]{1,0:T(8,128)S(1)} %sum_groups.3.own), channel_id=1, source_target_pairs={{0,4},{1,5},{2,6},{3,7},{4,0},{5,1},{6,2},{7,3},{8,12},{9,13},{10,... | collective-permute-start | bytes 49160 | tf_op jit(solution)/shard_map/ppermute | solution.py:392

commit v11 on v10

--- a/solution.py
+++ b/solution.py
@@ -65,23 +65,24 @@
     return scratch[pl.ds(half * SUB * SUB + j, SUB, stride=SUB), :]
 
 
-def gather_kernel(*refs):
-    sources = refs[:4]
-    xf, gf, residue_ref, decay_ref, segment, message, *scratch, x_ref, g_ref, sems = refs[4:]
-    staged = x_ref, g_ref, residue_ref, decay_ref
-    copies = [pltpu.make_async_copy(*pair, sems.at[i]) for i, pair in enumerate(zip(sources, staged))]
-    for copy in copies:
-        copy.start()
+def gather_kernel(x_hbm, g_hbm, residue_hbm, decay_hbm, *refs):
+    xf, gf, residue_ref, decay_ref, segment, message, *scratch, x_ref, g_ref, sems = refs
     modes, channels = decay_ref.shape
     tokens = x_ref.shape[0]
     chunks = tokens // (SUB * SUB)
     span = chunks * SUB
+    tiles = channels // LANES
+    groups = [slice(0, channels // 2), slice(channels // 2, channels)]
+    pairs = [(decay_hbm, decay_ref)]
+    for lanes in groups:
+        pairs += [(x_hbm.at[:, lanes], x_ref.at[:, lanes]), (g_hbm.at[:, lanes], g_ref.at[:, lanes])]
+    pairs.append((residue_hbm, residue_ref))
+    copies = [pltpu.make_async_copy(*pair, sems.at[i]) for i, pair in enumerate(pairs)]
+    for copy in copies:
+        copy.start()
     closing, opening, grad = (segment.at[pl.ds(i * modes, modes)] for i in range(3))
     order = token_order(tokens)
-    for copy in copies:
-        copy.wait()
-    xf[...] = jnp.dot(order, x_ref[...], preferred_element_type=F32)
-    gf[...] = jnp.dot(order, g_ref[...], preferred_element_type=F32)
+    copies[0].wait()
 
     def tile_step(tile):
         lanes = pl.ds(tile * LANES, LANES)
@@ -121,8 +122,13 @@
             opening[some, lanes] = leaving
             grad[some, lanes] = near + a * cross
 
-    for tile in range(channels // LANES):
-        tile_step(tile)
+    for which, lanes in enumerate(groups):
+        for copy, source, target in zip(copies[1 + 2 * which:], (x_ref, g_ref), (xf, gf)):
+            copy.wait()
+            target[:, lanes] = jnp.dot(order, source[:, lanes], preferred_element_type=F32)
+        for tile in range(which * tiles // 2, (which + 1) * tiles // 2):
+            tile_step(tile)
+    copies[-1].wait()
 
     own_high = owns_high()
     half = modes // 2
@@ -341,8 +347,8 @@
     finished[...] = jnp.zeros(finished.shape, F32)
 
 
-def sum_kernel(own, other, _, out_ref):
-    out_ref[...] = own[...] + other[...]
+def sum_kernel(own, other, *refs):
+    refs[-1][...] = own[...] + other[...]
 
 
 def assemble_kernel(scale, own, other, out_ref):
@@ -417,7 +423,7 @@
         + [vmem(2, modes * SUB, LANES)] * 3
         + [vmem(2, modes, chunks - 1, SUB, LANES)]
         + [pltpu.VMEM(signal.shape, signal.dtype)] * 2
-        + [pltpu.SemaphoreType.DMA((4,))],
+        + [pltpu.SemaphoreType.DMA((6,))],
         compiler_params=PARAMS,
         cost_estimate=cost(elements * modes * 5, modes * channels * 3, elements * 6),
         name="block_states",
@@ -462,10 +468,10 @@
         if stride == 1:
             received = swap(message[0], 1)
             near = near + near_part(2, grad)
-            pinned = near[-1]
+            pinned = near[-1:]
         stride *= 2
         if stride == groups:
-            conv_out, signal_grad, pinned = pl.pallas_call(
+            conv_out, signal_grad, *pinned = pl.pallas_call(
                 functools.partial(finish_kernel, ranges),
                 out_shape=[jax.ShapeDtypeStruct((tokens, channels), signal.dtype)] * 2 + [shaped(SUB, LANES)],
                 in_specs=[WHOLE] * (4 + 2 * len(ranges)) + [UNREAD],
@@ -481,10 +487,10 @@
         grad = pl.pallas_call(
             sum_kernel,
             out_shape=shaped(half, channels),
-            in_specs=[WHOLE] * 2 + [UNREAD],
+            in_specs=[WHOLE] * 2 + [UNREAD] * len(pinned),
             name="sum_groups",
             **small,
-        )(grad, other, pinned)
+        )(grad, other, *pinned)
     residue_grad = pl.pallas_call(
         functools.partial(assemble_kernel, 1.0 / (tokens * n)),
         out_shape=shaped(modes, channels),

time: 23.4 us -> 23.7 us (1.013)
  Pallas kernels: 9.27 us -> 9.6 us
    pallas_call x1, Pallas kernels: 2.91 us -> 3.24 us  [body(): pl.pallas_call(gather_kernel, out_shape=[values, values] + [shaped(modes,...]
where the time goes in v11:
time: 23.7 us; the launch traced here: 23.6 us
  Pallas kernels  9.6 us (41%)
  starting transfers between devices  9.26 us (39%)
  waiting for transfers between devices  4.04 us (17%)
  between operations  0.69 us (3%)
    ppermute x8, starting transfers between devices, swap(): lax.ppermute(x, ('ctx', 'ch'), [(i, i ^ mask) for i in range(n * groups)])  9.26 us
    ppermute x8, waiting for transfers between devices, swap(): lax.ppermute(x, ('ctx', 'ch'), [(i, i ^ mask) for i in range(n * groups)])  4.04 us
    pallas_call x1, Pallas kernels, body(): pl.pallas_call(gather_kernel, out_shape=[values, values] + [shaped(modes,...  3.24 us
    pallas_call x3, Pallas kernels, near_part(): pl.pallas_call(functools.partial(local_kernel, ranges[part]), out_shape=[...  3.11 us
    pallas_call x1, Pallas kernels, body(): pl.pallas_call(functools.partial(finish_kernel, ranges), out_shape=[jax.S...  2.53 us
    pallas_call x1, Pallas kernels, body(): pl.pallas_call(functools.partial(assemble_kernel, 1.0 / (tokens * n)), ou...  0.62 us
  transfers between devices with their start and end apart: 8, of which 5 were waited for; matrix products, arithmetic and copies ran while one was open for 0% of the time, Pallas kernels for 24%

profile of v11, /device:TPU:0, one launch (start us, length us, event | category | flops | bytes accessed | tf_op | source)
XLA Modules:
  0.0 23.6 jit_solution(16183596807846594359)
XLA Ops:
  0.6 3.2 %block_states.1 = (f32[256,512]{1,0:T(8,128)S(1)}, f32[256,512]{1,0:T(8,128)S(1)}, f32[16,512]{1,0:T(8,128)S(1)}, f32[16,512]{1,0:T(8,128)S(1)}, f32[48,512]{1,0:T(8,128)S(1)}, /*index=5*/f32[24,512]{1,0:T(8,128)S(1)}) custom-call(bf16[256,512]{1,0:T(8,128)(2,1)} %x_hbm.1, bf16[256,512]{1,0:T(8,128)(2,1)} %g_hbm.1, f32[16,512]{1,0:T(8,128)} %residue_hbm.1, ...), custom_call_target="tpu_custom_call" | custom-call | flops 10485760 | bytes 786432 | tf_op jit(solution)/shard_map/block_states/pallas_call | solution.py:416
  3.9 0.5 %collective-permute-start = (f32[24,512]{1,0:T(8,128)S(1)}, f32[24,512]{1,0:T(8,128)S(1)}, u32[]{:S(2)}, u32[]{:S(2)}) collective-permute-start(f32[24,512]{1,0:T(8,128)S(1)} %get-tuple-element.26), channel_id=1, source_target_pairs={{0,4},{1,5},{2,6},{3,7},{4,0},{5,1},{6,2},{7,3},{8,12},{9,13},{10,... | collective-permute-start | bytes 147464 | tf_op jit(solution)/shard_map/ppermute | solution.py:398
  4.4 0.8 %local_convolutions.3 = (f32[1,32,8,128]{3,2,1,0:T(8,128)S(1)}, f32[1,32,8,128]{3,2,1,0:T(8,128)S(1)}) custom-call(f32[256,512]{1,0:T(8,128)S(1)} %get-tuple-element.27.xf, f32[256,512]{1,0:T(8,128)S(1)} %get-tuple-element.28.gf, f32[16,512]{1,0:T(8,128)S(1)} %get-tuple-element.23.residue_ref, f32[16,512]{1,0:T(8,128)S(1)} %get-tuple-element.24.decay_ref.refs_5_, ...), custom_call_target="tpu_custom_call" | custom-call | flops 209715200 | bytes 524288 | tf_op jit(solution)/shard_map/local_convolutions/pallas_call | solution.py:403
  5.2 0.1 collective-permute-done.other
  5.3 3.9 %collective-permute-start.1 = (f32[24,512]{1,0:T(8,128)S(1)}, f32[24,512]{1,0:T(8,128)S(1)}, u32[]{:S(2)}, u32[]{:S(2)}) collective-permute-start(f32[24,512]{1,0:T(8,128)S(1)} %get-tuple-element.30._.refs_0_), channel_id=1, source_target_pairs={{0,24},{1,25},{2,26},{3,27},{4,28},{5,29},{6,30},{7,31},{8,16},{9,... | collective-permute-start | bytes 147464 | tf_op jit(solution)/shard_map/ppermute | solution.py:398
  9.2 0.0 collective-permute-start.2
  9.2 0.3 %collective-permute-start.3 = (f32[24,512]{1,0:T(8,128)S(1)}, f32[24,512]{1,0:T(8,128)S(1)}, u32[]{:S(2)}, u32[]{:S(2)}) collective-permute-start(f32[24,512]{1,0:T(8,128)S(1)} %get-tuple-element.30._.refs_0_), channel_id=1, source_target_pairs={{0,20},{1,21},{2,22},{3,23},{4,16},{5,17},{6,18},{7,19},{8,28},{9,... | collective-permute-start | bytes 147464 | tf_op jit(solution)/shard_map/ppermute | solution.py:398
  9.5 1.6 %local_convolutions.4 = (f32[2,32,8,128]{3,2,1,0:T(8,128)S(1)}, f32[2,32,8,128]{3,2,1,0:T(8,128)S(1)}) custom-call(f32[256,512]{1,0:T(8,128)S(1)} %get-tuple-element.27.xf, f32[256,512]{1,0:T(8,128)S(1)} %get-tuple-element.28.gf, f32[16,512]{1,0:T(8,128)S(1)} %get-tuple-element.23.residue_ref, f32[16,512]{1,0:T(8,128)S(1)} %get-tuple-element.24.decay_ref.refs_5_, ...), custom_call_target="tpu_custom_call" | custom-call | flops 419430400 | bytes 1048576 | tf_op jit(solution)/shard_map/local_convolutions/pallas_call | solution.py:403
  11.1 0.2 collective-permute-done.1.refs_1_
  11.3 1.9 %collective-permute-done.2.refs_2_ = f32[24,512]{1,0:T(8,128)S(1)} collective-permute-done((f32[24,512]{1,0:T(8,128)S(1)}, f32[24,512]{1,0:T(8,128)S(1)}, u32[]{:S(2)}, u32[]{:S(2)}) %collective-permute-start.2) | collective-permute-done | bytes 49184 | tf_op jit(solution)/shard_map/ppermute | solution.py:398
  13.1 0.0 collective-permute-done.3.refs_3_
  13.1 0.1 join_chips.1
  13.2 0.2 %collective-permute-start.4 = (f32[16,512]{1,0:T(8,128)S(1)}, f32[16,512]{1,0:T(8,128)S(1)}, u32[]{:S(2)}, u32[]{:S(2)}) collective-permute-start(f32[16,512]{1,0:T(8,128)S(1)} %get-tuple-element.34), channel_id=1, source_target_pairs={{0,4},{1,5},{2,6},{3,7},{4,0},{5,1},{6,2},{7,3},{8,12},{9,13},{10,... | collective-permute-start | bytes 98312 | tf_op jit(solution)/shard_map/ppermute | solution.py:398
  13.5 1.5 %collective-permute-start.5 = (f32[8,512]{1,0:T(8,128)S(1)}, f32[8,512]{1,0:T(8,128)S(1)}, u32[]{:S(2)}, u32[]{:S(2)}) collective-permute-start(f32[8,512]{1,0:T(8,128)S(1)} %get-tuple-element.37._.own), channel_id=1, source_target_pairs={{0,5},{1,4},{2,7},{3,6},{4,1},{5,0},{6,3},{7,2},{8,13},{9,12},{10,... | collective-permute-start | bytes 49160 | tf_op jit(solution)/shard_map/ppermute | solution.py:398
  15.0 0.8 %local_convolutions.5 = (f32[1,32,8,128]{3,2,1,0:T(8,128)S(1)}, f32[1,32,8,128]{3,2,1,0:T(8,128)S(1)}) custom-call(f32[256,512]{1,0:T(8,128)S(1)} %get-tuple-element.27.xf, f32[256,512]{1,0:T(8,128)S(1)} %get-tuple-element.28.gf, f32[16,512]{1,0:T(8,128)S(1)} %get-tuple-element.23.residue_ref, f32[16,512]{1,0:T(8,128)S(1)} %get-tuple-element.24.decay_ref.refs_5_, ...), custom_call_target="tpu_custom_call" | custom-call | flops 209715200 | bytes 524288 | tf_op jit(solution)/shard_map/local_convolutions/pallas_call | solution.py:403
  15.7 0.9 %collective-permute-done.5.other = f32[8,512]{1,0:T(8,128)S(1)} collective-permute-done((f32[8,512]{1,0:T(8,128)S(1)}, f32[8,512]{1,0:T(8,128)S(1)}, u32[]{:S(2)}, u32[]{:S(2)}) %collective-permute-start.5) | collective-permute-done | bytes 16416 | tf_op jit(solution)/shard_map/ppermute | solution.py:398
  16.6 2.5 %collective-permute-start.6 = (f32[8,512]{1,0:T(8,128)S(1)}, f32[8,512]{1,0:T(8,128)S(1)}, u32[]{:S(2)}, u32[]{:S(2)}) collective-permute-start(f32[8,512]{1,0:T(8,128)S(1)} %sum_groups.2.refs_6_.own), channel_id=1, source_target_pairs={{0,6},{1,7},{2,4},{3,5},{4,2},{5,3},{6,0},{7,1},{8,14},{9,15},{10,... | collective-permute-start | bytes 49160 | tf_op jit(solution)/shard_map/ppermute | solution.py:398
  19.2 0.0 collective-permute-done.4.other
  19.2 2.5 %add_arrivals.1 = (bf16[256,512]{1,0:T(8,128)(2,1)}, bf16[256,512]{1,0:T(8,128)(2,1)}, f32[8,128]{1,0:T(8,128)S(1)}) custom-call(f32[16,512]{1,0:T(8,128)S(1)} %get-tuple-element.23.residue_ref, f32[16,512]{1,0:T(8,128)S(1)} %get-tuple-element.24.decay_ref.refs_5_, f32[16,512]{1,0:T(8,128)S(1)} %get-tuple-element.33.own, ...), custom_call_target="tpu_custom_call" | custom-call | flops 1258291200 | bytes 1572864 | tf_op jit(solution)/shard_map/add_arrivals/pallas_call | solution.py:474
  21.7 0.0 collective-permute-done.6.other
  21.7 0.2 %collective-permute-start.7 = (f32[8,512]{1,0:T(8,128)S(1)}, f32[8,512]{1,0:T(8,128)S(1)}, u32[]{:S(2)}, u32[]{:S(2)}) collective-permute-start(f32[8,512]{1,0:T(8,128)S(1)} %sum_groups.3.own), channel_id=1, source_target_pairs={{0,4},{1,5},{2,6},{3,7},{4,0},{5,1},{6,2},{7,3},{8,12},{9,13},{10,... | collective-permute-start | bytes 49160 | tf_op jit(solution)/shard_map/ppermute | solution.py:398
  22.0 1.0 %collective-permute-done.7.other = f32[8,512]{1,0:T(8,128)S(1)} collective-permute-done((f32[8,512]{1,0:T(8,128)S(1)}, f32[8,512]{1,0:T(8,128)S(1)}, u32[]{:S(2)}, u32[]{:S(2)}) %collective-permute-start.7) | collective-permute-done | bytes 16416 | tf_op jit(solution)/shard_map/ppermute | solution.py:398
  23.0 0.6 %assemble_gradient.1 = f32[16,512]{1,0:T(8,128)} custom-call(f32[8,512]{1,0:T(8,128)S(1)} %sum_groups.3.own, f32[8,512]{1,0:T(8,128)S(1)} %collective-permute-done.7.other), custom_call_target="tpu_custom_call" | custom-call | flops 131072 | bytes 262144 | tf_op jit(solution)/shard_map/assemble_gradient/pallas_call | solution.py:494
  (3 shorter events, 0.0 us)
Async XLA Ops:
  3.9 1.4 %collective-permute-start = (f32[24,512]{1,0:T(8,128)S(1)}, f32[24,512]{1,0:T(8,128)S(1)}, u32[]{:S(2)}, u32[]{:S(2)}) collective-permute-start(f32[24,512]{1,0:T(8,128)S(1)} %get-tuple-element.26), channel_id=1, source_target_pairs={{0,4},{1,5},{2,6},{3,7},{4,0},{5,1},{6,2},{7,3},{8,12},{9,13},{10,... | collective-permute-start | bytes 147464 | tf_op jit(solution)/shard_map/ppermute | solution.py:398
  5.3 6.0 %collective-permute-start.1 = (f32[24,512]{1,0:T(8,128)S(1)}, f32[24,512]{1,0:T(8,128)S(1)}, u32[]{:S(2)}, u32[]{:S(2)}) collective-permute-start(f32[24,512]{1,0:T(8,128)S(1)} %get-tuple-element.30._.refs_0_), channel_id=1, source_target_pairs={{0,24},{1,25},{2,26},{3,27},{4,28},{5,29},{6,30},{7,31},{8,16},{9,... | collective-permute-start | bytes 147464 | tf_op jit(solution)/shard_map/ppermute | solution.py:398
  9.2 4.0 %collective-permute-start.2 = (f32[24,512]{1,0:T(8,128)S(1)}, f32[24,512]{1,0:T(8,128)S(1)}, u32[]{:S(2)}, u32[]{:S(2)}) collective-permute-start(f32[24,512]{1,0:T(8,128)S(1)} %get-tuple-element.30._.refs_0_), channel_id=1, source_target_pairs={{0,12},{1,13},{2,14},{3,15},{4,8},{5,9},{6,10},{7,11},{8,4},{9,5},... | collective-permute-start | bytes 147464 | tf_op jit(solution)/shard_map/ppermute | solution.py:398
  9.2 4.0 %collective-permute-start.3 = (f32[24,512]{1,0:T(8,128)S(1)}, f32[24,512]{1,0:T(8,128)S(1)}, u32[]{:S(2)}, u32[]{:S(2)}) collective-permute-start(f32[24,512]{1,0:T(8,128)S(1)} %get-tuple-element.30._.refs_0_), channel_id=1, source_target_pairs={{0,20},{1,21},{2,22},{3,23},{4,16},{5,17},{6,18},{7,19},{8,28},{9,... | collective-permute-start | bytes 147464 | tf_op jit(solution)/shard_map/ppermute | solution.py:398
  13.2 5.9 %collective-permute-start.4 = (f32[16,512]{1,0:T(8,128)S(1)}, f32[16,512]{1,0:T(8,128)S(1)}, u32[]{:S(2)}, u32[]{:S(2)}) collective-permute-start(f32[16,512]{1,0:T(8,128)S(1)} %get-tuple-element.34), channel_id=1, source_target_pairs={{0,4},{1,5},{2,6},{3,7},{4,0},{5,1},{6,2},{7,3},{8,12},{9,13},{10,... | collective-permute-start | bytes 98312 | tf_op jit(solution)/shard_map/ppermute | solution.py:398
  13.5 3.2 %collective-permute-start.5 = (f32[8,512]{1,0:T(8,128)S(1)}, f32[8,512]{1,0:T(8,128)S(1)}, u32[]{:S(2)}, u32[]{:S(2)}) collective-permute-start(f32[8,512]{1,0:T(8,128)S(1)} %get-tuple-element.37._.own), channel_id=1, source_target_pairs={{0,5},{1,4},{2,7},{3,6},{4,1},{5,0},{6,3},{7,2},{8,13},{9,12},{10,... | collective-permute-start | bytes 49160 | tf_op jit(solution)/shard_map/ppermute | solution.py:398
  16.6 5.1 %collective-permute-start.6 = (f32[8,512]{1,0:T(8,128)S(1)}, f32[8,512]{1,0:T(8,128)S(1)}, u32[]{:S(2)}, u32[]{:S(2)}) collective-permute-start(f32[8,512]{1,0:T(8,128)S(1)} %sum_groups.2.refs_6_.own), channel_id=1, source_target_pairs={{0,6},{1,7},{2,4},{3,5},{4,2},{5,3},{6,0},{7,1},{8,14},{9,15},{10,... | collective-permute-start | bytes 49160 | tf_op jit(solution)/shard_map/ppermute | solution.py:398
  21.7 1.2 %collective-permute-start.7 = (f32[8,512]{1,0:T(8,128)S(1)}, f32[8,512]{1,0:T(8,128)S(1)}, u32[]{:S(2)}, u32[]{:S(2)}) collective-permute-start(f32[8,512]{1,0:T(8,128)S(1)} %sum_groups.3.own), channel_id=1, source_target_pairs={{0,4},{1,5},{2,6},{3,7},{4,0},{5,1},{6,2},{7,3},{8,12},{9,13},{10,... | collective-permute-start | bytes 49160 | tf_op jit(solution)/shard_map/ppermute | solution.py:398

commit v12 on v10

--- a/solution.py
+++ b/solution.py
@@ -456,15 +456,15 @@
         size *= count
 
     grad = joined
-    stride = 1
-    while stride < groups:
+    stride = groups // 2
+    while stride:
         other = swap(grad, 0, stride)
-        if stride == 1:
+        if stride == groups // 2:
             received = swap(message[0], 1)
             near = near + near_part(2, grad)
             pinned = near[-1]
-        stride *= 2
-        if stride == groups:
+        stride //= 2
+        if not stride:
             conv_out, signal_grad, pinned = pl.pallas_call(
                 functools.partial(finish_kernel, ranges),
                 out_shape=[jax.ShapeDtypeStruct((tokens, channels), signal.dtype)] * 2 + [shaped(SUB, LANES)],

time: 23.4 us -> 23.3 us (level)
  no operation moved by 1% of the time
where the time goes in v12:
time: 23.3 us; the launch traced here: 23.1 us
  Pallas kernels  9.27 us (40%)
  starting transfers between devices  9.26 us (40%)
  waiting for transfers between devices  3.93 us (17%)
  between operations  0.69 us (3%)
    ppermute x8, starting transfers between devices, swap(): lax.ppermute(x, ('ctx', 'ch'), [(i, i ^ mask) for i in range(n * groups)])  9.26 us
    ppermute x8, waiting for transfers between devices, swap(): lax.ppermute(x, ('ctx', 'ch'), [(i, i ^ mask) for i in range(n * groups)])  3.93 us
    pallas_call x3, Pallas kernels, near_part(): pl.pallas_call(functools.partial(local_kernel, ranges[part]), out_shape=[...  3.11 us
    pallas_call x1, Pallas kernels, body(): pl.pallas_call(gather_kernel, out_shape=[values, values] + [shaped(modes,...  2.91 us
    pallas_call x1, Pallas kernels, body(): pl.pallas_call(functools.partial(finish_kernel, ranges), out_shape=[jax.S...  2.53 us
    pallas_call x1, Pallas kernels, body(): pl.pallas_call(functools.partial(assemble_kernel, 1.0 / (tokens * n)), ou...  0.62 us
  transfers between devices with their start and end apart: 8, of which 5 were waited for; matrix products, arithmetic and copies ran while one was open for 0% of the time, Pallas kernels for 24%

profile of v12, /device:TPU:0, one launch (start us, length us, event | category | flops | bytes accessed | tf_op | source)
XLA Modules:
  0.0 23.1 jit_solution(2632221482902475894)
XLA Ops:
  0.6 2.9 %block_states.1 = (f32[256,512]{1,0:T(8,128)S(1)}, f32[256,512]{1,0:T(8,128)S(1)}, f32[16,512]{1,0:T(8,128)S(1)}, f32[16,512]{1,0:T(8,128)S(1)}, f32[48,512]{1,0:T(8,128)S(1)}, /*index=5*/f32[24,512]{1,0:T(8,128)S(1)}) custom-call(bf16[256,512]{1,0:T(8,128)(2,1)} %refs_0_.1, bf16[256,512]{1,0:T(8,128)(2,1)} %refs_1_.1, f32[16,512]{1,0:T(8,128)} %refs_2_.1, ...), custom_call_target="tpu_custom_call" | custom-call | flops 10485760 | bytes 786432 | tf_op jit(solution)/shard_map/block_states/pallas_call | solution.py:410
  3.6 0.5 %collective-permute-start = (f32[24,512]{1,0:T(8,128)S(1)}, f32[24,512]{1,0:T(8,128)S(1)}, u32[]{:S(2)}, u32[]{:S(2)}) collective-permute-start(f32[24,512]{1,0:T(8,128)S(1)} %get-tuple-element.26), channel_id=1, source_target_pairs={{0,4},{1,5},{2,6},{3,7},{4,0},{5,1},{6,2},{7,3},{8,12},{9,13},{10,... | collective-permute-start | bytes 147464 | tf_op jit(solution)/shard_map/ppermute | solution.py:392
  4.1 0.8 %local_convolutions.3 = (f32[1,32,8,128]{3,2,1,0:T(8,128)S(1)}, f32[1,32,8,128]{3,2,1,0:T(8,128)S(1)}) custom-call(f32[256,512]{1,0:T(8,128)S(1)} %get-tuple-element.27.xf, f32[256,512]{1,0:T(8,128)S(1)} %get-tuple-element.28.gf, f32[16,512]{1,0:T(8,128)S(1)} %get-tuple-element.23.residue_ref, f32[16,512]{1,0:T(8,128)S(1)} %get-tuple-element.24.decay_ref.refs_5_, ...), custom_call_target="tpu_custom_call" | custom-call | flops 209715200 | bytes 524288 | tf_op jit(solution)/shard_map/local_convolutions/pallas_call | solution.py:397
  4.8 0.1 collective-permute-done.other
  5.0 3.9 %collective-permute-start.1 = (f32[24,512]{1,0:T(8,128)S(1)}, f32[24,512]{1,0:T(8,128)S(1)}, u32[]{:S(2)}, u32[]{:S(2)}) collective-permute-start(f32[24,512]{1,0:T(8,128)S(1)} %get-tuple-element.30._.refs_0_), channel_id=1, source_target_pairs={{0,24},{1,25},{2,26},{3,27},{4,28},{5,29},{6,30},{7,31},{8,16},{9,... | collective-permute-start | bytes 147464 | tf_op jit(solution)/shard_map/ppermute | solution.py:392
  8.8 0.0 collective-permute-start.2
  8.9 0.3 %collective-permute-start.3 = (f32[24,512]{1,0:T(8,128)S(1)}, f32[24,512]{1,0:T(8,128)S(1)}, u32[]{:S(2)}, u32[]{:S(2)}) collective-permute-start(f32[24,512]{1,0:T(8,128)S(1)} %get-tuple-element.30._.refs_0_), channel_id=1, source_target_pairs={{0,20},{1,21},{2,22},{3,23},{4,16},{5,17},{6,18},{7,19},{8,28},{9,... | collective-permute-start | bytes 147464 | tf_op jit(solution)/shard_map/ppermute | solution.py:392
  9.2 1.6 %local_convolutions.4 = (f32[2,32,8,128]{3,2,1,0:T(8,128)S(1)}, f32[2,32,8,128]{3,2,1,0:T(8,128)S(1)}) custom-call(f32[256,512]{1,0:T(8,128)S(1)} %get-tuple-element.27.xf, f32[256,512]{1,0:T(8,128)S(1)} %get-tuple-element.28.gf, f32[16,512]{1,0:T(8,128)S(1)} %get-tuple-element.23.residue_ref, f32[16,512]{1,0:T(8,128)S(1)} %get-tuple-element.24.decay_ref.refs_5_, ...), custom_call_target="tpu_custom_call" | custom-call | flops 419430400 | bytes 1048576 | tf_op jit(solution)/shard_map/local_convolutions/pallas_call | solution.py:397
  10.8 0.2 collective-permute-done.1.refs_1_
  11.0 1.9 %collective-permute-done.2.refs_2_ = f32[24,512]{1,0:T(8,128)S(1)} collective-permute-done((f32[24,512]{1,0:T(8,128)S(1)}, f32[24,512]{1,0:T(8,128)S(1)}, u32[]{:S(2)}, u32[]{:S(2)}) %collective-permute-start.2) | collective-permute-done | bytes 49184 | tf_op jit(solution)/shard_map/ppermute | solution.py:392
  12.8 0.0 collective-permute-done.3.refs_3_
  12.8 0.1 join_chips.1
  12.9 0.2 %collective-permute-start.4 = (f32[16,512]{1,0:T(8,128)S(1)}, f32[16,512]{1,0:T(8,128)S(1)}, u32[]{:S(2)}, u32[]{:S(2)}) collective-permute-start(f32[16,512]{1,0:T(8,128)S(1)} %get-tuple-element.34), channel_id=1, source_target_pairs={{0,4},{1,5},{2,6},{3,7},{4,0},{5,1},{6,2},{7,3},{8,12},{9,13},{10,... | collective-permute-start | bytes 98312 | tf_op jit(solution)/shard_map/ppermute | solution.py:392
  13.1 2.5 %collective-permute-start.5 = (f32[8,512]{1,0:T(8,128)S(1)}, f32[8,512]{1,0:T(8,128)S(1)}, u32[]{:S(2)}, u32[]{:S(2)}) collective-permute-start(f32[8,512]{1,0:T(8,128)S(1)} %get-tuple-element.37._.own), channel_id=1, source_target_pairs={{0,6},{1,7},{2,4},{3,5},{4,2},{5,3},{6,0},{7,1},{8,14},{9,15},{10,... | collective-permute-start | bytes 49160 | tf_op jit(solution)/shard_map/ppermute | solution.py:392
  15.7 0.8 %local_convolutions.5 = (f32[1,32,8,128]{3,2,1,0:T(8,128)S(1)}, f32[1,32,8,128]{3,2,1,0:T(8,128)S(1)}) custom-call(f32[256,512]{1,0:T(8,128)S(1)} %get-tuple-element.27.xf, f32[256,512]{1,0:T(8,128)S(1)} %get-tuple-element.28.gf, f32[16,512]{1,0:T(8,128)S(1)} %get-tuple-element.23.residue_ref, f32[16,512]{1,0:T(8,128)S(1)} %get-tuple-element.24.decay_ref.refs_5_, ...), custom_call_target="tpu_custom_call" | custom-call | flops 209715200 | bytes 524288 | tf_op jit(solution)/shard_map/local_convolutions/pallas_call | solution.py:397
  16.4 0.8 %collective-permute-done.5.other = f32[8,512]{1,0:T(8,128)S(1)} collective-permute-done((f32[8,512]{1,0:T(8,128)S(1)}, f32[8,512]{1,0:T(8,128)S(1)}, u32[]{:S(2)}, u32[]{:S(2)}) %collective-permute-start.5) | collective-permute-done | bytes 16416 | tf_op jit(solution)/shard_map/ppermute | solution.py:392
  17.2 1.5 %collective-permute-start.6 = (f32[8,512]{1,0:T(8,128)S(1)}, f32[8,512]{1,0:T(8,128)S(1)}, u32[]{:S(2)}, u32[]{:S(2)}) collective-permute-start(f32[8,512]{1,0:T(8,128)S(1)} %sum_groups.2.refs_6_.own), channel_id=1, source_target_pairs={{0,5},{1,4},{2,7},{3,6},{4,1},{5,0},{6,3},{7,2},{8,13},{9,12},{10,... | collective-permute-start | bytes 49160 | tf_op jit(solution)/shard_map/ppermute | solution.py:392
  18.7 0.0 collective-permute-done.4.other
  18.7 2.5 %add_arrivals.1 = (bf16[256,512]{1,0:T(8,128)(2,1)}, bf16[256,512]{1,0:T(8,128)(2,1)}, f32[8,128]{1,0:T(8,128)S(1)}) custom-call(f32[16,512]{1,0:T(8,128)S(1)} %get-tuple-element.23.residue_ref, f32[16,512]{1,0:T(8,128)S(1)} %get-tuple-element.24.decay_ref.refs_5_, f32[16,512]{1,0:T(8,128)S(1)} %get-tuple-element.33.own, ...), custom_call_target="tpu_custom_call" | custom-call | flops 1258291200 | bytes 1572864 | tf_op jit(solution)/shard_map/add_arrivals/pallas_call | solution.py:468
  21.3 0.0 collective-permute-done.6.other
  21.3 0.2 %collective-permute-start.7 = (f32[8,512]{1,0:T(8,128)S(1)}, f32[8,512]{1,0:T(8,128)S(1)}, u32[]{:S(2)}, u32[]{:S(2)}) collective-permute-start(f32[8,512]{1,0:T(8,128)S(1)} %sum_groups.3.own), channel_id=1, source_target_pairs={{0,4},{1,5},{2,6},{3,7},{4,0},{5,1},{6,2},{7,3},{8,12},{9,13},{10,... | collective-permute-start | bytes 49160 | tf_op jit(solution)/shard_map/ppermute | solution.py:392
  21.5 1.0 %collective-permute-done.7.other = f32[8,512]{1,0:T(8,128)S(1)} collective-permute-done((f32[8,512]{1,0:T(8,128)S(1)}, f32[8,512]{1,0:T(8,128)S(1)}, u32[]{:S(2)}, u32[]{:S(2)}) %collective-permute-start.7) | collective-permute-done | bytes 16416 | tf_op jit(solution)/shard_map/ppermute | solution.py:392
  22.5 0.6 %assemble_gradient.1 = f32[16,512]{1,0:T(8,128)} custom-call(f32[8,512]{1,0:T(8,128)S(1)} %sum_groups.3.own, f32[8,512]{1,0:T(8,128)S(1)} %collective-permute-done.7.other), custom_call_target="tpu_custom_call" | custom-call | flops 131072 | bytes 262144 | tf_op jit(solution)/shard_map/assemble_gradient/pallas_call | solution.py:488
  (3 shorter events, 0.0 us)
Async XLA Ops:
  3.6 1.4 %collective-permute-start = (f32[24,512]{1,0:T(8,128)S(1)}, f32[24,512]{1,0:T(8,128)S(1)}, u32[]{:S(2)}, u32[]{:S(2)}) collective-permute-start(f32[24,512]{1,0:T(8,128)S(1)} %get-tuple-element.26), channel_id=1, source_target_pairs={{0,4},{1,5},{2,6},{3,7},{4,0},{5,1},{6,2},{7,3},{8,12},{9,13},{10,... | collective-permute-start | bytes 147464 | tf_op jit(solution)/shard_map/ppermute | solution.py:392
  5.0 6.0 %collective-permute-start.1 = (f32[24,512]{1,0:T(8,128)S(1)}, f32[24,512]{1,0:T(8,128)S(1)}, u32[]{:S(2)}, u32[]{:S(2)}) collective-permute-start(f32[24,512]{1,0:T(8,128)S(1)} %get-tuple-element.30._.refs_0_), channel_id=1, source_target_pairs={{0,24},{1,25},{2,26},{3,27},{4,28},{5,29},{6,30},{7,31},{8,16},{9,... | collective-permute-start | bytes 147464 | tf_op jit(solution)/shard_map/ppermute | solution.py:392
  8.8 4.0 %collective-permute-start.2 = (f32[24,512]{1,0:T(8,128)S(1)}, f32[24,512]{1,0:T(8,128)S(1)}, u32[]{:S(2)}, u32[]{:S(2)}) collective-permute-start(f32[24,512]{1,0:T(8,128)S(1)} %get-tuple-element.30._.refs_0_), channel_id=1, source_target_pairs={{0,12},{1,13},{2,14},{3,15},{4,8},{5,9},{6,10},{7,11},{8,4},{9,5},... | collective-permute-start | bytes 147464 | tf_op jit(solution)/shard_map/ppermute | solution.py:392
  8.9 4.0 %collective-permute-start.3 = (f32[24,512]{1,0:T(8,128)S(1)}, f32[24,512]{1,0:T(8,128)S(1)}, u32[]{:S(2)}, u32[]{:S(2)}) collective-permute-start(f32[24,512]{1,0:T(8,128)S(1)} %get-tuple-element.30._.refs_0_), channel_id=1, source_target_pairs={{0,20},{1,21},{2,22},{3,23},{4,16},{5,17},{6,18},{7,19},{8,28},{9,... | collective-permute-start | bytes 147464 | tf_op jit(solution)/shard_map/ppermute | solution.py:392
  12.9 5.8 %collective-permute-start.4 = (f32[16,512]{1,0:T(8,128)S(1)}, f32[16,512]{1,0:T(8,128)S(1)}, u32[]{:S(2)}, u32[]{:S(2)}) collective-permute-start(f32[16,512]{1,0:T(8,128)S(1)} %get-tuple-element.34), channel_id=1, source_target_pairs={{0,4},{1,5},{2,6},{3,7},{4,0},{5,1},{6,2},{7,3},{8,12},{9,13},{10,... | collective-permute-start | bytes 98312 | tf_op jit(solution)/shard_map/ppermute | solution.py:392
  13.1 4.1 %collective-permute-start.5 = (f32[8,512]{1,0:T(8,128)S(1)}, f32[8,512]{1,0:T(8,128)S(1)}, u32[]{:S(2)}, u32[]{:S(2)}) collective-permute-start(f32[8,512]{1,0:T(8,128)S(1)} %get-tuple-element.37._.own), channel_id=1, source_target_pairs={{0,6},{1,7},{2,4},{3,5},{4,2},{5,3},{6,0},{7,1},{8,14},{9,15},{10,... | collective-permute-start | bytes 49160 | tf_op jit(solution)/shard_map/ppermute | solution.py:392
  17.2 4.1 %collective-permute-start.6 = (f32[8,512]{1,0:T(8,128)S(1)}, f32[8,512]{1,0:T(8,128)S(1)}, u32[]{:S(2)}, u32[]{:S(2)}) collective-permute-start(f32[8,512]{1,0:T(8,128)S(1)} %sum_groups.2.refs_6_.own), channel_id=1, source_target_pairs={{0,5},{1,4},{2,7},{3,6},{4,1},{5,0},{6,3},{7,2},{8,13},{9,12},{10,... | collective-permute-start | bytes 49160 | tf_op jit(solution)/shard_map/ppermute | solution.py:392
  21.3 1.2 %collective-permute-start.7 = (f32[8,512]{1,0:T(8,128)S(1)}, f32[8,512]{1,0:T(8,128)S(1)}, u32[]{:S(2)}, u32[]{:S(2)}) collective-permute-start(f32[8,512]{1,0:T(8,128)S(1)} %sum_groups.3.own), channel_id=1, source_target_pairs={{0,4},{1,5},{2,6},{3,7},{4,0},{5,1},{6,2},{7,3},{8,12},{9,13},{10,... | collective-permute-start | bytes 49160 | tf_op jit(solution)/shard_map/ppermute | solution.py:392

commit v13 on v12

--- a/solution.py
+++ b/solution.py
@@ -281,12 +281,11 @@
     message[half:] = jnp.where(second, out[0], out[1])
 
 
-def finish_kernel(ranges, residue_ref, decay_ref, own, other, *refs):
-    near = refs[:2 * len(ranges)]
-    _, out_hbm, back_hbm, finished, out_ref, back_ref, result, pw, arrive, leave, sems = refs[2 * len(ranges):]
+def finish_kernel(tiles, residue_ref, decay_ref, own, other, near_out, near_back, *refs):
+    out_hbm, back_hbm, finished, out_ref, back_ref, result, pw, arrive, leave, sems = refs[-10:]
     modes, channels = decay_ref.shape
     half = modes // 2
-    chunks = near[0].shape[1] // SUB
+    chunks = near_out.shape[1] // SUB
     span = chunks * SUB
     own_high = owns_high()
     first = residue_ref[...] * jnp.exp(-decay_ref[...])
@@ -300,49 +299,45 @@
         source, target = ((out_ref, out_hbm), (back_ref, back_hbm))[which]
         return pltpu.make_async_copy(source.at[:, lanes], target.at[:, lanes], sems.at[which, tile])
 
-    def run(tiles, near_out, near_back):
-        def tile_step(tile, _):
-            lanes = pl.ds(pl.multiple_of(tile * LANES, LANES), LANES)
-            decay = decay_ref[:, lanes]
-            powers(decay, pw)
-            pw[2] = decay * (-1.0 * span)
-            pw[3] = arrive[:, lanes]
-            pw[4] = leave[:, lanes]
-            level = lax.broadcasted_iota(jnp.int32, (SUB, LANES), 0).astype(F32)
-            for near, target, forward in ((near_out, out_ref, True), (near_back, back_ref, False)):
-                order = range(SUB) if forward else range(SUB - 1, -1, -1)
-                spans = level if forward else SUB - 1.0 - level
-                totals = [[near[tile - tiles[0], p * SUB + r] for r in range(SUB)] for p in range(chunks)]
-                for m in range(modes):
-                    a, a8, rate = (row(pw, i, pl.ds(m, 1)) for i in range(3))
-                    state = row(pw, 3 if forward else 4, pl.ds(m, 1)) * jnp.exp(rate * spans)
-                    for q in range(chunks):
-                        p = q if forward else chunks - 1 - q
-                        wave = state
-                        for r in order:
-                            totals[p][r] = totals[p][r] + wave
-                            wave = wave * a
-                        if q < chunks - 1:
-                            state = state * a8
-                for p in range(chunks):
-                    for r in range(SUB):
-                        result[pl.ds(p * SUB + r, SUB, stride=span), :] = totals[p][r]
-                target[:, lanes] = result[...].astype(target.dtype)
-                copy_out(tile, 0 if forward else 1).start()
-            return 0
-
-        lax.fori_loop(tiles[0], tiles[1], tile_step, 0)
-
-    for part, tiles in enumerate(ranges):
-        run(tiles, near[2 * part], near[2 * part + 1])
-    for tile in range(channels // LANES):
+    def tile_step(tile, _):
+        lanes = pl.ds(pl.multiple_of(tile * LANES, LANES), LANES)
+        decay = decay_ref[:, lanes]
+        powers(decay, pw)
+        pw[2] = decay * (-1.0 * span)
+        pw[3] = arrive[:, lanes]
+        pw[4] = leave[:, lanes]
+        level = lax.broadcasted_iota(jnp.int32, (SUB, LANES), 0).astype(F32)
+        for near, target, forward in ((near_out, out_ref, True), (near_back, back_ref, False)):
+            order = range(SUB) if forward else range(SUB - 1, -1, -1)
+            spans = level if forward else SUB - 1.0 - level
+            totals = [[near[tile - tiles[0], p * SUB + r] for r in range(SUB)] for p in range(chunks)]
+            for m in range(modes):
+                a, a8, rate = (row(pw, i, pl.ds(m, 1)) for i in range(3))
+                state = row(pw, 3 if forward else 4, pl.ds(m, 1)) * jnp.exp(rate * spans)
+                for q in range(chunks):
+                    p = q if forward else chunks - 1 - q
+                    wave = state
+                    for r in order:
+                        totals[p][r] = totals[p][r] + wave
+                        wave = wave * a
+                    if q < chunks - 1:
+                        state = state * a8
+            for p in range(chunks):
+                for r in range(SUB):
+                    result[pl.ds(p * SUB + r, SUB, stride=span), :] = totals[p][r]
+            target[:, lanes] = result[...].astype(target.dtype)
+            copy_out(tile, 0 if forward else 1).start()
+        return 0
+
+    lax.fori_loop(*tiles, tile_step, 0)
+    for tile in range(*tiles):
         for which in range(2):
             copy_out(tile, which).wait()
     finished[...] = jnp.zeros(finished.shape, F32)
 
 
-def sum_kernel(own, other, _, out_ref):
-    out_ref[...] = own[...] + other[...]
+def sum_kernel(own, other, *refs):
+    refs[-1][...] = own[...] + other[...]
 
 
 def assemble_kernel(scale, own, other, out_ref):
@@ -382,7 +377,7 @@
     spans = vmem(modes * SUB, LANES)
     tiles = channels // LANES
     quarter = tiles // 4
-    ranges = [(0, quarter), (quarter, 3 * quarter), (3 * quarter, tiles)]
+    ranges = [(0, quarter), (quarter, tiles)]
     small = dict(compiler_params=PARAMS, cost_estimate=cost(elements, modes * channels, modes * channels * 32))
 
     def swap(x, ctx_mask, ch_mask=0):
@@ -440,7 +435,7 @@
     while size < chips:
         count = min(4, chips // size)
         last = size * count == chips
-        masks = [3, 1, 2] if count == 4 else [1]
+        masks = [2, 1, 3] if count == 4 else [1]
         others = [swap(joined, 2 * size * m) for m in masks]
         if last:
             near = near + near_part(1, joined)
@@ -455,43 +450,50 @@
         )(joined, *others, core, decay, carried, near[-1])
         size *= count
 
+    def finish_part(part, after, written):
+        return pl.pallas_call(
+            functools.partial(finish_kernel, ranges[part]),
+            out_shape=[jax.ShapeDtypeStruct((tokens, channels), jnp.bfloat16)] * 2 + [shaped(SUB, LANES)],
+            in_specs=[WHOLE] * 6 + [UNREAD] + [HBM] * len(written),
+            out_specs=[HBM] * 2 + [WHOLE],
+            input_output_aliases={7 + i: i for i in range(len(written))},
+            scratch_shapes=[pltpu.VMEM((tokens, channels), jnp.bfloat16)] * 2
+            + [vmem(tokens, LANES), vmem(5, modes, LANES)]
+            + [vmem(modes, channels)] * 2
+            + [pltpu.SemaphoreType.DMA((2, tiles))],
+            compiler_params=PARAMS,
+            cost_estimate=cost(elements * modes * 300, 0, elements * 6),
+            name="add_arrivals",
+        )(residue, decay, carried, received, *near[2 * part:2 * part + 2], after, *written)
+
+    received = swap(message[0], 1)
     grad = joined
+    written = []
     stride = groups // 2
     while stride:
         other = swap(grad, 0, stride)
+        pinned = []
         if stride == groups // 2:
-            received = swap(message[0], 1)
-            near = near + near_part(2, grad)
-            pinned = near[-1]
-        stride //= 2
-        if not stride:
-            conv_out, signal_grad, pinned = pl.pallas_call(
-                functools.partial(finish_kernel, ranges),
-                out_shape=[jax.ShapeDtypeStruct((tokens, channels), signal.dtype)] * 2 + [shaped(SUB, LANES)],
-                in_specs=[WHOLE] * (4 + 2 * len(ranges)) + [UNREAD],
-                out_specs=[HBM] * 2 + [WHOLE],
-                scratch_shapes=[pltpu.VMEM((tokens, channels), signal.dtype)] * 2
-                + [vmem(tokens, LANES), vmem(5, modes, LANES)]
-                + [vmem(modes, channels)] * 2
-                + [pltpu.SemaphoreType.DMA((2, tiles))],
-                compiler_params=PARAMS,
-                cost_estimate=cost(elements * modes * 600, 0, elements * 12),
-                name="add_arrivals",
-            )(residue, decay, carried, received, *near, grad)
+            *written, finished = finish_part(0, grad, written)
+            pinned = [finished]
+        if stride == 1:
+            *written, finished = finish_part(1, grad, written)
+            pinned = [finished]
         grad = pl.pallas_call(
             sum_kernel,
             out_shape=shaped(half, channels),
-            in_specs=[WHOLE] * 2 + [UNREAD],
+            in_specs=[WHOLE] * 2 + [UNREAD] * len(pinned),
             name="sum_groups",
             **small,
-        )(grad, other, pinned)
+        )(grad, other, *pinned)
+        stride //= 2
     residue_grad = pl.pallas_call(
         functools.partial(assemble_kernel, 1.0 / (tokens * n)),
         out_shape=shaped(modes, channels),
         name="assemble_gradient",
         **small,
     )(grad, swap(grad, 1))
-    return conv_out, signal_grad, residue_grad
+    return *written, residue_grad
 
 
 def solution(mesh):

time: 23.3 us -> 22.9 us (0.983)
  waiting for transfers between devices: 3.93 us -> 2.7 us
  Pallas kernels: 9.27 us -> 10.1 us
    ppermute x8, waiting for transfers between devices: 3.93 us -> 2.7 us  [swap(): lax.ppermute(x, ('ctx', 'ch'), [(i, i ^ mask) for i in range(n * groups)])]
    pallas_call x1 -> x2, Pallas kernels: 2.53 us -> 3.36 us  [finish_part(): pl.pallas_call(functools.partial(finish_kernel, ranges[part]), out_shape=...]
    pallas_call x3 -> x2, Pallas kernels: 3.11 us -> 3.13 us  [near_part(): pl.pallas_call(functools.partial(local_kernel, ranges[part]), out_shape=[...]
  transfers between devices with their start and end apart: 8 -> 8, of which waited for: 5 -> 4; matrix products, arithmetic and copies ran while one was open for 0% -> 0% of each run, Pallas kernels for 24% -> 28%
where the time goes in v13:
time: 22.9 us; the launch traced here: 22.8 us
  Pallas kernels  10.1 us (44%)
  starting transfers between devices  9.26 us (40%)
  waiting for transfers between devices  2.7 us (12%)
  between operations  0.7 us (3%)
    ppermute x8, starting transfers between devices, swap(): lax.ppermute(x, ('ctx', 'ch'), [(i, i ^ mask) for i in range(n * groups)])  9.26 us
    pallas_call x2, Pallas kernels, finish_part(): pl.pallas_call(functools.partial(finish_kernel, ranges[part]), out_shape=...  3.36 us
    pallas_call x2, Pallas kernels, near_part(): pl.pallas_call(functools.partial(local_kernel, ranges[part]), out_shape=[...  3.13 us
    pallas_call x1, Pallas kernels, body(): pl.pallas_call(gather_kernel, out_shape=[values, values] + [shaped(modes,...  2.91 us
    ppermute x8, waiting for transfers between devices, swap(): lax.ppermute(x, ('ctx', 'ch'), [(i, i ^ mask) for i in range(n * groups)])  2.7 us
    pallas_call x1, Pallas kernels, body(): pl.pallas_call(functools.partial(assemble_kernel, 1.0 / (tokens * n)), ou...  0.62 us
  transfers between devices with their start and end apart: 8, of which 4 were waited for; matrix products, arithmetic and copies ran while one was open for 0% of the time, Pallas kernels for 28%

profile of v13, /device:TPU:0, one launch (start us, length us, event | category | flops | bytes accessed | tf_op | source)
XLA Modules:
  0.0 22.8 jit_solution(12076707231559527974)
XLA Ops:
  0.6 2.9 %block_states.1 = (f32[256,512]{1,0:T(8,128)S(1)}, f32[256,512]{1,0:T(8,128)S(1)}, f32[16,512]{1,0:T(8,128)S(1)}, f32[16,512]{1,0:T(8,128)S(1)}, f32[48,512]{1,0:T(8,128)S(1)}, /*index=5*/f32[24,512]{1,0:T(8,128)S(1)}) custom-call(bf16[256,512]{1,0:T(8,128)(2,1)} %refs_0_.1, bf16[256,512]{1,0:T(8,128)(2,1)} %refs_1_.1, f32[16,512]{1,0:T(8,128)} %refs_2_.1, ...), custom_call_target="tpu_custom_call" | custom-call | flops 10485760 | bytes 786432 | tf_op jit(solution)/shard_map/block_states/pallas_call | solution.py:405
  3.6 0.5 %collective-permute-start = (f32[24,512]{1,0:T(8,128)S(1)}, f32[24,512]{1,0:T(8,128)S(1)}, u32[]{:S(2)}, u32[]{:S(2)}) collective-permute-start(f32[24,512]{1,0:T(8,128)S(1)} %get-tuple-element.27), channel_id=1, source_target_pairs={{0,4},{1,5},{2,6},{3,7},{4,0},{5,1},{6,2},{7,3},{8,12},{9,13},{10,... | collective-permute-start | bytes 147464 | tf_op jit(solution)/shard_map/ppermute | solution.py:387
  4.1 0.8 %local_convolutions.2 = (f32[1,32,8,128]{3,2,1,0:T(8,128)S(1)}, f32[1,32,8,128]{3,2,1,0:T(8,128)S(1)}) custom-call(f32[256,512]{1,0:T(8,128)S(1)} %get-tuple-element.28.xf, f32[256,512]{1,0:T(8,128)S(1)} %get-tuple-element.29.gf, f32[16,512]{1,0:T(8,128)S(1)} %get-tuple-element.24.residue_ref, f32[16,512]{1,0:T(8,128)S(1)} %get-tuple-element.25.decay_ref.refs_5_, ...), custom_call_target="tpu_custom_call" | custom-call | flops 209715200 | bytes 524288 | tf_op jit(solution)/shard_map/local_convolutions/pallas_call | solution.py:392
  4.8 0.1 collective-permute-done.other
  5.0 3.9 %collective-permute-start.3 = (f32[24,512]{1,0:T(8,128)S(1)}, f32[24,512]{1,0:T(8,128)S(1)}, u32[]{:S(2)}, u32[]{:S(2)}) collective-permute-start(f32[24,512]{1,0:T(8,128)S(1)} %get-tuple-element.31._.refs_0_), channel_id=1, source_target_pairs={{0,24},{1,25},{2,26},{3,27},{4,28},{5,29},{6,30},{7,31},{8,16},{9,... | collective-permute-start | bytes 147464 | tf_op jit(solution)/shard_map/ppermute | solution.py:387
  8.8 0.0 collective-permute-start.2
  8.9 0.3 %collective-permute-start.1 = (f32[24,512]{1,0:T(8,128)S(1)}, f32[24,512]{1,0:T(8,128)S(1)}, u32[]{:S(2)}, u32[]{:S(2)}) collective-permute-start(f32[24,512]{1,0:T(8,128)S(1)} %get-tuple-element.31._.refs_0_), channel_id=1, source_target_pairs={{0,20},{1,21},{2,22},{3,23},{4,16},{5,17},{6,18},{7,19},{8,28},{9,... | collective-permute-start | bytes 147464 | tf_op jit(solution)/shard_map/ppermute | solution.py:387
  9.2 2.3 %local_convolutions.3 = (f32[3,32,8,128]{3,2,1,0:T(8,128)S(1)}, f32[3,32,8,128]{3,2,1,0:T(8,128)S(1)}) custom-call(f32[256,512]{1,0:T(8,128)S(1)} %get-tuple-element.28.xf, f32[256,512]{1,0:T(8,128)S(1)} %get-tuple-element.29.gf, f32[16,512]{1,0:T(8,128)S(1)} %get-tuple-element.24.residue_ref, f32[16,512]{1,0:T(8,128)S(1)} %get-tuple-element.25.decay_ref.refs_5_, ...), custom_call_target="tpu_custom_call" | custom-call | flops 629145600 | bytes 1572864 | tf_op jit(solution)/shard_map/local_convolutions/pallas_call | solution.py:392
  11.6 0.0 collective-permute-done.3.refs_3_
  11.6 1.3 %collective-permute-done.2.refs_2_ = f32[24,512]{1,0:T(8,128)S(1)} collective-permute-done((f32[24,512]{1,0:T(8,128)S(1)}, f32[24,512]{1,0:T(8,128)S(1)}, u32[]{:S(2)}, u32[]{:S(2)}) %collective-permute-start.2) | collective-permute-done | bytes 49184 | tf_op jit(solution)/shard_map/ppermute | solution.py:387
  12.8 0.0 collective-permute-done.1.refs_1_
  12.8 0.1 join_chips.1
  12.9 0.2 %collective-permute-start.4 = (f32[16,512]{1,0:T(8,128)S(1)}, f32[16,512]{1,0:T(8,128)S(1)}, u32[]{:S(2)}, u32[]{:S(2)}) collective-permute-start(f32[16,512]{1,0:T(8,128)S(1)} %get-tuple-element.35), channel_id=1, source_target_pairs={{0,4},{1,5},{2,6},{3,7},{4,0},{5,1},{6,2},{7,3},{8,12},{9,13},{10,... | collective-permute-start | bytes 98312 | tf_op jit(solution)/shard_map/ppermute | solution.py:387
  13.1 2.5 %collective-permute-start.5 = (f32[8,512]{1,0:T(8,128)S(1)}, f32[8,512]{1,0:T(8,128)S(1)}, u32[]{:S(2)}, u32[]{:S(2)}) collective-permute-start(f32[8,512]{1,0:T(8,128)S(1)} %get-tuple-element.37.refs_0_.own), channel_id=1, source_target_pairs={{0,6},{1,7},{2,4},{3,5},{4,2},{5,3},{6,0},{7,1},{8,14},{9,15},{10,... | collective-permute-start | bytes 49160 | tf_op jit(solution)/shard_map/ppermute | solution.py:387
  15.7 0.0 collective-permute-done.4.other
  15.7 1.2 %add_arrivals.2 = (bf16[256,512]{1,0:T(8,128)(2,1)}, bf16[256,512]{1,0:T(8,128)(2,1)}, f32[8,128]{1,0:T(8,128)S(1)}) custom-call(f32[16,512]{1,0:T(8,128)S(1)} %get-tuple-element.24.residue_ref, f32[16,512]{1,0:T(8,128)S(1)} %get-tuple-element.25.decay_ref.refs_5_, f32[16,512]{1,0:T(8,128)S(1)} %get-tuple-element.34.own, ...), custom_call_target="tpu_custom_call" | custom-call | flops 629145600 | bytes 786432 | tf_op jit(solution)/shard_map/add_arrivals/pallas_call | solution.py:454
  16.9 0.3 %collective-permute-done.5.other = f32[8,512]{1,0:T(8,128)S(1)} collective-permute-done((f32[8,512]{1,0:T(8,128)S(1)}, f32[8,512]{1,0:T(8,128)S(1)}, u32[]{:S(2)}, u32[]{:S(2)}) %collective-permute-start.5) | collective-permute-done | bytes 16416 | tf_op jit(solution)/shard_map/ppermute | solution.py:387
  17.2 1.5 %collective-permute-start.6 = (f32[8,512]{1,0:T(8,128)S(1)}, f32[8,512]{1,0:T(8,128)S(1)}, u32[]{:S(2)}, u32[]{:S(2)}) collective-permute-start(f32[8,512]{1,0:T(8,128)S(1)} %sum_groups.2.refs_0_.own), channel_id=1, source_target_pairs={{0,5},{1,4},{2,7},{3,6},{4,1},{5,0},{6,3},{7,2},{8,13},{9,12},{10,... | collective-permute-start | bytes 49160 | tf_op jit(solution)/shard_map/ppermute | solution.py:387
  18.7 2.2 %add_arrivals.3 = (bf16[256,512]{1,0:T(8,128)(2,1)}, bf16[256,512]{1,0:T(8,128)(2,1)}, f32[8,128]{1,0:T(8,128)S(1)}) custom-call(f32[16,512]{1,0:T(8,128)S(1)} %get-tuple-element.24.residue_ref, f32[16,512]{1,0:T(8,128)S(1)} %get-tuple-element.25.decay_ref.refs_5_, ...), custom_call_target="tpu_custom_call", output_to_operand_aliasing={{0}: (7, {}), {1}: (8, {})} | custom-call | flops 629145600 | bytes 786432 | tf_op jit(solution)/shard_map/add_arrivals/pallas_call | solution.py:454
  20.9 0.0 collective-permute-done.6.other
  20.9 0.2 %collective-permute-start.7 = (f32[8,512]{1,0:T(8,128)S(1)}, f32[8,512]{1,0:T(8,128)S(1)}, u32[]{:S(2)}, u32[]{:S(2)}) collective-permute-start(f32[8,512]{1,0:T(8,128)S(1)} %sum_groups.3.own), channel_id=1, source_target_pairs={{0,4},{1,5},{2,6},{3,7},{4,0},{5,1},{6,2},{7,3},{8,12},{9,13},{10,... | collective-permute-start | bytes 49160 | tf_op jit(solution)/shard_map/ppermute | solution.py:387
  21.2 1.0 %collective-permute-done.7.other = f32[8,512]{1,0:T(8,128)S(1)} collective-permute-done((f32[8,512]{1,0:T(8,128)S(1)}, f32[8,512]{1,0:T(8,128)S(1)}, u32[]{:S(2)}, u32[]{:S(2)}) %collective-permute-start.7) | collective-permute-done | bytes 16416 | tf_op jit(solution)/shard_map/ppermute | solution.py:387
  22.2 0.6 %assemble_gradient.1 = f32[16,512]{1,0:T(8,128)} custom-call(f32[8,512]{1,0:T(8,128)S(1)} %sum_groups.3.own, f32[8,512]{1,0:T(8,128)S(1)} %collective-permute-done.7.other), custom_call_target="tpu_custom_call" | custom-call | flops 131072 | bytes 262144 | tf_op jit(solution)/shard_map/assemble_gradient/pallas_call | solution.py:490
  (3 shorter events, 0.0 us)
Async XLA Ops:
  3.6 1.4 %collective-permute-start = (f32[24,512]{1,0:T(8,128)S(1)}, f32[24,512]{1,0:T(8,128)S(1)}, u32[]{:S(2)}, u32[]{:S(2)}) collective-permute-start(f32[24,512]{1,0:T(8,128)S(1)} %get-tuple-element.27), channel_id=1, source_target_pairs={{0,4},{1,5},{2,6},{3,7},{4,0},{5,1},{6,2},{7,3},{8,12},{9,13},{10,... | collective-permute-start | bytes 147464 | tf_op jit(solution)/shard_map/ppermute | solution.py:387
  5.0 6.6 %collective-permute-start.3 = (f32[24,512]{1,0:T(8,128)S(1)}, f32[24,512]{1,0:T(8,128)S(1)}, u32[]{:S(2)}, u32[]{:S(2)}) collective-permute-start(f32[24,512]{1,0:T(8,128)S(1)} %get-tuple-element.31._.refs_0_), channel_id=1, source_target_pairs={{0,24},{1,25},{2,26},{3,27},{4,28},{5,29},{6,30},{7,31},{8,16},{9,... | collective-permute-start | bytes 147464 | tf_op jit(solution)/shard_map/ppermute | solution.py:387
  8.8 4.0 %collective-permute-start.2 = (f32[24,512]{1,0:T(8,128)S(1)}, f32[24,512]{1,0:T(8,128)S(1)}, u32[]{:S(2)}, u32[]{:S(2)}) collective-permute-start(f32[24,512]{1,0:T(8,128)S(1)} %get-tuple-element.31._.refs_0_), channel_id=1, source_target_pairs={{0,12},{1,13},{2,14},{3,15},{4,8},{5,9},{6,10},{7,11},{8,4},{9,5},... | collective-permute-start | bytes 147464 | tf_op jit(solution)/shard_map/ppermute | solution.py:387
  8.9 4.0 %collective-permute-start.1 = (f32[24,512]{1,0:T(8,128)S(1)}, f32[24,512]{1,0:T(8,128)S(1)}, u32[]{:S(2)}, u32[]{:S(2)}) collective-permute-start(f32[24,512]{1,0:T(8,128)S(1)} %get-tuple-element.31._.refs_0_), channel_id=1, source_target_pairs={{0,20},{1,21},{2,22},{3,23},{4,16},{5,17},{6,18},{7,19},{8,28},{9,... | collective-permute-start | bytes 147464 | tf_op jit(solution)/shard_map/ppermute | solution.py:387
  12.9 2.8 %collective-permute-start.4 = (f32[16,512]{1,0:T(8,128)S(1)}, f32[16,512]{1,0:T(8,128)S(1)}, u32[]{:S(2)}, u32[]{:S(2)}) collective-permute-start(f32[16,512]{1,0:T(8,128)S(1)} %get-tuple-element.35), channel_id=1, source_target_pairs={{0,4},{1,5},{2,6},{3,7},{4,0},{5,1},{6,2},{7,3},{8,12},{9,13},{10,... | collective-permute-start | bytes 98312 | tf_op jit(solution)/shard_map/ppermute | solution.py:387
  13.1 4.1 %collective-permute-start.5 = (f32[8,512]{1,0:T(8,128)S(1)}, f32[8,512]{1,0:T(8,128)S(1)}, u32[]{:S(2)}, u32[]{:S(2)}) collective-permute-start(f32[8,512]{1,0:T(8,128)S(1)} %get-tuple-element.37.refs_0_.own), channel_id=1, source_target_pairs={{0,6},{1,7},{2,4},{3,5},{4,2},{5,3},{6,0},{7,1},{8,14},{9,15},{10,... | collective-permute-start | bytes 49160 | tf_op jit(solution)/shard_map/ppermute | solution.py:387
  17.2 3.7 %collective-permute-start.6 = (f32[8,512]{1,0:T(8,128)S(1)}, f32[8,512]{1,0:T(8,128)S(1)}, u32[]{:S(2)}, u32[]{:S(2)}) collective-permute-start(f32[8,512]{1,0:T(8,128)S(1)} %sum_groups.2.refs_0_.own), channel_id=1, source_target_pairs={{0,5},{1,4},{2,7},{3,6},{4,1},{5,0},{6,3},{7,2},{8,13},{9,12},{10,... | collective-permute-start | bytes 49160 | tf_op jit(solution)/shard_map/ppermute | solution.py:387
  20.9 1.2 %collective-permute-start.7 = (f32[8,512]{1,0:T(8,128)S(1)}, f32[8,512]{1,0:T(8,128)S(1)}, u32[]{:S(2)}, u32[]{:S(2)}) collective-permute-start(f32[8,512]{1,0:T(8,128)S(1)} %sum_groups.3.own), channel_id=1, source_target_pairs={{0,4},{1,5},{2,6},{3,7},{4,0},{5,1},{6,2},{7,3},{8,12},{9,13},{10,... | collective-permute-start | bytes 49160 | tf_op jit(solution)/shard_map/ppermute | solution.py:387

commit v14 on v13

--- a/solution.py
+++ b/solution.py
@@ -340,9 +340,9 @@
     refs[-1][...] = own[...] + other[...]
 
 
-def assemble_kernel(scale, own, other, out_ref):
+def assemble_kernel(scale, own, same, across, beside, _, out_ref):
     half = own.shape[0]
-    low, high = in_order(owns_high(), own[...], other[...])
+    low, high = in_order(owns_high(), own[...] + same[...], beside[...] + across[...])
     out_ref[0:half] = low * scale
     out_ref[half:] = high * scale
 
@@ -381,10 +381,11 @@
     small = dict(compiler_params=PARAMS, cost_estimate=cost(elements, modes * channels, modes * channels * 32))
 
     def swap(x, ctx_mask, ch_mask=0):
-        if ctx_mask != 1:
-            ctx_mask |= (ctx_mask.bit_count() + ch_mask.bit_count()) % 2
         mask = ctx_mask * groups + ch_mask
         return lax.ppermute(x, ("ctx", "ch"), [(i, i ^ mask) for i in range(n * groups)])
+
+    def swap_halves(x, ctx_mask, ch_mask=0):
+        return swap(x, ctx_mask | (ctx_mask.bit_count() + ch_mask.bit_count()) % 2, ch_mask)
 
     def near_part(part, after):
         first, last = ranges[part]
@@ -436,7 +437,7 @@
         count = min(4, chips // size)
         last = size * count == chips
         masks = [2, 1, 3] if count == 4 else [1]
-        others = [swap(joined, 2 * size * m) for m in masks]
+        others = [swap_halves(joined, 2 * size * m) for m in masks]
         if last:
             near = near + near_part(1, joined)
         rows = [half, 2 * half, 2 * half] if last else [3 * half, 2 * half]
@@ -470,14 +471,11 @@
     grad = joined
     written = []
     stride = groups // 2
-    while stride:
-        other = swap(grad, 0, stride)
+    while stride > 1:
+        other = swap_halves(grad, 0, stride)
         pinned = []
-        if stride == groups // 2:
+        if not written:
             *written, finished = finish_part(0, grad, written)
-            pinned = [finished]
-        if stride == 1:
-            *written, finished = finish_part(1, grad, written)
             pinned = [finished]
         grad = pl.pallas_call(
             sum_kernel,
@@ -487,12 +485,18 @@
             **small,
         )(grad, other, *pinned)
         stride //= 2
+
+    if not written:
+        *written, finished = finish_part(0, grad, written)
+    same, across, beside = swap_halves(grad, 0, 1), swap(grad, 0, 1), swap(grad, 1)
+    *written, finished = finish_part(1, grad, written)
     residue_grad = pl.pallas_call(
         functools.partial(assemble_kernel, 1.0 / (tokens * n)),
         out_shape=shaped(modes, channels),
+        in_specs=[WHOLE] * 4 + [UNREAD],
         name="assemble_gradient",
         **small,
-    )(grad, swap(grad, 1))
+    )(grad, same, across, beside, finished)
     return *written, residue_grad
 
 

time: 22.9 us -> 23.1 us (level)
    ppermute x8 -> x9, starting transfers between devices: 9.26 us -> 9.41 us  [swap(): lax.ppermute(x, ('ctx', 'ch'), [(i, i ^ mask) for i in range(n * groups)])]
    ppermute x8 -> x9, waiting for transfers between devices: 2.7 us -> 2.76 us  [swap(): lax.ppermute(x, ('ctx', 'ch'), [(i, i ^ mask) for i in range(n * groups)])]
  transfers between devices with their start and end apart: 8 -> 9, of which waited for: 4 -> 4; matrix products, arithmetic and copies ran while one was open for 0% -> 0% of each run, Pallas kernels for 28% -> 28%
where the time goes in v14:
time: 23.1 us; the launch traced here: 23 us
  Pallas kernels  10.1 us (44%)
  starting transfers between devices  9.41 us (41%)
  waiting for transfers between devices  2.76 us (12%)
  between operations  0.7 us (3%)
    ppermute x9, starting transfers between devices, swap(): lax.ppermute(x, ('ctx', 'ch'), [(i, i ^ mask) for i in range(n * groups)])  9.41 us
    pallas_call x2, Pallas kernels, finish_part(): pl.pallas_call(functools.partial(finish_kernel, ranges[part]), out_shape=...  3.36 us
    pallas_call x2, Pallas kernels, near_part(): pl.pallas_call(functools.partial(local_kernel, ranges[part]), out_shape=[...  3.13 us
    pallas_call x1, Pallas kernels, body(): pl.pallas_call(gather_kernel, out_shape=[values, values] + [shaped(modes,...  2.91 us
    ppermute x9, waiting for transfers between devices, swap(): lax.ppermute(x, ('ctx', 'ch'), [(i, i ^ mask) for i in range(n * groups)])  2.76 us
    pallas_call x1, Pallas kernels, body(): pl.pallas_call(functools.partial(assemble_kernel, 1.0 / (tokens * n)), ou...  0.62 us
  transfers between devices with their start and end apart: 9, of which 4 were waited for; matrix products, arithmetic and copies ran while one was open for 0% of the time, Pallas kernels for 28%

profile of v14, /device:TPU:0, one launch (start us, length us, event | category | flops | bytes accessed | tf_op | source)
XLA Modules:
  0.0 23.0 jit_solution(17044075576982045035)
XLA Ops:
  0.6 2.9 %block_states.1 = (f32[256,512]{1,0:T(8,128)S(1)}, f32[256,512]{1,0:T(8,128)S(1)}, f32[16,512]{1,0:T(8,128)S(1)}, f32[16,512]{1,0:T(8,128)S(1)}, f32[48,512]{1,0:T(8,128)S(1)}, /*index=5*/f32[24,512]{1,0:T(8,128)S(1)}) custom-call(bf16[256,512]{1,0:T(8,128)(2,1)} %refs_0_.1, bf16[256,512]{1,0:T(8,128)(2,1)} %refs_1_.1, f32[16,512]{1,0:T(8,128)} %refs_2_.1, ...), custom_call_target="tpu_custom_call" | custom-call | flops 10485760 | bytes 786432 | tf_op jit(solution)/shard_map/block_states/pallas_call | solution.py:406
  3.6 0.5 %collective-permute-start = (f32[24,512]{1,0:T(8,128)S(1)}, f32[24,512]{1,0:T(8,128)S(1)}, u32[]{:S(2)}, u32[]{:S(2)}) collective-permute-start(f32[24,512]{1,0:T(8,128)S(1)} %get-tuple-element.27), channel_id=1, source_target_pairs={{0,4},{1,5},{2,6},{3,7},{4,0},{5,1},{6,2},{7,3},{8,12},{9,13},{10,... | collective-permute-start | bytes 147464 | tf_op jit(solution)/shard_map/ppermute | solution.py:385
  4.1 0.8 %local_convolutions.2 = (f32[1,32,8,128]{3,2,1,0:T(8,128)S(1)}, f32[1,32,8,128]{3,2,1,0:T(8,128)S(1)}) custom-call(f32[256,512]{1,0:T(8,128)S(1)} %get-tuple-element.28.xf, f32[256,512]{1,0:T(8,128)S(1)} %get-tuple-element.29.gf, f32[16,512]{1,0:T(8,128)S(1)} %get-tuple-element.24.residue_ref, f32[16,512]{1,0:T(8,128)S(1)} %get-tuple-element.25.decay_ref.refs_5_, ...), custom_call_target="tpu_custom_call" | custom-call | flops 209715200 | bytes 524288 | tf_op jit(solution)/shard_map/local_convolutions/pallas_call | solution.py:393
  4.8 0.1 collective-permute-done.other
  5.0 3.9 %collective-permute-start.3 = (f32[24,512]{1,0:T(8,128)S(1)}, f32[24,512]{1,0:T(8,128)S(1)}, u32[]{:S(2)}, u32[]{:S(2)}) collective-permute-start(f32[24,512]{1,0:T(8,128)S(1)} %get-tuple-element.31._.refs_0_), channel_id=1, source_target_pairs={{0,24},{1,25},{2,26},{3,27},{4,28},{5,29},{6,30},{7,31},{8,16},{9,... | collective-permute-start | bytes 147464 | tf_op jit(solution)/shard_map/ppermute | solution.py:385
  8.8 0.0 collective-permute-start.2
  8.9 0.3 %collective-permute-start.1 = (f32[24,512]{1,0:T(8,128)S(1)}, f32[24,512]{1,0:T(8,128)S(1)}, u32[]{:S(2)}, u32[]{:S(2)}) collective-permute-start(f32[24,512]{1,0:T(8,128)S(1)} %get-tuple-element.31._.refs_0_), channel_id=1, source_target_pairs={{0,20},{1,21},{2,22},{3,23},{4,16},{5,17},{6,18},{7,19},{8,28},{9,... | collective-permute-start | bytes 147464 | tf_op jit(solution)/shard_map/ppermute | solution.py:385
  9.2 2.3 %local_convolutions.3 = (f32[3,32,8,128]{3,2,1,0:T(8,128)S(1)}, f32[3,32,8,128]{3,2,1,0:T(8,128)S(1)}) custom-call(f32[256,512]{1,0:T(8,128)S(1)} %get-tuple-element.28.xf, f32[256,512]{1,0:T(8,128)S(1)} %get-tuple-element.29.gf, f32[16,512]{1,0:T(8,128)S(1)} %get-tuple-element.24.residue_ref, f32[16,512]{1,0:T(8,128)S(1)} %get-tuple-element.25.decay_ref.refs_5_, ...), custom_call_target="tpu_custom_call" | custom-call | flops 629145600 | bytes 1572864 | tf_op jit(solution)/shard_map/local_convolutions/pallas_call | solution.py:393
  11.6 0.0 collective-permute-done.3.refs_3_
  11.6 1.3 %collective-permute-done.2.refs_2_ = f32[24,512]{1,0:T(8,128)S(1)} collective-permute-done((f32[24,512]{1,0:T(8,128)S(1)}, f32[24,512]{1,0:T(8,128)S(1)}, u32[]{:S(2)}, u32[]{:S(2)}) %collective-permute-start.2) | collective-permute-done | bytes 49184 | tf_op jit(solution)/shard_map/ppermute | solution.py:385
  12.8 0.0 collective-permute-done.1.refs_1_
  12.8 0.1 join_chips.1
  12.9 0.2 %collective-permute-start.4 = (f32[16,512]{1,0:T(8,128)S(1)}, f32[16,512]{1,0:T(8,128)S(1)}, u32[]{:S(2)}, u32[]{:S(2)}) collective-permute-start(f32[16,512]{1,0:T(8,128)S(1)} %get-tuple-element.35), channel_id=1, source_target_pairs={{0,4},{1,5},{2,6},{3,7},{4,0},{5,1},{6,2},{7,3},{8,12},{9,13},{10,... | collective-permute-start | bytes 98312 | tf_op jit(solution)/shard_map/ppermute | solution.py:385
  13.1 2.5 %collective-permute-start.5 = (f32[8,512]{1,0:T(8,128)S(1)}, f32[8,512]{1,0:T(8,128)S(1)}, u32[]{:S(2)}, u32[]{:S(2)}) collective-permute-start(f32[8,512]{1,0:T(8,128)S(1)} %get-tuple-element.37.refs_0_.own), channel_id=1, source_target_pairs={{0,6},{1,7},{2,4},{3,5},{4,2},{5,3},{6,0},{7,1},{8,14},{9,15},{10,... | collective-permute-start | bytes 49160 | tf_op jit(solution)/shard_map/ppermute | solution.py:385
  15.7 0.0 collective-permute-done.4.other
  15.7 1.2 %add_arrivals.2 = (bf16[256,512]{1,0:T(8,128)(2,1)}, bf16[256,512]{1,0:T(8,128)(2,1)}, f32[8,128]{1,0:T(8,128)S(1)}) custom-call(f32[16,512]{1,0:T(8,128)S(1)} %get-tuple-element.24.residue_ref, f32[16,512]{1,0:T(8,128)S(1)} %get-tuple-element.25.decay_ref.refs_5_, f32[16,512]{1,0:T(8,128)S(1)} %get-tuple-element.34.own, ...), custom_call_target="tpu_custom_call" | custom-call | flops 629145600 | bytes 786432 | tf_op jit(solution)/shard_map/add_arrivals/pallas_call | solution.py:455
  16.9 0.3 %collective-permute-done.5.other = f32[8,512]{1,0:T(8,128)S(1)} collective-permute-done((f32[8,512]{1,0:T(8,128)S(1)}, f32[8,512]{1,0:T(8,128)S(1)}, u32[]{:S(2)}, u32[]{:S(2)}) %collective-permute-start.5) | collective-permute-done | bytes 16416 | tf_op jit(solution)/shard_map/ppermute | solution.py:385
  17.2 0.3 %collective-permute-start.8 = (f32[8,512]{1,0:T(8,128)S(1)}, f32[8,512]{1,0:T(8,128)S(1)}, u32[]{:S(2)}, u32[]{:S(2)}) collective-permute-start(f32[8,512]{1,0:T(8,128)S(1)} %sum_groups.1.refs_0_.own), channel_id=1, source_target_pairs={{0,4},{1,5},{2,6},{3,7},{4,0},{5,1},{6,2},{7,3},{8,12},{9,13},{10,... | collective-permute-start | bytes 49160 | tf_op jit(solution)/shard_map/ppermute | solution.py:385
  17.5 1.6 %collective-permute-start.7 = (f32[8,512]{1,0:T(8,128)S(1)}, f32[8,512]{1,0:T(8,128)S(1)}, u32[]{:S(2)}, u32[]{:S(2)}) collective-permute-start(f32[8,512]{1,0:T(8,128)S(1)} %sum_groups.1.refs_0_.own), channel_id=1, source_target_pairs={{0,1},{1,0},{2,3},{3,2},{4,5},{5,4},{6,7},{7,6},{8,9},{9,8},{10,11... | collective-permute-start | bytes 49160 | tf_op jit(solution)/shard_map/ppermute | solution.py:385
  19.1 0.0 collective-permute-start.6
  19.1 2.2 %add_arrivals.3 = (bf16[256,512]{1,0:T(8,128)(2,1)}, bf16[256,512]{1,0:T(8,128)(2,1)}, f32[8,128]{1,0:T(8,128)S(1)}) custom-call(f32[16,512]{1,0:T(8,128)S(1)} %get-tuple-element.24.residue_ref, f32[16,512]{1,0:T(8,128)S(1)} %get-tuple-element.25.decay_ref.refs_5_, ...), custom_call_target="tpu_custom_call", output_to_operand_aliasing={{0}: (7, {}), {1}: (8, {})} | custom-call | flops 629145600 | bytes 786432 | tf_op jit(solution)/shard_map/add_arrivals/pallas_call | solution.py:455
  21.3 0.0 collective-permute-done.8.beside
  21.3 0.0 collective-permute-done.7.across
  21.3 1.1 %collective-permute-done.6.same = f32[8,512]{1,0:T(8,128)S(1)} collective-permute-done((f32[8,512]{1,0:T(8,128)S(1)}, f32[8,512]{1,0:T(8,128)S(1)}, u32[]{:S(2)}, u32[]{:S(2)}) %collective-permute-start.6) | collective-permute-done | bytes 16416 | tf_op jit(solution)/shard_map/ppermute | solution.py:385
  22.4 0.6 %assemble_gradient.1 = f32[16,512]{1,0:T(8,128)} custom-call(f32[8,512]{1,0:T(8,128)S(1)} %sum_groups.1.refs_0_.own, f32[8,512]{1,0:T(8,128)S(1)} %collective-permute-done.6.same, f32[8,512]{1,0:T(8,128)S(1)} %collective-permute-done.7.across, f32[8,512]{1,0:T(8,128)S(1)} %collective-permute-done.8.beside, f32[8,128]{1,0:T(8,128)S(1)} %get-tuple-element.44._), custom_call_target="tpu_custom_call" | custom-call | flops 131072 | bytes 262144 | tf_op jit(solution)/shard_map/assemble_gradient/pallas_call | solution.py:493
  (2 shorter events, 0.0 us)
Async XLA Ops:
  3.6 1.4 %collective-permute-start = (f32[24,512]{1,0:T(8,128)S(1)}, f32[24,512]{1,0:T(8,128)S(1)}, u32[]{:S(2)}, u32[]{:S(2)}) collective-permute-start(f32[24,512]{1,0:T(8,128)S(1)} %get-tuple-element.27), channel_id=1, source_target_pairs={{0,4},{1,5},{2,6},{3,7},{4,0},{5,1},{6,2},{7,3},{8,12},{9,13},{10,... | collective-permute-start | bytes 147464 | tf_op jit(solution)/shard_map/ppermute | solution.py:385
  5.0 6.6 %collective-permute-start.3 = (f32[24,512]{1,0:T(8,128)S(1)}, f32[24,512]{1,0:T(8,128)S(1)}, u32[]{:S(2)}, u32[]{:S(2)}) collective-permute-start(f32[24,512]{1,0:T(8,128)S(1)} %get-tuple-element.31._.refs_0_), channel_id=1, source_target_pairs={{0,24},{1,25},{2,26},{3,27},{4,28},{5,29},{6,30},{7,31},{8,16},{9,... | collective-permute-start | bytes 147464 | tf_op jit(solution)/shard_map/ppermute | solution.py:385
  8.8 4.0 %collective-permute-start.2 = (f32[24,512]{1,0:T(8,128)S(1)}, f32[24,512]{1,0:T(8,128)S(1)}, u32[]{:S(2)}, u32[]{:S(2)}) collective-permute-start(f32[24,512]{1,0:T(8,128)S(1)} %get-tuple-element.31._.refs_0_), channel_id=1, source_target_pairs={{0,12},{1,13},{2,14},{3,15},{4,8},{5,9},{6,10},{7,11},{8,4},{9,5},... | collective-permute-start | bytes 147464 | tf_op jit(solution)/shard_map/ppermute | solution.py:385
  8.9 4.0 %collective-permute-start.1 = (f32[24,512]{1,0:T(8,128)S(1)}, f32[24,512]{1,0:T(8,128)S(1)}, u32[]{:S(2)}, u32[]{:S(2)}) collective-permute-start(f32[24,512]{1,0:T(8,128)S(1)} %get-tuple-element.31._.refs_0_), channel_id=1, source_target_pairs={{0,20},{1,21},{2,22},{3,23},{4,16},{5,17},{6,18},{7,19},{8,28},{9,... | collective-permute-start | bytes 147464 | tf_op jit(solution)/shard_map/ppermute | solution.py:385
  12.9 2.8 %collective-permute-start.4 = (f32[16,512]{1,0:T(8,128)S(1)}, f32[16,512]{1,0:T(8,128)S(1)}, u32[]{:S(2)}, u32[]{:S(2)}) collective-permute-start(f32[16,512]{1,0:T(8,128)S(1)} %get-tuple-element.35), channel_id=1, source_target_pairs={{0,4},{1,5},{2,6},{3,7},{4,0},{5,1},{6,2},{7,3},{8,12},{9,13},{10,... | collective-permute-start | bytes 98312 | tf_op jit(solution)/shard_map/ppermute | solution.py:385
  13.1 4.1 %collective-permute-start.5 = (f32[8,512]{1,0:T(8,128)S(1)}, f32[8,512]{1,0:T(8,128)S(1)}, u32[]{:S(2)}, u32[]{:S(2)}) collective-permute-start(f32[8,512]{1,0:T(8,128)S(1)} %get-tuple-element.37.refs_0_.own), channel_id=1, source_target_pairs={{0,6},{1,7},{2,4},{3,5},{4,2},{5,3},{6,0},{7,1},{8,14},{9,15},{10,... | collective-permute-start | bytes 49160 | tf_op jit(solution)/shard_map/ppermute | solution.py:385
  17.2 4.1 %collective-permute-start.8 = (f32[8,512]{1,0:T(8,128)S(1)}, f32[8,512]{1,0:T(8,128)S(1)}, u32[]{:S(2)}, u32[]{:S(2)}) collective-permute-start(f32[8,512]{1,0:T(8,128)S(1)} %sum_groups.1.refs_0_.own), channel_id=1, source_target_pairs={{0,4},{1,5},{2,6},{3,7},{4,0},{5,1},{6,2},{7,3},{8,12},{9,13},{10,... | collective-permute-start | bytes 49160 | tf_op jit(solution)/shard_map/ppermute | solution.py:385
  17.5 3.8 %collective-permute-start.7 = (f32[8,512]{1,0:T(8,128)S(1)}, f32[8,512]{1,0:T(8,128)S(1)}, u32[]{:S(2)}, u32[]{:S(2)}) collective-permute-start(f32[8,512]{1,0:T(8,128)S(1)} %sum_groups.1.refs_0_.own), channel_id=1, source_target_pairs={{0,1},{1,0},{2,3},{3,2},{4,5},{5,4},{6,7},{7,6},{8,9},{9,8},{10,11... | collective-permute-start | bytes 49160 | tf_op jit(solution)/shard_map/ppermute | solution.py:385
  19.1 3.3 %collective-permute-start.6 = (f32[8,512]{1,0:T(8,128)S(1)}, f32[8,512]{1,0:T(8,128)S(1)}, u32[]{:S(2)}, u32[]{:S(2)}) collective-permute-start(f32[8,512]{1,0:T(8,128)S(1)} %sum_groups.1.refs_0_.own), channel_id=1, source_target_pairs={{0,5},{1,4},{2,7},{3,6},{4,1},{5,0},{6,3},{7,2},{8,13},{9,12},{10,... | collective-permute-start | bytes 49160 | tf_op jit(solution)/shard_map/ppermute | solution.py:385

commit v15 on v13

--- a/solution.py
+++ b/solution.py
@@ -78,10 +78,11 @@
     span = chunks * SUB
     closing, opening, grad = (segment.at[pl.ds(i * modes, modes)] for i in range(3))
     order = token_order(tokens)
-    for copy in copies:
-        copy.wait()
+    copies[0].wait()
     xf[...] = jnp.dot(order, x_ref[...], preferred_element_type=F32)
+    copies[1].wait()
     gf[...] = jnp.dot(order, g_ref[...], preferred_element_type=F32)
+    copies[3].wait()
 
     def tile_step(tile):
         lanes = pl.ds(tile * LANES, LANES)
@@ -123,6 +124,7 @@
 
     for tile in range(channels // LANES):
         tile_step(tile)
+    copies[2].wait()
 
     own_high = owns_high()
     half = modes // 2
@@ -281,11 +283,12 @@
     message[half:] = jnp.where(second, out[0], out[1])
 
 
-def finish_kernel(tiles, residue_ref, decay_ref, own, other, near_out, near_back, *refs):
-    out_hbm, back_hbm, finished, out_ref, back_ref, result, pw, arrive, leave, sems = refs[-10:]
+def finish_kernel(tiles, ranges, residue_ref, decay_ref, own, other, *refs):
+    nears = refs[:2 * len(ranges)]
+    out_hbm, back_hbm, finished, out_ref, back_ref, results, pws, arrive, leave, sems = refs[-10:]
     modes, channels = decay_ref.shape
     half = modes // 2
-    chunks = near_out.shape[1] // SUB
+    chunks = nears[0].shape[1] // SUB
     span = chunks * SUB
     own_high = owns_high()
     first = residue_ref[...] * jnp.exp(-decay_ref[...])
@@ -295,12 +298,15 @@
         target[half:] = high * first[half:]
 
     def copy_out(tile, which):
-        lanes = pl.ds(pl.multiple_of(tile * LANES, LANES), LANES)
+        lanes = pl.ds(tile * LANES, LANES)
         source, target = ((out_ref, out_hbm), (back_ref, back_hbm))[which]
         return pltpu.make_async_copy(source.at[:, lanes], target.at[:, lanes], sems.at[which, tile])
 
-    def tile_step(tile, _):
-        lanes = pl.ds(pl.multiple_of(tile * LANES, LANES), LANES)
+    def tile_step(tile):
+        part, = [i for i, (first, last) in enumerate(ranges) if first <= tile < last]
+        near_out, near_back = (near.at[tile - ranges[part][0]] for near in nears[2 * part:2 * part + 2])
+        pw = pws.at[tile % 2]
+        lanes = pl.ds(tile * LANES, LANES)
         decay = decay_ref[:, lanes]
         powers(decay, pw)
         pw[2] = decay * (-1.0 * span)
@@ -308,9 +314,10 @@
         pw[4] = leave[:, lanes]
         level = lax.broadcasted_iota(jnp.int32, (SUB, LANES), 0).astype(F32)
         for near, target, forward in ((near_out, out_ref, True), (near_back, back_ref, False)):
+            result = results.at[2 * (tile % 2) + forward]
             order = range(SUB) if forward else range(SUB - 1, -1, -1)
             spans = level if forward else SUB - 1.0 - level
-            totals = [[near[tile - tiles[0], p * SUB + r] for r in range(SUB)] for p in range(chunks)]
+            totals = [[near[p * SUB + r] for r in range(SUB)] for p in range(chunks)]
             for m in range(modes):
                 a, a8, rate = (row(pw, i, pl.ds(m, 1)) for i in range(3))
                 state = row(pw, 3 if forward else 4, pl.ds(m, 1)) * jnp.exp(rate * spans)
@@ -327,9 +334,9 @@
                     result[pl.ds(p * SUB + r, SUB, stride=span), :] = totals[p][r]
             target[:, lanes] = result[...].astype(target.dtype)
             copy_out(tile, 0 if forward else 1).start()
-        return 0
-
-    lax.fori_loop(*tiles, tile_step, 0)
+
+    for tile in range(*tiles):
+        tile_step(tile)
     for tile in range(*tiles):
         for which in range(2):
             copy_out(tile, which).wait()
@@ -452,19 +459,19 @@
 
     def finish_part(part, after, written):
         return pl.pallas_call(
-            functools.partial(finish_kernel, ranges[part]),
+            functools.partial(finish_kernel, (part * tiles // 2, (part + 1) * tiles // 2), ranges),
             out_shape=[jax.ShapeDtypeStruct((tokens, channels), jnp.bfloat16)] * 2 + [shaped(SUB, LANES)],
-            in_specs=[WHOLE] * 6 + [UNREAD] + [HBM] * len(written),
+            in_specs=[WHOLE] * (4 + len(near)) + [UNREAD] + [HBM] * len(written),
             out_specs=[HBM] * 2 + [WHOLE],
-            input_output_aliases={7 + i: i for i in range(len(written))},
+            input_output_aliases={5 + len(near) + i: i for i in range(len(written))},
             scratch_shapes=[pltpu.VMEM((tokens, channels), jnp.bfloat16)] * 2
-            + [vmem(tokens, LANES), vmem(5, modes, LANES)]
+            + [vmem(4, tokens, LANES), vmem(2, 5, modes, LANES)]
             + [vmem(modes, channels)] * 2
             + [pltpu.SemaphoreType.DMA((2, tiles))],
             compiler_params=PARAMS,
             cost_estimate=cost(elements * modes * 300, 0, elements * 6),
             name="add_arrivals",
-        )(residue, decay, carried, received, *near[2 * part:2 * part + 2], after, *written)
+        )(residue, decay, carried, received, *near, after, *written)
 
     received = swap(message[0], 1)
     grad = joined

time: 22.9 us -> 22.6 us (0.987)
  waiting for transfers between devices: 2.7 us -> 2.39 us
    ppermute x8, waiting for transfers between devices: 2.7 us -> 2.39 us  [swap(): lax.ppermute(x, ('ctx', 'ch'), [(i, i ^ mask) for i in range(n * groups)])]
  transfers between devices with their start and end apart: 8 -> 8, of which waited for: 4 -> 4; matrix products, arithmetic and copies ran while one was open for 0% -> 0% of each run, Pallas kernels for 28% -> 29%
where the time goes in v15:
time: 22.6 us; the launch traced here: 22.5 us
  Pallas kernels  10.1 us (45%)
  starting transfers between devices  9.22 us (41%)
  waiting for transfers between devices  2.39 us (11%)
  between operations  0.7 us (3%)
    ppermute x8, starting transfers between devices, swap(): lax.ppermute(x, ('ctx', 'ch'), [(i, i ^ mask) for i in range(n * groups)])  9.22 us
    pallas_call x2, Pallas kernels, finish_part(): pl.pallas_call(functools.partial(finish_kernel, (part * tiles // 2, (part...  3.34 us
    pallas_call x2, Pallas kernels, near_part(): pl.pallas_call(functools.partial(local_kernel, ranges[part]), out_shape=[...  3.13 us
    pallas_call x1, Pallas kernels, body(): pl.pallas_call(gather_kernel, out_shape=[values, values] + [shaped(modes,...  2.97 us
    ppermute x8, waiting for transfers between devices, swap(): lax.ppermute(x, ('ctx', 'ch'), [(i, i ^ mask) for i in range(n * groups)])  2.39 us
    pallas_call x1, Pallas kernels, body(): pl.pallas_call(functools.partial(assemble_kernel, 1.0 / (tokens * n)), ou...  0.62 us
  transfers between devices with their start and end apart: 8, of which 4 were waited for; matrix products, arithmetic and copies ran while one was open for 0% of the time, Pallas kernels for 29%

profile of v15, /device:TPU:0, one launch (start us, length us, event | category | flops | bytes accessed | tf_op | source)
XLA Modules:
  0.0 22.5 jit_solution(5518521079840410074)
XLA Ops:
  0.6 3.0 %block_states.1 = (f32[256,512]{1,0:T(8,128)S(1)}, f32[256,512]{1,0:T(8,128)S(1)}, f32[16,512]{1,0:T(8,128)S(1)}, f32[16,512]{1,0:T(8,128)S(1)}, f32[48,512]{1,0:T(8,128)S(1)}, /*index=5*/f32[24,512]{1,0:T(8,128)S(1)}) custom-call(bf16[256,512]{1,0:T(8,128)(2,1)} %refs_0_.1, bf16[256,512]{1,0:T(8,128)(2,1)} %refs_1_.1, f32[16,512]{1,0:T(8,128)} %refs_2_.1, ...), custom_call_target="tpu_custom_call" | custom-call | flops 10485760 | bytes 786432 | tf_op jit(solution)/shard_map/block_states/pallas_call | solution.py:412
  3.6 0.5 %collective-permute-start = (f32[24,512]{1,0:T(8,128)S(1)}, f32[24,512]{1,0:T(8,128)S(1)}, u32[]{:S(2)}, u32[]{:S(2)}) collective-permute-start(f32[24,512]{1,0:T(8,128)S(1)} %get-tuple-element.27), channel_id=1, source_target_pairs={{0,4},{1,5},{2,6},{3,7},{4,0},{5,1},{6,2},{7,3},{8,12},{9,13},{10,... | collective-permute-start | bytes 147464 | tf_op jit(solution)/shard_map/ppermute | solution.py:394
  4.1 0.8 %local_convolutions.2 = (f32[1,32,8,128]{3,2,1,0:T(8,128)S(1)}, f32[1,32,8,128]{3,2,1,0:T(8,128)S(1)}) custom-call(f32[256,512]{1,0:T(8,128)S(1)} %get-tuple-element.28.xf, f32[256,512]{1,0:T(8,128)S(1)} %get-tuple-element.29.gf, f32[16,512]{1,0:T(8,128)S(1)} %get-tuple-element.24.residue_ref, f32[16,512]{1,0:T(8,128)S(1)} %get-tuple-element.25.decay_ref.refs_5_, ...), custom_call_target="tpu_custom_call" | custom-call | flops 209715200 | bytes 524288 | tf_op jit(solution)/shard_map/local_convolutions/pallas_call | solution.py:399
  4.9 0.1 collective-permute-done.other
  5.0 3.9 %collective-permute-start.3 = (f32[24,512]{1,0:T(8,128)S(1)}, f32[24,512]{1,0:T(8,128)S(1)}, u32[]{:S(2)}, u32[]{:S(2)}) collective-permute-start(f32[24,512]{1,0:T(8,128)S(1)} %get-tuple-element.31._.refs_0_), channel_id=1, source_target_pairs={{0,24},{1,25},{2,26},{3,27},{4,28},{5,29},{6,30},{7,31},{8,16},{9,... | collective-permute-start | bytes 147464 | tf_op jit(solution)/shard_map/ppermute | solution.py:394
  8.9 0.0 collective-permute-start.2
  8.9 0.4 %collective-permute-start.1 = (f32[24,512]{1,0:T(8,128)S(1)}, f32[24,512]{1,0:T(8,128)S(1)}, u32[]{:S(2)}, u32[]{:S(2)}) collective-permute-start(f32[24,512]{1,0:T(8,128)S(1)} %get-tuple-element.31._.refs_0_), channel_id=1, source_target_pairs={{0,20},{1,21},{2,22},{3,23},{4,16},{5,17},{6,18},{7,19},{8,28},{9,... | collective-permute-start | bytes 147464 | tf_op jit(solution)/shard_map/ppermute | solution.py:394
  9.3 2.3 %local_convolutions.3 = (f32[3,32,8,128]{3,2,1,0:T(8,128)S(1)}, f32[3,32,8,128]{3,2,1,0:T(8,128)S(1)}) custom-call(f32[256,512]{1,0:T(8,128)S(1)} %get-tuple-element.28.xf, f32[256,512]{1,0:T(8,128)S(1)} %get-tuple-element.29.gf, f32[16,512]{1,0:T(8,128)S(1)} %get-tuple-element.24.residue_ref, f32[16,512]{1,0:T(8,128)S(1)} %get-tuple-element.25.decay_ref.refs_5_, ...), custom_call_target="tpu_custom_call" | custom-call | flops 629145600 | bytes 1572864 | tf_op jit(solution)/shard_map/local_convolutions/pallas_call | solution.py:399
  11.6 0.0 collective-permute-done.3.refs_3_
  11.6 1.3 %collective-permute-done.2.refs_2_ = f32[24,512]{1,0:T(8,128)S(1)} collective-permute-done((f32[24,512]{1,0:T(8,128)S(1)}, f32[24,512]{1,0:T(8,128)S(1)}, u32[]{:S(2)}, u32[]{:S(2)}) %collective-permute-start.2) | collective-permute-done | bytes 49184 | tf_op jit(solution)/shard_map/ppermute | solution.py:394
  12.9 0.0 collective-permute-done.1.refs_1_
  12.9 0.1 join_chips.1
  13.0 0.2 %collective-permute-start.4 = (f32[16,512]{1,0:T(8,128)S(1)}, f32[16,512]{1,0:T(8,128)S(1)}, u32[]{:S(2)}, u32[]{:S(2)}) collective-permute-start(f32[16,512]{1,0:T(8,128)S(1)} %get-tuple-element.35), channel_id=1, source_target_pairs={{0,4},{1,5},{2,6},{3,7},{4,0},{5,1},{6,2},{7,3},{8,12},{9,13},{10,... | collective-permute-start | bytes 98312 | tf_op jit(solution)/shard_map/ppermute | solution.py:394
  13.2 2.5 %collective-permute-start.5 = (f32[8,512]{1,0:T(8,128)S(1)}, f32[8,512]{1,0:T(8,128)S(1)}, u32[]{:S(2)}, u32[]{:S(2)}) collective-permute-start(f32[8,512]{1,0:T(8,128)S(1)} %get-tuple-element.38.refs_4_.own), channel_id=1, source_target_pairs={{0,6},{1,7},{2,4},{3,5},{4,2},{5,3},{6,0},{7,1},{8,14},{9,15},{10,... | collective-permute-start | bytes 49160 | tf_op jit(solution)/shard_map/ppermute | solution.py:394
  15.7 0.0 collective-permute-done.4.other
  15.7 1.7 %add_arrivals.2 = (bf16[256,512]{1,0:T(8,128)(2,1)}, bf16[256,512]{1,0:T(8,128)(2,1)}, f32[8,128]{1,0:T(8,128)S(1)}) custom-call(f32[16,512]{1,0:T(8,128)S(1)} %get-tuple-element.24.residue_ref, f32[16,512]{1,0:T(8,128)S(1)} %get-tuple-element.25.decay_ref.refs_5_, f32[16,512]{1,0:T(8,128)S(1)} %get-tuple-element.34.own, ...), custom_call_target="tpu_custom_call" | custom-call | flops 629145600 | bytes 786432 | tf_op jit(solution)/shard_map/add_arrivals/pallas_call | solution.py:461
  17.4 0.0 collective-permute-done.5.other
  17.4 1.4 %collective-permute-start.6 = (f32[8,512]{1,0:T(8,128)S(1)}, f32[8,512]{1,0:T(8,128)S(1)}, u32[]{:S(2)}, u32[]{:S(2)}) collective-permute-start(f32[8,512]{1,0:T(8,128)S(1)} %sum_groups.2.refs_4_.own), channel_id=1, source_target_pairs={{0,5},{1,4},{2,7},{3,6},{4,1},{5,0},{6,3},{7,2},{8,13},{9,12},{10,... | collective-permute-start | bytes 49160 | tf_op jit(solution)/shard_map/ppermute | solution.py:394
  18.9 1.7 %add_arrivals.3 = (bf16[256,512]{1,0:T(8,128)(2,1)}, bf16[256,512]{1,0:T(8,128)(2,1)}, f32[8,128]{1,0:T(8,128)S(1)}) custom-call(f32[16,512]{1,0:T(8,128)S(1)} %get-tuple-element.24.residue_ref, f32[16,512]{1,0:T(8,128)S(1)} %get-tuple-element.25.decay_ref.refs_5_, ...), custom_call_target="tpu_custom_call", output_to_operand_aliasing={{0}: (9, {}), {1}: (10, {})} | custom-call | flops 629145600 | bytes 786432 | tf_op jit(solution)/shard_map/add_arrivals/pallas_call | solution.py:461
  20.5 0.1 collective-permute-done.6.other
  20.7 0.3 %collective-permute-start.7 = (f32[8,512]{1,0:T(8,128)S(1)}, f32[8,512]{1,0:T(8,128)S(1)}, u32[]{:S(2)}, u32[]{:S(2)}) collective-permute-start(f32[8,512]{1,0:T(8,128)S(1)} %sum_groups.3.own), channel_id=1, source_target_pairs={{0,4},{1,5},{2,6},{3,7},{4,0},{5,1},{6,2},{7,3},{8,12},{9,13},{10,... | collective-permute-start | bytes 49160 | tf_op jit(solution)/shard_map/ppermute | solution.py:394
  20.9 0.9 %collective-permute-done.7.other = f32[8,512]{1,0:T(8,128)S(1)} collective-permute-done((f32[8,512]{1,0:T(8,128)S(1)}, f32[8,512]{1,0:T(8,128)S(1)}, u32[]{:S(2)}, u32[]{:S(2)}) %collective-permute-start.7) | collective-permute-done | bytes 16416 | tf_op jit(solution)/shard_map/ppermute | solution.py:394
  21.8 0.6 %assemble_gradient.1 = f32[16,512]{1,0:T(8,128)} custom-call(f32[8,512]{1,0:T(8,128)S(1)} %sum_groups.3.own, f32[8,512]{1,0:T(8,128)S(1)} %collective-permute-done.7.other), custom_call_target="tpu_custom_call" | custom-call | flops 131072 | bytes 262144 | tf_op jit(solution)/shard_map/assemble_gradient/pallas_call | solution.py:497
  (3 shorter events, 0.0 us)
Async XLA Ops:
  3.6 1.4 %collective-permute-start = (f32[24,512]{1,0:T(8,128)S(1)}, f32[24,512]{1,0:T(8,128)S(1)}, u32[]{:S(2)}, u32[]{:S(2)}) collective-permute-start(f32[24,512]{1,0:T(8,128)S(1)} %get-tuple-element.27), channel_id=1, source_target_pairs={{0,4},{1,5},{2,6},{3,7},{4,0},{5,1},{6,2},{7,3},{8,12},{9,13},{10,... | collective-permute-start | bytes 147464 | tf_op jit(solution)/shard_map/ppermute | solution.py:394
  5.0 6.6 %collective-permute-start.3 = (f32[24,512]{1,0:T(8,128)S(1)}, f32[24,512]{1,0:T(8,128)S(1)}, u32[]{:S(2)}, u32[]{:S(2)}) collective-permute-start(f32[24,512]{1,0:T(8,128)S(1)} %get-tuple-element.31._.refs_0_), channel_id=1, source_target_pairs={{0,24},{1,25},{2,26},{3,27},{4,28},{5,29},{6,30},{7,31},{8,16},{9,... | collective-permute-start | bytes 147464 | tf_op jit(solution)/shard_map/ppermute | solution.py:394
  8.9 4.0 %collective-permute-start.2 = (f32[24,512]{1,0:T(8,128)S(1)}, f32[24,512]{1,0:T(8,128)S(1)}, u32[]{:S(2)}, u32[]{:S(2)}) collective-permute-start(f32[24,512]{1,0:T(8,128)S(1)} %get-tuple-element.31._.refs_0_), channel_id=1, source_target_pairs={{0,12},{1,13},{2,14},{3,15},{4,8},{5,9},{6,10},{7,11},{8,4},{9,5},... | collective-permute-start | bytes 147464 | tf_op jit(solution)/shard_map/ppermute | solution.py:394
  8.9 4.0 %collective-permute-start.1 = (f32[24,512]{1,0:T(8,128)S(1)}, f32[24,512]{1,0:T(8,128)S(1)}, u32[]{:S(2)}, u32[]{:S(2)}) collective-permute-start(f32[24,512]{1,0:T(8,128)S(1)} %get-tuple-element.31._.refs_0_), channel_id=1, source_target_pairs={{0,20},{1,21},{2,22},{3,23},{4,16},{5,17},{6,18},{7,19},{8,28},{9,... | collective-permute-start | bytes 147464 | tf_op jit(solution)/shard_map/ppermute | solution.py:394
  13.0 2.8 %collective-permute-start.4 = (f32[16,512]{1,0:T(8,128)S(1)}, f32[16,512]{1,0:T(8,128)S(1)}, u32[]{:S(2)}, u32[]{:S(2)}) collective-permute-start(f32[16,512]{1,0:T(8,128)S(1)} %get-tuple-element.35), channel_id=1, source_target_pairs={{0,4},{1,5},{2,6},{3,7},{4,0},{5,1},{6,2},{7,3},{8,12},{9,13},{10,... | collective-permute-start | bytes 98312 | tf_op jit(solution)/shard_map/ppermute | solution.py:394
  13.2 4.2 %collective-permute-start.5 = (f32[8,512]{1,0:T(8,128)S(1)}, f32[8,512]{1,0:T(8,128)S(1)}, u32[]{:S(2)}, u32[]{:S(2)}) collective-permute-start(f32[8,512]{1,0:T(8,128)S(1)} %get-tuple-element.38.refs_4_.own), channel_id=1, source_target_pairs={{0,6},{1,7},{2,4},{3,5},{4,2},{5,3},{6,0},{7,1},{8,14},{9,15},{10,... | collective-permute-start | bytes 49160 | tf_op jit(solution)/shard_map/ppermute | solution.py:394
  17.4 3.2 %collective-permute-start.6 = (f32[8,512]{1,0:T(8,128)S(1)}, f32[8,512]{1,0:T(8,128)S(1)}, u32[]{:S(2)}, u32[]{:S(2)}) collective-permute-start(f32[8,512]{1,0:T(8,128)S(1)} %sum_groups.2.refs_4_.own), channel_id=1, source_target_pairs={{0,5},{1,4},{2,7},{3,6},{4,1},{5,0},{6,3},{7,2},{8,13},{9,12},{10,... | collective-permute-start | bytes 49160 | tf_op jit(solution)/shard_map/ppermute | solution.py:394
  20.7 1.2 %collective-permute-start.7 = (f32[8,512]{1,0:T(8,128)S(1)}, f32[8,512]{1,0:T(8,128)S(1)}, u32[]{:S(2)}, u32[]{:S(2)}) collective-permute-start(f32[8,512]{1,0:T(8,128)S(1)} %sum_groups.3.own), channel_id=1, source_target_pairs={{0,4},{1,5},{2,6},{3,7},{4,0},{5,1},{6,2},{7,3},{8,12},{9,13},{10,... | collective-permute-start | bytes 49160 | tf_op jit(solution)/shard_map/ppermute | solution.py:394

commit v16 on v15

--- a/solution.py
+++ b/solution.py
@@ -78,11 +78,10 @@
     span = chunks * SUB
     closing, opening, grad = (segment.at[pl.ds(i * modes, modes)] for i in range(3))
     order = token_order(tokens)
-    copies[0].wait()
+    for copy in copies:
+        copy.wait()
     xf[...] = jnp.dot(order, x_ref[...], preferred_element_type=F32)
-    copies[1].wait()
     gf[...] = jnp.dot(order, g_ref[...], preferred_element_type=F32)
-    copies[3].wait()
 
     def tile_step(tile):
         lanes = pl.ds(tile * LANES, LANES)
@@ -124,7 +123,6 @@
 
     for tile in range(channels // LANES):
         tile_step(tile)
-    copies[2].wait()
 
     own_high = owns_high()
     half = modes // 2
@@ -459,7 +457,7 @@
 
     def finish_part(part, after, written):
         return pl.pallas_call(
-            functools.partial(finish_kernel, (part * tiles // 2, (part + 1) * tiles // 2), ranges),
+            functools.partial(finish_kernel, ranges[part], ranges),
             out_shape=[jax.ShapeDtypeStruct((tokens, channels), jnp.bfloat16)] * 2 + [shaped(SUB, LANES)],
             in_specs=[WHOLE] * (4 + len(near)) + [UNREAD] + [HBM] * len(written),
             out_specs=[HBM] * 2 + [WHOLE],

time: 22.6 us -> 22.9 us (1.013)
  waiting for transfers between devices: 2.39 us -> 2.7 us
    ppermute x8, waiting for transfers between devices: 2.39 us -> 2.7 us  [swap(): lax.ppermute(x, ('ctx', 'ch'), [(i, i ^ mask) for i in range(n * groups)])]
  transfers between devices with their start and end apart: 8 -> 8, of which waited for: 4 -> 4; matrix products, arithmetic and copies ran while one was open for 0% -> 0% of each run, Pallas kernels for 29% -> 28%
where the time goes in v16:
time: 22.9 us; the launch traced here: 22.7 us
  Pallas kernels  10 us (44%)
  starting transfers between devices  9.26 us (40%)
  waiting for transfers between devices  2.7 us (12%)
  between operations  0.7 us (3%)
    ppermute x8, starting transfers between devices, swap(): lax.ppermute(x, ('ctx', 'ch'), [(i, i ^ mask) for i in range(n * groups)])  9.26 us
    pallas_call x2, Pallas kernels, finish_part(): pl.pallas_call(functools.partial(finish_kernel, ranges[part], ranges), ou...  3.29 us
    pallas_call x2, Pallas kernels, near_part(): pl.pallas_call(functools.partial(local_kernel, ranges[part]), out_shape=[...  3.13 us
    pallas_call x1, Pallas kernels, body(): pl.pallas_call(gather_kernel, out_shape=[values, values] + [shaped(modes,...  2.91 us
    ppermute x8, waiting for transfers between devices, swap(): lax.ppermute(x, ('ctx', 'ch'), [(i, i ^ mask) for i in range(n * groups)])  2.7 us
    pallas_call x1, Pallas kernels, body(): pl.pallas_call(functools.partial(assemble_kernel, 1.0 / (tokens * n)), ou...  0.62 us
  transfers between devices with their start and end apart: 8, of which 4 were waited for; matrix products, arithmetic and copies ran while one was open for 0% of the time, Pallas kernels for 28%

profile of v16, /device:TPU:0, one launch (start us, length us, event | category | flops | bytes accessed | tf_op | source)
XLA Modules:
  0.0 22.7 jit_solution(7686981660722507516)
XLA Ops:
  0.6 2.9 %block_states.1 = (f32[256,512]{1,0:T(8,128)S(1)}, f32[256,512]{1,0:T(8,128)S(1)}, f32[16,512]{1,0:T(8,128)S(1)}, f32[16,512]{1,0:T(8,128)S(1)}, f32[48,512]{1,0:T(8,128)S(1)}, /*index=5*/f32[24,512]{1,0:T(8,128)S(1)}) custom-call(bf16[256,512]{1,0:T(8,128)(2,1)} %refs_0_.1, bf16[256,512]{1,0:T(8,128)(2,1)} %refs_1_.1, f32[16,512]{1,0:T(8,128)} %refs_2_.1, ...), custom_call_target="tpu_custom_call" | custom-call | flops 10485760 | bytes 786432 | tf_op jit(solution)/shard_map/block_states/pallas_call | solution.py:410
  3.6 0.5 %collective-permute-start = (f32[24,512]{1,0:T(8,128)S(1)}, f32[24,512]{1,0:T(8,128)S(1)}, u32[]{:S(2)}, u32[]{:S(2)}) collective-permute-start(f32[24,512]{1,0:T(8,128)S(1)} %get-tuple-element.27), channel_id=1, source_target_pairs={{0,4},{1,5},{2,6},{3,7},{4,0},{5,1},{6,2},{7,3},{8,12},{9,13},{10,... | collective-permute-start | bytes 147464 | tf_op jit(solution)/shard_map/ppermute | solution.py:392
  4.1 0.8 %local_convolutions.2 = (f32[1,32,8,128]{3,2,1,0:T(8,128)S(1)}, f32[1,32,8,128]{3,2,1,0:T(8,128)S(1)}) custom-call(f32[256,512]{1,0:T(8,128)S(1)} %get-tuple-element.28.xf, f32[256,512]{1,0:T(8,128)S(1)} %get-tuple-element.29.gf, f32[16,512]{1,0:T(8,128)S(1)} %get-tuple-element.24.residue_ref, f32[16,512]{1,0:T(8,128)S(1)} %get-tuple-element.25.decay_ref.refs_5_, ...), custom_call_target="tpu_custom_call" | custom-call | flops 209715200 | bytes 524288 | tf_op jit(solution)/shard_map/local_convolutions/pallas_call | solution.py:397
  4.8 0.1 collective-permute-done.other
  5.0 3.9 %collective-permute-start.3 = (f32[24,512]{1,0:T(8,128)S(1)}, f32[24,512]{1,0:T(8,128)S(1)}, u32[]{:S(2)}, u32[]{:S(2)}) collective-permute-start(f32[24,512]{1,0:T(8,128)S(1)} %get-tuple-element.31._.refs_0_), channel_id=1, source_target_pairs={{0,24},{1,25},{2,26},{3,27},{4,28},{5,29},{6,30},{7,31},{8,16},{9,... | collective-permute-start | bytes 147464 | tf_op jit(solution)/shard_map/ppermute | solution.py:392
  8.8 0.0 collective-permute-start.2
  8.9 0.3 %collective-permute-start.1 = (f32[24,512]{1,0:T(8,128)S(1)}, f32[24,512]{1,0:T(8,128)S(1)}, u32[]{:S(2)}, u32[]{:S(2)}) collective-permute-start(f32[24,512]{1,0:T(8,128)S(1)} %get-tuple-element.31._.refs_0_), channel_id=1, source_target_pairs={{0,20},{1,21},{2,22},{3,23},{4,16},{5,17},{6,18},{7,19},{8,28},{9,... | collective-permute-start | bytes 147464 | tf_op jit(solution)/shard_map/ppermute | solution.py:392
  9.2 2.3 %local_convolutions.3 = (f32[3,32,8,128]{3,2,1,0:T(8,128)S(1)}, f32[3,32,8,128]{3,2,1,0:T(8,128)S(1)}) custom-call(f32[256,512]{1,0:T(8,128)S(1)} %get-tuple-element.28.xf, f32[256,512]{1,0:T(8,128)S(1)} %get-tuple-element.29.gf, f32[16,512]{1,0:T(8,128)S(1)} %get-tuple-element.24.residue_ref, f32[16,512]{1,0:T(8,128)S(1)} %get-tuple-element.25.decay_ref.refs_5_, ...), custom_call_target="tpu_custom_call" | custom-call | flops 629145600 | bytes 1572864 | tf_op jit(solution)/shard_map/local_convolutions/pallas_call | solution.py:397
  11.6 0.0 collective-permute-done.3.refs_3_
  11.6 1.3 %collective-permute-done.2.refs_2_ = f32[24,512]{1,0:T(8,128)S(1)} collective-permute-done((f32[24,512]{1,0:T(8,128)S(1)}, f32[24,512]{1,0:T(8,128)S(1)}, u32[]{:S(2)}, u32[]{:S(2)}) %collective-permute-start.2) | collective-permute-done | bytes 49184 | tf_op jit(solution)/shard_map/ppermute | solution.py:392
  12.8 0.0 collective-permute-done.1.refs_1_
  12.8 0.1 join_chips.1
  12.9 0.2 %collective-permute-start.4 = (f32[16,512]{1,0:T(8,128)S(1)}, f32[16,512]{1,0:T(8,128)S(1)}, u32[]{:S(2)}, u32[]{:S(2)}) collective-permute-start(f32[16,512]{1,0:T(8,128)S(1)} %get-tuple-element.35), channel_id=1, source_target_pairs={{0,4},{1,5},{2,6},{3,7},{4,0},{5,1},{6,2},{7,3},{8,12},{9,13},{10,... | collective-permute-start | bytes 98312 | tf_op jit(solution)/shard_map/ppermute | solution.py:392
  13.1 2.5 %collective-permute-start.5 = (f32[8,512]{1,0:T(8,128)S(1)}, f32[8,512]{1,0:T(8,128)S(1)}, u32[]{:S(2)}, u32[]{:S(2)}) collective-permute-start(f32[8,512]{1,0:T(8,128)S(1)} %get-tuple-element.38.refs_4_.own), channel_id=1, source_target_pairs={{0,6},{1,7},{2,4},{3,5},{4,2},{5,3},{6,0},{7,1},{8,14},{9,15},{10,... | collective-permute-start | bytes 49160 | tf_op jit(solution)/shard_map/ppermute | solution.py:392
  15.7 0.0 collective-permute-done.4.other
  15.7 1.2 %add_arrivals.2 = (bf16[256,512]{1,0:T(8,128)(2,1)}, bf16[256,512]{1,0:T(8,128)(2,1)}, f32[8,128]{1,0:T(8,128)S(1)}) custom-call(f32[16,512]{1,0:T(8,128)S(1)} %get-tuple-element.24.residue_ref, f32[16,512]{1,0:T(8,128)S(1)} %get-tuple-element.25.decay_ref.refs_5_, f32[16,512]{1,0:T(8,128)S(1)} %get-tuple-element.34.own, ...), custom_call_target="tpu_custom_call" | custom-call | flops 629145600 | bytes 786432 | tf_op jit(solution)/shard_map/add_arrivals/pallas_call | solution.py:459
  16.9 0.3 %collective-permute-done.5.other = f32[8,512]{1,0:T(8,128)S(1)} collective-permute-done((f32[8,512]{1,0:T(8,128)S(1)}, f32[8,512]{1,0:T(8,128)S(1)}, u32[]{:S(2)}, u32[]{:S(2)}) %collective-permute-start.5) | collective-permute-done | bytes 16416 | tf_op jit(solution)/shard_map/ppermute | solution.py:392
  17.2 1.5 %collective-permute-start.6 = (f32[8,512]{1,0:T(8,128)S(1)}, f32[8,512]{1,0:T(8,128)S(1)}, u32[]{:S(2)}, u32[]{:S(2)}) collective-permute-start(f32[8,512]{1,0:T(8,128)S(1)} %sum_groups.2.refs_4_.own), channel_id=1, source_target_pairs={{0,5},{1,4},{2,7},{3,6},{4,1},{5,0},{6,3},{7,2},{8,13},{9,12},{10,... | collective-permute-start | bytes 49160 | tf_op jit(solution)/shard_map/ppermute | solution.py:392
  18.7 2.1 %add_arrivals.3 = (bf16[256,512]{1,0:T(8,128)(2,1)}, bf16[256,512]{1,0:T(8,128)(2,1)}, f32[8,128]{1,0:T(8,128)S(1)}) custom-call(f32[16,512]{1,0:T(8,128)S(1)} %get-tuple-element.24.residue_ref, f32[16,512]{1,0:T(8,128)S(1)} %get-tuple-element.25.decay_ref.refs_5_, ...), custom_call_target="tpu_custom_call", output_to_operand_aliasing={{0}: (9, {}), {1}: (10, {})} | custom-call | flops 629145600 | bytes 786432 | tf_op jit(solution)/shard_map/add_arrivals/pallas_call | solution.py:459
  20.8 0.0 collective-permute-done.6.other
  20.8 0.2 %collective-permute-start.7 = (f32[8,512]{1,0:T(8,128)S(1)}, f32[8,512]{1,0:T(8,128)S(1)}, u32[]{:S(2)}, u32[]{:S(2)}) collective-permute-start(f32[8,512]{1,0:T(8,128)S(1)} %sum_groups.3.own), channel_id=1, source_target_pairs={{0,4},{1,5},{2,6},{3,7},{4,0},{5,1},{6,2},{7,3},{8,12},{9,13},{10,... | collective-permute-start | bytes 49160 | tf_op jit(solution)/shard_map/ppermute | solution.py:392
  21.1 1.0 %collective-permute-done.7.other = f32[8,512]{1,0:T(8,128)S(1)} collective-permute-done((f32[8,512]{1,0:T(8,128)S(1)}, f32[8,512]{1,0:T(8,128)S(1)}, u32[]{:S(2)}, u32[]{:S(2)}) %collective-permute-start.7) | collective-permute-done | bytes 16416 | tf_op jit(solution)/shard_map/ppermute | solution.py:392
  22.1 0.6 %assemble_gradient.1 = f32[16,512]{1,0:T(8,128)} custom-call(f32[8,512]{1,0:T(8,128)S(1)} %sum_groups.3.own, f32[8,512]{1,0:T(8,128)S(1)} %collective-permute-done.7.other), custom_call_target="tpu_custom_call" | custom-call | flops 131072 | bytes 262144 | tf_op jit(solution)/shard_map/assemble_gradient/pallas_call | solution.py:495
  (3 shorter events, 0.0 us)
Async XLA Ops:
  3.6 1.4 %collective-permute-start = (f32[24,512]{1,0:T(8,128)S(1)}, f32[24,512]{1,0:T(8,128)S(1)}, u32[]{:S(2)}, u32[]{:S(2)}) collective-permute-start(f32[24,512]{1,0:T(8,128)S(1)} %get-tuple-element.27), channel_id=1, source_target_pairs={{0,4},{1,5},{2,6},{3,7},{4,0},{5,1},{6,2},{7,3},{8,12},{9,13},{10,... | collective-permute-start | bytes 147464 | tf_op jit(solution)/shard_map/ppermute | solution.py:392
  5.0 6.6 %collective-permute-start.3 = (f32[24,512]{1,0:T(8,128)S(1)}, f32[24,512]{1,0:T(8,128)S(1)}, u32[]{:S(2)}, u32[]{:S(2)}) collective-permute-start(f32[24,512]{1,0:T(8,128)S(1)} %get-tuple-element.31._.refs_0_), channel_id=1, source_target_pairs={{0,24},{1,25},{2,26},{3,27},{4,28},{5,29},{6,30},{7,31},{8,16},{9,... | collective-permute-start | bytes 147464 | tf_op jit(solution)/shard_map/ppermute | solution.py:392
  8.8 4.0 %collective-permute-start.2 = (f32[24,512]{1,0:T(8,128)S(1)}, f32[24,512]{1,0:T(8,128)S(1)}, u32[]{:S(2)}, u32[]{:S(2)}) collective-permute-start(f32[24,512]{1,0:T(8,128)S(1)} %get-tuple-element.31._.refs_0_), channel_id=1, source_target_pairs={{0,12},{1,13},{2,14},{3,15},{4,8},{5,9},{6,10},{7,11},{8,4},{9,5},... | collective-permute-start | bytes 147464 | tf_op jit(solution)/shard_map/ppermute | solution.py:392
  8.9 4.0 %collective-permute-start.1 = (f32[24,512]{1,0:T(8,128)S(1)}, f32[24,512]{1,0:T(8,128)S(1)}, u32[]{:S(2)}, u32[]{:S(2)}) collective-permute-start(f32[24,512]{1,0:T(8,128)S(1)} %get-tuple-element.31._.refs_0_), channel_id=1, source_target_pairs={{0,20},{1,21},{2,22},{3,23},{4,16},{5,17},{6,18},{7,19},{8,28},{9,... | collective-permute-start | bytes 147464 | tf_op jit(solution)/shard_map/ppermute | solution.py:392
  12.9 2.8 %collective-permute-start.4 = (f32[16,512]{1,0:T(8,128)S(1)}, f32[16,512]{1,0:T(8,128)S(1)}, u32[]{:S(2)}, u32[]{:S(2)}) collective-permute-start(f32[16,512]{1,0:T(8,128)S(1)} %get-tuple-element.35), channel_id=1, source_target_pairs={{0,4},{1,5},{2,6},{3,7},{4,0},{5,1},{6,2},{7,3},{8,12},{9,13},{10,... | collective-permute-start | bytes 98312 | tf_op jit(solution)/shard_map/ppermute | solution.py:392
  13.1 4.1 %collective-permute-start.5 = (f32[8,512]{1,0:T(8,128)S(1)}, f32[8,512]{1,0:T(8,128)S(1)}, u32[]{:S(2)}, u32[]{:S(2)}) collective-permute-start(f32[8,512]{1,0:T(8,128)S(1)} %get-tuple-element.38.refs_4_.own), channel_id=1, source_target_pairs={{0,6},{1,7},{2,4},{3,5},{4,2},{5,3},{6,0},{7,1},{8,14},{9,15},{10,... | collective-permute-start | bytes 49160 | tf_op jit(solution)/shard_map/ppermute | solution.py:392
  17.2 3.6 %collective-permute-start.6 = (f32[8,512]{1,0:T(8,128)S(1)}, f32[8,512]{1,0:T(8,128)S(1)}, u32[]{:S(2)}, u32[]{:S(2)}) collective-permute-start(f32[8,512]{1,0:T(8,128)S(1)} %sum_groups.2.refs_4_.own), channel_id=1, source_target_pairs={{0,5},{1,4},{2,7},{3,6},{4,1},{5,0},{6,3},{7,2},{8,13},{9,12},{10,... | collective-permute-start | bytes 49160 | tf_op jit(solution)/shard_map/ppermute | solution.py:392
  20.8 1.2 %collective-permute-start.7 = (f32[8,512]{1,0:T(8,128)S(1)}, f32[8,512]{1,0:T(8,128)S(1)}, u32[]{:S(2)}, u32[]{:S(2)}) collective-permute-start(f32[8,512]{1,0:T(8,128)S(1)} %sum_groups.3.own), channel_id=1, source_target_pairs={{0,4},{1,5},{2,6},{3,7},{4,0},{5,1},{6,2},{7,3},{8,12},{9,13},{10,... | collective-permute-start | bytes 49160 | tf_op jit(solution)/shard_map/ppermute | solution.py:392

commit v17 on v16

--- a/solution.py
+++ b/solution.py
@@ -457,7 +457,7 @@
 
     def finish_part(part, after, written):
         return pl.pallas_call(
-            functools.partial(finish_kernel, ranges[part], ranges),
+            functools.partial(finish_kernel, (part * tiles // 2, (part + 1) * tiles // 2), ranges),
             out_shape=[jax.ShapeDtypeStruct((tokens, channels), jnp.bfloat16)] * 2 + [shaped(SUB, LANES)],
             in_specs=[WHOLE] * (4 + len(near)) + [UNREAD] + [HBM] * len(written),
             out_specs=[HBM] * 2 + [WHOLE],

time: 22.9 us -> 22.5 us (0.983)
  waiting for transfers between devices: 2.7 us -> 2.39 us
    ppermute x8, waiting for transfers between devices: 2.7 us -> 2.39 us  [swap(): lax.ppermute(x, ('ctx', 'ch'), [(i, i ^ mask) for i in range(n * groups)])]
  transfers between devices with their start and end apart: 8 -> 8, of which waited for: 4 -> 4; matrix products, arithmetic and copies ran while one was open for 0% -> 0% of each run, Pallas kernels for 28% -> 29%
where the time goes in v17:
time: 22.5 us; the launch traced here: 22.4 us
  Pallas kernels  10.1 us (45%)
  starting transfers between devices  9.22 us (41%)
  waiting for transfers between devices  2.39 us (11%)
  between operations  0.7 us (3%)
    ppermute x8, starting transfers between devices, swap(): lax.ppermute(x, ('ctx', 'ch'), [(i, i ^ mask) for i in range(n * groups)])  9.22 us
    pallas_call x2, Pallas kernels, finish_part(): pl.pallas_call(functools.partial(finish_kernel, (part * tiles // 2, (part...  3.34 us
    pallas_call x2, Pallas kernels, near_part(): pl.pallas_call(functools.partial(local_kernel, ranges[part]), out_shape=[...  3.13 us
    pallas_call x1, Pallas kernels, body(): pl.pallas_call(gather_kernel, out_shape=[values, values] + [shaped(modes,...  2.91 us
    ppermute x8, waiting for transfers between devices, swap(): lax.ppermute(x, ('ctx', 'ch'), [(i, i ^ mask) for i in range(n * groups)])  2.39 us
    pallas_call x1, Pallas kernels, body(): pl.pallas_call(functools.partial(assemble_kernel, 1.0 / (tokens * n)), ou...  0.62 us
  transfers between devices with their start and end apart: 8, of which 4 were waited for; matrix products, arithmetic and copies ran while one was open for 0% of the time, Pallas kernels for 29%

profile of v17, /device:TPU:0, one launch (start us, length us, event | category | flops | bytes accessed | tf_op | source)
XLA Modules:
  0.0 22.4 jit_solution(3017102787661391013)
XLA Ops:
  0.6 2.9 %block_states.1 = (f32[256,512]{1,0:T(8,128)S(1)}, f32[256,512]{1,0:T(8,128)S(1)}, f32[16,512]{1,0:T(8,128)S(1)}, f32[16,512]{1,0:T(8,128)S(1)}, f32[48,512]{1,0:T(8,128)S(1)}, /*index=5*/f32[24,512]{1,0:T(8,128)S(1)}) custom-call(bf16[256,512]{1,0:T(8,128)(2,1)} %refs_0_.1, bf16[256,512]{1,0:T(8,128)(2,1)} %refs_1_.1, f32[16,512]{1,0:T(8,128)} %refs_2_.1, ...), custom_call_target="tpu_custom_call" | custom-call | flops 10485760 | bytes 786432 | tf_op jit(solution)/shard_map/block_states/pallas_call | solution.py:410
  3.6 0.5 %collective-permute-start = (f32[24,512]{1,0:T(8,128)S(1)}, f32[24,512]{1,0:T(8,128)S(1)}, u32[]{:S(2)}, u32[]{:S(2)}) collective-permute-start(f32[24,512]{1,0:T(8,128)S(1)} %get-tuple-element.27), channel_id=1, source_target_pairs={{0,4},{1,5},{2,6},{3,7},{4,0},{5,1},{6,2},{7,3},{8,12},{9,13},{10,... | collective-permute-start | bytes 147464 | tf_op jit(solution)/shard_map/ppermute | solution.py:392
  4.1 0.8 %local_convolutions.2 = (f32[1,32,8,128]{3,2,1,0:T(8,128)S(1)}, f32[1,32,8,128]{3,2,1,0:T(8,128)S(1)}) custom-call(f32[256,512]{1,0:T(8,128)S(1)} %get-tuple-element.28.xf, f32[256,512]{1,0:T(8,128)S(1)} %get-tuple-element.29.gf, f32[16,512]{1,0:T(8,128)S(1)} %get-tuple-element.24.residue_ref, f32[16,512]{1,0:T(8,128)S(1)} %get-tuple-element.25.decay_ref.refs_5_, ...), custom_call_target="tpu_custom_call" | custom-call | flops 209715200 | bytes 524288 | tf_op jit(solution)/shard_map/local_convolutions/pallas_call | solution.py:397
  4.8 0.1 collective-permute-done.other
  5.0 3.9 %collective-permute-start.3 = (f32[24,512]{1,0:T(8,128)S(1)}, f32[24,512]{1,0:T(8,128)S(1)}, u32[]{:S(2)}, u32[]{:S(2)}) collective-permute-start(f32[24,512]{1,0:T(8,128)S(1)} %get-tuple-element.31._.refs_0_), channel_id=1, source_target_pairs={{0,24},{1,25},{2,26},{3,27},{4,28},{5,29},{6,30},{7,31},{8,16},{9,... | collective-permute-start | bytes 147464 | tf_op jit(solution)/shard_map/ppermute | solution.py:392
  8.8 0.0 collective-permute-start.2
  8.9 0.3 %collective-permute-start.1 = (f32[24,512]{1,0:T(8,128)S(1)}, f32[24,512]{1,0:T(8,128)S(1)}, u32[]{:S(2)}, u32[]{:S(2)}) collective-permute-start(f32[24,512]{1,0:T(8,128)S(1)} %get-tuple-element.31._.refs_0_), channel_id=1, source_target_pairs={{0,20},{1,21},{2,22},{3,23},{4,16},{5,17},{6,18},{7,19},{8,28},{9,... | collective-permute-start | bytes 147464 | tf_op jit(solution)/shard_map/ppermute | solution.py:392
  9.2 2.3 %local_convolutions.3 = (f32[3,32,8,128]{3,2,1,0:T(8,128)S(1)}, f32[3,32,8,128]{3,2,1,0:T(8,128)S(1)}) custom-call(f32[256,512]{1,0:T(8,128)S(1)} %get-tuple-element.28.xf, f32[256,512]{1,0:T(8,128)S(1)} %get-tuple-element.29.gf, f32[16,512]{1,0:T(8,128)S(1)} %get-tuple-element.24.residue_ref, f32[16,512]{1,0:T(8,128)S(1)} %get-tuple-element.25.decay_ref.refs_5_, ...), custom_call_target="tpu_custom_call" | custom-call | flops 629145600 | bytes 1572864 | tf_op jit(solution)/shard_map/local_convolutions/pallas_call | solution.py:397
  11.6 0.0 collective-permute-done.3.refs_3_
  11.6 1.3 %collective-permute-done.2.refs_2_ = f32[24,512]{1,0:T(8,128)S(1)} collective-permute-done((f32[24,512]{1,0:T(8,128)S(1)}, f32[24,512]{1,0:T(8,128)S(1)}, u32[]{:S(2)}, u32[]{:S(2)}) %collective-permute-start.2) | collective-permute-done | bytes 49184 | tf_op jit(solution)/shard_map/ppermute | solution.py:392
  12.8 0.0 collective-permute-done.1.refs_1_
  12.8 0.1 join_chips.1
  12.9 0.2 %collective-permute-start.4 = (f32[16,512]{1,0:T(8,128)S(1)}, f32[16,512]{1,0:T(8,128)S(1)}, u32[]{:S(2)}, u32[]{:S(2)}) collective-permute-start(f32[16,512]{1,0:T(8,128)S(1)} %get-tuple-element.35), channel_id=1, source_target_pairs={{0,4},{1,5},{2,6},{3,7},{4,0},{5,1},{6,2},{7,3},{8,12},{9,13},{10,... | collective-permute-start | bytes 98312 | tf_op jit(solution)/shard_map/ppermute | solution.py:392
  13.1 2.5 %collective-permute-start.5 = (f32[8,512]{1,0:T(8,128)S(1)}, f32[8,512]{1,0:T(8,128)S(1)}, u32[]{:S(2)}, u32[]{:S(2)}) collective-permute-start(f32[8,512]{1,0:T(8,128)S(1)} %get-tuple-element.38.refs_4_.own), channel_id=1, source_target_pairs={{0,6},{1,7},{2,4},{3,5},{4,2},{5,3},{6,0},{7,1},{8,14},{9,15},{10,... | collective-permute-start | bytes 49160 | tf_op jit(solution)/shard_map/ppermute | solution.py:392
  15.7 0.0 collective-permute-done.4.other
  15.7 1.7 %add_arrivals.2 = (bf16[256,512]{1,0:T(8,128)(2,1)}, bf16[256,512]{1,0:T(8,128)(2,1)}, f32[8,128]{1,0:T(8,128)S(1)}) custom-call(f32[16,512]{1,0:T(8,128)S(1)} %get-tuple-element.24.residue_ref, f32[16,512]{1,0:T(8,128)S(1)} %get-tuple-element.25.decay_ref.refs_5_, f32[16,512]{1,0:T(8,128)S(1)} %get-tuple-element.34.own, ...), custom_call_target="tpu_custom_call" | custom-call | flops 629145600 | bytes 786432 | tf_op jit(solution)/shard_map/add_arrivals/pallas_call | solution.py:459
  17.3 0.0 collective-permute-done.5.other
  17.4 1.4 %collective-permute-start.6 = (f32[8,512]{1,0:T(8,128)S(1)}, f32[8,512]{1,0:T(8,128)S(1)}, u32[]{:S(2)}, u32[]{:S(2)}) collective-permute-start(f32[8,512]{1,0:T(8,128)S(1)} %sum_groups.2.refs_4_.own), channel_id=1, source_target_pairs={{0,5},{1,4},{2,7},{3,6},{4,1},{5,0},{6,3},{7,2},{8,13},{9,12},{10,... | collective-permute-start | bytes 49160 | tf_op jit(solution)/shard_map/ppermute | solution.py:392
  18.8 1.7 %add_arrivals.3 = (bf16[256,512]{1,0:T(8,128)(2,1)}, bf16[256,512]{1,0:T(8,128)(2,1)}, f32[8,128]{1,0:T(8,128)S(1)}) custom-call(f32[16,512]{1,0:T(8,128)S(1)} %get-tuple-element.24.residue_ref, f32[16,512]{1,0:T(8,128)S(1)} %get-tuple-element.25.decay_ref.refs_5_, ...), custom_call_target="tpu_custom_call", output_to_operand_aliasing={{0}: (9, {}), {1}: (10, {})} | custom-call | flops 629145600 | bytes 786432 | tf_op jit(solution)/shard_map/add_arrivals/pallas_call | solution.py:459
  20.5 0.1 collective-permute-done.6.other
  20.6 0.3 %collective-permute-start.7 = (f32[8,512]{1,0:T(8,128)S(1)}, f32[8,512]{1,0:T(8,128)S(1)}, u32[]{:S(2)}, u32[]{:S(2)}) collective-permute-start(f32[8,512]{1,0:T(8,128)S(1)} %sum_groups.3.own), channel_id=1, source_target_pairs={{0,4},{1,5},{2,6},{3,7},{4,0},{5,1},{6,2},{7,3},{8,12},{9,13},{10,... | collective-permute-start | bytes 49160 | tf_op jit(solution)/shard_map/ppermute | solution.py:392
  20.9 0.9 %collective-permute-done.7.other = f32[8,512]{1,0:T(8,128)S(1)} collective-permute-done((f32[8,512]{1,0:T(8,128)S(1)}, f32[8,512]{1,0:T(8,128)S(1)}, u32[]{:S(2)}, u32[]{:S(2)}) %collective-permute-start.7) | collective-permute-done | bytes 16416 | tf_op jit(solution)/shard_map/ppermute | solution.py:392
  21.8 0.6 %assemble_gradient.1 = f32[16,512]{1,0:T(8,128)} custom-call(f32[8,512]{1,0:T(8,128)S(1)} %sum_groups.3.own, f32[8,512]{1,0:T(8,128)S(1)} %collective-permute-done.7.other), custom_call_target="tpu_custom_call" | custom-call | flops 131072 | bytes 262144 | tf_op jit(solution)/shard_map/assemble_gradient/pallas_call | solution.py:495
  (3 shorter events, 0.0 us)
Async XLA Ops:
  3.6 1.4 %collective-permute-start = (f32[24,512]{1,0:T(8,128)S(1)}, f32[24,512]{1,0:T(8,128)S(1)}, u32[]{:S(2)}, u32[]{:S(2)}) collective-permute-start(f32[24,512]{1,0:T(8,128)S(1)} %get-tuple-element.27), channel_id=1, source_target_pairs={{0,4},{1,5},{2,6},{3,7},{4,0},{5,1},{6,2},{7,3},{8,12},{9,13},{10,... | collective-permute-start | bytes 147464 | tf_op jit(solution)/shard_map/ppermute | solution.py:392
  5.0 6.6 %collective-permute-start.3 = (f32[24,512]{1,0:T(8,128)S(1)}, f32[24,512]{1,0:T(8,128)S(1)}, u32[]{:S(2)}, u32[]{:S(2)}) collective-permute-start(f32[24,512]{1,0:T(8,128)S(1)} %get-tuple-element.31._.refs_0_), channel_id=1, source_target_pairs={{0,24},{1,25},{2,26},{3,27},{4,28},{5,29},{6,30},{7,31},{8,16},{9,... | collective-permute-start | bytes 147464 | tf_op jit(solution)/shard_map/ppermute | solution.py:392
  8.8 4.0 %collective-permute-start.2 = (f32[24,512]{1,0:T(8,128)S(1)}, f32[24,512]{1,0:T(8,128)S(1)}, u32[]{:S(2)}, u32[]{:S(2)}) collective-permute-start(f32[24,512]{1,0:T(8,128)S(1)} %get-tuple-element.31._.refs_0_), channel_id=1, source_target_pairs={{0,12},{1,13},{2,14},{3,15},{4,8},{5,9},{6,10},{7,11},{8,4},{9,5},... | collective-permute-start | bytes 147464 | tf_op jit(solution)/shard_map/ppermute | solution.py:392
  8.9 4.0 %collective-permute-start.1 = (f32[24,512]{1,0:T(8,128)S(1)}, f32[24,512]{1,0:T(8,128)S(1)}, u32[]{:S(2)}, u32[]{:S(2)}) collective-permute-start(f32[24,512]{1,0:T(8,128)S(1)} %get-tuple-element.31._.refs_0_), channel_id=1, source_target_pairs={{0,20},{1,21},{2,22},{3,23},{4,16},{5,17},{6,18},{7,19},{8,28},{9,... | collective-permute-start | bytes 147464 | tf_op jit(solution)/shard_map/ppermute | solution.py:392
  12.9 2.8 %collective-permute-start.4 = (f32[16,512]{1,0:T(8,128)S(1)}, f32[16,512]{1,0:T(8,128)S(1)}, u32[]{:S(2)}, u32[]{:S(2)}) collective-permute-start(f32[16,512]{1,0:T(8,128)S(1)} %get-tuple-element.35), channel_id=1, source_target_pairs={{0,4},{1,5},{2,6},{3,7},{4,0},{5,1},{6,2},{7,3},{8,12},{9,13},{10,... | collective-permute-start | bytes 98312 | tf_op jit(solution)/shard_map/ppermute | solution.py:392
  13.1 4.2 %collective-permute-start.5 = (f32[8,512]{1,0:T(8,128)S(1)}, f32[8,512]{1,0:T(8,128)S(1)}, u32[]{:S(2)}, u32[]{:S(2)}) collective-permute-start(f32[8,512]{1,0:T(8,128)S(1)} %get-tuple-element.38.refs_4_.own), channel_id=1, source_target_pairs={{0,6},{1,7},{2,4},{3,5},{4,2},{5,3},{6,0},{7,1},{8,14},{9,15},{10,... | collective-permute-start | bytes 49160 | tf_op jit(solution)/shard_map/ppermute | solution.py:392
  17.4 3.2 %collective-permute-start.6 = (f32[8,512]{1,0:T(8,128)S(1)}, f32[8,512]{1,0:T(8,128)S(1)}, u32[]{:S(2)}, u32[]{:S(2)}) collective-permute-start(f32[8,512]{1,0:T(8,128)S(1)} %sum_groups.2.refs_4_.own), channel_id=1, source_target_pairs={{0,5},{1,4},{2,7},{3,6},{4,1},{5,0},{6,3},{7,2},{8,13},{9,12},{10,... | collective-permute-start | bytes 49160 | tf_op jit(solution)/shard_map/ppermute | solution.py:392
  20.6 1.2 %collective-permute-start.7 = (f32[8,512]{1,0:T(8,128)S(1)}, f32[8,512]{1,0:T(8,128)S(1)}, u32[]{:S(2)}, u32[]{:S(2)}) collective-permute-start(f32[8,512]{1,0:T(8,128)S(1)} %sum_groups.3.own), channel_id=1, source_target_pairs={{0,4},{1,5},{2,6},{3,7},{4,0},{5,1},{6,2},{7,3},{8,12},{9,13},{10,... | collective-permute-start | bytes 49160 | tf_op jit(solution)/shard_map/ppermute | solution.py:392
